TPU v7x, 32 devices: a whole 2x2x4 slice. The times are simulated.
32 devices in a mesh: doc: 4 (over x, core), topic: 4 (over z), vocab: 2 (over y).
Axes of the slice: x: 2, y: 2, z: 4, core: 2. Of those that a mesh axis runs over, the one named last changes fastest.
Arguments:
- doc_topics: bfloat16 [2048, 16384], P('doc', 'topic'), may hold values from 0 to 1, as said below
- word_logits: bfloat16 [512, 16384], P('vocab', 'topic'), may hold values from -6 to 11
- log_norm: float32 [16384], P('topic'), may hold values from 12 to 16
- tile_doc: int32 [128], P(('doc', 'vocab')), may hold values from 0 to 3, as said below
- tile_word: int32 [128], P(('doc', 'vocab')), may hold values from 0 to 3
- word_counts: int32 [128, 64, 128], P(('doc', 'vocab')), may hold values from 0 to 3, as said below
Outputs:
- doc_topic_grad: float32 [2048, 16384], P('doc', ('topic', 'vocab'))
- word_logit_grad: bfloat16 [512, 16384], P('vocab', 'topic')
Inputs may be any that keep to these rules, and one draw needn't show every extreme that they name: `doc_topics`: each document's row is a softmax over the 16384 topics. Within the 16 slots of one doc and vocab index pair no (tile_doc, tile_word) pair repeats. `word_counts`: A slot whose counts are all zero is empty; occupied slots come first in each pair's list, and in every draw some pair has all 16 slots occupied.
All inputs are finite; a program needn't handle non-finite values.
Results may differ from a plain program's by a relative error of at most 0.018.
Values may be sent and summed in bfloat16 or wider, within the bound.
No kernel may reach another device: no remote copies, remote signals or barrier semaphores. Data moves between devices by JAX's collectives and lax.ppermute only.
A program may use at most 128 MiB of HBM per device.

v0:
```python
import jax
import jax.numpy as jnp
from jax import lax
from jax.sharding import PartitionSpec as P

tiles_per_step = 8


def on_device(doc_topics, word_logits, log_norm, tile_doc, tile_word, word_counts):
    tile_total, word_span, doc_span = word_counts.shape
    topic_width = doc_topics.shape[1]
    word_prob = jnp.exp(word_logits.astype(jnp.float32) - log_norm[None, :]).astype(jnp.bfloat16)
    topic_blocks = doc_topics.reshape(-1, doc_span, topic_width)
    prob_blocks = word_prob.reshape(-1, word_span, topic_width)
    doc_rows = topic_blocks[tile_doc]
    word_rows = prob_blocks[tile_word]
    word_part = word_rows
    doc_part = doc_rows
    rate_full = lax.psum(
        jnp.einsum("gwk,gdk->gwd", word_part, doc_part, preferred_element_type=jnp.float32).astype(
            jnp.bfloat16
        ),
        "topic",
    ).astype(jnp.float32)
    ratios = (word_counts.astype(jnp.float32) / (word_span * rate_full)).astype(jnp.bfloat16)

    def accumulate(state_pair, group_index):
        theta_acc, beta_acc = state_pair
        first_row = group_index * tiles_per_step
        ratio_part = lax.dynamic_slice_in_dim(ratios, first_row, tiles_per_step, 0)
        word_part = lax.dynamic_slice_in_dim(word_rows, first_row, tiles_per_step, 0)
        doc_part = lax.dynamic_slice_in_dim(doc_rows, first_row, tiles_per_step, 0)
        doc_index = lax.dynamic_slice_in_dim(tile_doc, first_row, tiles_per_step, 0)
        word_index = lax.dynamic_slice_in_dim(tile_word, first_row, tiles_per_step, 0)
        toward_theta = jnp.einsum(
            "gwd,gwk->gdk", ratio_part, word_part, preferred_element_type=jnp.float32
        )
        toward_beta = jnp.einsum(
            "gwd,gdk->gwk", ratio_part, doc_part, preferred_element_type=jnp.float32
        )
        return (
            (theta_acc.at[doc_index].add(toward_theta), beta_acc.at[word_index].add(toward_beta)),
            None,
        )

    initial = (
        jnp.zeros(topic_blocks.shape, jnp.float32),
        jnp.zeros(prob_blocks.shape, jnp.float32),
    )
    steps_all = jnp.arange(tile_total // tiles_per_step, dtype=jnp.int32)
    (theta_acc, beta_acc), _ = lax.scan(accumulate, initial, steps_all)
    theta_term = -theta_acc.reshape(doc_topics.shape)
    doc_topic_grad = lax.psum_scatter(
        theta_term.astype(jnp.bfloat16), "vocab", scatter_dimension=1, tiled=True
    ).astype(jnp.float32)
    beta_term = -word_prob.astype(jnp.float32) * beta_acc.reshape(word_prob.shape)
    word_logit_grad = lax.psum(beta_term.astype(jnp.bfloat16), "doc")
    return (doc_topic_grad, word_logit_grad)


def solution(mesh):
    placed = (
        P("doc", "topic"),
        P("vocab", "topic"),
        P("topic"),
        P(("doc", "vocab")),
        P(("doc", "vocab")),
        P(("doc", "vocab"), None, None),
    )
    return jax.shard_map(
        on_device,
        mesh=mesh,
        in_specs=placed,
        out_specs=(P("doc", ("topic", "vocab")), P("vocab", "topic")),
        check_vma=False,
    )
```

profile of v0, /device:TPU:0, one launch (start us, length us, event | category | flops | bytes accessed | tf_op | source)
XLA Modules:
  0.0 341.3 jit_solution(14141265949409256518)
XLA Ops:
  7.2 0.0 all-reduce.3.cloned.1.call-start
  7.2 0.7 compare_select_fusion.2
  7.9 0.7 compare_select_fusion.3
  8.5 2.2 exponential_convert_fusion
  10.8 4.7 %gather_fusion = bf16[16,64,4096]{2,1,0:T(8,128)(2,1)} fusion(bf16[4,64,4096]{2,1,0:T(8,128)(2,1)S(1)} %bitcast.13, s32[1024]{0:T(1024)S(1)} %pad_clamp_fusion.1), kind=kCustom, calls=%fused_computation | custom fusion | bytes 16777280 | tf_op jit(solution)/shard_map/gather | solution.py:16
  15.4 9.3 %gather_fusion.1 = bf16[16,128,4096]{2,1,0:T(8,128)(2,1)} fusion(bf16[4,128,4096]{2,1,0:T(8,128)(2,1)} %bitcast.12, s32[1024]{0:T(1024)S(1)} %pad_clamp_fusion), kind=kCustom, calls=%fused_computation.1 | custom fusion | bytes 33554496 | tf_op jit(solution)/shard_map/gather | solution.py:15
  24.7 12.0 %convolution_convert_fusion = bf16[16,64,128]{2,1,0:T(8,128)(2,1)} fusion(bf16[16,64,4096]{2,1,0:T(8,128)(2,1)} %gather_fusion, bf16[16,128,4096]{2,1,0:T(8,128)(2,1)} %gather_fusion.1), kind=kOutput, calls=%fused_computation.18 | convolution fusion | flops 1073872896 | bytes 25427968 | tf_op jit(solution)/shard_map/gwk,gdk->gwd/dot_general | solution.py:20
  36.8 0.0 reduce-scatter.2.cloned.1.call-start
  36.8 38.4 %all-reduce.3.cloned.1.call-done = bf16[16,64,128]{2,1,0:T(8,128)(2,1)} async-done(((bf16[16,64,128]{2,1,0:T(8,128)(2,1)}), bf16[16,64,128]{2,1,0:T(8,128)(2,1)}) %all-reduce.3.cloned.1.call-update) | async-done | bytes 262160 | tf_op jit(solution)/shard_map/psum | solution.py:19
  75.2 1.1 divide_convert_fusion
  76.3 2.5 broadcast_in_dim.20
  78.8 4.2 %broadcast_in_dim.19 = f32[4,128,4096]{2,1,0:T(8,128)} broadcast(f32[]{:T(128)} %constant.5.clone.1), dimensions={} | broadcast | bytes 8388612 | tf_op jit(solution)/shard_map/broadcast_in_dim | solution.py:47
  83.0 133.6 %while.12 = (s32[]{:T(128)}, f32[4,128,4096]{2,1,0:T(8,128)}, f32[4,64,4096]{2,1,0:T(8,128)}, s32[2]{0:T(128)S(1)}, s32[16]{0:T(128)S(1)}, /*index=5*/bf16[16,64...) while((s32[]{:T(128)}, f32[4,128,4096]{2,1,0:T(8,128)}, ...), condition=%wide.region_4.5_spmd, body=%wide.region_1.4_spmd.sunk | while | flops 1080033280 | bytes 113510784 | solution.py:51
  83.0 0.6 dynamic_slice.40
  84.2 0.1 compare_select_fusion.5
  84.3 7.8 %fusion.22 = f32[8,64,4096]{2,1,0:T(8,128)} fusion(bf16[16,128,4096]{2,1,0:T(8,128)(2,1)} %get-tuple-element.165, s32[]{:T(128)S(6)} %select_n.28, bf16[16,64,128]{2,1,0:T(8,128)(2,1)S(1)} %get-tuple-element.162), kind=kOutput, calls=%fused_computation.4.clone.1 | convolution fusion | flops 536870912 | bytes 16909312 | tf_op jit(solution)/shard_map/while/body/eval_jaxpr/gwd,gdk->gwk/dot_general | solution.py:38
  92.2 17.0 %scatter_fusion.1 = f32[4,64,4096]{2,1,0:T(8,128)} fusion(f32[4,64,4096]{2,1,0:T(8,128)} %get-tuple-element.146, s32[8]{0:T(128)S(1)} %get-tuple-element.130, f32[8,64,4096]{2,1,0:T(8,128)} %fusion.22), kind=kCustom, calls=%fused_computation.3.clone.1 | custom fusion | flops 2097152 | bytes 25165856 | tf_op jit(solution)/shard_map/while/body/eval_jaxpr/scatter-add | solution.py:42
  109.1 10.3 %fusion.21 = f32[8,128,4096]{2,1,0:T(8,128)} fusion(bf16[16,64,4096]{2,1,0:T(8,128)(2,1)} %get-tuple-element.163, s32[]{:T(128)S(6)} %select_n.28, bf16[16,64,128]{2,1,0:T(8,128)(2,1)S(1)} %get-tuple-element.162), kind=kOutput, calls=%fused_computation.6.clone.1 | convolution fusion | flops 536870912 | bytes 21103616 | tf_op jit(solution)/shard_map/while/body/eval_jaxpr/gwd,gwk->gdk/dot_general | solution.py:35
  119.4 30.5 %scatter_fusion = f32[4,128,4096]{2,1,0:T(8,128)} fusion(f32[4,128,4096]{2,1,0:T(8,128)} %get-tuple-element.145, s32[8]{0:T(128)S(1)} %get-tuple-element.129, f32[8,128,4096]{2,1,0:T(8,128)} %fusion.21), kind=kCustom, calls=%fused_computation.2.clone.1 | custom fusion | flops 4194304 | bytes 50331680 | tf_op jit(solution)/shard_map/while/body/eval_jaxpr/scatter-add | solution.py:42
  149.9 0.6 dynamic_slice.40
  151.1 0.1 compare_select_fusion.5
  151.2 7.8 %fusion.22 = f32[8,64,4096]{2,1,0:T(8,128)} fusion(bf16[16,128,4096]{2,1,0:T(8,128)(2,1)} %get-tuple-element.165, s32[]{:T(128)S(6)} %select_n.28, bf16[16,64,128]{2,1,0:T(8,128)(2,1)S(1)} %get-tuple-element.162), kind=kOutput, calls=%fused_computation.4.clone.1 | convolution fusion | flops 536870912 | bytes 16909312 | tf_op jit(solution)/shard_map/while/body/eval_jaxpr/gwd,gdk->gwk/dot_general | solution.py:38
  159.0 16.6 %scatter_fusion.1 = f32[4,64,4096]{2,1,0:T(8,128)} fusion(f32[4,64,4096]{2,1,0:T(8,128)} %get-tuple-element.146, s32[8]{0:T(128)S(1)} %get-tuple-element.130, f32[8,64,4096]{2,1,0:T(8,128)} %fusion.22), kind=kCustom, calls=%fused_computation.3.clone.1 | custom fusion | flops 2097152 | bytes 25165856 | tf_op jit(solution)/shard_map/while/body/eval_jaxpr/scatter-add | solution.py:42
  175.7 10.3 %fusion.21 = f32[8,128,4096]{2,1,0:T(8,128)} fusion(bf16[16,64,4096]{2,1,0:T(8,128)(2,1)} %get-tuple-element.163, s32[]{:T(128)S(6)} %select_n.28, bf16[16,64,128]{2,1,0:T(8,128)(2,1)S(1)} %get-tuple-element.162), kind=kOutput, calls=%fused_computation.6.clone.1 | convolution fusion | flops 536870912 | bytes 21103616 | tf_op jit(solution)/shard_map/while/body/eval_jaxpr/gwd,gwk->gdk/dot_general | solution.py:35
  186.0 30.7 %scatter_fusion = f32[4,128,4096]{2,1,0:T(8,128)} fusion(f32[4,128,4096]{2,1,0:T(8,128)} %get-tuple-element.145, s32[8]{0:T(128)S(1)} %get-tuple-element.129, f32[8,128,4096]{2,1,0:T(8,128)} %fusion.21), kind=kCustom, calls=%fused_computation.2.clone.1 | custom fusion | flops 4194304 | bytes 50331680 | tf_op jit(solution)/shard_map/while/body/eval_jaxpr/scatter-add | solution.py:42
  216.6 6.4 %negate_convert_fusion = bf16[4,128,4096]{2,1,0:T(8,128)(2,1)} fusion(f32[4,128,4096]{2,1,0:T(8,128)} %get-tuple-element.50), kind=kLoop, calls=%fused_computation.14 | loop fusion | flops 4194304 | bytes 12582912 | tf_op jit(solution)/shard_map/convert_element_type | solution.py:54
  223.1 0.0 all-reduce.5.cloned.1.call-start
  223.2 4.4 %fusion.8 = bf16[256,4096]{1,0:T(8,128)(2,1)} fusion(f32[4,64,4096]{2,1,0:T(8,128)} %get-tuple-element.51, f32[4096]{0:T(1024)S(1)} %copy-done.2, bf16[256,4096]{1,0:T(8,128)(2,1)S(1)} %copy-done), kind=kLoop, calls=%fused_computation.16 | loop fusion | flops 7340032 | bytes 8404992 | tf_op jit(solution)/shard_map/convert_element_type | solution.py:57
  227.6 49.7 %reduce-scatter.2.cloned.1.call-done = bf16[512,2048]{1,0:T(8,128)(2,1)} async-done(((bf16[512,4096]{1,0:T(8,128)(2,1)}), bf16[512,2048]{1,0:T(8,128)(2,1)}) %reduce-scatter.2.cloned.1.call-update) | async-done | bytes 2097168 | tf_op jit(solution)/shard_map/reduce_scatter | solution.py:53
  277.3 4.1 %convert_element_type.41 = f32[512,2048]{1,0:T(8,128)} convert(bf16[512,2048]{1,0:T(8,128)(2,1)} %reduce-scatter.2.cloned.1.call-done) | non-fusion elementwise | flops 1048576 | bytes 6291456 | tf_op jit(solution)/shard_map/convert_element_type | solution.py:55
  281.4 50.2 %all-reduce.5.cloned.1.call-done = bf16[256,4096]{1,0:T(8,128)(2,1)} async-done(((bf16[256,4096]{1,0:T(8,128)(2,1)}), bf16[256,4096]{1,0:T(8,128)(2,1)}) %all-reduce.5.cloned.1.call-update) | async-done | bytes 2097168 | tf_op jit(solution)/shard_map/psum | solution.py:57
  331.6 3.1 copy.21
  (16 shorter events, 0.1 us)
Async XLA Ops:
  7.2 68.0 %all-reduce.3.cloned.1.call-start = ((), (), s32[]{:S(2)}) async-start(), calls=%async_computation.1 | async-start | bytes 524288 | tf_op jit(solution)/shard_map/psum | solution.py:19
  24.7 50.5 %copy-start.1 = (s32[16,64,128]{2,1,0:T(8,128)S(1)}, s32[16,64,128]{2,1,0:T(8,128)}, u32[]{:S(2)}) copy-start(s32[16,64,128]{2,1,0:T(8,128)} %param.13) | copy-start | bytes 1572868
  36.7 46.3 %copy-start.3 = (s32[16]{0:T(128)S(1)}, s32[16]{0:T(128)}, u32[]{:S(2)}) copy-start(s32[16]{0:T(128)} %param.12) | copy-start | bytes 196
  36.7 46.3 %copy-start.4 = (s32[16]{0:T(128)S(1)}, s32[16]{0:T(128)}, u32[]{:S(2)}) copy-start(s32[16]{0:T(128)} %param.11) | copy-start | bytes 196
  36.8 240.5 %reduce-scatter.2.cloned.1.call-start = ((), (), s32[]{:S(2)}) async-start(), calls=%async_computation.2 | async-start | bytes 6291456 | tf_op jit(solution)/shard_map/reduce_scatter | solution.py:53
  216.6 6.5 %copy-start = (bf16[256,4096]{1,0:T(8,128)(2,1)S(1)}, bf16[256,4096]{1,0:T(8,128)(2,1)}, u32[]{:S(2)}) copy-start(bf16[256,4096]{1,0:T(8,128)(2,1)} %param.9) | copy-start | bytes 6291460
  216.6 6.5 %copy-start.2 = (f32[4096]{0:T(1024)S(1)}, f32[4096]{0:T(1024)}, u32[]{:S(2)}) copy-start(f32[4096]{0:T(1024)} %param.10) | copy-start | bytes 49156
  223.1 108.6 %all-reduce.5.cloned.1.call-start = ((), (), s32[]{:S(2)}) async-start(), calls=%async_computation.3 | async-start | bytes 4194304 | tf_op jit(solution)/shard_map/psum | solution.py:57
Sparse Core Ops, SparseCore 0:
  36.9 38.2 all-reduce.2
  223.2 54.0 reduce-scatter.1
  280.2 51.3 all-reduce.4
where the time goes:
time: 342 us; the launch traced here: 341 us
  waiting for transfers between devices  138 us (40%)
  other arithmetic  114 us (33%)
  matrix products  48.2 us (14%)
  local copies, waits for them, and re-layouts  25 us (7%)
  between operations  13.8 us (4%)
    scatter-add x2, other arithmetic, accumulate(): theta_acc.at[doc_index].add(toward_theta)  61.1 us
    psum x1, waiting for transfers between devices, on_device(): word_logit_grad = lax.psum(beta_term.astype(jnp.bfloat16), 'doc')  50.2 us
    reduce_scatter x1, waiting for transfers between devices, on_device(): lax.psum_scatter(theta_term.astype(jnp.bfloat16), 'vocab', scatter_dimens...  49.7 us
    psum x1, waiting for transfers between devices, on_device(): lax.psum(jnp.einsum('gwk,gdk->gwd', word_part, doc_part, preferred_elemen...  38.4 us
    scatter-add x2, other arithmetic, accumulate(): beta_acc.at[word_index].add(toward_beta)  33.6 us
    dot_general x2, matrix products, accumulate(): jnp.einsum('gwd,gwk->gdk', ratio_part, word_part, preferred_element_type=...  20.5 us
    dot_general x2, matrix products, accumulate(): jnp.einsum('gwd,gdk->gwk', ratio_part, doc_part, preferred_element_type=j...  15.7 us
    dot_general x1, matrix products, on_device(): jnp.einsum('gwk,gdk->gwd', word_part, doc_part, preferred_element_type=jn...  12 us
  transfers between devices with their start and end apart: 3, of which 3 were waited for; matrix products, arithmetic and copies ran while one was open for 2% of the time, Pallas kernels for 0%

commit v1 on v0

v1 whole, which is shorter than its diff:
```python
import functools

import jax
import jax.numpy as jnp
from jax import lax
from jax.experimental import pallas as pl
from jax.experimental.pallas import tpu as pltpu
from jax.sharding import PartitionSpec as P

BF16 = jnp.bfloat16
F32 = jnp.float32
VMEM_LIMIT = 24 * 1024 * 1024


def block_width(width, most):
    return min(width, most)


def call_params():
    return pltpu.CompilerParams(vmem_limit_bytes=VMEM_LIMIT)


def rate_partial(doc_topics, word_logits, log_norm, place, n_topic):
    docs, width = doc_topics.shape
    words = word_logits.shape[0]
    step_width = block_width(width, 1024)
    steps = width // step_width
    chunk = words // n_topic

    def kernel(place_ref, doc_ref, logit_ref, norm_ref, *rest):
        outs, acc = rest[:-1], rest[-1]
        step = pl.program_id(0)
        prob = jnp.exp(logit_ref[...].astype(F32) - norm_ref[...]).astype(BF16)
        part = lax.dot_general(prob, doc_ref[...], (((1,), (1,)), ((), ())), preferred_element_type=F32)

        @pl.when(step == 0)
        def _():
            acc[...] = part

        @pl.when(step > 0)
        def _():
            acc[...] += part

        @pl.when(step == steps - 1)
        def _():
            for s in range(n_topic):
                owner = lax.rem(place_ref[0] + s, n_topic)
                outs[s][...] = acc[pl.ds(pl.multiple_of(owner * chunk, chunk), chunk), :].astype(BF16)

    return pl.pallas_call(
        kernel,
        out_shape=[jax.ShapeDtypeStruct((chunk, docs), BF16)] * n_topic,
        grid_spec=pltpu.PrefetchScalarGridSpec(
            num_scalar_prefetch=1,
            grid=(steps,),
            in_specs=[
                pl.BlockSpec((docs, step_width), lambda j, p: (0, j)),
                pl.BlockSpec((words, step_width), lambda j, p: (0, j)),
                pl.BlockSpec((1, step_width), lambda j, p: (0, j)),
            ],
            out_specs=[pl.BlockSpec((chunk, docs), lambda j, p: (0, 0))] * n_topic,
            scratch_shapes=[pltpu.VMEM((words, docs), F32)],
        ),
        compiler_params=call_params(),
        cost_estimate=pl.CostEstimate(
            flops=2 * words * docs * width, bytes_accessed=2 * (words + docs) * width, transcendentals=words * width
        ),
        name="rate_partial",
    )(place, doc_topics, word_logits, log_norm)


def chunk_counts(word_counts, tile_doc, tile_word, place, n_topic, docs, words):
    slots, word_tile, doc_tile = word_counts.shape
    chunk = words // n_topic

    def kernel(place_ref, doc_at, word_at, count_ref, out_ref):
        first = place_ref[0] * chunk
        block = first // word_tile
        row = pl.multiple_of(lax.rem(first, word_tile), chunk)
        out_ref[...] = jnp.zeros_like(out_ref)
        for s in range(slots):
            @pl.when(word_at[s] == block)
            def _():
                column = pl.multiple_of(doc_at[s] * doc_tile, doc_tile)
                out_ref[:, pl.ds(column, doc_tile)] = count_ref[s, pl.ds(row, chunk), :].astype(F32)

    return pl.pallas_call(
        kernel,
        out_shape=jax.ShapeDtypeStruct((chunk, docs), F32),
        grid_spec=pltpu.PrefetchScalarGridSpec(
            num_scalar_prefetch=3,
            grid=(1,),
            in_specs=[pl.BlockSpec(word_counts.shape, lambda j, *_: (0, 0, 0))],
            out_specs=pl.BlockSpec((chunk, docs), lambda j, *_: (0, 0)),
        ),
        compiler_params=call_params(),
        cost_estimate=pl.CostEstimate(flops=words * docs, bytes_accessed=4 * words * docs, transcendentals=0),
        name="chunk_counts",
    )(place, tile_doc, tile_word, word_counts)


def ratio_chunk(parts, counts, word_tile):
    def kernel(*refs):
        part_refs, count_ref, out_ref = refs[:-2], refs[-2], refs[-1]
        rate = part_refs[0][...].astype(F32)
        for ref in part_refs[1:]:
            rate += ref[...].astype(F32)
        out_ref[...] = (count_ref[...] / (word_tile * rate)).astype(BF16)

    return pl.pallas_call(
        kernel,
        out_shape=jax.ShapeDtypeStruct(counts.shape, BF16),
        compiler_params=call_params(),
        cost_estimate=pl.CostEstimate(flops=10 * counts.size, bytes_accessed=16 * counts.size, transcendentals=0),
        name="ratio_chunk",
    )(*parts, counts)


def join_ratio(chunks, place, n_topic):
    rows, docs = chunks[0].shape

    def kernel(place_ref, *refs):
        out_ref = refs[-1]
        for s in range(n_topic):
            owner = lax.rem(place_ref[0] + n_topic - s, n_topic)
            out_ref[pl.ds(pl.multiple_of(owner * rows, rows), rows), :] = refs[s][...]

    return pl.pallas_call(
        kernel,
        out_shape=jax.ShapeDtypeStruct((rows * n_topic, docs), BF16),
        grid_spec=pltpu.PrefetchScalarGridSpec(
            num_scalar_prefetch=1,
            grid=(1,),
            in_specs=[pl.BlockSpec((rows, docs), lambda j, p: (0, 0))] * n_topic,
            out_specs=pl.BlockSpec((rows * n_topic, docs), lambda j, p: (0, 0)),
        ),
        compiler_params=call_params(),
        cost_estimate=pl.CostEstimate(flops=0, bytes_accessed=4 * rows * docs * n_topic, transcendentals=0),
        name="join_ratio",
    )(place, *chunks)


def beta_piece(ratio, doc_topics, word_logits, log_norm, side, piece, pieces):
    docs, width = doc_topics.shape
    words = word_logits.shape[0]
    span = width // pieces
    half = words // 2

    def kernel(side_ref, ratio_ref, doc_ref, logit_ref, norm_ref, keep_ref, send_ref):
        for out_ref, which in ((send_ref, 1 - side_ref[0]), (keep_ref, side_ref[0])):
            rows = pl.ds(pl.multiple_of(which * half, half), half)
            summed = jnp.dot(ratio_ref[rows, :], doc_ref[...], preferred_element_type=F32)
            prob = jnp.exp(logit_ref[rows, :].astype(F32) - norm_ref[...]).astype(BF16).astype(F32)
            out_ref[...] = (-prob * summed).astype(BF16)

    return pl.pallas_call(
        kernel,
        out_shape=[jax.ShapeDtypeStruct((half, span), BF16)] * 2,
        grid_spec=pltpu.PrefetchScalarGridSpec(
            num_scalar_prefetch=1,
            grid=(1,),
            in_specs=[
                pl.BlockSpec((words, docs), lambda j, p: (0, 0)),
                pl.BlockSpec((docs, span), lambda j, p: (0, piece)),
                pl.BlockSpec((words, span), lambda j, p: (0, piece)),
                pl.BlockSpec((1, span), lambda j, p: (0, piece)),
            ],
            out_specs=[pl.BlockSpec((half, span), lambda j, p: (0, 0))] * 2,
        ),
        compiler_params=call_params(),
        cost_estimate=pl.CostEstimate(
            flops=2 * words * docs * span, bytes_accessed=2 * (2 * words + docs) * span, transcendentals=words * span
        ),
        name="beta_piece",
    )(side, ratio, doc_topics, word_logits, log_norm)


def theta_grad(ratios, logits, log_norm):
    words, docs = ratios[0].shape
    width = logits[0].shape[1]
    span = block_width(width, 512)
    count = len(ratios)

    def kernel(*refs):
        ratio_refs, logit_refs = refs[:count], refs[count : 2 * count]
        norm_ref, out_ref, turned = refs[2 * count :]

        @pl.when(pl.program_id(0) == 0)
        def _():
            for l in range(count):
                turned[:, l * words : (l + 1) * words] = (-ratio_refs[l][...].astype(F32)).T.astype(BF16)

        prob = jnp.concatenate(
            [jnp.exp(ref[...].astype(F32) - norm_ref[...]).astype(BF16) for ref in logit_refs], axis=0
        )
        out_ref[...] = jnp.dot(turned[...], prob, preferred_element_type=F32)

    return pl.pallas_call(
        kernel,
        out_shape=jax.ShapeDtypeStruct((docs, width), F32),
        grid=(width // span,),
        in_specs=[pl.BlockSpec((words, docs), lambda j: (0, 0))] * count
        + [pl.BlockSpec((words, span), lambda j: (0, j))] * count
        + [pl.BlockSpec((1, span), lambda j: (0, j))],
        out_specs=pl.BlockSpec((docs, span), lambda j: (0, j)),
        scratch_shapes=[pltpu.VMEM((docs, count * words), BF16)],
        compiler_params=call_params(),
        cost_estimate=pl.CostEstimate(
            flops=2 * count * words * docs * width,
            bytes_accessed=(4 * docs + 2 * count * words) * width,
            transcendentals=count * words * width,
        ),
        name="theta_grad",
    )(*ratios, *logits, log_norm)


def place_piece(own, other, side, piece, pieces, so_far):
    half, span = own.shape

    def kernel(side_ref, own_ref, other_ref, *rest):
        out_ref = rest[-1]
        step = pl.program_id(0)

        @pl.when(step == 0)
        def _():
            out_ref[...] = own_ref[...]

        @pl.when(step == 1)
        def _():
            out_ref[...] = other_ref[...]

    first = so_far is None
    return pl.pallas_call(
        kernel,
        out_shape=jax.ShapeDtypeStruct((2 * half, span * pieces), BF16),
        grid_spec=pltpu.PrefetchScalarGridSpec(
            num_scalar_prefetch=1,
            grid=(2,),
            in_specs=[pl.BlockSpec((half, span), lambda j, p: (0, 0))] * 2
            + ([] if first else [pl.BlockSpec(memory_space=pl.ANY)]),
            out_specs=pl.BlockSpec((half, span), lambda j, p: (lax.rem(p[0] + j, 2), piece)),
        ),
        input_output_aliases={} if first else {3: 0},
        compiler_params=call_params(),
        cost_estimate=pl.CostEstimate(flops=0, bytes_accessed=8 * half * span, transcendentals=0),
        name="place_piece",
    )(side, own, other, *([] if first else [so_far]))


def on_device(sizes, doc_topics, word_logits, log_norm, tile_doc, tile_word, word_counts):
    n_doc, n_topic, n_vocab = sizes
    docs, width = doc_topics.shape
    words = word_logits.shape[0]
    word_tile = word_counts.shape[1]
    norm = log_norm[None, :]
    topic_at = lax.axis_index("topic").astype(jnp.int32)
    vocab_at = lax.axis_index("vocab").astype(jnp.int32)
    place = topic_at[None]
    side = lax.rem(lax.axis_index("doc").astype(jnp.int32), 2)[None]

    def shift(array, axis, count, by):
        return lax.ppermute(array, axis, [(i, (i + by) % count) for i in range(count)])

    def swap(array, bit):
        return lax.ppermute(array, "doc", [(i, i ^ bit) for i in range(n_doc)])

    share = width // n_vocab
    own_logits = lax.dynamic_slice_in_dim(word_logits, vocab_at * share, share, 1)
    own_norm = lax.dynamic_slice_in_dim(norm, vocab_at * share, share, 1)
    logits_all = [own_logits]
    for s in range(1, n_vocab):
        target = lax.rem(vocab_at + s, n_vocab)
        logits_all.append(shift(lax.dynamic_slice_in_dim(word_logits, target * share, share, 1), "vocab", n_vocab, s))

    parts = rate_partial(doc_topics, word_logits, norm, place, n_topic)
    arrived = [parts[0]] + [shift(parts[s], "topic", n_topic, s) for s in range(1, n_topic)]
    counts = chunk_counts(word_counts, tile_doc, tile_word, place, n_topic, docs, words)
    own_ratio = ratio_chunk(arrived, counts, word_tile)
    chunks = [own_ratio] + [shift(own_ratio, "topic", n_topic, s) for s in range(1, n_topic)]
    ratio = join_ratio(chunks, place, n_topic)

    ratios = [ratio] + [shift(ratio, "vocab", n_vocab, s) for s in range(1, n_vocab)]

    pieces = 4
    out = None
    for piece in range(pieces):
        keep, send = beta_piece(ratio, doc_topics, word_logits, norm, side, piece, pieces)
        held = keep.astype(F32) + swap(send, 1).astype(F32)
        bit = 2
        while bit < n_doc:
            held = held.astype(BF16)
            held = held.astype(F32) + swap(held, bit).astype(F32)
            bit *= 2
        held = held.astype(BF16)
        out = place_piece(held, swap(held, 1), side, piece, pieces, out)

    theta = theta_grad(ratios, logits_all, own_norm)
    return theta, out


def solution(mesh):
    placed = (
        P("doc", "topic"),
        P("vocab", "topic"),
        P("topic"),
        P(("doc", "vocab")),
        P(("doc", "vocab")),
        P(("doc", "vocab"), None, None),
    )
    sizes = (mesh.shape["doc"], mesh.shape["topic"], mesh.shape["vocab"])
    return jax.shard_map(
        functools.partial(on_device, sizes),
        mesh=mesh,
        in_specs=placed,
        out_specs=(P("doc", ("topic", "vocab")), P("vocab", "topic")),
        check_vma=False,
    )
```

time: 342 us -> 72.9 us (0.21)
  other arithmetic: 114 us -> 0.53 us
  waiting for transfers between devices: 138 us -> 33.5 us
  matrix products: 48.2 us -> 0 us
  starting transfers between devices: 0.12 us -> 18.5 us
  local copies, waits for them, and re-layouts: 25 us -> 6.89 us
  between operations: 13.8 us -> 0.86 us
  Pallas kernels: 0 us -> 12.4 us
    scatter-add x4 -> x0, other arithmetic: 94.7 us -> none  [the longest x2 61.1 us: accumulate(): theta_acc.at[doc_index].add(toward_theta)]
    psum x2 -> x0, waiting for transfers between devices: 88.6 us -> none  [the longest x1 50.2 us: on_device(): word_logit_grad = lax.psum(beta_term.astype(jnp.bfloat16), 'doc')]
    reduce_scatter x1 -> x0, waiting for transfers between devices: 49.7 us -> none  [on_device(): lax.psum_scatter(theta_term.astype(jnp.bfloat16), 'vocab', scatter_dimens...]
    dot_general x5 -> x0, matrix products: 48.2 us -> none  [the longest x2 20.5 us: accumulate(): jnp.einsum('gwd,gwk->gdk', ratio_part, word_part, preferred_element_type=...]
    ppermute x0 -> x20, waiting for transfers between devices: none -> 33.5 us  [the longest x12 20.5 us: swap(): return lax.ppermute(array, 'doc', [(i, i ^ bit) for i in range(n_doc)])]
    ppermute x0 -> x20, starting transfers between devices: none -> 18.5 us  [the longest x8 12.9 us: shift(): lax.ppermute(array, axis, [(i, (i + by) % count) for i in range(count)])]
    convert_element_type x5 -> x8, other arithmetic: 18.2 us -> 0.53 us  [on_device(): held = held.astype(BF16)]
    gather x2 -> x0, local copies, waits for them, and re-layouts: 14 us -> none  [the longest x1 9.28 us: on_device(): doc_rows = topic_blocks[tile_doc]]
  transfers between devices with their start and end apart: 3 -> 20, of which waited for: 3 -> 9; matrix products, arithmetic and copies ran while one was open for 2% -> 1% of each run, Pallas kernels for 0% -> 7%
where the time goes in v1:
time: 72.9 us; the launch traced here: 72.6 us
  waiting for transfers between devices  33.5 us (46%)
  starting transfers between devices  18.5 us (25%)
  Pallas kernels  12.4 us (17%)
  local copies, waits for them, and re-layouts  6.89 us (9%)
  between operations  0.86 us (1%)
    ppermute x12, waiting for transfers between devices, swap(): return lax.ppermute(array, 'doc', [(i, i ^ bit) for i in range(n_doc)])  20.5 us
    ppermute x8, waiting for transfers between devices, shift(): lax.ppermute(array, axis, [(i, (i + by) % count) for i in range(count)])  13 us
    ppermute x8, starting transfers between devices, shift(): lax.ppermute(array, axis, [(i, (i + by) % count) for i in range(count)])  12.9 us
    unnamed x18, local copies, waits for them, and re-layouts  6.69 us
    ppermute x12, starting transfers between devices, swap(): return lax.ppermute(array, 'doc', [(i, i ^ bit) for i in range(n_doc)])  5.57 us
    pallas_call x1, Pallas kernels, theta_grad(): pl.pallas_call(kernel, out_shape=jax.ShapeDtypeStruct((docs, width), F32)...  3.78 us
    pallas_call x4, Pallas kernels, place_piece(): pl.pallas_call(kernel, out_shape=jax.ShapeDtypeStruct((2 * half, span * p...  3.26 us
    pallas_call x1, Pallas kernels, rate_partial(): pl.pallas_call(kernel, out_shape=[jax.ShapeDtypeStruct((chunk, docs), BF1...  2.64 us
  transfers between devices with their start and end apart: 20, of which 9 were waited for; matrix products, arithmetic and copies ran while one was open for 1% of the time, Pallas kernels for 7%

profile of v1, /device:TPU:0, one launch (start us, length us, event | category | flops | bytes accessed | tf_op | source)
XLA Modules:
  0.0 72.6 jit_solution(4058033868062050854)
XLA Ops:
  0.6 2.2 %copy-done = bf16[512,4096]{1,0:T(8,128)(2,1)S(1)} copy-done((bf16[512,4096]{1,0:T(8,128)(2,1)S(1)}, bf16[512,4096]{1,0:T(8,128)(2,1)}, u32[]{:S(2)}) %copy-start) | copy-done | bytes 4194328
  2.8 1.6 %copy-done.2 = bf16[256,4096]{1,0:T(8,128)(2,1)S(1)} copy-done((bf16[256,4096]{1,0:T(8,128)(2,1)S(1)}, bf16[256,4096]{1,0:T(8,128)(2,1)}, u32[]{:S(2)}) %copy-start.2) | copy-done | bytes 2097176
  4.4 0.7 copy-done.5
  5.2 2.6 %rate_partial.1 = (bf16[64,512]{1,0:T(8,128)(2,1)S(1)}, bf16[64,512]{1,0:T(8,128)(2,1)S(1)}, bf16[64,512]{1,0:T(8,128)(2,1)S(1)}, bf16[64,512]{1,0:T(8,128)(2,1)S(1)}) custom-call(s32[1]{0:T(128)} %bitcast.place_ref, bf16[512,4096]{1,0:T(8,128)(2,1)S(1)} %copy-done, bf16[256,4096]{1,0:T(8,128)(2,1)S(1)} %copy-done.2, f32[1,4096]{1,0:T(1,128)S(1)} %bitcast.4), custom_call_target="tpu_custom_call" | custom-call | flops 1073741824 | bytes 6291456 | tf_op jit(solution)/shard_map/rate_partial/pallas_call | solution.py:50
  7.8 3.1 %collective-permute-start = (bf16[64,512]{1,0:T(8,128)(2,1)S(1)}, bf16[64,512]{1,0:T(8,128)(2,1)S(1)}, u32[]{:S(2)}, u32[]{:S(2)}) collective-permute-start(bf16[64,512]{1,0:T(8,128)(2,1)S(1)} %get-tuple-element.15), channel_id=1, source_target_pairs={{0,2},{2,4},{4,6},{6,0},{1,3},{3,5},{5,7},{7,1},{8,10},{10,12},{12... | collective-permute-start | bytes 196616 | tf_op jit(solution)/shard_map/ppermute | solution.py:262
  10.9 2.6 %collective-permute-start.1 = (bf16[64,512]{1,0:T(8,128)(2,1)S(1)}, bf16[64,512]{1,0:T(8,128)(2,1)S(1)}, u32[]{:S(2)}, u32[]{:S(2)}) collective-permute-start(bf16[64,512]{1,0:T(8,128)(2,1)S(1)} %get-tuple-element.16), channel_id=1, source_target_pairs={{0,4},{2,6},{4,0},{6,2},{1,5},{3,7},{5,1},{7,3},{8,12},{10,14},{12... | collective-permute-start | bytes 196616 | tf_op jit(solution)/shard_map/ppermute | solution.py:262
  13.5 1.4 %collective-permute-start.2 = (bf16[64,512]{1,0:T(8,128)(2,1)S(1)}, bf16[64,512]{1,0:T(8,128)(2,1)S(1)}, u32[]{:S(2)}, u32[]{:S(2)}) collective-permute-start(bf16[64,512]{1,0:T(8,128)(2,1)S(1)} %get-tuple-element.17), channel_id=1, source_target_pairs={{0,6},{2,0},{4,2},{6,4},{1,7},{3,1},{5,3},{7,5},{8,14},{10,8},{12,... | collective-permute-start | bytes 196616 | tf_op jit(solution)/shard_map/ppermute | solution.py:262
  14.8 0.7 chunk_counts.1.refs_4_
  15.5 2.4 %collective-permute-done.1.refs_2_ = bf16[64,512]{1,0:T(8,128)(2,1)S(1)} collective-permute-done((bf16[64,512]{1,0:T(8,128)(2,1)S(1)}, bf16[64,512]{1,0:T(8,128)(2,1)S(1)}, u32[]{:S(2)}, u32[]{:S(2)}) %collective-permute-start.1) | collective-permute-done | bytes 65568 | tf_op jit(solution)/shard_map/ppermute | solution.py:262
  18.2 3.1 %collective-permute-start.5 = (bf16[64,512]{1,0:T(8,128)(2,1)S(1)}, bf16[64,512]{1,0:T(8,128)(2,1)S(1)}, u32[]{:S(2)}, u32[]{:S(2)}) collective-permute-start(bf16[64,512]{1,0:T(8,128)(2,1)S(1)} %ratio_chunk.1.refs_0_), channel_id=1, source_target_pairs={{0,6},{2,0},{4,2},{6,4},{1,7},{3,1},{5,3},{7,5},{8,14},{10,8},{12,... | collective-permute-start | bytes 196616 | tf_op jit(solution)/shard_map/ppermute | solution.py:262
  21.3 0.6 collective-permute-start.3
  22.0 1.3 %collective-permute-done.5.refs_3_ = bf16[64,512]{1,0:T(8,128)(2,1)S(1)} collective-permute-done((bf16[64,512]{1,0:T(8,128)(2,1)S(1)}, bf16[64,512]{1,0:T(8,128)(2,1)S(1)}, u32[]{:S(2)}, u32[]{:S(2)}) %collective-permute-start.5) | collective-permute-done | bytes 65568 | tf_op jit(solution)/shard_map/ppermute | solution.py:262
  23.3 4.3 %collective-permute-done.4.refs_2_ = bf16[64,512]{1,0:T(8,128)(2,1)S(1)} collective-permute-done((bf16[64,512]{1,0:T(8,128)(2,1)S(1)}, bf16[64,512]{1,0:T(8,128)(2,1)S(1)}, u32[]{:S(2)}, u32[]{:S(2)}) %collective-permute-start.4) | collective-permute-done | bytes 65568 | tf_op jit(solution)/shard_map/ppermute | solution.py:262
  27.7 2.2 %copy-done.1 = bf16[512,4096]{1,0:T(8,128)(2,1)S(1)} copy-done((bf16[512,4096]{1,0:T(8,128)(2,1)S(1)}, bf16[512,4096]{1,0:T(8,128)(2,1)}, u32[]{:S(2)}) %copy-start.1) | copy-done | bytes 4194328
  29.9 0.5 beta_piece.7
  30.6 1.5 %collective-permute-start.7 = (bf16[256,2048]{1,0:T(8,128)(2,1)S(1)}, bf16[256,2048]{1,0:T(8,128)(2,1)S(1)}, u32[]{:S(2)}, u32[]{:S(2)}) collective-permute-start(bf16[256,2048]{1,0:T(8,128)(2,1)S(1)} %get-tuple-element.26), channel_id=1, source_target_pairs={{0,1},{1,0},{2,3},{3,2},{4,5},{5,4},{6,7},{7,6},{8,9},{9,8},{10,11... | collective-permute-start | bytes 3145736 | tf_op jit(solution)/shard_map/ppermute | solution.py:262
  32.1 0.5 beta_piece.6
  34.5 1.6 %collective-permute-start.18 = (bf16[128,1024]{1,0:T(8,128)(2,1)S(1)}, bf16[128,1024]{1,0:T(8,128)(2,1)S(1)}, u32[]{:S(2)}, u32[]{:S(2)}) collective-permute-start(bf16[128,1024]{1,0:T(8,128)(2,1)S(1)} %add_convert_fusion.1), channel_id=1, source_target_pairs={{0,16},{8,24},{16,0},{24,8},{1,17},{9,25},{17,1},{25,9},{2,18},{10... | collective-permute-start | bytes 786440 | tf_op jit(solution)/shard_map/ppermute | solution.py:265
  36.2 0.6 collective-permute-start.15
  36.8 1.6 %collective-permute-start.12 = (bf16[128,1024]{1,0:T(8,128)(2,1)S(1)}, bf16[128,1024]{1,0:T(8,128)(2,1)S(1)}, u32[]{:S(2)}, u32[]{:S(2)}) collective-permute-start(bf16[128,1024]{1,0:T(8,128)(2,1)S(1)} %add_convert_fusion.5), channel_id=1, source_target_pairs={{0,16},{8,24},{16,0},{24,8},{1,17},{9,25},{17,1},{25,9},{2,18},{10... | collective-permute-start | bytes 786440 | tf_op jit(solution)/shard_map/ppermute | solution.py:265
  38.5 0.6 collective-permute-start.9
  39.1 4.7 %collective-permute-done.18 = bf16[128,1024]{1,0:T(8,128)(2,1)S(1)} collective-permute-done((bf16[128,1024]{1,0:T(8,128)(2,1)S(1)}, bf16[128,1024]{1,0:T(8,128)(2,1)S(1)}, u32[]{:S(2)}, u32[]{:S(2)}) %collective-permute-start.18) | collective-permute-done | bytes 262176 | tf_op jit(solution)/shard_map/ppermute | solution.py:265
  43.9 5.5 %collective-permute-done.15 = bf16[128,1024]{1,0:T(8,128)(2,1)S(1)} collective-permute-done((bf16[128,1024]{1,0:T(8,128)(2,1)S(1)}, bf16[128,1024]{1,0:T(8,128)(2,1)S(1)}, u32[]{:S(2)}, u32[]{:S(2)}) %collective-permute-start.15) | collective-permute-done | bytes 262176 | tf_op jit(solution)/shard_map/ppermute | solution.py:265
  49.5 5.5 %collective-permute-done.12 = bf16[128,1024]{1,0:T(8,128)(2,1)S(1)} collective-permute-done((bf16[128,1024]{1,0:T(8,128)(2,1)S(1)}, bf16[128,1024]{1,0:T(8,128)(2,1)S(1)}, u32[]{:S(2)}, u32[]{:S(2)}) %collective-permute-start.12) | collective-permute-done | bytes 262176 | tf_op jit(solution)/shard_map/ppermute | solution.py:265
  55.1 4.9 %collective-permute-done.9 = bf16[128,1024]{1,0:T(8,128)(2,1)S(1)} collective-permute-done((bf16[128,1024]{1,0:T(8,128)(2,1)S(1)}, bf16[128,1024]{1,0:T(8,128)(2,1)S(1)}, u32[]{:S(2)}, u32[]{:S(2)}) %collective-permute-start.9) | collective-permute-done | bytes 262176 | tf_op jit(solution)/shard_map/ppermute | solution.py:265
  60.1 0.7 collective-permute-start.6
  60.8 0.8 %place_piece.4.rest_0_ = bf16[256,4096]{1,0:T(8,128)(2,1)} custom-call(s32[1]{0:T(128)} %bitcast.3.side_ref, bf16[128,1024]{1,0:T(8,128)(2,1)S(1)} %add_convert_fusion.own_ref, bf16[128,1024]{1,0:T(8,128)(2,1)S(1)} %collective-permute-done.19.other_ref), custom_call_target="tpu_custom_call" | custom-call | bytes 1048576 | tf_op jit(solution)/shard_map/place_piece/pallas_call | solution.py:233
  61.7 0.8 %place_piece.5.rest_0_ = bf16[256,4096]{1,0:T(8,128)(2,1)} custom-call(s32[1]{0:T(128)} %bitcast.3.side_ref, bf16[128,1024]{1,0:T(8,128)(2,1)S(1)} %add_convert_fusion.2.own_ref, bf16[128,1024]{1,0:T(8,128)(2,1)S(1)} %collective-permute-done.16.other_ref, bf16[256,4096]{1,0:T(8,128)(2,1)} %place_piece.4.rest_0_), custom_call_target="tpu_custom_call", output_to_operand_aliasing={{}: (3, {})} | custom-call | bytes 1048576 | tf_op jit(solution)/shard_map/place_piece/pallas_call | solution.py:233
  62.5 0.8 %place_piece.6.rest_0_ = bf16[256,4096]{1,0:T(8,128)(2,1)} custom-call(s32[1]{0:T(128)} %bitcast.3.side_ref, bf16[128,1024]{1,0:T(8,128)(2,1)S(1)} %add_convert_fusion.4.own_ref, bf16[128,1024]{1,0:T(8,128)(2,1)S(1)} %collective-permute-done.13.other_ref, bf16[256,4096]{1,0:T(8,128)(2,1)} %place_piece.5.rest_0_), custom_call_target="tpu_custom_call", output_to_operand_aliasing={{}: (3, {})} | custom-call | bytes 1048576 | tf_op jit(solution)/shard_map/place_piece/pallas_call | solution.py:233
  63.3 0.8 %place_piece.7 = bf16[256,4096]{1,0:T(8,128)(2,1)} custom-call(s32[1]{0:T(128)} %bitcast.3.side_ref, bf16[128,1024]{1,0:T(8,128)(2,1)S(1)} %add_convert_fusion.6.own_ref, bf16[128,1024]{1,0:T(8,128)(2,1)S(1)} %collective-permute-done.10.other_ref, bf16[256,4096]{1,0:T(8,128)(2,1)} %place_piece.6.rest_0_), custom_call_target="tpu_custom_call", output_to_operand_aliasing={{}: (3, {})} | custom-call | bytes 1048576 | tf_op jit(solution)/shard_map/place_piece/pallas_call | solution.py:233
  64.1 4.7 %collective-permute-done.6.refs_1_ = bf16[256,512]{1,0:T(8,128)(2,1)S(1)} collective-permute-done((bf16[256,512]{1,0:T(8,128)(2,1)S(1)}, bf16[256,512]{1,0:T(8,128)(2,1)S(1)}, u32[]{:S(2)}, u32[]{:S(2)}) %collective-permute-start.6) | collective-permute-done | bytes 262176 | tf_op jit(solution)/shard_map/ppermute | solution.py:262
  68.9 3.8 %theta_grad.1 = f32[512,2048]{1,0:T(8,128)} custom-call(bf16[256,512]{1,0:T(8,128)(2,1)S(1)} %join_ratio.1.refs_0_.ratio_ref, bf16[256,512]{1,0:T(8,128)(2,1)S(1)} %collective-permute-done.6.refs_1_, bf16[256,2048]{1,0:T(8,128)(2,1)S(1)} %get-tuple-element.27.refs_2_, bf16[256,2048]{1,0:T(8,128)(2,1)S(1)} %collective-permute-done.7.refs_3_, ...), custom_call_target="tpu_custom_call" | custom-call | flops 1073741824 | bytes 6291456 | tf_op jit(solution)/shard_map/theta_grad/pallas_call | solution.py:198
  (49 shorter events, 3.3 us)
Async XLA Ops:
  0.6 2.2 %copy-start = (bf16[512,4096]{1,0:T(8,128)(2,1)S(1)}, bf16[512,4096]{1,0:T(8,128)(2,1)}, u32[]{:S(2)}) copy-start(bf16[512,4096]{1,0:T(8,128)(2,1)} %doc_ref.9) | copy-start | bytes 12582916
  2.8 1.6 %copy-start.2 = (bf16[256,4096]{1,0:T(8,128)(2,1)S(1)}, bf16[256,4096]{1,0:T(8,128)(2,1)}, u32[]{:S(2)}) copy-start(bf16[256,4096]{1,0:T(8,128)(2,1)} %logit_ref.9) | copy-start | bytes 6291460
  4.4 0.7 copy-start.5
  5.1 9.7 %copy-start.4 = (s32[16,64,128]{2,1,0:T(8,128)S(1)}, s32[16,64,128]{2,1,0:T(8,128)}, u32[]{:S(2)}) copy-start(s32[16,64,128]{2,1,0:T(8,128)} %count_ref.1) | copy-start | bytes 1572868
  5.1 9.7 %copy-start.7 = (s32[16]{0:T(128)S(1)}, s32[16]{0:T(128)}, u32[]{:S(2)}) copy-start(s32[16]{0:T(128)} %doc_at.1) | copy-start | bytes 196
  5.1 9.7 %copy-start.8 = (s32[16]{0:T(128)S(1)}, s32[16]{0:T(128)}, u32[]{:S(2)}) copy-start(s32[16]{0:T(128)} %word_at.1) | copy-start | bytes 196
  5.1 22.5 %copy-start.3 = (bf16[256,4096]{1,0:T(8,128)(2,1)S(1)}, bf16[256,4096]{1,0:T(8,128)(2,1)}, u32[]{:S(2)}) copy-start(bf16[256,4096]{1,0:T(8,128)(2,1)} %logit_ref.9) | copy-start | bytes 6291460
  5.1 22.5 %copy-start.6 = (f32[4096]{0:T(1024)S(1)}, f32[4096]{0:T(1024)}, u32[]{:S(2)}) copy-start(f32[4096]{0:T(1024)} %param.8) | copy-start | bytes 49156
  7.8 7.7 %collective-permute-start = (bf16[64,512]{1,0:T(8,128)(2,1)S(1)}, bf16[64,512]{1,0:T(8,128)(2,1)S(1)}, u32[]{:S(2)}, u32[]{:S(2)}) collective-permute-start(bf16[64,512]{1,0:T(8,128)(2,1)S(1)} %get-tuple-element.15), channel_id=1, source_target_pairs={{0,2},{2,4},{4,6},{6,0},{1,3},{3,5},{5,7},{7,1},{8,10},{10,12},{12... | collective-permute-start | bytes 196616 | tf_op jit(solution)/shard_map/ppermute | solution.py:262
  10.9 7.1 %collective-permute-start.1 = (bf16[64,512]{1,0:T(8,128)(2,1)S(1)}, bf16[64,512]{1,0:T(8,128)(2,1)S(1)}, u32[]{:S(2)}, u32[]{:S(2)}) collective-permute-start(bf16[64,512]{1,0:T(8,128)(2,1)S(1)} %get-tuple-element.16), channel_id=1, source_target_pairs={{0,4},{2,6},{4,0},{6,2},{1,5},{3,7},{5,1},{7,3},{8,12},{10,14},{12... | collective-permute-start | bytes 196616 | tf_op jit(solution)/shard_map/ppermute | solution.py:262
  13.5 4.7 %collective-permute-start.2 = (bf16[64,512]{1,0:T(8,128)(2,1)S(1)}, bf16[64,512]{1,0:T(8,128)(2,1)S(1)}, u32[]{:S(2)}, u32[]{:S(2)}) collective-permute-start(bf16[64,512]{1,0:T(8,128)(2,1)S(1)} %get-tuple-element.17), channel_id=1, source_target_pairs={{0,6},{2,0},{4,2},{6,4},{1,7},{3,1},{5,3},{7,5},{8,14},{10,8},{12,... | collective-permute-start | bytes 196616 | tf_op jit(solution)/shard_map/ppermute | solution.py:262
  18.2 5.0 %collective-permute-start.5 = (bf16[64,512]{1,0:T(8,128)(2,1)S(1)}, bf16[64,512]{1,0:T(8,128)(2,1)S(1)}, u32[]{:S(2)}, u32[]{:S(2)}) collective-permute-start(bf16[64,512]{1,0:T(8,128)(2,1)S(1)} %ratio_chunk.1.refs_0_), channel_id=1, source_target_pairs={{0,6},{2,0},{4,2},{6,4},{1,7},{3,1},{5,3},{7,5},{8,14},{10,8},{12,... | collective-permute-start | bytes 196616 | tf_op jit(solution)/shard_map/ppermute | solution.py:262
  21.3 6.3 %collective-permute-start.4 = (bf16[64,512]{1,0:T(8,128)(2,1)S(1)}, bf16[64,512]{1,0:T(8,128)(2,1)S(1)}, u32[]{:S(2)}, u32[]{:S(2)}) collective-permute-start(bf16[64,512]{1,0:T(8,128)(2,1)S(1)} %ratio_chunk.1.refs_0_), channel_id=1, source_target_pairs={{0,4},{2,6},{4,0},{6,2},{1,5},{3,7},{5,1},{7,3},{8,12},{10,14},{12... | collective-permute-start | bytes 196616 | tf_op jit(solution)/shard_map/ppermute | solution.py:262
  21.3 6.3 %collective-permute-start.3 = (bf16[64,512]{1,0:T(8,128)(2,1)S(1)}, bf16[64,512]{1,0:T(8,128)(2,1)S(1)}, u32[]{:S(2)}, u32[]{:S(2)}) collective-permute-start(bf16[64,512]{1,0:T(8,128)(2,1)S(1)} %ratio_chunk.1.refs_0_), channel_id=1, source_target_pairs={{0,2},{2,4},{4,6},{6,0},{1,3},{3,5},{5,7},{7,1},{8,10},{10,12},{12... | collective-permute-start | bytes 196616 | tf_op jit(solution)/shard_map/ppermute | solution.py:262
  27.7 2.2 %copy-start.1 = (bf16[512,4096]{1,0:T(8,128)(2,1)S(1)}, bf16[512,4096]{1,0:T(8,128)(2,1)}, u32[]{:S(2)}) copy-start(bf16[512,4096]{1,0:T(8,128)(2,1)} %doc_ref.9) | copy-start | bytes 12582916
  30.3 4.1 %collective-permute-start.17 = (bf16[128,1024]{1,0:T(8,128)(2,1)S(1)}, bf16[128,1024]{1,0:T(8,128)(2,1)S(1)}, u32[]{:S(2)}, u32[]{:S(2)}) collective-permute-start(bf16[128,1024]{1,0:T(8,128)(2,1)S(1)} %get-tuple-element.25), channel_id=1, source_target_pairs={{0,8},{8,0},{16,24},{24,16},{1,9},{9,1},{17,25},{25,17},{2,10},{10... | collective-permute-start | bytes 786440 | tf_op jit(solution)/shard_map/ppermute | solution.py:265
  30.6 38.2 %collective-permute-start.7 = (bf16[256,2048]{1,0:T(8,128)(2,1)S(1)}, bf16[256,2048]{1,0:T(8,128)(2,1)S(1)}, u32[]{:S(2)}, u32[]{:S(2)}) collective-permute-start(bf16[256,2048]{1,0:T(8,128)(2,1)S(1)} %get-tuple-element.26), channel_id=1, source_target_pairs={{0,1},{1,0},{2,3},{3,2},{4,5},{5,4},{6,7},{7,6},{8,9},{9,8},{10,11... | collective-permute-start | bytes 3145736 | tf_op jit(solution)/shard_map/ppermute | solution.py:262
  32.6 3.5 %collective-permute-start.14 = (bf16[128,1024]{1,0:T(8,128)(2,1)S(1)}, bf16[128,1024]{1,0:T(8,128)(2,1)S(1)}, u32[]{:S(2)}, u32[]{:S(2)}) collective-permute-start(bf16[128,1024]{1,0:T(8,128)(2,1)S(1)} %get-tuple-element.23), channel_id=1, source_target_pairs={{0,8},{8,0},{16,24},{24,16},{1,9},{9,1},{17,25},{25,17},{2,10},{10... | collective-permute-start | bytes 786440 | tf_op jit(solution)/shard_map/ppermute | solution.py:265
  33.3 3.4 %collective-permute-start.11 = (bf16[128,1024]{1,0:T(8,128)(2,1)S(1)}, bf16[128,1024]{1,0:T(8,128)(2,1)S(1)}, u32[]{:S(2)}, u32[]{:S(2)}) collective-permute-start(bf16[128,1024]{1,0:T(8,128)(2,1)S(1)} %get-tuple-element.21), channel_id=1, source_target_pairs={{0,8},{8,0},{16,24},{24,16},{1,9},{9,1},{17,25},{25,17},{2,10},{10... | collective-permute-start | bytes 786440 | tf_op jit(solution)/shard_map/ppermute | solution.py:265
  34.2 4.2 %collective-permute-start.8 = (bf16[128,1024]{1,0:T(8,128)(2,1)S(1)}, bf16[128,1024]{1,0:T(8,128)(2,1)S(1)}, u32[]{:S(2)}, u32[]{:S(2)}) collective-permute-start(bf16[128,1024]{1,0:T(8,128)(2,1)S(1)} %get-tuple-element.19), channel_id=1, source_target_pairs={{0,8},{8,0},{16,24},{24,16},{1,9},{9,1},{17,25},{25,17},{2,10},{10... | collective-permute-start | bytes 786440 | tf_op jit(solution)/shard_map/ppermute | solution.py:265
  34.5 9.2 %collective-permute-start.18 = (bf16[128,1024]{1,0:T(8,128)(2,1)S(1)}, bf16[128,1024]{1,0:T(8,128)(2,1)S(1)}, u32[]{:S(2)}, u32[]{:S(2)}) collective-permute-start(bf16[128,1024]{1,0:T(8,128)(2,1)S(1)} %add_convert_fusion.1), channel_id=1, source_target_pairs={{0,16},{8,24},{16,0},{24,8},{1,17},{9,25},{17,1},{25,9},{2,18},{10... | collective-permute-start | bytes 786440 | tf_op jit(solution)/shard_map/ppermute | solution.py:265
  36.2 13.2 %collective-permute-start.15 = (bf16[128,1024]{1,0:T(8,128)(2,1)S(1)}, bf16[128,1024]{1,0:T(8,128)(2,1)S(1)}, u32[]{:S(2)}, u32[]{:S(2)}) collective-permute-start(bf16[128,1024]{1,0:T(8,128)(2,1)S(1)} %add_convert_fusion.3), channel_id=1, source_target_pairs={{0,16},{8,24},{16,0},{24,8},{1,17},{9,25},{17,1},{25,9},{2,18},{10... | collective-permute-start | bytes 786440 | tf_op jit(solution)/shard_map/ppermute | solution.py:265
  36.8 18.1 %collective-permute-start.12 = (bf16[128,1024]{1,0:T(8,128)(2,1)S(1)}, bf16[128,1024]{1,0:T(8,128)(2,1)S(1)}, u32[]{:S(2)}, u32[]{:S(2)}) collective-permute-start(bf16[128,1024]{1,0:T(8,128)(2,1)S(1)} %add_convert_fusion.5), channel_id=1, source_target_pairs={{0,16},{8,24},{16,0},{24,8},{1,17},{9,25},{17,1},{25,9},{2,18},{10... | collective-permute-start | bytes 786440 | tf_op jit(solution)/shard_map/ppermute | solution.py:265
  38.5 21.5 %collective-permute-start.9 = (bf16[128,1024]{1,0:T(8,128)(2,1)S(1)}, bf16[128,1024]{1,0:T(8,128)(2,1)S(1)}, u32[]{:S(2)}, u32[]{:S(2)}) collective-permute-start(bf16[128,1024]{1,0:T(8,128)(2,1)S(1)} %add_convert_fusion.7), channel_id=1, source_target_pairs={{0,16},{8,24},{16,0},{24,8},{1,17},{9,25},{17,1},{25,9},{2,18},{10... | collective-permute-start | bytes 786440 | tf_op jit(solution)/shard_map/ppermute | solution.py:265
  43.8 16.3 %collective-permute-start.19 = (bf16[128,1024]{1,0:T(8,128)(2,1)S(1)}, bf16[128,1024]{1,0:T(8,128)(2,1)S(1)}, u32[]{:S(2)}, u32[]{:S(2)}) collective-permute-start(bf16[128,1024]{1,0:T(8,128)(2,1)S(1)} %add_convert_fusion.own_ref), channel_id=1, source_target_pairs={{0,8},{8,0},{16,24},{24,16},{1,9},{9,1},{17,25},{25,17},{2,10},{10... | collective-permute-start | bytes 786440 | tf_op jit(solution)/shard_map/ppermute | solution.py:265
  49.4 12.2 %collective-permute-start.16 = (bf16[128,1024]{1,0:T(8,128)(2,1)S(1)}, bf16[128,1024]{1,0:T(8,128)(2,1)S(1)}, u32[]{:S(2)}, u32[]{:S(2)}) collective-permute-start(bf16[128,1024]{1,0:T(8,128)(2,1)S(1)} %add_convert_fusion.2.own_ref), channel_id=1, source_target_pairs={{0,8},{8,0},{16,24},{24,16},{1,9},{9,1},{17,25},{25,17},{2,10},{10... | collective-permute-start | bytes 786440 | tf_op jit(solution)/shard_map/ppermute | solution.py:265
  55.0 7.4 %collective-permute-start.13 = (bf16[128,1024]{1,0:T(8,128)(2,1)S(1)}, bf16[128,1024]{1,0:T(8,128)(2,1)S(1)}, u32[]{:S(2)}, u32[]{:S(2)}) collective-permute-start(bf16[128,1024]{1,0:T(8,128)(2,1)S(1)} %add_convert_fusion.4.own_ref), channel_id=1, source_target_pairs={{0,8},{8,0},{16,24},{24,16},{1,9},{9,1},{17,25},{25,17},{2,10},{10... | collective-permute-start | bytes 786440 | tf_op jit(solution)/shard_map/ppermute | solution.py:265
  60.1 3.2 %collective-permute-start.10 = (bf16[128,1024]{1,0:T(8,128)(2,1)S(1)}, bf16[128,1024]{1,0:T(8,128)(2,1)S(1)}, u32[]{:S(2)}, u32[]{:S(2)}) collective-permute-start(bf16[128,1024]{1,0:T(8,128)(2,1)S(1)} %add_convert_fusion.6.own_ref), channel_id=1, source_target_pairs={{0,8},{8,0},{16,24},{24,16},{1,9},{9,1},{17,25},{25,17},{2,10},{10... | collective-permute-start | bytes 786440 | tf_op jit(solution)/shard_map/ppermute | solution.py:265
  60.1 8.7 %collective-permute-start.6 = (bf16[256,512]{1,0:T(8,128)(2,1)S(1)}, bf16[256,512]{1,0:T(8,128)(2,1)S(1)}, u32[]{:S(2)}, u32[]{:S(2)}) collective-permute-start(bf16[256,512]{1,0:T(8,128)(2,1)S(1)} %join_ratio.1.refs_0_.ratio_ref), channel_id=1, source_target_pairs={{0,1},{1,0},{2,3},{3,2},{4,5},{5,4},{6,7},{7,6},{8,9},{9,8},{10,11... | collective-permute-start | bytes 786440 | tf_op jit(solution)/shard_map/ppermute | solution.py:262

commit v2 on v1

v2 whole, which is shorter than its diff:
```python
import functools

import jax
import jax.numpy as jnp
from jax import lax
from jax.experimental import pallas as pl
from jax.experimental.pallas import tpu as pltpu
from jax.sharding import PartitionSpec as P

BF16 = jnp.bfloat16
F32 = jnp.float32
VMEM_LIMIT = 28 * 1024 * 1024
ANY = pl.BlockSpec(memory_space=pl.ANY)
HBM = pl.BlockSpec(memory_space=pltpu.HBM)
VMEM = pl.BlockSpec(memory_space=pltpu.VMEM)
SMEM = pl.BlockSpec(memory_space=pltpu.SMEM)


def call_params():
    return pltpu.CompilerParams(vmem_limit_bytes=VMEM_LIMIT)


def cost(flops, bytes_accessed, transcendentals=0):
    return pl.CostEstimate(flops=flops, bytes_accessed=bytes_accessed, transcendentals=transcendentals)


def in_hbm(array):
    return pltpu.with_memory_space_constraint(array, pltpu.HBM)


def first_row(index, rows):
    return pl.multiple_of(index * rows, rows)


def rate_partial(doc_topics, word_logits, log_norm, place, n_topic):
    docs, width = doc_topics.shape
    words = word_logits.shape[0]
    span = min(width, 1024)
    steps = width // span
    chunk = words // n_topic

    def kernel(place_ref, doc_in, logit_in, norm_ref, *rest):
        parts, (doc_ref, prob_ref, logit_ref, acc, sems) = rest[:n_topic], rest[n_topic:]
        copies = []
        for j in range(steps):
            at = pl.ds(j * span, span)
            copies.append(
                (
                    pltpu.make_async_copy(logit_in.at[:, at], logit_ref.at[:, at], sems.at[0, j]),
                    pltpu.make_async_copy(doc_in.at[:, at], doc_ref.at[:, at], sems.at[1, j]),
                )
            )
        for pair in copies:
            for copy in pair:
                copy.start()
        for j in range(steps):
            at = pl.ds(j * span, span)
            copies[j][0].wait()
            prob = jnp.exp(logit_ref[:, at].astype(F32) - norm_ref[:, at]).astype(BF16)
            prob_ref[:, at] = prob
            copies[j][1].wait()
            part = lax.dot_general(
                prob, doc_ref[:, at], (((1,), (1,)), ((), ())), preferred_element_type=F32
            )
            if j == 0:
                acc[...] = part
            else:
                acc[...] += part
        for s in range(n_topic):
            owner = lax.rem(place_ref[0] + s, n_topic)
            parts[s][...] = acc[pl.ds(first_row(owner, chunk), chunk), :].astype(BF16)

    out = pl.pallas_call(
        kernel,
        out_shape=[jax.ShapeDtypeStruct((chunk, docs), BF16)] * n_topic
        + [jax.ShapeDtypeStruct(doc_topics.shape, BF16), jax.ShapeDtypeStruct(word_logits.shape, BF16)],
        in_specs=[SMEM, HBM, HBM, VMEM],
        out_specs=[VMEM] * (n_topic + 2),
        scratch_shapes=[
            pltpu.VMEM(word_logits.shape, BF16),
            pltpu.VMEM((words, docs), F32),
            pltpu.SemaphoreType.DMA((2, steps)),
        ],
        compiler_params=call_params(),
        cost_estimate=cost(2 * words * docs * width, 2 * (words + docs) * width, words * width),
        name="rate_partial",
    )(place, in_hbm(doc_topics), in_hbm(word_logits), log_norm)
    return out[:n_topic], out[n_topic], out[n_topic + 1]


def chunk_counts(word_counts, tile_doc, tile_word, place, n_topic, docs, words):
    slots, word_tile, doc_tile = word_counts.shape
    chunk = words // n_topic

    def kernel(place_ref, doc_at, word_at, count_ref, out_ref):
        first = place_ref[0] * chunk
        block = first // word_tile
        row = pl.multiple_of(lax.rem(first, word_tile), chunk)
        out_ref[...] = jnp.zeros_like(out_ref)
        for s in range(slots):
            @pl.when(word_at[s] == block)
            def _():
                column = first_row(doc_at[s], doc_tile)
                out_ref[:, pl.ds(column, doc_tile)] = count_ref[s, pl.ds(row, chunk), :].astype(F32)

    return pl.pallas_call(
        kernel,
        out_shape=jax.ShapeDtypeStruct((chunk, docs), F32),
        in_specs=[SMEM, SMEM, SMEM, VMEM],
        out_specs=VMEM,
        compiler_params=call_params(),
        cost_estimate=cost(words * docs, 4 * words * docs),
        name="chunk_counts",
    )(place, tile_doc, tile_word, word_counts)


def ratio_chunk(parts, counts, word_tile):
    def kernel(*refs):
        part_refs, count_ref, out_ref = refs[:-2], refs[-2], refs[-1]
        rate = part_refs[0][...].astype(F32)
        for ref in part_refs[1:]:
            rate += ref[...].astype(F32)
        out_ref[...] = (count_ref[...] / (word_tile * rate)).astype(BF16)

    return pl.pallas_call(
        kernel,
        out_shape=jax.ShapeDtypeStruct(counts.shape, BF16),
        compiler_params=call_params(),
        cost_estimate=cost(10 * counts.size, 16 * counts.size),
        name="ratio_chunk",
    )(*parts, counts)


def join_ratio(chunks, place, n_topic):
    rows, docs = chunks[0].shape

    def kernel(place_ref, *refs):
        out_ref = refs[-1]
        for s in range(n_topic):
            owner = lax.rem(place_ref[0] + n_topic - s, n_topic)
            out_ref[pl.ds(first_row(owner, rows), rows), :] = refs[s][...]

    return pl.pallas_call(
        kernel,
        out_shape=jax.ShapeDtypeStruct((rows * n_topic, docs), BF16),
        in_specs=[SMEM] + [VMEM] * n_topic,
        out_specs=VMEM,
        compiler_params=call_params(),
        cost_estimate=cost(0, 4 * rows * docs * n_topic),
        name="join_ratio",
    )(place, *chunks)


def beta_piece(ratio, docs_held, prob_held, side, piece, pieces, after):
    docs, width = docs_held.shape
    words = prob_held.shape[0]
    span = width // pieces
    half = words // 2

    def kernel(side_ref, ratio_ref, doc_ref, prob_ref, *rest):
        keep_ref, send_ref = rest[-2:]
        for out_ref, which in ((send_ref, 1 - side_ref[0]), (keep_ref, side_ref[0])):
            rows = pl.ds(first_row(which, half), half)
            summed = jnp.dot(ratio_ref[rows, :], doc_ref[...], preferred_element_type=F32)
            out_ref[...] = (-prob_ref[rows, :].astype(F32) * summed).astype(BF16)

    return pl.pallas_call(
        kernel,
        out_shape=[jax.ShapeDtypeStruct((half, span), BF16)] * 2,
        grid=(1,),
        in_specs=[
            SMEM,
            pl.BlockSpec((words, docs), lambda j: (0, 0)),
            pl.BlockSpec((docs, span), lambda j: (0, piece)),
            pl.BlockSpec((words, span), lambda j: (0, piece)),
        ]
        + [ANY] * len(after),
        out_specs=[pl.BlockSpec((half, span), lambda j: (0, 0))] * 2,
        compiler_params=call_params(),
        cost_estimate=cost(2 * words * docs * span, 2 * (2 * words + docs) * span),
        name="beta_piece",
    )(side, ratio, docs_held, prob_held, *after)


def add_pair(own, other, after=()):
    def kernel(own_ref, other_ref, *rest):
        rest[-1][...] = (own_ref[...].astype(F32) + other_ref[...].astype(F32)).astype(BF16)

    return pl.pallas_call(
        kernel,
        out_shape=jax.ShapeDtypeStruct(own.shape, BF16),
        in_specs=[VMEM, VMEM] + [ANY] * len(after),
        out_specs=VMEM,
        compiler_params=call_params(),
        cost_estimate=cost(own.size, 6 * own.size),
        name="add_pair",
    )(own, other, *after)


def theta_grad(ratio, far_ratios, prob_held, far_logits, log_norm, vocab_at, side):
    words, docs = ratio.shape
    half = words // 2
    share = log_norm.shape[1]
    far = len(far_ratios)
    count = far + 1
    span = min(share, 512)

    def kernel(vocab_ref, side_ref, ratio_ref, *refs):
        far_refs, prob_ref = refs[:far], refs[far]
        logit_refs, norm_ref = refs[far + 1 : 3 * far + 1], refs[3 * far + 1]
        out_ref, done_ref, turned = refs[-3:]
        done_ref[...] = jnp.zeros_like(done_ref)

        @pl.when(pl.program_id(0) == 0)
        def _():
            def put(rows, at):
                turned[:, at : at + rows.shape[0]] = (-rows.astype(F32)).T.astype(BF16)

            put(ratio_ref[...], 0)
            for l in range(far):
                for h in range(2):
                    which = side_ref[0] if h == 0 else 1 - side_ref[0]
                    put(far_refs[l][pl.ds(first_row(which, half), half), :], (l + 1) * words + h * half)

        prob = jnp.concatenate(
            [prob_ref[...]] + [jnp.exp(ref[...].astype(F32) - norm_ref[...]).astype(BF16) for ref in logit_refs],
            axis=0,
        )
        out_ref[...] = jnp.dot(turned[...], prob, preferred_element_type=F32)

    blocks = share // span
    return pl.pallas_call(
        kernel,
        out_shape=[jax.ShapeDtypeStruct((docs, share), F32), jax.ShapeDtypeStruct((8, 128), F32)],
        grid_spec=pltpu.PrefetchScalarGridSpec(
            num_scalar_prefetch=2,
            grid=(blocks,),
            in_specs=[pl.BlockSpec((words, docs), lambda j, v, s: (0, 0))] * count
            + [pl.BlockSpec((words, span), lambda j, v, s: (0, v[0] * blocks + j))]
            + [pl.BlockSpec((half, span), lambda j, v, s: (0, j))] * (2 * far)
            + [pl.BlockSpec((1, span), lambda j, v, s: (0, j))],
            out_specs=[
                pl.BlockSpec((docs, span), lambda j, v, s: (0, j)),
                pl.BlockSpec((8, 128), lambda j, v, s: (0, 0)),
            ],
            scratch_shapes=[pltpu.VMEM((docs, count * words), BF16)],
        ),
        compiler_params=call_params(),
        cost_estimate=cost(
            2 * count * words * docs * share, (4 * docs + 2 * count * words) * share, count * words * share
        ),
        name="theta_grad",
    )(vocab_at, side, ratio, *far_ratios, prob_held, *far_logits, log_norm)


def place_pieces(own, other, side):
    pieces = len(own)
    half, span = own[0].shape

    def kernel(side_ref, *refs):
        out_ref, sems = refs[-2:]
        copies = []
        for p in range(pieces):
            for h, which in ((0, side_ref[0]), (1, 1 - side_ref[0])):
                target = out_ref.at[pl.ds(first_row(which, half), half), pl.ds(p * span, span)]
                copies.append(pltpu.make_async_copy(refs[h * pieces + p], target, sems.at[h, p]))
        for copy in copies:
            copy.start()
        for copy in copies:
            copy.wait()

    return pl.pallas_call(
        kernel,
        out_shape=jax.ShapeDtypeStruct((2 * half, span * pieces), BF16),
        in_specs=[SMEM] + [VMEM] * (2 * pieces),
        out_specs=HBM,
        scratch_shapes=[pltpu.SemaphoreType.DMA((2, pieces))],
        compiler_params=call_params(),
        cost_estimate=cost(0, 8 * half * span * pieces),
        name="place_pieces",
    )(side, *own, *other)


def on_device(sizes, doc_topics, word_logits, log_norm, tile_doc, tile_word, word_counts):
    n_doc, n_topic, n_vocab = sizes
    docs, width = doc_topics.shape
    words = word_logits.shape[0]
    word_tile = word_counts.shape[1]
    norm = log_norm[None, :]
    place = lax.axis_index("topic").astype(jnp.int32)[None]
    vocab_at = lax.axis_index("vocab").astype(jnp.int32)
    side = lax.rem(lax.axis_index("doc").astype(jnp.int32), 2)

    def shift(array, axis, count, by):
        return lax.ppermute(array, axis, [(i, (i + by) % count) for i in range(count)])

    def swap(array, bit):
        return lax.ppermute(array, "doc", [(i, i ^ bit) for i in range(n_doc)])

    share = width // n_vocab
    half = words // 2
    own_norm = lax.dynamic_slice_in_dim(norm, vocab_at * share, share, 1)
    far_logits = []
    for s in range(1, n_vocab):
        target = lax.rem(vocab_at + s, n_vocab)
        near_half = shift(
            lax.dynamic_slice(word_logits, (side * half, target * share), (half, share)), "vocab", n_vocab, s
        )
        far_logits += [near_half, swap(near_half, 1)]

    parts, docs_held, prob_held = rate_partial(doc_topics, word_logits, norm, place, n_topic)
    arrived = [parts[0]] + [shift(parts[s], "topic", n_topic, s) for s in range(1, n_topic)]
    counts = chunk_counts(word_counts, tile_doc, tile_word, place, n_topic, docs, words)
    own_ratio = ratio_chunk(arrived, counts, word_tile)
    chunks = [own_ratio] + [shift(own_ratio, "topic", n_topic, s) for s in range(1, n_topic)]
    ratio = join_ratio(chunks, place, n_topic)
    far_ratios = [shift(ratio, "vocab", n_vocab, s) for s in range(1, n_vocab)]
    theta, theta_done = theta_grad(ratio, far_ratios, prob_held, far_logits, own_norm, vocab_at[None], side[None])

    pieces = 4
    halves, sums = [], []
    for p in range(pieces):
        after = [sums[p - 2]] if p >= 2 else []
        keep, send = beta_piece(ratio, docs_held, prob_held, side[None], p, pieces, after)
        halves.append((keep, swap(send, 1)))
        if p >= 1:
            sums.append(add_pair(*halves[p - 1]))
    sums.append(add_pair(*halves[-1]))
    bit = 2
    while bit < n_doc:
        sums = [add_pair(part, swap(part, bit), [theta_done] if p == 2 else []) for p, part in enumerate(sums)]
        bit *= 2
    out = place_pieces(sums, [swap(part, 1) for part in sums], side[None])
    return theta, out


def solution(mesh):
    placed = (
        P("doc", "topic"),
        P("vocab", "topic"),
        P("topic"),
        P(("doc", "vocab")),
        P(("doc", "vocab")),
        P(("doc", "vocab"), None, None),
    )
    sizes = (mesh.shape["doc"], mesh.shape["topic"], mesh.shape["vocab"])
    return jax.shard_map(
        functools.partial(on_device, sizes),
        mesh=mesh,
        in_specs=placed,
        out_specs=(P("doc", ("topic", "vocab")), P("vocab", "topic")),
        check_vma=False,
    )
```

time: 72.9 us -> 62.8 us (0.86)
  waiting for transfers between devices: 33.5 us -> 20.9 us
  Pallas kernels: 12.4 us -> 16.3 us
  local copies, waits for them, and re-layouts: 6.89 us -> 4.33 us
  starting transfers between devices: 18.5 us -> 20.1 us
    ppermute x12 -> x13, waiting for transfers between devices: 20.5 us -> 14 us  [swap(): return lax.ppermute(array, 'doc', [(i, i ^ bit) for i in range(n_doc)])]
    ppermute x8, waiting for transfers between devices: 13 us -> 6.96 us  [shift(): lax.ppermute(array, axis, [(i, (i + by) % count) for i in range(count)])]
    unnamed x18 -> x14, local copies, waits for them, and re-layouts: 6.69 us -> 2.39 us
    pallas_call x5 -> x10, Pallas kernels: 7.04 us -> 9.91 us  [the longest x1 5.18 us: theta_grad(): pl.pallas_call(kernel, out_shape=[jax.ShapeDtypeStruct((docs, share), F32...]
    dynamic_slice x1, local copies, waits for them, and re-layouts: 0.19 us -> 1.94 us  [on_device(): lax.dynamic_slice(word_logits, (side * half, target * share), (half, share))]
    ppermute x12 -> x13, starting transfers between devices: 5.57 us -> 7.19 us  [swap(): return lax.ppermute(array, 'doc', [(i, i ^ bit) for i in range(n_doc)])]
    pallas_call x1, Pallas kernels: 2.64 us -> 3.59 us  [rate_partial(): pl.pallas_call(kernel, out_shape=[jax.ShapeDtypeStruct((chunk, docs), BF1...]
  transfers between devices with their start and end apart: 20 -> 21, of which waited for: 9 -> 9; matrix products, arithmetic and copies ran while one was open for 1% -> 0% of each run, Pallas kernels for 7% -> 24%
where the time goes in v2:
time: 62.8 us; the launch traced here: 62.4 us
  waiting for transfers between devices  20.9 us (33%)
  starting transfers between devices  20.1 us (32%)
  Pallas kernels  16.3 us (26%)
  local copies, waits for them, and re-layouts  4.33 us (7%)
  between operations  0.79 us (1%)
    ppermute x13, waiting for transfers between devices, swap(): return lax.ppermute(array, 'doc', [(i, i ^ bit) for i in range(n_doc)])  14 us
    ppermute x8, starting transfers between devices, shift(): lax.ppermute(array, axis, [(i, (i + by) % count) for i in range(count)])  12.9 us
    ppermute x13, starting transfers between devices, swap(): return lax.ppermute(array, 'doc', [(i, i ^ bit) for i in range(n_doc)])  7.19 us
    ppermute x8, waiting for transfers between devices, shift(): lax.ppermute(array, axis, [(i, (i + by) % count) for i in range(count)])  6.96 us
    pallas_call x1, Pallas kernels, theta_grad(): pl.pallas_call(kernel, out_shape=[jax.ShapeDtypeStruct((docs, share), F32...  5.18 us
    pallas_call x1, Pallas kernels, rate_partial(): pl.pallas_call(kernel, out_shape=[jax.ShapeDtypeStruct((chunk, docs), BF1...  3.59 us
    pallas_call x8, Pallas kernels, add_pair(): pl.pallas_call(kernel, out_shape=jax.ShapeDtypeStruct(own.shape, BF16), i...  3.36 us
    unnamed x14, local copies, waits for them, and re-layouts  2.39 us
  transfers between devices with their start and end apart: 21, of which 9 were waited for; matrix products, arithmetic and copies ran while one was open for 0% of the time, Pallas kernels for 24%

profile of v2, /device:TPU:0, one launch (start us, length us, event | category | flops | bytes accessed | tf_op | source)
XLA Modules:
  0.0 62.4 jit_solution(11671861830181889772)
XLA Ops:
  0.7 1.9 %dynamic_slice.6 = bf16[128,2048]{1,0:T(8,128)(2,1)} dynamic-slice(bf16[256,4096]{1,0:T(8,128)(2,1)} %logit_in.1, s32[]{:T(128)S(6)} %select_n.9, s32[]{:T(128)S(6)} %select_n.10), dynamic_slice_sizes={128,2048} | dynamic-slice | bytes 1048580 | tf_op jit(solution)/shard_map/dynamic_slice | solution.py:307
  2.6 3.0 %collective-permute-start.7 = (bf16[128,2048]{1,0:T(8,128)(2,1)}, bf16[128,2048]{1,0:T(8,128)(2,1)}, u32[]{:S(2)}, u32[]{:S(2)}) collective-permute-start(bf16[128,2048]{1,0:T(8,128)(2,1)} %dynamic_slice.6), channel_id=1, source_target_pairs={{0,1},{1,0},{2,3},{3,2},{4,5},{5,4},{6,7},{7,6},{8,9},{9,8},{10,11... | collective-permute-start | bytes 1572872 | tf_op jit(solution)/shard_map/ppermute | solution.py:295
  5.6 0.7 %copy-done.3 = f32[4096]{0:T(1024)S(1)} copy-done((f32[4096]{0:T(1024)S(1)}, f32[4096]{0:T(1024)}, u32[]{:S(2)}) %copy-start.3) | copy-done | bytes 16408
  6.3 3.6 %rate_partial.1 = (bf16[64,512]{1,0:T(8,128)(2,1)S(1)}, bf16[64,512]{1,0:T(8,128)(2,1)S(1)}, bf16[64,512]{1,0:T(8,128)(2,1)S(1)}, bf16[64,512]{1,0:T(8,128)(2,1)...) custom-call(s32[1]{0:T(128)} %bitcast.2.place_ref, bf16[512,4096]{1,0:T(8,128)(2,1)} %doc_in.1, ...), custom_call_target="tpu_custom_call" | custom-call | flops 1073741824 | bytes 6291456 | tf_op jit(solution)/shard_map/rate_partial/pallas_call | solution.py:73
  9.9 1.6 %collective-permute-start = (bf16[64,512]{1,0:T(8,128)(2,1)S(1)}, bf16[64,512]{1,0:T(8,128)(2,1)S(1)}, u32[]{:S(2)}, u32[]{:S(2)}) collective-permute-start(bf16[64,512]{1,0:T(8,128)(2,1)S(1)} %get-tuple-element.19), channel_id=1, source_target_pairs={{0,2},{2,4},{4,6},{6,0},{1,3},{3,5},{5,7},{7,1},{8,10},{10,12},{12... | collective-permute-start | bytes 196616 | tf_op jit(solution)/shard_map/ppermute | solution.py:295
  11.5 2.6 %collective-permute-start.1 = (bf16[64,512]{1,0:T(8,128)(2,1)S(1)}, bf16[64,512]{1,0:T(8,128)(2,1)S(1)}, u32[]{:S(2)}, u32[]{:S(2)}) collective-permute-start(bf16[64,512]{1,0:T(8,128)(2,1)S(1)} %get-tuple-element.20), channel_id=1, source_target_pairs={{0,4},{2,6},{4,0},{6,2},{1,5},{3,7},{5,1},{7,3},{8,12},{10,14},{12... | collective-permute-start | bytes 196616 | tf_op jit(solution)/shard_map/ppermute | solution.py:295
  14.1 1.3 %collective-permute-start.2 = (bf16[64,512]{1,0:T(8,128)(2,1)S(1)}, bf16[64,512]{1,0:T(8,128)(2,1)S(1)}, u32[]{:S(2)}, u32[]{:S(2)}) collective-permute-start(bf16[64,512]{1,0:T(8,128)(2,1)S(1)} %get-tuple-element.21), channel_id=1, source_target_pairs={{0,6},{2,0},{4,2},{6,4},{1,7},{3,1},{5,3},{7,5},{8,14},{10,8},{12,... | collective-permute-start | bytes 196616 | tf_op jit(solution)/shard_map/ppermute | solution.py:295
  15.5 0.7 %chunk_counts.1.refs_4_ = f32[64,512]{1,0:T(8,128)S(1)} custom-call(s32[1]{0:T(128)} %bitcast.2.place_ref, s32[16]{0:T(128)S(1)} %copy-done.5, s32[16]{0:T(128)S(1)} %copy-done.6, s32[16,64,128]{2,1,0:T(8,128)S(1)} %copy-done), custom_call_target="tpu_custom_call" | custom-call | flops 131072 | bytes 524288 | tf_op jit(solution)/shard_map/chunk_counts/pallas_call | solution.py:106
  16.2 0.6 %collective-permute-done.refs_1_ = bf16[64,512]{1,0:T(8,128)(2,1)S(1)} collective-permute-done((bf16[64,512]{1,0:T(8,128)(2,1)S(1)}, bf16[64,512]{1,0:T(8,128)(2,1)S(1)}, u32[]{:S(2)}, u32[]{:S(2)}) %collective-permute-start) | collective-permute-done | bytes 65568 | tf_op jit(solution)/shard_map/ppermute | solution.py:295
  16.8 2.1 %collective-permute-done.1.refs_2_ = bf16[64,512]{1,0:T(8,128)(2,1)S(1)} collective-permute-done((bf16[64,512]{1,0:T(8,128)(2,1)S(1)}, bf16[64,512]{1,0:T(8,128)(2,1)S(1)}, u32[]{:S(2)}, u32[]{:S(2)}) %collective-permute-start.1) | collective-permute-done | bytes 65568 | tf_op jit(solution)/shard_map/ppermute | solution.py:295
  18.9 1.3 %collective-permute-start.3 = (bf16[64,512]{1,0:T(8,128)(2,1)S(1)}, bf16[64,512]{1,0:T(8,128)(2,1)S(1)}, u32[]{:S(2)}, u32[]{:S(2)}) collective-permute-start(bf16[64,512]{1,0:T(8,128)(2,1)S(1)} %ratio_chunk.1.refs_0_), channel_id=1, source_target_pairs={{0,2},{2,4},{4,6},{6,0},{1,3},{3,5},{5,7},{7,1},{8,10},{10,12},{12... | collective-permute-start | bytes 196616 | tf_op jit(solution)/shard_map/ppermute | solution.py:295
  20.3 2.0 %collective-permute-start.4 = (bf16[64,512]{1,0:T(8,128)(2,1)S(1)}, bf16[64,512]{1,0:T(8,128)(2,1)S(1)}, u32[]{:S(2)}, u32[]{:S(2)}) collective-permute-start(bf16[64,512]{1,0:T(8,128)(2,1)S(1)} %ratio_chunk.1.refs_0_), channel_id=1, source_target_pairs={{0,4},{2,6},{4,0},{6,2},{1,5},{3,7},{5,1},{7,3},{8,12},{10,14},{12... | collective-permute-start | bytes 196616 | tf_op jit(solution)/shard_map/ppermute | solution.py:295
  22.3 0.5 collective-permute-start.5
  22.8 2.8 %collective-permute-done.3.refs_1_ = bf16[64,512]{1,0:T(8,128)(2,1)S(1)} collective-permute-done((bf16[64,512]{1,0:T(8,128)(2,1)S(1)}, bf16[64,512]{1,0:T(8,128)(2,1)S(1)}, u32[]{:S(2)}, u32[]{:S(2)}) %collective-permute-start.3) | collective-permute-done | bytes 65568 | tf_op jit(solution)/shard_map/ppermute | solution.py:295
  25.6 1.4 %collective-permute-done.4.refs_2_ = bf16[64,512]{1,0:T(8,128)(2,1)S(1)} collective-permute-done((bf16[64,512]{1,0:T(8,128)(2,1)S(1)}, bf16[64,512]{1,0:T(8,128)(2,1)S(1)}, u32[]{:S(2)}, u32[]{:S(2)}) %collective-permute-start.4) | collective-permute-done | bytes 65568 | tf_op jit(solution)/shard_map/ppermute | solution.py:295
  28.2 0.6 collective-permute-start.9
  31.2 1.5 %collective-permute-start.12 = (bf16[128,1024]{1,0:T(8,128)(2,1)S(1)}, bf16[128,1024]{1,0:T(8,128)(2,1)S(1)}, u32[]{:S(2)}, u32[]{:S(2)}) collective-permute-start(bf16[128,1024]{1,0:T(8,128)(2,1)S(1)} %add_pair.10.own_ref.rest_0_), channel_id=1, source_target_pairs={{0,16},{8,24},{16,0},{24,8},{1,17},{9,25},{17,1},{25,9},{2,18},{10... | collective-permute-start | bytes 786440 | tf_op jit(solution)/shard_map/ppermute | solution.py:298
  32.7 0.5 collective-permute-start.10
  33.3 1.6 %collective-permute-start.16 = (bf16[128,1024]{1,0:T(8,128)(2,1)S(1)}, bf16[128,1024]{1,0:T(8,128)(2,1)}, u32[]{:S(2)}, u32[]{:S(2)}) collective-permute-start(bf16[128,1024]{1,0:T(8,128)(2,1)S(1)} %add_pair.14.own_ref), channel_id=1, source_target_pairs={{0,16},{8,24},{16,0},{24,8},{1,17},{9,25},{17,1},{25,9},{2,18},{10... | collective-permute-start | bytes 786440 | tf_op jit(solution)/shard_map/ppermute | solution.py:298
  35.4 4.9 %collective-permute-done.12.other_ref = bf16[128,1024]{1,0:T(8,128)(2,1)S(1)} collective-permute-done((bf16[128,1024]{1,0:T(8,128)(2,1)S(1)}, bf16[128,1024]{1,0:T(8,128)(2,1)S(1)}, u32[]{:S(2)}, u32[]{:S(2)}) %collective-permute-start.12) | collective-permute-done | bytes 262176 | tf_op jit(solution)/shard_map/ppermute | solution.py:298
  40.3 0.7 %copy-done.1 = bf16[128,1024]{1,0:T(8,128)(2,1)} copy-done((bf16[128,1024]{1,0:T(8,128)(2,1)}, bf16[128,1024]{1,0:T(8,128)(2,1)S(1)}, u32[]{:S(2)}) %copy-start.1) | copy-done | bytes 262168
  41.0 1.5 %collective-permute-start.14 = (bf16[128,1024]{1,0:T(8,128)(2,1)S(1)}, bf16[128,1024]{1,0:T(8,128)(2,1)}, u32[]{:S(2)}, u32[]{:S(2)}) collective-permute-start(bf16[128,1024]{1,0:T(8,128)(2,1)S(1)} %add_pair.12.own_ref), channel_id=1, source_target_pairs={{0,16},{8,24},{16,0},{24,8},{1,17},{9,25},{17,1},{25,9},{2,18},{10... | collective-permute-start | bytes 786440 | tf_op jit(solution)/shard_map/ppermute | solution.py:298
  42.5 0.9 %copy-done.2 = bf16[128,1024]{1,0:T(8,128)(2,1)S(1)} copy-done((bf16[128,1024]{1,0:T(8,128)(2,1)S(1)}, bf16[128,1024]{1,0:T(8,128)(2,1)}, u32[]{:S(2)}) %copy-start.2) | copy-done | bytes 262168
  43.5 2.5 %collective-permute-done.10.other_ref = bf16[128,1024]{1,0:T(8,128)(2,1)} collective-permute-done((bf16[128,1024]{1,0:T(8,128)(2,1)S(1)}, bf16[128,1024]{1,0:T(8,128)(2,1)}, u32[]{:S(2)}, u32[]{:S(2)}) %collective-permute-start.10) | collective-permute-done | bytes 262176 | tf_op jit(solution)/shard_map/ppermute | solution.py:298
  46.0 1.0 %add_pair.9.refs_0_ = bf16[128,1024]{1,0:T(8,128)(2,1)S(1)} custom-call(bf16[128,1024]{1,0:T(8,128)(2,1)S(1)} %add_pair.8.own_ref.rest_0_, bf16[128,1024]{1,0:T(8,128)(2,1)} %collective-permute-done.10.other_ref), custom_call_target="tpu_custom_call" | custom-call | flops 131072 | bytes 786432 | tf_op jit(solution)/shard_map/add_pair/pallas_call | solution.py:189
  47.0 4.6 %collective-permute-done.16.other_ref = bf16[128,1024]{1,0:T(8,128)(2,1)} collective-permute-done((bf16[128,1024]{1,0:T(8,128)(2,1)S(1)}, bf16[128,1024]{1,0:T(8,128)(2,1)}, u32[]{:S(2)}, u32[]{:S(2)}) %collective-permute-start.16) | collective-permute-done | bytes 262176 | tf_op jit(solution)/shard_map/ppermute | solution.py:298
  51.6 1.0 %add_pair.15.refs_3_ = bf16[128,1024]{1,0:T(8,128)(2,1)S(1)} custom-call(bf16[128,1024]{1,0:T(8,128)(2,1)S(1)} %add_pair.14.own_ref, bf16[128,1024]{1,0:T(8,128)(2,1)} %collective-permute-done.16.other_ref), custom_call_target="tpu_custom_call" | custom-call | flops 131072 | bytes 786432 | tf_op jit(solution)/shard_map/add_pair/pallas_call | solution.py:189
  52.7 0.6 collective-permute-start.20
  53.2 5.2 %theta_grad.1 = (f32[512,2048]{1,0:T(8,128)}, f32[8,128]{1,0:T(8,128)S(1)}) custom-call(s32[1]{0:T(128)} %bitcast.vocab_ref, s32[1]{0:T(128)} %bitcast.1.side_ref, bf16[256,512]{1,0:T(8,128)(2,1)S(1)} %join_ratio.1.ratio_ref, bf16[256,512]{1,0:T(8,128)(2,1)} %collective-permute-done.6.refs_0_, bf16[256,4096]{1,0:T(8,128)(2,1)S(1)} %get-tuple-element.22.refs_1_.prob_ref, ...), custom_call_target="tpu_custom_call" | custom-call | flops 1073741824 | bytes 6291456 | tf_op jit(solution)/shard_map/theta_grad/pallas_call | solution.py:232
  58.4 1.0 %add_pair.13.refs_2_ = bf16[128,1024]{1,0:T(8,128)(2,1)S(1)} custom-call(bf16[128,1024]{1,0:T(8,128)(2,1)S(1)} %add_pair.12.own_ref, bf16[128,1024]{1,0:T(8,128)(2,1)} %collective-permute-done.14.other_ref, f32[8,128]{1,0:T(8,128)S(1)} %get-tuple-element.31.rest_0_), custom_call_target="tpu_custom_call" | custom-call | flops 131072 | bytes 786432 | tf_op jit(solution)/shard_map/add_pair/pallas_call | solution.py:189
  59.6 1.5 %collective-permute-done.19.refs_6_ = bf16[128,1024]{1,0:T(8,128)(2,1)S(1)} collective-permute-done((bf16[128,1024]{1,0:T(8,128)(2,1)S(1)}, bf16[128,1024]{1,0:T(8,128)(2,1)S(1)}, u32[]{:S(2)}, u32[]{:S(2)}) %collective-permute-start.19) | collective-permute-done | bytes 262176 | tf_op jit(solution)/shard_map/ppermute | solution.py:298
  61.0 1.4 %place_pieces.1 = bf16[256,4096]{1,0:T(8,128)(2,1)} custom-call(s32[1]{0:T(128)} %bitcast.1.side_ref, bf16[128,1024]{1,0:T(8,128)(2,1)S(1)} %add_pair.9.refs_0_, bf16[128,1024]{1,0:T(8,128)(2,1)S(1)} %add_pair.11.refs_1_, bf16[128,1024]{1,0:T(8,128)(2,1)S(1)} %add_pair.13.refs_2_, bf16[128,1024]{1,0:T(8,128)(2,1)S(1)} %add_pair.15.refs_3_, ...), custom_call_target="tpu_custom_call" | custom-call | bytes 4194304 | tf_op jit(solution)/shard_map/place_pieces/pallas_call | solution.py:272
  (44 shorter events, 4.4 us)
Async XLA Ops:
  0.6 14.8 %copy-start.6 = (s32[16]{0:T(128)S(1)}, s32[16]{0:T(128)}, u32[]{:S(2)}) copy-start(s32[16]{0:T(128)} %word_at.1) | copy-start | bytes 196
  0.6 14.8 %copy-start = (s32[16,64,128]{2,1,0:T(8,128)S(1)}, s32[16,64,128]{2,1,0:T(8,128)}, u32[]{:S(2)}) copy-start(s32[16,64,128]{2,1,0:T(8,128)} %count_ref.1) | copy-start | bytes 1572868
  0.7 14.8 %copy-start.5 = (s32[16]{0:T(128)S(1)}, s32[16]{0:T(128)}, u32[]{:S(2)}) copy-start(s32[16]{0:T(128)} %doc_at.1) | copy-start | bytes 196
  2.6 28.4 %collective-permute-start.7 = (bf16[128,2048]{1,0:T(8,128)(2,1)}, bf16[128,2048]{1,0:T(8,128)(2,1)}, u32[]{:S(2)}, u32[]{:S(2)}) collective-permute-start(bf16[128,2048]{1,0:T(8,128)(2,1)} %dynamic_slice.6), channel_id=1, source_target_pairs={{0,1},{1,0},{2,3},{3,2},{4,5},{5,4},{6,7},{7,6},{8,9},{9,8},{10,11... | collective-permute-start | bytes 1572872 | tf_op jit(solution)/shard_map/ppermute | solution.py:295
  5.6 0.7 %copy-start.3 = (f32[4096]{0:T(1024)S(1)}, f32[4096]{0:T(1024)}, u32[]{:S(2)}) copy-start(f32[4096]{0:T(1024)} %param.8) | copy-start | bytes 49156
  9.9 6.9 %collective-permute-start = (bf16[64,512]{1,0:T(8,128)(2,1)S(1)}, bf16[64,512]{1,0:T(8,128)(2,1)S(1)}, u32[]{:S(2)}, u32[]{:S(2)}) collective-permute-start(bf16[64,512]{1,0:T(8,128)(2,1)S(1)} %get-tuple-element.19), channel_id=1, source_target_pairs={{0,2},{2,4},{4,6},{6,0},{1,3},{3,5},{5,7},{7,1},{8,10},{10,12},{12... | collective-permute-start | bytes 196616 | tf_op jit(solution)/shard_map/ppermute | solution.py:295
  11.5 7.3 %collective-permute-start.1 = (bf16[64,512]{1,0:T(8,128)(2,1)S(1)}, bf16[64,512]{1,0:T(8,128)(2,1)S(1)}, u32[]{:S(2)}, u32[]{:S(2)}) collective-permute-start(bf16[64,512]{1,0:T(8,128)(2,1)S(1)} %get-tuple-element.20), channel_id=1, source_target_pairs={{0,4},{2,6},{4,0},{6,2},{1,5},{3,7},{5,1},{7,3},{8,12},{10,14},{12... | collective-permute-start | bytes 196616 | tf_op jit(solution)/shard_map/ppermute | solution.py:295
  14.1 4.8 %collective-permute-start.2 = (bf16[64,512]{1,0:T(8,128)(2,1)S(1)}, bf16[64,512]{1,0:T(8,128)(2,1)S(1)}, u32[]{:S(2)}, u32[]{:S(2)}) collective-permute-start(bf16[64,512]{1,0:T(8,128)(2,1)S(1)} %get-tuple-element.21), channel_id=1, source_target_pairs={{0,6},{2,0},{4,2},{6,4},{1,7},{3,1},{5,3},{7,5},{8,14},{10,8},{12,... | collective-permute-start | bytes 196616 | tf_op jit(solution)/shard_map/ppermute | solution.py:295
  18.9 6.7 %collective-permute-start.3 = (bf16[64,512]{1,0:T(8,128)(2,1)S(1)}, bf16[64,512]{1,0:T(8,128)(2,1)S(1)}, u32[]{:S(2)}, u32[]{:S(2)}) collective-permute-start(bf16[64,512]{1,0:T(8,128)(2,1)S(1)} %ratio_chunk.1.refs_0_), channel_id=1, source_target_pairs={{0,2},{2,4},{4,6},{6,0},{1,3},{3,5},{5,7},{7,1},{8,10},{10,12},{12... | collective-permute-start | bytes 196616 | tf_op jit(solution)/shard_map/ppermute | solution.py:295
  20.3 6.8 %collective-permute-start.4 = (bf16[64,512]{1,0:T(8,128)(2,1)S(1)}, bf16[64,512]{1,0:T(8,128)(2,1)S(1)}, u32[]{:S(2)}, u32[]{:S(2)}) collective-permute-start(bf16[64,512]{1,0:T(8,128)(2,1)S(1)} %ratio_chunk.1.refs_0_), channel_id=1, source_target_pairs={{0,4},{2,6},{4,0},{6,2},{1,5},{3,7},{5,1},{7,3},{8,12},{10,14},{12... | collective-permute-start | bytes 196616 | tf_op jit(solution)/shard_map/ppermute | solution.py:295
  22.3 4.8 %collective-permute-start.5 = (bf16[64,512]{1,0:T(8,128)(2,1)S(1)}, bf16[64,512]{1,0:T(8,128)(2,1)S(1)}, u32[]{:S(2)}, u32[]{:S(2)}) collective-permute-start(bf16[64,512]{1,0:T(8,128)(2,1)S(1)} %ratio_chunk.1.refs_0_), channel_id=1, source_target_pairs={{0,6},{2,0},{4,2},{6,4},{1,7},{3,1},{5,3},{7,5},{8,14},{10,8},{12,... | collective-permute-start | bytes 196616 | tf_op jit(solution)/shard_map/ppermute | solution.py:295
  27.6 1.6 %collective-permute-start.11 = (bf16[128,1024]{1,0:T(8,128)(2,1)S(1)}, bf16[128,1024]{1,0:T(8,128)(2,1)S(1)}, u32[]{:S(2)}, u32[]{:S(2)}) collective-permute-start(bf16[128,1024]{1,0:T(8,128)(2,1)S(1)} %get-tuple-element.28), channel_id=1, source_target_pairs={{0,8},{8,0},{16,24},{24,16},{1,9},{9,1},{17,25},{25,17},{2,10},{10... | collective-permute-start | bytes 786440 | tf_op jit(solution)/shard_map/ppermute | solution.py:298
  28.2 1.8 %collective-permute-start.9 = (bf16[128,1024]{1,0:T(8,128)(2,1)S(1)}, bf16[128,1024]{1,0:T(8,128)(2,1)S(1)}, u32[]{:S(2)}, u32[]{:S(2)}) collective-permute-start(bf16[128,1024]{1,0:T(8,128)(2,1)S(1)} %get-tuple-element.26), channel_id=1, source_target_pairs={{0,8},{8,0},{16,24},{24,16},{1,9},{9,1},{17,25},{25,17},{2,10},{10... | collective-permute-start | bytes 786440 | tf_op jit(solution)/shard_map/ppermute | solution.py:298
  29.8 3.4 %collective-permute-start.15 = (bf16[128,1024]{1,0:T(8,128)(2,1)S(1)}, bf16[128,1024]{1,0:T(8,128)(2,1)S(1)}, u32[]{:S(2)}, u32[]{:S(2)}) collective-permute-start(bf16[128,1024]{1,0:T(8,128)(2,1)S(1)} %get-tuple-element.33), channel_id=1, source_target_pairs={{0,8},{8,0},{16,24},{24,16},{1,9},{9,1},{17,25},{25,17},{2,10},{10... | collective-permute-start | bytes 786440 | tf_op jit(solution)/shard_map/ppermute | solution.py:298
  30.1 12.4 %copy-start.4 = (f32[4096]{0:T(1024)S(1)}, f32[4096]{0:T(1024)}, u32[]{:S(2)}) copy-start(f32[4096]{0:T(1024)} %param.8) | copy-start | bytes 49156
  30.6 4.3 %collective-permute-start.13 = (bf16[128,1024]{1,0:T(8,128)(2,1)S(1)}, bf16[128,1024]{1,0:T(8,128)(2,1)S(1)}, u32[]{:S(2)}, u32[]{:S(2)}) collective-permute-start(bf16[128,1024]{1,0:T(8,128)(2,1)S(1)} %get-tuple-element.30), channel_id=1, source_target_pairs={{0,8},{8,0},{16,24},{24,16},{1,9},{9,1},{17,25},{25,17},{2,10},{10... | collective-permute-start | bytes 786440 | tf_op jit(solution)/shard_map/ppermute | solution.py:298
  31.0 22.2 %collective-permute-start.8 = (bf16[128,2048]{1,0:T(8,128)(2,1)}, bf16[128,2048]{1,0:T(8,128)(2,1)}, u32[]{:S(2)}, u32[]{:S(2)}) collective-permute-start(bf16[128,2048]{1,0:T(8,128)(2,1)} %collective-permute-done.7.refs_2_), channel_id=1, source_target_pairs={{0,8},{8,0},{16,24},{24,16},{1,9},{9,1},{17,25},{25,17},{2,10},{10... | collective-permute-start | bytes 1572872 | tf_op jit(solution)/shard_map/ppermute | solution.py:298
  31.2 9.1 %collective-permute-start.12 = (bf16[128,1024]{1,0:T(8,128)(2,1)S(1)}, bf16[128,1024]{1,0:T(8,128)(2,1)S(1)}, u32[]{:S(2)}, u32[]{:S(2)}) collective-permute-start(bf16[128,1024]{1,0:T(8,128)(2,1)S(1)} %add_pair.10.own_ref.rest_0_), channel_id=1, source_target_pairs={{0,16},{8,24},{16,0},{24,8},{1,17},{9,25},{17,1},{25,9},{2,18},{10... | collective-permute-start | bytes 786440 | tf_op jit(solution)/shard_map/ppermute | solution.py:298
  32.7 13.4 %collective-permute-start.10 = (bf16[128,1024]{1,0:T(8,128)(2,1)S(1)}, bf16[128,1024]{1,0:T(8,128)(2,1)}, u32[]{:S(2)}, u32[]{:S(2)}) collective-permute-start(bf16[128,1024]{1,0:T(8,128)(2,1)S(1)} %add_pair.8.own_ref.rest_0_), channel_id=1, source_target_pairs={{0,16},{8,24},{16,0},{24,8},{1,17},{9,25},{17,1},{25,9},{2,18},{10... | collective-permute-start | bytes 786440 | tf_op jit(solution)/shard_map/ppermute | solution.py:298
  33.3 18.4 %collective-permute-start.16 = (bf16[128,1024]{1,0:T(8,128)(2,1)S(1)}, bf16[128,1024]{1,0:T(8,128)(2,1)}, u32[]{:S(2)}, u32[]{:S(2)}) collective-permute-start(bf16[128,1024]{1,0:T(8,128)(2,1)S(1)} %add_pair.14.own_ref), channel_id=1, source_target_pairs={{0,16},{8,24},{16,0},{24,8},{1,17},{9,25},{17,1},{25,9},{2,18},{10... | collective-permute-start | bytes 786440 | tf_op jit(solution)/shard_map/ppermute | solution.py:298
  34.8 17.8 %collective-permute-start.6 = (bf16[256,512]{1,0:T(8,128)(2,1)S(1)}, bf16[256,512]{1,0:T(8,128)(2,1)}, u32[]{:S(2)}, u32[]{:S(2)}) collective-permute-start(bf16[256,512]{1,0:T(8,128)(2,1)S(1)} %join_ratio.1.ratio_ref), channel_id=1, source_target_pairs={{0,1},{1,0},{2,3},{3,2},{4,5},{5,4},{6,7},{7,6},{8,9},{9,8},{10,11... | collective-permute-start | bytes 786440 | tf_op jit(solution)/shard_map/ppermute | solution.py:295
  40.3 0.7 %copy-start.1 = (bf16[128,1024]{1,0:T(8,128)(2,1)}, bf16[128,1024]{1,0:T(8,128)(2,1)S(1)}, u32[]{:S(2)}) copy-start(bf16[128,1024]{1,0:T(8,128)(2,1)S(1)} %collective-permute-done.12.other_ref) | copy-start | bytes 786436
  41.0 17.4 %collective-permute-start.14 = (bf16[128,1024]{1,0:T(8,128)(2,1)S(1)}, bf16[128,1024]{1,0:T(8,128)(2,1)}, u32[]{:S(2)}, u32[]{:S(2)}) collective-permute-start(bf16[128,1024]{1,0:T(8,128)(2,1)S(1)} %add_pair.12.own_ref), channel_id=1, source_target_pairs={{0,16},{8,24},{16,0},{24,8},{1,17},{9,25},{17,1},{25,9},{2,18},{10... | collective-permute-start | bytes 786440 | tf_op jit(solution)/shard_map/ppermute | solution.py:298
  42.5 1.0 %copy-start.2 = (bf16[128,1024]{1,0:T(8,128)(2,1)S(1)}, bf16[128,1024]{1,0:T(8,128)(2,1)}, u32[]{:S(2)}) copy-start(bf16[128,1024]{1,0:T(8,128)(2,1)} %copy-done.1) | copy-start | bytes 786436
  46.0 13.5 %collective-permute-start.18 = (bf16[128,1024]{1,0:T(8,128)(2,1)S(1)}, bf16[128,1024]{1,0:T(8,128)(2,1)S(1)}, u32[]{:S(2)}, u32[]{:S(2)}) collective-permute-start(bf16[128,1024]{1,0:T(8,128)(2,1)S(1)} %add_pair.11.refs_1_), channel_id=1, source_target_pairs={{0,8},{8,0},{16,24},{24,16},{1,9},{9,1},{17,25},{25,17},{2,10},{10... | collective-permute-start | bytes 786440 | tf_op jit(solution)/shard_map/ppermute | solution.py:298
  51.6 7.9 %collective-permute-start.17 = (bf16[128,1024]{1,0:T(8,128)(2,1)S(1)}, bf16[128,1024]{1,0:T(8,128)(2,1)S(1)}, u32[]{:S(2)}, u32[]{:S(2)}) collective-permute-start(bf16[128,1024]{1,0:T(8,128)(2,1)S(1)} %add_pair.9.refs_0_), channel_id=1, source_target_pairs={{0,8},{8,0},{16,24},{24,16},{1,9},{9,1},{17,25},{25,17},{2,10},{10... | collective-permute-start | bytes 786440 | tf_op jit(solution)/shard_map/ppermute | solution.py:298
  52.7 6.9 %collective-permute-start.20 = (bf16[128,1024]{1,0:T(8,128)(2,1)S(1)}, bf16[128,1024]{1,0:T(8,128)(2,1)S(1)}, u32[]{:S(2)}, u32[]{:S(2)}) collective-permute-start(bf16[128,1024]{1,0:T(8,128)(2,1)S(1)} %add_pair.15.refs_3_), channel_id=1, source_target_pairs={{0,8},{8,0},{16,24},{24,16},{1,9},{9,1},{17,25},{25,17},{2,10},{10... | collective-permute-start | bytes 786440 | tf_op jit(solution)/shard_map/ppermute | solution.py:298
  59.4 1.6 %collective-permute-start.19 = (bf16[128,1024]{1,0:T(8,128)(2,1)S(1)}, bf16[128,1024]{1,0:T(8,128)(2,1)S(1)}, u32[]{:S(2)}, u32[]{:S(2)}) collective-permute-start(bf16[128,1024]{1,0:T(8,128)(2,1)S(1)} %add_pair.13.refs_2_), channel_id=1, source_target_pairs={{0,8},{8,0},{16,24},{24,16},{1,9},{9,1},{17,25},{25,17},{2,10},{10... | collective-permute-start | bytes 786440 | tf_op jit(solution)/shard_map/ppermute | solution.py:298

commit v3 on v2

--- a/solution.py
+++ b/solution.py
@@ -9,15 +9,15 @@
 
 BF16 = jnp.bfloat16
 F32 = jnp.float32
-VMEM_LIMIT = 28 * 1024 * 1024
+MIB = 1024 * 1024
 ANY = pl.BlockSpec(memory_space=pl.ANY)
 HBM = pl.BlockSpec(memory_space=pltpu.HBM)
 VMEM = pl.BlockSpec(memory_space=pltpu.VMEM)
 SMEM = pl.BlockSpec(memory_space=pltpu.SMEM)
 
 
-def call_params():
-    return pltpu.CompilerParams(vmem_limit_bytes=VMEM_LIMIT)
+def call_params(mib=8):
+    return pltpu.CompilerParams(vmem_limit_bytes=mib * MIB)
 
 
 def cost(flops, bytes_accessed, transcendentals=0):
@@ -32,15 +32,16 @@
     return pl.multiple_of(index * rows, rows)
 
 
-def rate_partial(doc_topics, word_logits, log_norm, place, n_topic):
+def rate_partial(doc_topics, word_logits, log_norm, n_topic):
     docs, width = doc_topics.shape
     words = word_logits.shape[0]
     span = min(width, 1024)
     steps = width // span
     chunk = words // n_topic
 
-    def kernel(place_ref, doc_in, logit_in, norm_ref, *rest):
-        parts, (doc_ref, prob_ref, logit_ref, acc, sems) = rest[:n_topic], rest[n_topic:]
+    def kernel(doc_in, logit_in, norm_in, part_ref, doc_ref, prob_ref, norm_ref, logit_ref, acc, sems, norm_sem):
+        norm_copy = pltpu.make_async_copy(norm_in, norm_ref, norm_sem)
+        norm_copy.start()
         copies = []
         for j in range(steps):
             at = pl.ds(j * span, span)
@@ -53,6 +54,7 @@
         for pair in copies:
             for copy in pair:
                 copy.start()
+        norm_copy.wait()
         for j in range(steps):
             at = pl.ds(j * span, span)
             copies[j][0].wait()
@@ -67,25 +69,28 @@
             else:
                 acc[...] += part
         for s in range(n_topic):
-            owner = lax.rem(place_ref[0] + s, n_topic)
-            parts[s][...] = acc[pl.ds(first_row(owner, chunk), chunk), :].astype(BF16)
-
-    out = pl.pallas_call(
-        kernel,
-        out_shape=[jax.ShapeDtypeStruct((chunk, docs), BF16)] * n_topic
-        + [jax.ShapeDtypeStruct(doc_topics.shape, BF16), jax.ShapeDtypeStruct(word_logits.shape, BF16)],
-        in_specs=[SMEM, HBM, HBM, VMEM],
-        out_specs=[VMEM] * (n_topic + 2),
+            part_ref[s] = acc[s * chunk : (s + 1) * chunk, :].astype(BF16)
+
+    return pl.pallas_call(
+        kernel,
+        out_shape=[
+            jax.ShapeDtypeStruct((n_topic, chunk, docs), BF16),
+            jax.ShapeDtypeStruct(doc_topics.shape, BF16),
+            jax.ShapeDtypeStruct(word_logits.shape, BF16),
+            jax.ShapeDtypeStruct(log_norm.shape, F32),
+        ],
+        in_specs=[HBM, HBM, HBM],
+        out_specs=[VMEM] * 4,
         scratch_shapes=[
             pltpu.VMEM(word_logits.shape, BF16),
             pltpu.VMEM((words, docs), F32),
             pltpu.SemaphoreType.DMA((2, steps)),
+            pltpu.SemaphoreType.DMA,
         ],
-        compiler_params=call_params(),
+        compiler_params=call_params(16),
         cost_estimate=cost(2 * words * docs * width, 2 * (words + docs) * width, words * width),
         name="rate_partial",
-    )(place, in_hbm(doc_topics), in_hbm(word_logits), log_norm)
-    return out[:n_topic], out[n_topic], out[n_topic + 1]
+    )(in_hbm(doc_topics), in_hbm(word_logits), in_hbm(log_norm))
 
 
 def chunk_counts(word_counts, tile_doc, tile_word, place, n_topic, docs, words):
@@ -115,40 +120,23 @@
 
 
 def ratio_chunk(parts, counts, word_tile):
-    def kernel(*refs):
-        part_refs, count_ref, out_ref = refs[:-2], refs[-2], refs[-1]
-        rate = part_refs[0][...].astype(F32)
-        for ref in part_refs[1:]:
-            rate += ref[...].astype(F32)
-        out_ref[...] = (count_ref[...] / (word_tile * rate)).astype(BF16)
-
-    return pl.pallas_call(
-        kernel,
-        out_shape=jax.ShapeDtypeStruct(counts.shape, BF16),
-        compiler_params=call_params(),
-        cost_estimate=cost(10 * counts.size, 16 * counts.size),
+    n_topic = parts.shape[0]
+
+    def kernel(part_ref, count_ref, out_ref):
+        rate = part_ref[0].astype(F32)
+        for s in range(1, n_topic):
+            rate += part_ref[s].astype(F32)
+        ratio = (count_ref[...] / (word_tile * rate)).astype(BF16)
+        for s in range(n_topic):
+            out_ref[s] = ratio
+
+    return pl.pallas_call(
+        kernel,
+        out_shape=jax.ShapeDtypeStruct(parts.shape, BF16),
+        compiler_params=call_params(),
+        cost_estimate=cost(10 * counts.size, 4 * parts.size),
         name="ratio_chunk",
-    )(*parts, counts)
-
-
-def join_ratio(chunks, place, n_topic):
-    rows, docs = chunks[0].shape
-
-    def kernel(place_ref, *refs):
-        out_ref = refs[-1]
-        for s in range(n_topic):
-            owner = lax.rem(place_ref[0] + n_topic - s, n_topic)
-            out_ref[pl.ds(first_row(owner, rows), rows), :] = refs[s][...]
-
-    return pl.pallas_call(
-        kernel,
-        out_shape=jax.ShapeDtypeStruct((rows * n_topic, docs), BF16),
-        in_specs=[SMEM] + [VMEM] * n_topic,
-        out_specs=VMEM,
-        compiler_params=call_params(),
-        cost_estimate=cost(0, 4 * rows * docs * n_topic),
-        name="join_ratio",
-    )(place, *chunks)
+    )(parts, counts)
 
 
 def beta_piece(ratio, docs_held, prob_held, side, piece, pieces, after):
@@ -200,7 +188,7 @@
 def theta_grad(ratio, far_ratios, prob_held, far_logits, log_norm, vocab_at, side):
     words, docs = ratio.shape
     half = words // 2
-    share = log_norm.shape[1]
+    share = far_logits[0].shape[1]
     far = len(far_ratios)
     count = far + 1
     span = min(share, 512)
@@ -238,14 +226,14 @@
             in_specs=[pl.BlockSpec((words, docs), lambda j, v, s: (0, 0))] * count
             + [pl.BlockSpec((words, span), lambda j, v, s: (0, v[0] * blocks + j))]
             + [pl.BlockSpec((half, span), lambda j, v, s: (0, j))] * (2 * far)
-            + [pl.BlockSpec((1, span), lambda j, v, s: (0, j))],
+            + [pl.BlockSpec((1, span), lambda j, v, s: (0, v[0] * blocks + j))],
             out_specs=[
                 pl.BlockSpec((docs, span), lambda j, v, s: (0, j)),
                 pl.BlockSpec((8, 128), lambda j, v, s: (0, 0)),
             ],
             scratch_shapes=[pltpu.VMEM((docs, count * words), BF16)],
         ),
-        compiler_params=call_params(),
+        compiler_params=call_params(16),
         cost_estimate=cost(
             2 * count * words * docs * share, (4 * docs + 2 * count * words) * share, count * words * share
         ),
@@ -299,7 +287,6 @@
 
     share = width // n_vocab
     half = words // 2
-    own_norm = lax.dynamic_slice_in_dim(norm, vocab_at * share, share, 1)
     far_logits = []
     for s in range(1, n_vocab):
         target = lax.rem(vocab_at + s, n_vocab)
@@ -308,14 +295,13 @@
         )
         far_logits += [near_half, swap(near_half, 1)]
 
-    parts, docs_held, prob_held = rate_partial(doc_topics, word_logits, norm, place, n_topic)
-    arrived = [parts[0]] + [shift(parts[s], "topic", n_topic, s) for s in range(1, n_topic)]
+    parts, docs_held, prob_held, norm_held = rate_partial(doc_topics, word_logits, norm, n_topic)
+    parts = lax.all_to_all(parts, "topic", 0, 0)
     counts = chunk_counts(word_counts, tile_doc, tile_word, place, n_topic, docs, words)
-    own_ratio = ratio_chunk(arrived, counts, word_tile)
-    chunks = [own_ratio] + [shift(own_ratio, "topic", n_topic, s) for s in range(1, n_topic)]
-    ratio = join_ratio(chunks, place, n_topic)
+    chunks = lax.all_to_all(ratio_chunk(parts, counts, word_tile), "topic", 0, 0)
+    ratio = chunks.reshape(words, docs)
     far_ratios = [shift(ratio, "vocab", n_vocab, s) for s in range(1, n_vocab)]
-    theta, theta_done = theta_grad(ratio, far_ratios, prob_held, far_logits, own_norm, vocab_at[None], side[None])
+    theta, theta_done = theta_grad(ratio, far_ratios, prob_held, far_logits, norm_held, vocab_at[None], side[None])
 
     pieces = 4
     halves, sums = [], []

time: 62.8 us -> 70.4 us (1.12)
  blocking collectives: 0 us -> 10.6 us
  starting transfers between devices: 20.1 us -> 15.1 us
  Pallas kernels: 16.3 us -> 13.7 us
  local copies, waits for them, and re-layouts: 4.33 us -> 6.61 us
  waiting for transfers between devices: 20.9 us -> 23.1 us
    all_to_all x0 -> x1, blocking collectives: none -> 10.6 us  [on_device(): lax.all_to_all(ratio_chunk(parts, counts, word_tile), 'topic', 0, 0)]
    ppermute x8 -> x2, starting transfers between devices: 12.9 us -> 3.04 us  [shift(): lax.ppermute(array, axis, [(i, (i + by) % count) for i in range(count)])]
    all_to_all x0 -> x1, starting transfers between devices: none -> 6.32 us  [on_device(): parts = lax.all_to_all(parts, 'topic', 0, 0)]
    all_to_all x0 -> x1, waiting for transfers between devices: none -> 4.8 us  [on_device(): parts = lax.all_to_all(parts, 'topic', 0, 0)]
    ppermute x8 -> x2, waiting for transfers between devices: 6.96 us -> 2.43 us  [shift(): lax.ppermute(array, axis, [(i, (i + by) % count) for i in range(count)])]
    pallas_call x8, Pallas kernels: 3.36 us -> 0.52 us  [add_pair(): pl.pallas_call(kernel, out_shape=jax.ShapeDtypeStruct(own.shape, BF16), i...]
    unnamed x14 -> x16, local copies, waits for them, and re-layouts: 2.39 us -> 4.73 us
    ppermute x13, waiting for transfers between devices: 14 us -> 15.8 us  [swap(): return lax.ppermute(array, 'doc', [(i, i ^ bit) for i in range(n_doc)])]
  transfers between devices with their start and end apart: 21 -> 16, of which waited for: 9 -> 7; matrix products, arithmetic and copies ran while one was open for 0% -> 3% of each run, Pallas kernels for 24% -> 10%
where the time goes in v3:
time: 70.4 us; the launch traced here: 70 us
  waiting for transfers between devices  23.1 us (33%)
  starting transfers between devices  15.1 us (21%)
  Pallas kernels  13.7 us (19%)
  blocking collectives  10.6 us (15%)
  local copies, waits for them, and re-layouts  6.61 us (9%)
  between operations  0.86 us (1%)
    ppermute x13, waiting for transfers between devices, swap(): return lax.ppermute(array, 'doc', [(i, i ^ bit) for i in range(n_doc)])  15.8 us
    all_to_all x1, blocking collectives, on_device(): lax.all_to_all(ratio_chunk(parts, counts, word_tile), 'topic', 0, 0)  10.6 us
    all_to_all x1, starting transfers between devices, on_device(): parts = lax.all_to_all(parts, 'topic', 0, 0)  6.32 us
    ppermute x13, starting transfers between devices, swap(): return lax.ppermute(array, 'doc', [(i, i ^ bit) for i in range(n_doc)])  5.78 us
    pallas_call x1, Pallas kernels, rate_partial(): pl.pallas_call(kernel, out_shape=[jax.ShapeDtypeStruct((n_topic, chunk, d...  5.4 us
    all_to_all x1, waiting for transfers between devices, on_device(): parts = lax.all_to_all(parts, 'topic', 0, 0)  4.8 us
    unnamed x16, local copies, waits for them, and re-layouts  4.73 us
    pallas_call x1, Pallas kernels, theta_grad(): pl.pallas_call(kernel, out_shape=[jax.ShapeDtypeStruct((docs, share), F32...  3.68 us
  transfers between devices with their start and end apart: 16, of which 7 were waited for; matrix products, arithmetic and copies ran while one was open for 3% of the time, Pallas kernels for 10%

profile of v3, /device:TPU:0, one launch (start us, length us, event | category | flops | bytes accessed | tf_op | source)
XLA Modules:
  0.0 70.0 jit_solution(405367202171993932)
XLA Ops:
  0.7 5.4 %rate_partial.1 = (bf16[4,64,512]{2,1,0:T(8,128)(2,1)}, bf16[512,4096]{1,0:T(8,128)(2,1)S(1)}, bf16[256,4096]{1,0:T(8,128)(2,1)S(1)}, f32[1,4096]{1,0:T(1,128)S(1)}) custom-call(bf16[512,4096]{1,0:T(8,128)(2,1)} %doc_in.1, bf16[256,4096]{1,0:T(8,128)(2,1)} %logit_in.1, f32[1,4096]{1,0:T(1,128)} %bitcast.11), custom_call_target="tpu_custom_call" | custom-call | flops 1073741824 | bytes 6291456 | tf_op jit(solution)/shard_map/rate_partial/pallas_call | solution.py:74
  6.1 2.0 %copy-done = bf16[512,4096]{1,0:T(8,128)(2,1)} copy-done((bf16[512,4096]{1,0:T(8,128)(2,1)}, bf16[512,4096]{1,0:T(8,128)(2,1)S(1)}, u32[]{:S(2)}) %copy-start) | copy-done | bytes 4194328
  8.1 6.3 %all-to-all-start = ((bf16[4,64,512]{2,1,0:T(8,128)(2,1)}), bf16[4,64,512]{2,1,0:T(8,128)(2,1)S(1)}, u32[]{:S(2)}, u32[]{:S(2)}) async-start(bf16[4,64,512]{2,1,0:T(8,128)(2,1)} %get-tuple-element.16), calls=%async_computation | async-start | bytes 524288 | tf_op jit(solution)/shard_map/all_to_all | solution.py:299
  14.4 1.9 %dynamic_slice.3 = bf16[128,2048]{1,0:T(8,128)(2,1)} dynamic-slice(bf16[256,4096]{1,0:T(8,128)(2,1)} %logit_in.1, s32[]{:T(128)S(6)} %select_n.6, s32[]{:T(128)S(6)} %select_n.7), dynamic_slice_sizes={128,2048} | dynamic-slice | bytes 1048580 | tf_op jit(solution)/shard_map/dynamic_slice | solution.py:294
  16.3 1.5 %collective-permute-start.1 = (bf16[128,2048]{1,0:T(8,128)(2,1)}, bf16[128,2048]{1,0:T(8,128)(2,1)S(1)}, u32[]{:S(2)}, u32[]{:S(2)}) collective-permute-start(bf16[128,2048]{1,0:T(8,128)(2,1)} %dynamic_slice.3), channel_id=1, source_target_pairs={{0,1},{1,0},{2,3},{3,2},{4,5},{5,4},{6,7},{7,6},{8,9},{9,8},{10,11... | collective-permute-start | bytes 1572872 | tf_op jit(solution)/shard_map/ppermute | solution.py:283
  17.8 0.7 chunk_counts.1.count_ref
  18.5 4.8 %all-to-all-done.part_ref = bf16[4,64,512]{2,1,0:T(8,128)(2,1)S(1)} async-done(((bf16[4,64,512]{2,1,0:T(8,128)(2,1)}), bf16[4,64,512]{2,1,0:T(8,128)(2,1)S(1)}, u32[]{:S(2)}, u32[]{:S(2)}) %all-to-all-start) | async-done | bytes 262176 | tf_op jit(solution)/shard_map/all_to_all | solution.py:299
  23.4 10.6 %all_to_all.10 = bf16[4,64,512]{2,1,0:T(8,128)(2,1)S(1)} all-to-all(bf16[4,64,512]{2,1,0:T(8,128)(2,1)S(1)} %ratio_chunk.1), channel_id=1, replica_groups=mesh['doc'=4,'topic'=4,'vocab'=2] {'topic'}, dimensions={0} | all-to-all | bytes 524288 | tf_op jit(solution)/shard_map/all_to_all | solution.py:301
  34.0 2.2 %copy-done.1 = bf16[512,4096]{1,0:T(8,128)(2,1)S(1)} copy-done((bf16[512,4096]{1,0:T(8,128)(2,1)S(1)}, bf16[512,4096]{1,0:T(8,128)(2,1)}, u32[]{:S(2)}) %copy-start.1) | copy-done | bytes 4194328
  36.2 0.5 beta_piece.5
  36.7 0.1 collective-permute-start.5
  36.8 0.5 beta_piece.4
  37.3 0.6 collective-permute-start.3
  37.8 0.1 collective-permute-start.2
  37.9 0.4 collective-permute-done.5.other_ref
  38.4 0.5 copy-done.2
  38.9 0.5 beta_piece.7
  39.5 0.5 beta_piece.6
  40.1 0.5 collective-permute-start.7
  40.6 1.5 %collective-permute-start = (bf16[256,512]{1,0:T(8,128)(2,1)S(1)}, bf16[256,512]{1,0:T(8,128)(2,1)S(1)}, u32[]{:S(2)}, u32[]{:S(2)}) collective-permute-start(bf16[256,512]{1,0:T(8,128)(2,1)S(1)} %bitcast.9), channel_id=1, source_target_pairs={{0,1},{1,0},{2,3},{3,2},{4,5},{5,4},{6,7},{7,6},{8,9},{9,8},{10,11... | collective-permute-start | bytes 786440 | tf_op jit(solution)/shard_map/ppermute | solution.py:283
  42.1 1.5 %collective-permute-start.6 = (bf16[128,1024]{1,0:T(8,128)(2,1)S(1)}, bf16[128,1024]{1,0:T(8,128)(2,1)S(1)}, u32[]{:S(2)}, u32[]{:S(2)}) collective-permute-start(bf16[128,1024]{1,0:T(8,128)(2,1)S(1)} %add_pair.10.own_ref.rest_0_), channel_id=1, source_target_pairs={{0,16},{8,24},{16,0},{24,8},{1,17},{9,25},{17,1},{25,9},{2,18},{10... | collective-permute-start | bytes 786440 | tf_op jit(solution)/shard_map/ppermute | solution.py:286
  43.6 0.5 collective-permute-start.4
  44.2 1.6 %collective-permute-start.10 = (bf16[128,1024]{1,0:T(8,128)(2,1)S(1)}, bf16[128,1024]{1,0:T(8,128)(2,1)S(1)}, u32[]{:S(2)}, u32[]{:S(2)}) collective-permute-start(bf16[128,1024]{1,0:T(8,128)(2,1)S(1)} %add_pair.14.own_ref), channel_id=1, source_target_pairs={{0,16},{8,24},{16,0},{24,8},{1,17},{9,25},{17,1},{25,9},{2,18},{10... | collective-permute-start | bytes 786440 | tf_op jit(solution)/shard_map/ppermute | solution.py:286
  45.9 0.6 collective-permute-start.8
  46.5 2.4 %collective-permute-done.refs_0_ = bf16[256,512]{1,0:T(8,128)(2,1)S(1)} collective-permute-done((bf16[256,512]{1,0:T(8,128)(2,1)S(1)}, bf16[256,512]{1,0:T(8,128)(2,1)S(1)}, u32[]{:S(2)}, u32[]{:S(2)}) %collective-permute-start) | collective-permute-done | bytes 262176 | tf_op jit(solution)/shard_map/ppermute | solution.py:283
  48.9 3.7 %theta_grad.1 = (f32[512,2048]{1,0:T(8,128)}, f32[8,128]{1,0:T(8,128)S(1)}) custom-call(s32[1]{0:T(128)} %bitcast.vocab_ref, s32[1]{0:T(128)} %bitcast.1.side_ref, bf16[256,512]{1,0:T(8,128)(2,1)S(1)} %bitcast.10, bf16[256,512]{1,0:T(8,128)(2,1)S(1)} %collective-permute-done.refs_0_, bf16[256,4096]{1,0:T(8,128)(2,1)S(1)} %get-tuple-element.17.refs_1_.prob_ref, ...), custom_call_target="tpu_custom_call" | custom-call | flops 1073741824 | bytes 6291456 | tf_op jit(solution)/shard_map/theta_grad/pallas_call | solution.py:220
  52.7 4.2 %collective-permute-done.4.other_ref = bf16[128,1024]{1,0:T(8,128)(2,1)S(1)} collective-permute-done((bf16[128,1024]{1,0:T(8,128)(2,1)S(1)}, bf16[128,1024]{1,0:T(8,128)(2,1)S(1)}, u32[]{:S(2)}, u32[]{:S(2)}) %collective-permute-start.4) | collective-permute-done | bytes 262176 | tf_op jit(solution)/shard_map/ppermute | solution.py:286
  57.1 5.5 %collective-permute-done.10.other_ref = bf16[128,1024]{1,0:T(8,128)(2,1)S(1)} collective-permute-done((bf16[128,1024]{1,0:T(8,128)(2,1)S(1)}, bf16[128,1024]{1,0:T(8,128)(2,1)S(1)}, u32[]{:S(2)}, u32[]{:S(2)}) %collective-permute-start.10) | collective-permute-done | bytes 262176 | tf_op jit(solution)/shard_map/ppermute | solution.py:286
  62.6 0.1 collective-permute-start.14
  62.7 4.3 %collective-permute-done.8.other_ref = bf16[128,1024]{1,0:T(8,128)(2,1)S(1)} collective-permute-done((bf16[128,1024]{1,0:T(8,128)(2,1)S(1)}, bf16[128,1024]{1,0:T(8,128)(2,1)S(1)}, u32[]{:S(2)}, u32[]{:S(2)}) %collective-permute-start.8) | collective-permute-done | bytes 262176 | tf_op jit(solution)/shard_map/ppermute | solution.py:286
  67.2 1.5 %collective-permute-done.13.refs_6_ = bf16[128,1024]{1,0:T(8,128)(2,1)S(1)} collective-permute-done((bf16[128,1024]{1,0:T(8,128)(2,1)S(1)}, bf16[128,1024]{1,0:T(8,128)(2,1)S(1)}, u32[]{:S(2)}, u32[]{:S(2)}) %collective-permute-start.13) | collective-permute-done | bytes 262176 | tf_op jit(solution)/shard_map/ppermute | solution.py:286
  68.7 1.4 %place_pieces.1 = bf16[256,4096]{1,0:T(8,128)(2,1)} custom-call(s32[1]{0:T(128)} %bitcast.1.side_ref, bf16[128,1024]{1,0:T(8,128)(2,1)S(1)} %add_pair.9.refs_0_, bf16[128,1024]{1,0:T(8,128)(2,1)S(1)} %add_pair.11.refs_1_, bf16[128,1024]{1,0:T(8,128)(2,1)S(1)} %add_pair.13.refs_2_, bf16[128,1024]{1,0:T(8,128)(2,1)S(1)} %add_pair.15.refs_3_, ...), custom_call_target="tpu_custom_call" | custom-call | bytes 4194304 | tf_op jit(solution)/shard_map/place_pieces/pallas_call | solution.py:260
  (35 shorter events, 0.9 us)
Async XLA Ops:
  0.6 17.2 %copy-start.5 = (s32[16]{0:T(128)S(1)}, s32[16]{0:T(128)}, u32[]{:S(2)}) copy-start(s32[16]{0:T(128)} %word_at.1) | copy-start | bytes 196
  0.6 17.2 %copy-start.3 = (s32[16,64,128]{2,1,0:T(8,128)S(1)}, s32[16,64,128]{2,1,0:T(8,128)}, u32[]{:S(2)}) copy-start(s32[16,64,128]{2,1,0:T(8,128)} %count_ref.1) | copy-start | bytes 1572868
  0.7 17.2 %copy-start.4 = (s32[16]{0:T(128)S(1)}, s32[16]{0:T(128)}, u32[]{:S(2)}) copy-start(s32[16]{0:T(128)} %doc_at.1) | copy-start | bytes 196
  6.1 2.0 %copy-start = (bf16[512,4096]{1,0:T(8,128)(2,1)}, bf16[512,4096]{1,0:T(8,128)(2,1)S(1)}, u32[]{:S(2)}) copy-start(bf16[512,4096]{1,0:T(8,128)(2,1)S(1)} %get-tuple-element.20.doc_ref) | copy-start | bytes 12582916
  8.1 9.7 %copy-start.6 = (f32[1,4096]{1,0:T(1,128)}, f32[1,4096]{1,0:T(1,128)S(1)}, u32[]{:S(2)}) copy-start(f32[1,4096]{1,0:T(1,128)S(1)} %get-tuple-element.18.refs_4_) | copy-start | bytes 49156
  8.1 15.2 %all-to-all-start = ((bf16[4,64,512]{2,1,0:T(8,128)(2,1)}), bf16[4,64,512]{2,1,0:T(8,128)(2,1)S(1)}, u32[]{:S(2)}, u32[]{:S(2)}) async-start(bf16[4,64,512]{2,1,0:T(8,128)(2,1)} %get-tuple-element.16), calls=%async_computation | async-start | bytes 524288 | tf_op jit(solution)/shard_map/all_to_all | solution.py:299
  16.3 21.5 %collective-permute-start.1 = (bf16[128,2048]{1,0:T(8,128)(2,1)}, bf16[128,2048]{1,0:T(8,128)(2,1)S(1)}, u32[]{:S(2)}, u32[]{:S(2)}) collective-permute-start(bf16[128,2048]{1,0:T(8,128)(2,1)} %dynamic_slice.3), channel_id=1, source_target_pairs={{0,1},{1,0},{2,3},{3,2},{4,5},{5,4},{6,7},{7,6},{8,9},{9,8},{10,11... | collective-permute-start | bytes 1572872 | tf_op jit(solution)/shard_map/ppermute | solution.py:283
  34.0 2.2 %copy-start.1 = (bf16[512,4096]{1,0:T(8,128)(2,1)S(1)}, bf16[512,4096]{1,0:T(8,128)(2,1)}, u32[]{:S(2)}) copy-start(bf16[512,4096]{1,0:T(8,128)(2,1)} %copy-done) | copy-start | bytes 12582916
  36.7 2.2 %copy-start.2 = (bf16[512,4096]{1,0:T(8,128)(2,1)S(1)}, bf16[512,4096]{1,0:T(8,128)(2,1)}, u32[]{:S(2)}) copy-start(bf16[512,4096]{1,0:T(8,128)(2,1)} %copy-done) | copy-start | bytes 12582916
  36.7 1.6 %collective-permute-start.5 = (bf16[128,1024]{1,0:T(8,128)(2,1)S(1)}, bf16[128,1024]{1,0:T(8,128)(2,1)S(1)}, u32[]{:S(2)}, u32[]{:S(2)}) collective-permute-start(bf16[128,1024]{1,0:T(8,128)(2,1)S(1)} %get-tuple-element.24), channel_id=1, source_target_pairs={{0,8},{8,0},{16,24},{24,16},{1,9},{9,1},{17,25},{25,17},{2,10},{10... | collective-permute-start | bytes 786440 | tf_op jit(solution)/shard_map/ppermute | solution.py:286
  37.3 2.2 %collective-permute-start.3 = (bf16[128,1024]{1,0:T(8,128)(2,1)S(1)}, bf16[128,1024]{1,0:T(8,128)(2,1)S(1)}, u32[]{:S(2)}, u32[]{:S(2)}) collective-permute-start(bf16[128,1024]{1,0:T(8,128)(2,1)S(1)} %get-tuple-element.22), channel_id=1, source_target_pairs={{0,8},{8,0},{16,24},{24,16},{1,9},{9,1},{17,25},{25,17},{2,10},{10... | collective-permute-start | bytes 786440 | tf_op jit(solution)/shard_map/ppermute | solution.py:286
  37.8 8.0 %collective-permute-start.2 = (bf16[128,2048]{1,0:T(8,128)(2,1)S(1)}, bf16[128,2048]{1,0:T(8,128)(2,1)S(1)}, u32[]{:S(2)}, u32[]{:S(2)}) collective-permute-start(bf16[128,2048]{1,0:T(8,128)(2,1)S(1)} %collective-permute-done.1.refs_2_), channel_id=1, source_target_pairs={{0,8},{8,0},{16,24},{24,16},{1,9},{9,1},{17,25},{25,17},{2,10},{10... | collective-permute-start | bytes 1572872 | tf_op jit(solution)/shard_map/ppermute | solution.py:286
  39.4 4.2 %collective-permute-start.9 = (bf16[128,1024]{1,0:T(8,128)(2,1)S(1)}, bf16[128,1024]{1,0:T(8,128)(2,1)S(1)}, u32[]{:S(2)}, u32[]{:S(2)}) collective-permute-start(bf16[128,1024]{1,0:T(8,128)(2,1)S(1)} %get-tuple-element.29), channel_id=1, source_target_pairs={{0,8},{8,0},{16,24},{24,16},{1,9},{9,1},{17,25},{25,17},{2,10},{10... | collective-permute-start | bytes 786440 | tf_op jit(solution)/shard_map/ppermute | solution.py:286
  39.5 9.4 %copy-start.7 = (f32[1,4096]{1,0:T(1,128)S(1)}, f32[1,4096]{1,0:T(1,128)}, u32[]{:S(2)}) copy-start(f32[1,4096]{1,0:T(1,128)} %copy-done.6) | copy-start | bytes 49156
  40.1 4.2 %collective-permute-start.7 = (bf16[128,1024]{1,0:T(8,128)(2,1)S(1)}, bf16[128,1024]{1,0:T(8,128)(2,1)S(1)}, u32[]{:S(2)}, u32[]{:S(2)}) collective-permute-start(bf16[128,1024]{1,0:T(8,128)(2,1)S(1)} %get-tuple-element.26), channel_id=1, source_target_pairs={{0,8},{8,0},{16,24},{24,16},{1,9},{9,1},{17,25},{25,17},{2,10},{10... | collective-permute-start | bytes 786440 | tf_op jit(solution)/shard_map/ppermute | solution.py:286
  40.6 8.3 %collective-permute-start = (bf16[256,512]{1,0:T(8,128)(2,1)S(1)}, bf16[256,512]{1,0:T(8,128)(2,1)S(1)}, u32[]{:S(2)}, u32[]{:S(2)}) collective-permute-start(bf16[256,512]{1,0:T(8,128)(2,1)S(1)} %bitcast.9), channel_id=1, source_target_pairs={{0,1},{1,0},{2,3},{3,2},{4,5},{5,4},{6,7},{7,6},{8,9},{9,8},{10,11... | collective-permute-start | bytes 786440 | tf_op jit(solution)/shard_map/ppermute | solution.py:283
  42.1 10.5 %collective-permute-start.6 = (bf16[128,1024]{1,0:T(8,128)(2,1)S(1)}, bf16[128,1024]{1,0:T(8,128)(2,1)S(1)}, u32[]{:S(2)}, u32[]{:S(2)}) collective-permute-start(bf16[128,1024]{1,0:T(8,128)(2,1)S(1)} %add_pair.10.own_ref.rest_0_), channel_id=1, source_target_pairs={{0,16},{8,24},{16,0},{24,8},{1,17},{9,25},{17,1},{25,9},{2,18},{10... | collective-permute-start | bytes 786440 | tf_op jit(solution)/shard_map/ppermute | solution.py:286
  43.6 13.3 %collective-permute-start.4 = (bf16[128,1024]{1,0:T(8,128)(2,1)S(1)}, bf16[128,1024]{1,0:T(8,128)(2,1)S(1)}, u32[]{:S(2)}, u32[]{:S(2)}) collective-permute-start(bf16[128,1024]{1,0:T(8,128)(2,1)S(1)} %add_pair.8.own_ref.rest_0_), channel_id=1, source_target_pairs={{0,16},{8,24},{16,0},{24,8},{1,17},{9,25},{17,1},{25,9},{2,18},{10... | collective-permute-start | bytes 786440 | tf_op jit(solution)/shard_map/ppermute | solution.py:286
  44.2 18.3 %collective-permute-start.10 = (bf16[128,1024]{1,0:T(8,128)(2,1)S(1)}, bf16[128,1024]{1,0:T(8,128)(2,1)S(1)}, u32[]{:S(2)}, u32[]{:S(2)}) collective-permute-start(bf16[128,1024]{1,0:T(8,128)(2,1)S(1)} %add_pair.14.own_ref), channel_id=1, source_target_pairs={{0,16},{8,24},{16,0},{24,8},{1,17},{9,25},{17,1},{25,9},{2,18},{10... | collective-permute-start | bytes 786440 | tf_op jit(solution)/shard_map/ppermute | solution.py:286
  45.9 21.1 %collective-permute-start.8 = (bf16[128,1024]{1,0:T(8,128)(2,1)S(1)}, bf16[128,1024]{1,0:T(8,128)(2,1)S(1)}, u32[]{:S(2)}, u32[]{:S(2)}) collective-permute-start(bf16[128,1024]{1,0:T(8,128)(2,1)S(1)} %add_pair.12.own_ref), channel_id=1, source_target_pairs={{0,16},{8,24},{16,0},{24,8},{1,17},{9,25},{17,1},{25,9},{2,18},{10... | collective-permute-start | bytes 786440 | tf_op jit(solution)/shard_map/ppermute | solution.py:286
  52.6 14.5 %collective-permute-start.12 = (bf16[128,1024]{1,0:T(8,128)(2,1)S(1)}, bf16[128,1024]{1,0:T(8,128)(2,1)S(1)}, u32[]{:S(2)}, u32[]{:S(2)}) collective-permute-start(bf16[128,1024]{1,0:T(8,128)(2,1)S(1)} %add_pair.11.refs_1_), channel_id=1, source_target_pairs={{0,8},{8,0},{16,24},{24,16},{1,9},{9,1},{17,25},{25,17},{2,10},{10... | collective-permute-start | bytes 786440 | tf_op jit(solution)/shard_map/ppermute | solution.py:286
  57.0 10.1 %collective-permute-start.11 = (bf16[128,1024]{1,0:T(8,128)(2,1)S(1)}, bf16[128,1024]{1,0:T(8,128)(2,1)S(1)}, u32[]{:S(2)}, u32[]{:S(2)}) collective-permute-start(bf16[128,1024]{1,0:T(8,128)(2,1)S(1)} %add_pair.9.refs_0_), channel_id=1, source_target_pairs={{0,8},{8,0},{16,24},{24,16},{1,9},{9,1},{17,25},{25,17},{2,10},{10... | collective-permute-start | bytes 786440 | tf_op jit(solution)/shard_map/ppermute | solution.py:286
  62.6 4.5 %collective-permute-start.14 = (bf16[128,1024]{1,0:T(8,128)(2,1)S(1)}, bf16[128,1024]{1,0:T(8,128)(2,1)S(1)}, u32[]{:S(2)}, u32[]{:S(2)}) collective-permute-start(bf16[128,1024]{1,0:T(8,128)(2,1)S(1)} %add_pair.15.refs_3_), channel_id=1, source_target_pairs={{0,8},{8,0},{16,24},{24,16},{1,9},{9,1},{17,25},{25,17},{2,10},{10... | collective-permute-start | bytes 786440 | tf_op jit(solution)/shard_map/ppermute | solution.py:286
  67.1 1.6 %collective-permute-start.13 = (bf16[128,1024]{1,0:T(8,128)(2,1)S(1)}, bf16[128,1024]{1,0:T(8,128)(2,1)S(1)}, u32[]{:S(2)}, u32[]{:S(2)}) collective-permute-start(bf16[128,1024]{1,0:T(8,128)(2,1)S(1)} %add_pair.13.refs_2_), channel_id=1, source_target_pairs={{0,8},{8,0},{16,24},{24,16},{1,9},{9,1},{17,25},{25,17},{2,10},{10... | collective-permute-start | bytes 786440 | tf_op jit(solution)/shard_map/ppermute | solution.py:286

commit v4 on v3

v4 whole, which is shorter than its diff:
```python
import functools

import jax
import jax.numpy as jnp
from jax import lax
from jax.experimental import pallas as pl
from jax.experimental.pallas import tpu as pltpu
from jax.sharding import PartitionSpec as P

BF16 = jnp.bfloat16
F32 = jnp.float32
MIB = 1024 * 1024
ANY = pl.BlockSpec(memory_space=pl.ANY)
HBM = pl.BlockSpec(memory_space=pltpu.HBM)
VMEM = pl.BlockSpec(memory_space=pltpu.VMEM)
SMEM = pl.BlockSpec(memory_space=pltpu.SMEM)


def call_params(mib=8):
    return pltpu.CompilerParams(vmem_limit_bytes=mib * MIB)


def cost(flops, bytes_accessed, transcendentals=0):
    return pl.CostEstimate(flops=flops, bytes_accessed=bytes_accessed, transcendentals=transcendentals)


def in_hbm(array):
    return pltpu.with_memory_space_constraint(array, pltpu.HBM)


def first_row(index, rows):
    return pl.multiple_of(index * rows, rows)


def fetch(doc_topics, word_logits, log_norm, vocab_at, side, n_vocab, early, plain):
    docs, width = doc_topics.shape
    half, share = word_logits.shape[0] // 2, width // n_vocab
    far = n_vocab - 1
    widths = [w for w in (early, plain) if w]

    def kernel(vocab_ref, side_ref, doc_in, logit_in, norm_in, *rest):
        outs, sems = rest[:-1], rest[-1]
        sources = []
        if early:
            sources.append(doc_in.at[:, pl.ds(first_row(vocab_ref[0], early), early)])
        if plain:
            sources.append(doc_in.at[:, pl.ds(early * n_vocab, plain)])
        for s in range(1, n_vocab):
            target = lax.rem(vocab_ref[0] + s, n_vocab)
            rows, columns = pl.ds(first_row(side_ref[0], half), half), pl.ds(first_row(target, share), share)
            sources.append(logit_in.at[rows, columns])
        sources.append(norm_in)
        copies = [pltpu.make_async_copy(source, out, sems.at[i]) for i, (source, out) in enumerate(zip(sources, outs))]
        for copy in copies:
            copy.start()
        for copy in copies:
            copy.wait()

    count = len(widths) + far + 1
    out = pl.pallas_call(
        kernel,
        out_shape=[jax.ShapeDtypeStruct((docs, w), BF16) for w in widths]
        + [jax.ShapeDtypeStruct((half, share), BF16)] * far
        + [jax.ShapeDtypeStruct(log_norm.shape, F32)],
        in_specs=[SMEM, SMEM, HBM, HBM, HBM],
        out_specs=[VMEM] * count,
        scratch_shapes=[pltpu.SemaphoreType.DMA((count,))],
        compiler_params=call_params(),
        cost_estimate=cost(0, 4 * docs * sum(widths) + 4 * half * share * far),
        name="fetch",
    )(vocab_at, side, in_hbm(doc_topics), in_hbm(word_logits), in_hbm(log_norm))
    return out[: len(widths)], out[len(widths) : -1], out[-1]


def rate_partial(doc_topics, word_logits, log_norm, bit):
    docs, width = doc_topics.shape
    words = word_logits.shape[0]
    span = min(width, 1024)
    steps = width // span
    half = words // 2

    def kernel(bit_ref, doc_in, logit_in, norm_ref, keep_ref, send_ref, doc_ref, prob_ref, logit_ref, acc, sems):
        copies = []
        for j in range(steps):
            at = pl.ds(j * span, span)
            copies.append(
                (
                    pltpu.make_async_copy(logit_in.at[:, at], logit_ref.at[:, at], sems.at[0, j]),
                    pltpu.make_async_copy(doc_in.at[:, at], doc_ref.at[:, at], sems.at[1, j]),
                )
            )
        for pair in copies:
            for copy in pair:
                copy.start()
        for j in range(steps):
            at = pl.ds(j * span, span)
            copies[j][0].wait()
            prob = jnp.exp(logit_ref[:, at].astype(F32) - norm_ref[:, at]).astype(BF16)
            prob_ref[:, at] = prob
            copies[j][1].wait()
            part = lax.dot_general(
                prob, doc_ref[:, at], (((1,), (1,)), ((), ())), preferred_element_type=F32
            )
            if j == 0:
                acc[...] = part
            else:
                acc[...] += part
        send_ref[...] = acc[pl.ds(first_row(1 - bit_ref[0], half), half), :].astype(BF16)
        keep_ref[...] = acc[pl.ds(first_row(bit_ref[0], half), half), :]

    return pl.pallas_call(
        kernel,
        out_shape=[
            jax.ShapeDtypeStruct((half, docs), F32),
            jax.ShapeDtypeStruct((half, docs), BF16),
            jax.ShapeDtypeStruct(doc_topics.shape, BF16),
            jax.ShapeDtypeStruct(word_logits.shape, BF16),
        ],
        in_specs=[SMEM, HBM, HBM, VMEM],
        out_specs=[VMEM] * 4,
        scratch_shapes=[
            pltpu.VMEM(word_logits.shape, BF16),
            pltpu.VMEM((words, docs), F32),
            pltpu.SemaphoreType.DMA((2, steps)),
        ],
        compiler_params=call_params(16),
        cost_estimate=cost(2 * words * docs * width, 2 * (words + docs) * width, words * width),
        name="rate_partial",
    )(bit, in_hbm(doc_topics), in_hbm(word_logits), log_norm)


def fold_rates(own, other, bit):
    rows, docs = own.shape
    half = rows // 2

    def kernel(bit_ref, own_ref, other_ref, keep_ref, send_ref):
        for which, out_ref in ((1 - bit_ref[0], send_ref), (bit_ref[0], keep_ref)):
            at = pl.ds(first_row(which, half), half)
            out_ref[...] = (own_ref[at, :] + other_ref[at, :].astype(F32)).astype(out_ref.dtype)

    return pl.pallas_call(
        kernel,
        out_shape=[jax.ShapeDtypeStruct((half, docs), F32), jax.ShapeDtypeStruct((half, docs), BF16)],
        in_specs=[SMEM, VMEM, VMEM],
        out_specs=[VMEM, VMEM],
        compiler_params=call_params(),
        cost_estimate=cost(own.size, 8 * own.size),
        name="fold_rates",
    )(bit, own, other)


def chunk_counts(word_counts, tile_doc, tile_word, place, n_topic, docs, words):
    slots, word_tile, doc_tile = word_counts.shape
    chunk = words // n_topic

    def kernel(place_ref, doc_at, word_at, count_ref, out_ref):
        first = place_ref[0] * chunk
        block = first // word_tile
        row = pl.multiple_of(lax.rem(first, word_tile), chunk)
        out_ref[...] = jnp.zeros_like(out_ref)
        for s in range(slots):
            @pl.when(word_at[s] == block)
            def _():
                column = first_row(doc_at[s], doc_tile)
                out_ref[:, pl.ds(column, doc_tile)] = count_ref[s, pl.ds(row, chunk), :].astype(F32)

    return pl.pallas_call(
        kernel,
        out_shape=jax.ShapeDtypeStruct((chunk, docs), F32),
        in_specs=[SMEM, SMEM, SMEM, VMEM],
        out_specs=VMEM,
        compiler_params=call_params(),
        cost_estimate=cost(words * docs, 4 * words * docs),
        name="chunk_counts",
    )(place, tile_doc, tile_word, word_counts)


def ratio_chunk(own, other, counts, word_tile):
    def kernel(own_ref, other_ref, count_ref, out_ref):
        rate = own_ref[...] + other_ref[...].astype(F32)
        out_ref[...] = (count_ref[...] / (word_tile * rate)).astype(BF16)

    return pl.pallas_call(
        kernel,
        out_shape=jax.ShapeDtypeStruct(counts.shape, BF16),
        in_specs=[VMEM] * 3,
        out_specs=VMEM,
        compiler_params=call_params(),
        cost_estimate=cost(10 * counts.size, 12 * counts.size),
        name="ratio_chunk",
    )(own, other, counts)


def join_rows(own, other, bit, after=()):
    rows, docs = own.shape

    def kernel(bit_ref, own_ref, other_ref, *rest):
        out_ref = rest[-1]
        out_ref[pl.ds(first_row(bit_ref[0], rows), rows), :] = own_ref[...]
        out_ref[pl.ds(first_row(1 - bit_ref[0], rows), rows), :] = other_ref[...]

    return pl.pallas_call(
        kernel,
        out_shape=jax.ShapeDtypeStruct((2 * rows, docs), BF16),
        in_specs=[SMEM, VMEM, VMEM] + [ANY] * len(after),
        out_specs=VMEM,
        compiler_params=call_params(),
        cost_estimate=cost(0, 8 * own.size),
        name="join_rows",
    )(bit, own, other, *after)


def hold(array, after):
    def kernel(in_ref, *rest):
        rest[-1][...] = in_ref[...]

    return pl.pallas_call(
        kernel,
        out_shape=jax.ShapeDtypeStruct(array.shape, array.dtype),
        in_specs=[VMEM] + [ANY] * len(after),
        out_specs=VMEM,
        compiler_params=call_params(),
        cost_estimate=cost(0, 4 * array.size),
        name="hold",
    )(array, *after)


def beta_piece(ratios, docs_held, far_docs, prob_held, side, column, span, after=()):
    docs = docs_held.shape[0]
    words = prob_held.shape[0]
    half = words // 2
    count = len(ratios)

    def kernel(column_ref, side_ref, *refs):
        ratio_refs, doc_ref, prob_ref, far_refs = refs[:count], refs[count], refs[count + 1], refs[count + 2 :]
        keep_ref, send_ref = refs[-2:]
        at = pl.ds(pl.multiple_of(column_ref[0], 128), span)
        for out_ref, which in ((send_ref, 1 - side_ref[0]), (keep_ref, side_ref[0])):
            rows = pl.ds(first_row(which, half), half)
            summed = jnp.dot(ratio_refs[0][rows, :], doc_ref[:, at], preferred_element_type=F32)
            if count > 1:
                summed += jnp.dot(ratio_refs[1][rows, :], far_refs[0][...], preferred_element_type=F32)
            out_ref[...] = (-prob_ref[rows, at].astype(F32) * summed).astype(BF16)

    return pl.pallas_call(
        kernel,
        out_shape=[jax.ShapeDtypeStruct((half, span), BF16)] * 2,
        in_specs=[SMEM, SMEM] + [VMEM] * (count + 2 + len(far_docs)) + [ANY] * len(after),
        out_specs=[VMEM, VMEM],
        compiler_params=call_params(16),
        cost_estimate=cost(2 * count * words * docs * span, 2 * (2 * words + count * docs) * span),
        name="beta_piece",
    )(column, side, *ratios, docs_held, prob_held, *far_docs, *after)


def add_pair(own, other, after=()):
    def kernel(own_ref, other_ref, *rest):
        rest[-1][...] = (own_ref[...].astype(F32) + other_ref[...].astype(F32)).astype(BF16)

    return pl.pallas_call(
        kernel,
        out_shape=jax.ShapeDtypeStruct(own.shape, BF16),
        in_specs=[VMEM, VMEM] + [ANY] * len(after),
        out_specs=VMEM,
        compiler_params=call_params(),
        cost_estimate=cost(own.size, 6 * own.size),
        name="add_pair",
    )(own, other, *after)


def theta_grad(ratio, far_ratios, prob_held, far_logits, log_norm, vocab_at, side, after):
    words, docs = ratio.shape
    half = words // 2
    share = far_logits[0].shape[1]
    far = len(far_ratios)
    count = far + 1
    span = min(share, 512)

    def kernel(vocab_ref, side_ref, ratio_ref, *refs):
        far_refs, prob_ref = refs[:far], refs[far]
        logit_refs, norm_ref = refs[far + 1 : 3 * far + 1], refs[3 * far + 1]
        out_ref, done_ref, turned = refs[-3:]
        done_ref[...] = jnp.zeros_like(done_ref)

        @pl.when(pl.program_id(0) == 0)
        def _():
            def put(rows, at):
                turned[:, at : at + rows.shape[0]] = (-rows.astype(F32)).T.astype(BF16)

            put(ratio_ref[...], 0)
            for l in range(far):
                for h in range(2):
                    which = side_ref[0] if h == 0 else 1 - side_ref[0]
                    put(far_refs[l][pl.ds(first_row(which, half), half), :], (l + 1) * words + h * half)

        prob = jnp.concatenate(
            [prob_ref[...]] + [jnp.exp(ref[...].astype(F32) - norm_ref[...]).astype(BF16) for ref in logit_refs],
            axis=0,
        )
        out_ref[...] = jnp.dot(turned[...], prob, preferred_element_type=F32)

    blocks = share // span
    return pl.pallas_call(
        kernel,
        out_shape=[jax.ShapeDtypeStruct((docs, share), F32), jax.ShapeDtypeStruct((8, 128), F32)],
        grid_spec=pltpu.PrefetchScalarGridSpec(
            num_scalar_prefetch=2,
            grid=(blocks,),
            in_specs=[pl.BlockSpec((words, docs), lambda j, v, s: (0, 0))] * count
            + [pl.BlockSpec((words, span), lambda j, v, s: (0, v[0] * blocks + j))]
            + [pl.BlockSpec((half, span), lambda j, v, s: (0, j))] * (2 * far)
            + [pl.BlockSpec((1, span), lambda j, v, s: (0, v[0] * blocks + j))]
            + [ANY] * len(after),
            out_specs=[
                pl.BlockSpec((docs, span), lambda j, v, s: (0, j)),
                pl.BlockSpec((8, 128), lambda j, v, s: (0, 0)),
            ],
            scratch_shapes=[pltpu.VMEM((docs, count * words), BF16)],
        ),
        compiler_params=call_params(16),
        cost_estimate=cost(
            2 * count * words * docs * share, (4 * docs + 2 * count * words) * share, count * words * share
        ),
        name="theta_grad",
    )(vocab_at, side, ratio, *far_ratios, prob_held, *far_logits, log_norm, *after)


def place_pieces(own, other, starts, side, shape):
    pieces = len(own)
    half = own[0].shape[0]

    def kernel(side_ref, *refs):
        start_refs, own_refs, other_refs = (refs[i * pieces : (i + 1) * pieces] for i in range(3))
        out_ref, sems = refs[-2:]
        copies = []
        for p in range(pieces):
            span = own_refs[p].shape[1]
            columns = pl.ds(pl.multiple_of(start_refs[p][0], 128), span)
            for h, (ref, which) in enumerate(((own_refs[p], side_ref[0]), (other_refs[p], 1 - side_ref[0]))):
                target = out_ref.at[pl.ds(first_row(which, half), half), columns]
                copies.append(pltpu.make_async_copy(ref, target, sems.at[h, p]))
        for copy in copies:
            copy.start()
        for copy in copies:
            copy.wait()

    return pl.pallas_call(
        kernel,
        out_shape=jax.ShapeDtypeStruct(shape, BF16),
        in_specs=[SMEM] * (1 + pieces) + [VMEM] * (2 * pieces),
        out_specs=HBM,
        scratch_shapes=[pltpu.SemaphoreType.DMA((2, pieces))],
        compiler_params=call_params(),
        cost_estimate=cost(0, 4 * shape[0] * shape[1]),
        name="place_pieces",
    )(side, *starts, *own, *other)


def on_device(sizes, doc_topics, word_logits, log_norm, tile_doc, tile_word, word_counts):
    n_doc, n_topic, n_vocab = sizes
    docs, width = doc_topics.shape
    words = word_logits.shape[0]
    word_tile = word_counts.shape[1]
    topic_at = lax.axis_index("topic").astype(jnp.int32)
    vocab_at = lax.axis_index("vocab").astype(jnp.int32)[None]
    side = lax.rem(lax.axis_index("doc").astype(jnp.int32), 2)[None]
    levels = n_topic.bit_length() - 1
    assert n_topic == 1 << levels and levels > 0
    bits = [lax.rem(lax.div(topic_at, jnp.int32(1 << b)), 2)[None] for b in range(levels)]
    place = sum(bits[b] << (levels - 1 - b) for b in range(levels))

    def shift(array, by):
        return lax.ppermute(array, "vocab", [(i, (i + by) % n_vocab) for i in range(n_vocab)])

    def swap(array, bit):
        return lax.ppermute(array, "doc", [(i, i ^ bit) for i in range(n_doc)])

    def swap_topic(array, level):
        return lax.ppermute(array, "topic", [(i, i ^ (1 << level)) for i in range(n_topic)])

    early, plain = width * 3 // 8 // n_vocab // 128 * 128, width // 16 // 128 * 128
    if n_doc != 4:
        early = plain = 0
    near_docs, near_logits, norm = fetch(
        doc_topics, word_logits, log_norm[None, :], vocab_at, side, n_vocab, early, plain
    )
    passed = [swap(part, 2) for part in near_docs]
    far_logits = []
    for s in range(1, n_vocab):
        part = shift(near_logits[s - 1], s)
        far_logits += [part, swap(part, 1)]

    keep, send, docs_held, prob_held = rate_partial(doc_topics, word_logits, norm, bits[0])
    for level in range(1, levels):
        keep, send = fold_rates(keep, swap_topic(send, level - 1), bits[level])
    counts = chunk_counts(word_counts, tile_doc, tile_word, place, n_topic, docs, words)
    own_ratio = ratio_chunk(keep, swap_topic(send, levels - 1), counts, word_tile)

    def gather(chunk, after=()):
        for level in reversed(range(levels)):
            chunk = join_rows(chunk, swap_topic(chunk, level), bits[level], () if level else after)
        return chunk

    ratio = gather(own_ratio, passed[1:])
    far_ratios = [shift(ratio, s) for s in range(1, n_vocab)]

    begin = early * n_vocab + plain
    pieces = 2 if begin else 4
    span = (width - begin) // pieces
    starts = [jnp.full((1,), begin + p * span, jnp.int32) for p in range(pieces)]
    halves, sums = [], []
    for p in range(pieces):
        after = [sums[p - 2]] if p >= 2 else []
        keep, send = beta_piece([ratio], docs_held, [], prob_held, side, starts[p], span, after)
        halves.append((keep, swap(send, 1)))
        if p >= 1:
            sums.append(add_pair(*halves[p - 1]))
    sums.append(add_pair(*halves[-1]))

    near_sums = []
    if begin:
        far_ratio = gather(hold(swap(own_ratio, 2), [sums[-1]]))
        groups = []
        if plain:
            groups.append((jnp.full((1,), early * n_vocab, jnp.int32), passed[-1]))
        if early:
            groups.append((vocab_at * early, passed[0]))
            ready = hold(passed[0], [own_ratio])
            for s in range(1, n_vocab):
                groups.append((lax.rem(vocab_at + n_vocab - s, n_vocab) * early, shift(ready, s)))
        for start, part in groups:
            keep, send = beta_piece([ratio, far_ratio], docs_held, [part], prob_held, side, start, part.shape[1])
            near_sums.append(add_pair(keep, swap(send, 1)))
            starts.append(start)
    theta, theta_done = theta_grad(
        ratio, far_ratios, prob_held, far_logits, norm, vocab_at, side, near_sums[: len(passed)]
    )
    bit = 2
    while bit < n_doc:
        sums = [
            add_pair(part, swap(part, bit), [theta_done] if p == pieces - 1 else []) for p, part in enumerate(sums)
        ]
        bit *= 2
    sums += near_sums
    out = place_pieces(sums, [swap(part, 1) for part in sums], starts, side, word_logits.shape)
    return theta, out


def solution(mesh):
    placed = (
        P("doc", "topic"),
        P("vocab", "topic"),
        P("topic"),
        P(("doc", "vocab")),
        P(("doc", "vocab")),
        P(("doc", "vocab"), None, None),
    )
    sizes = (mesh.shape["doc"], mesh.shape["topic"], mesh.shape["vocab"])
    return jax.shard_map(
        functools.partial(on_device, sizes),
        mesh=mesh,
        in_specs=placed,
        out_specs=(P("doc", ("topic", "vocab")), P("vocab", "topic")),
        check_vma=False,
    )
```

time: 70.4 us -> 74 us (1.051)
  blocking collectives: 10.6 us -> 0 us
  starting transfers between devices: 15.1 us -> 25.1 us
  local copies, waits for them, and re-layouts: 6.61 us -> 8.65 us
  Pallas kernels: 13.7 us -> 15.5 us
    ppermute x2 -> x9, waiting for transfers between devices: 2.43 us -> 20 us  [the longest x6 16.9 us: swap_topic(): lax.ppermute(array, 'topic', [(i, i ^ 1 << level) for i in range(n_topic)])]
    ppermute x13 -> x16, waiting for transfers between devices: 15.8 us -> 3.61 us  [swap(): return lax.ppermute(array, 'doc', [(i, i ^ bit) for i in range(n_doc)])]
    ppermute x2 -> x9, starting transfers between devices: 3.04 us -> 15.3 us  [the longest x6 11.6 us: swap_topic(): lax.ppermute(array, 'topic', [(i, i ^ 1 << level) for i in range(n_topic)])]
    all_to_all x1 -> x0, blocking collectives: 10.6 us -> none  [on_device(): lax.all_to_all(ratio_chunk(parts, counts, word_tile), 'topic', 0, 0)]
    all_to_all x1 -> x0, starting transfers between devices: 6.32 us -> none  [on_device(): parts = lax.all_to_all(parts, 'topic', 0, 0)]
    all_to_all x1 -> x0, waiting for transfers between devices: 4.8 us -> none  [on_device(): parts = lax.all_to_all(parts, 'topic', 0, 0)]
    ppermute x13 -> x16, starting transfers between devices: 5.78 us -> 9.89 us  [swap(): return lax.ppermute(array, 'doc', [(i, i ^ bit) for i in range(n_doc)])]
    unnamed x16 -> x18, local copies, waits for them, and re-layouts: 4.73 us -> 8.65 us
  transfers between devices with their start and end apart: 16 -> 25, of which waited for: 7 -> 8; matrix products, arithmetic and copies ran while one was open for 3% -> 0% of each run, Pallas kernels for 10% -> 16%
where the time goes in v4:
time: 74 us; the launch traced here: 73.7 us
  starting transfers between devices  25.1 us (34%)
  waiting for transfers between devices  23.6 us (32%)
  Pallas kernels  15.5 us (21%)
  local copies, waits for them, and re-layouts  8.65 us (12%)
  between operations  0.87 us (1%)
    ppermute x6, waiting for transfers between devices, swap_topic(): lax.ppermute(array, 'topic', [(i, i ^ 1 << level) for i in range(n_topic)])  16.9 us
    ppermute x6, starting transfers between devices, swap_topic(): lax.ppermute(array, 'topic', [(i, i ^ 1 << level) for i in range(n_topic)])  11.6 us
    ppermute x16, starting transfers between devices, swap(): return lax.ppermute(array, 'doc', [(i, i ^ bit) for i in range(n_doc)])  9.89 us
    unnamed x18, local copies, waits for them, and re-layouts  8.65 us
    pallas_call x1, Pallas kernels, rate_partial(): pl.pallas_call(kernel, out_shape=[jax.ShapeDtypeStruct((half, docs), F32)...  4.21 us
    pallas_call x1, Pallas kernels, theta_grad(): pl.pallas_call(kernel, out_shape=[jax.ShapeDtypeStruct((docs, share), F32...  3.68 us
    ppermute x3, starting transfers between devices, shift(): lax.ppermute(array, 'vocab', [(i, (i + by) % n_vocab) for i in range(n_vo...  3.65 us
    ppermute x16, waiting for transfers between devices, swap(): return lax.ppermute(array, 'doc', [(i, i ^ bit) for i in range(n_doc)])  3.61 us
  transfers between devices with their start and end apart: 25, of which 8 were waited for; matrix products, arithmetic and copies ran while one was open for 0% of the time, Pallas kernels for 16%

profile of v4, /device:TPU:0, one launch (start us, length us, event | category | flops | bytes accessed | tf_op | source)
XLA Modules:
  0.0 73.7 jit_solution(1635775118269264688)
XLA Ops:
  0.6 2.3 %fetch.1 = (bf16[512,768]{1,0:T(8,128)(2,1)}, bf16[512,256]{1,0:T(8,128)(2,1)S(1)}, bf16[128,2048]{1,0:T(8,128)(2,1)S(1)}, f32[1,4096]{1,0:T(1,128)S(1)}) custom-call(s32[1]{0:T(128)} %bitcast.vocab_ref, s32[1]{0:T(128)} %bitcast.1.side_ref, bf16[512,4096]{1,0:T(8,128)(2,1)} %doc_in.3, bf16[256,4096]{1,0:T(8,128)(2,1)} %logit_in.3, f32[1,4096]{1,0:T(1,128)} %bitcast.5), custom_call_target="tpu_custom_call" | custom-call | bytes 3145728 | tf_op jit(solution)/shard_map/fetch/pallas_call | solution.py:60
  2.9 0.8 %copy-done.7 = bf16[128,2048]{1,0:T(8,128)(2,1)} copy-done((bf16[128,2048]{1,0:T(8,128)(2,1)}, bf16[128,2048]{1,0:T(8,128)(2,1)S(1)}, u32[]{:S(2)}) %copy-start.7) | copy-done | bytes 524312
  3.7 0.7 copy-done.8
  4.4 2.9 %collective-permute-start.13 = (bf16[512,768]{1,0:T(8,128)(2,1)}, bf16[512,768]{1,0:T(8,128)(2,1)S(1)}, u32[]{:S(2)}, u32[]{:S(2)}) collective-permute-start(bf16[512,768]{1,0:T(8,128)(2,1)} %get-tuple-element.37), channel_id=1, source_target_pairs={{0,16},{8,24},{16,0},{24,8},{1,17},{9,25},{17,1},{25,9},{2,18},{10... | collective-permute-start | bytes 2359304 | tf_op jit(solution)/shard_map/ppermute | solution.py:376
  7.4 4.2 %rate_partial.1 = (f32[128,512]{1,0:T(8,128)S(1)}, bf16[128,512]{1,0:T(8,128)(2,1)}, bf16[512,4096]{1,0:T(8,128)(2,1)S(1)}, bf16[256,4096]{1,0:T(8,128)(2,1)S(1)}) custom-call(s32[1]{0:T(128)} %bitcast.2.bit_ref, bf16[512,4096]{1,0:T(8,128)(2,1)} %doc_in.3, bf16[256,4096]{1,0:T(8,128)(2,1)} %logit_in.3, f32[1,4096]{1,0:T(1,128)S(1)} %get-tuple-element.24.norm_ref.refs_4_), custom_call_target="tpu_custom_call" | custom-call | flops 1073741824 | bytes 6291456 | tf_op jit(solution)/shard_map/rate_partial/pallas_call | solution.py:111
  11.6 2.0 %copy-done = bf16[512,4096]{1,0:T(8,128)(2,1)} copy-done((bf16[512,4096]{1,0:T(8,128)(2,1)}, bf16[512,4096]{1,0:T(8,128)(2,1)S(1)}, u32[]{:S(2)}) %copy-start) | copy-done | bytes 4194328
  13.6 0.7 copy-done.3
  14.3 1.6 %collective-permute-start = (bf16[128,512]{1,0:T(8,128)(2,1)}, bf16[128,512]{1,0:T(8,128)(2,1)S(1)}, u32[]{:S(2)}, u32[]{:S(2)}) collective-permute-start(bf16[128,512]{1,0:T(8,128)(2,1)} %get-tuple-element.26), channel_id=1, source_target_pairs={{0,2},{2,0},{4,6},{6,4},{1,3},{3,1},{5,7},{7,5},{8,10},{10,8},{12,... | collective-permute-start | bytes 393224 | tf_op jit(solution)/shard_map/ppermute | solution.py:379
  15.9 3.6 %collective-permute-done.other_ref = bf16[128,512]{1,0:T(8,128)(2,1)S(1)} collective-permute-done((bf16[128,512]{1,0:T(8,128)(2,1)}, bf16[128,512]{1,0:T(8,128)(2,1)S(1)}, u32[]{:S(2)}, u32[]{:S(2)}) %collective-permute-start) | collective-permute-done | bytes 131104 | tf_op jit(solution)/shard_map/ppermute | solution.py:379
  19.5 0.9 %copy-done.4 = f32[128,512]{1,0:T(8,128)S(1)} copy-done((f32[128,512]{1,0:T(8,128)S(1)}, f32[128,512]{1,0:T(8,128)}, u32[]{:S(2)}) %copy-start.4) | copy-done | bytes 262168
  20.5 2.6 %collective-permute-start.1 = (bf16[64,512]{1,0:T(8,128)(2,1)S(1)}, bf16[64,512]{1,0:T(8,128)(2,1)S(1)}, u32[]{:S(2)}, u32[]{:S(2)}) collective-permute-start(bf16[64,512]{1,0:T(8,128)(2,1)S(1)} %get-tuple-element.28), channel_id=1, source_target_pairs={{0,4},{2,6},{4,0},{6,2},{1,5},{3,7},{5,1},{7,3},{8,12},{10,14},{12... | collective-permute-start | bytes 196616 | tf_op jit(solution)/shard_map/ppermute | solution.py:379
  23.7 1.5 %collective-permute-start.6 = (bf16[128,2048]{1,0:T(8,128)(2,1)}, bf16[128,2048]{1,0:T(8,128)(2,1)S(1)}, u32[]{:S(2)}, u32[]{:S(2)}) collective-permute-start(bf16[128,2048]{1,0:T(8,128)(2,1)} %copy-done.7), channel_id=1, source_target_pairs={{0,1},{1,0},{2,3},{3,2},{4,5},{5,4},{6,7},{7,6},{8,9},{9,8},{10,11... | collective-permute-start | bytes 1572872 | tf_op jit(solution)/shard_map/ppermute | solution.py:373
  25.2 0.7 copy-done.5
  25.8 0.7 copy-done.6
  26.5 0.7 chunk_counts.1.count_ref
  27.2 1.2 %collective-permute-start.2 = (bf16[64,512]{1,0:T(8,128)(2,1)S(1)}, bf16[64,512]{1,0:T(8,128)(2,1)S(1)}, u32[]{:S(2)}, u32[]{:S(2)}) collective-permute-start(bf16[64,512]{1,0:T(8,128)(2,1)S(1)} %ratio_chunk.1.own_ref.rest_0_), channel_id=1, source_target_pairs={{0,4},{2,6},{4,0},{6,2},{1,5},{3,7},{5,1},{7,3},{8,12},{10,14},{12... | collective-permute-start | bytes 196616 | tf_op jit(solution)/shard_map/ppermute | solution.py:379
  28.4 4.1 %collective-permute-done.2.other_ref = bf16[64,512]{1,0:T(8,128)(2,1)S(1)} collective-permute-done((bf16[64,512]{1,0:T(8,128)(2,1)S(1)}, bf16[64,512]{1,0:T(8,128)(2,1)S(1)}, u32[]{:S(2)}, u32[]{:S(2)}) %collective-permute-start.2) | collective-permute-done | bytes 65568 | tf_op jit(solution)/shard_map/ppermute | solution.py:379
  32.5 2.3 %collective-permute-start.3 = (bf16[128,512]{1,0:T(8,128)(2,1)S(1)}, bf16[128,512]{1,0:T(8,128)(2,1)S(1)}, u32[]{:S(2)}, u32[]{:S(2)}) collective-permute-start(bf16[128,512]{1,0:T(8,128)(2,1)S(1)} %join_rows.4.own_ref), channel_id=1, source_target_pairs={{0,2},{2,0},{4,6},{6,4},{1,3},{3,1},{5,7},{7,5},{8,10},{10,8},{12,... | collective-permute-start | bytes 393224 | tf_op jit(solution)/shard_map/ppermute | solution.py:379
  34.8 2.9 %collective-permute-done.3.other_ref = bf16[128,512]{1,0:T(8,128)(2,1)S(1)} collective-permute-done((bf16[128,512]{1,0:T(8,128)(2,1)S(1)}, bf16[128,512]{1,0:T(8,128)(2,1)S(1)}, u32[]{:S(2)}, u32[]{:S(2)}) %collective-permute-start.3) | collective-permute-done | bytes 131104 | tf_op jit(solution)/shard_map/ppermute | solution.py:379
  38.3 2.2 %copy-done.1 = bf16[512,4096]{1,0:T(8,128)(2,1)S(1)} copy-done((bf16[512,4096]{1,0:T(8,128)(2,1)S(1)}, bf16[512,4096]{1,0:T(8,128)(2,1)}, u32[]{:S(2)}) %copy-start.1) | copy-done | bytes 4194328
  42.2 1.7 %collective-permute-start.8 = (bf16[64,512]{1,0:T(8,128)(2,1)S(1)}, bf16[64,512]{1,0:T(8,128)(2,1)S(1)}, u32[]{:S(2)}, u32[]{:S(2)}) collective-permute-start(bf16[64,512]{1,0:T(8,128)(2,1)S(1)} %ratio_chunk.1.own_ref.rest_0_), channel_id=1, source_target_pairs={{0,16},{8,24},{16,0},{24,8},{1,17},{9,25},{17,1},{25,9},{2,18},{10... | collective-permute-start | bytes 196616 | tf_op jit(solution)/shard_map/ppermute | solution.py:376
  44.0 2.5 %collective-permute-done.8.in_ref = bf16[64,512]{1,0:T(8,128)(2,1)S(1)} collective-permute-done((bf16[64,512]{1,0:T(8,128)(2,1)S(1)}, bf16[64,512]{1,0:T(8,128)(2,1)S(1)}, u32[]{:S(2)}, u32[]{:S(2)}) %collective-permute-start.8) | collective-permute-done | bytes 65568 | tf_op jit(solution)/shard_map/ppermute | solution.py:376
  46.5 2.5 %collective-permute-start.10 = (bf16[64,512]{1,0:T(8,128)(2,1)S(1)}, bf16[64,512]{1,0:T(8,128)(2,1)S(1)}, u32[]{:S(2)}, u32[]{:S(2)}) collective-permute-start(bf16[64,512]{1,0:T(8,128)(2,1)S(1)} %hold.2.own_ref), channel_id=1, source_target_pairs={{0,4},{2,6},{4,0},{6,2},{1,5},{3,7},{5,1},{7,3},{8,12},{10,14},{12... | collective-permute-start | bytes 196616 | tf_op jit(solution)/shard_map/ppermute | solution.py:379
  49.5 2.6 %collective-permute-done.10.other_ref = bf16[64,512]{1,0:T(8,128)(2,1)S(1)} collective-permute-done((bf16[64,512]{1,0:T(8,128)(2,1)S(1)}, bf16[64,512]{1,0:T(8,128)(2,1)S(1)}, u32[]{:S(2)}, u32[]{:S(2)}) %collective-permute-start.10) | collective-permute-done | bytes 65568 | tf_op jit(solution)/shard_map/ppermute | solution.py:379
  52.1 1.4 %collective-permute-start.11 = (bf16[128,512]{1,0:T(8,128)(2,1)S(1)}, bf16[128,512]{1,0:T(8,128)(2,1)S(1)}, u32[]{:S(2)}, u32[]{:S(2)}) collective-permute-start(bf16[128,512]{1,0:T(8,128)(2,1)S(1)} %join_rows.6.own_ref), channel_id=1, source_target_pairs={{0,2},{2,0},{4,6},{6,4},{1,3},{3,1},{5,7},{7,5},{8,10},{10,8},{12,... | collective-permute-start | bytes 393224 | tf_op jit(solution)/shard_map/ppermute | solution.py:379
  53.5 3.6 %collective-permute-done.11.other_ref = bf16[128,512]{1,0:T(8,128)(2,1)S(1)} collective-permute-done((bf16[128,512]{1,0:T(8,128)(2,1)S(1)}, bf16[128,512]{1,0:T(8,128)(2,1)S(1)}, u32[]{:S(2)}, u32[]{:S(2)}) %collective-permute-start.11) | collective-permute-done | bytes 131104 | tf_op jit(solution)/shard_map/ppermute | solution.py:379
  57.5 1.8 %collective-permute-start.5 = (bf16[256,512]{1,0:T(8,128)(2,1)S(1)}, bf16[256,512]{1,0:T(8,128)(2,1)S(1)}, u32[]{:S(2)}, u32[]{:S(2)}) collective-permute-start(bf16[256,512]{1,0:T(8,128)(2,1)S(1)} %join_rows.5.refs_0_.ratio_ref), channel_id=1, source_target_pairs={{0,1},{1,0},{2,3},{3,2},{4,5},{5,4},{6,7},{7,6},{8,9},{9,8},{10,11... | collective-permute-start | bytes 786440 | tf_op jit(solution)/shard_map/ppermute | solution.py:373
  60.1 1.6 %collective-permute-start.17 = (bf16[128,1152]{1,0:T(8,128)(2,1)S(1)}, bf16[128,1152]{1,0:T(8,128)(2,1)S(1)}, u32[]{:S(2)}, u32[]{:S(2)}) collective-permute-start(bf16[128,1152]{1,0:T(8,128)(2,1)S(1)} %add_pair.7.rest_0_.own_ref), channel_id=1, source_target_pairs={{0,16},{8,24},{16,0},{24,8},{1,17},{9,25},{17,1},{25,9},{2,18},{10... | collective-permute-start | bytes 884744 | tf_op jit(solution)/shard_map/ppermute | solution.py:376
  63.2 3.1 %collective-permute-done.5.refs_0_ = bf16[256,512]{1,0:T(8,128)(2,1)S(1)} collective-permute-done((bf16[256,512]{1,0:T(8,128)(2,1)S(1)}, bf16[256,512]{1,0:T(8,128)(2,1)S(1)}, u32[]{:S(2)}, u32[]{:S(2)}) %collective-permute-start.5) | collective-permute-done | bytes 262176 | tf_op jit(solution)/shard_map/ppermute | solution.py:373
  66.3 3.7 %theta_grad.1 = (f32[512,2048]{1,0:T(8,128)}, f32[8,128]{1,0:T(8,128)S(1)}) custom-call(s32[1]{0:T(128)} %bitcast.vocab_ref, s32[1]{0:T(128)} %bitcast.1.side_ref, bf16[256,512]{1,0:T(8,128)(2,1)S(1)} %join_rows.5.refs_0_.ratio_ref, bf16[256,512]{1,0:T(8,128)(2,1)S(1)} %collective-permute-done.5.refs_0_, ...), custom_call_target="tpu_custom_call" | custom-call | flops 1073741824 | bytes 6291456 | tf_op jit(solution)/shard_map/theta_grad/pallas_call | solution.py:303
  71.2 1.1 %collective-permute-done.22.refs_12_ = bf16[128,256]{1,0:T(8,128)(2,1)S(1)} collective-permute-done((bf16[128,256]{1,0:T(8,128)(2,1)S(1)}, bf16[128,256]{1,0:T(8,128)(2,1)S(1)}, u32[]{:S(2)}, u32[]{:S(2)}) %collective-permute-start.22) | collective-permute-done | bytes 65568 | tf_op jit(solution)/shard_map/ppermute | solution.py:376
  72.3 1.4 %place_pieces.1 = bf16[256,4096]{1,0:T(8,128)(2,1)} custom-call(s32[1]{0:T(128)} %bitcast.1.side_ref, s32[1]{0:T(128)} %constant.41.clone.1.column_ref.refs_0_, s32[1]{0:T(128)} %constant.39.clone.1.column_ref.refs_1_, s32[1]{0:T(128)} %constant.38.clone.1.column_ref.refs_2_, s32[1]{0:T(128)S(6)} %mul.6.column_ref.refs_3_, s32[1]{0:T(128)S(6)} %mul.7.column_ref.refs_4_, ...), custom_call_target="tpu_custom_call" | custom-call | bytes 4194304 | tf_op jit(solution)/shard_map/place_pieces/pallas_call | solution.py:347
  (61 shorter events, 7.4 us)
Async XLA Ops:
  2.9 0.8 %copy-start.7 = (bf16[128,2048]{1,0:T(8,128)(2,1)}, bf16[128,2048]{1,0:T(8,128)(2,1)S(1)}, u32[]{:S(2)}) copy-start(bf16[128,2048]{1,0:T(8,128)(2,1)S(1)} %get-tuple-element.31) | copy-start | bytes 1572868
  3.7 0.7 copy-start.8
  4.4 20.8 %copy-start.2 = (s32[16,64,128]{2,1,0:T(8,128)S(1)}, s32[16,64,128]{2,1,0:T(8,128)}, u32[]{:S(2)}) copy-start(s32[16,64,128]{2,1,0:T(8,128)} %count_ref.1) | copy-start | bytes 1572868
  4.4 33.4 %collective-permute-start.13 = (bf16[512,768]{1,0:T(8,128)(2,1)}, bf16[512,768]{1,0:T(8,128)(2,1)S(1)}, u32[]{:S(2)}, u32[]{:S(2)}) collective-permute-start(bf16[512,768]{1,0:T(8,128)(2,1)} %get-tuple-element.37), channel_id=1, source_target_pairs={{0,16},{8,24},{16,0},{24,8},{1,17},{9,25},{17,1},{25,9},{2,18},{10... | collective-permute-start | bytes 2359304 | tf_op jit(solution)/shard_map/ppermute | solution.py:376
  11.6 2.0 %copy-start = (bf16[512,4096]{1,0:T(8,128)(2,1)}, bf16[512,4096]{1,0:T(8,128)(2,1)S(1)}, u32[]{:S(2)}) copy-start(bf16[512,4096]{1,0:T(8,128)(2,1)S(1)} %get-tuple-element.32.refs_1_.refs_2_) | copy-start | bytes 12582916
  13.6 0.7 copy-start.3
  14.3 5.2 %collective-permute-start = (bf16[128,512]{1,0:T(8,128)(2,1)}, bf16[128,512]{1,0:T(8,128)(2,1)S(1)}, u32[]{:S(2)}, u32[]{:S(2)}) collective-permute-start(bf16[128,512]{1,0:T(8,128)(2,1)} %get-tuple-element.26), channel_id=1, source_target_pairs={{0,2},{2,0},{4,6},{6,4},{1,3},{3,1},{5,7},{7,5},{8,10},{10,8},{12,... | collective-permute-start | bytes 393224 | tf_op jit(solution)/shard_map/ppermute | solution.py:379
  19.5 1.0 %copy-start.4 = (f32[128,512]{1,0:T(8,128)S(1)}, f32[128,512]{1,0:T(8,128)}, u32[]{:S(2)}) copy-start(f32[128,512]{1,0:T(8,128)} %copy-done.3) | copy-start | bytes 786436
  20.5 6.7 %collective-permute-start.1 = (bf16[64,512]{1,0:T(8,128)(2,1)S(1)}, bf16[64,512]{1,0:T(8,128)(2,1)S(1)}, u32[]{:S(2)}, u32[]{:S(2)}) collective-permute-start(bf16[64,512]{1,0:T(8,128)(2,1)S(1)} %get-tuple-element.28), channel_id=1, source_target_pairs={{0,4},{2,6},{4,0},{6,2},{1,5},{3,7},{5,1},{7,3},{8,12},{10,14},{12... | collective-permute-start | bytes 196616 | tf_op jit(solution)/shard_map/ppermute | solution.py:379
  23.1 11.7 %collective-permute-start.4 = (bf16[512,256]{1,0:T(8,128)(2,1)}, bf16[512,256]{1,0:T(8,128)(2,1)S(1)}, u32[]{:S(2)}, u32[]{:S(2)}) collective-permute-start(bf16[512,256]{1,0:T(8,128)(2,1)} %copy-done.8), channel_id=1, source_target_pairs={{0,16},{8,24},{16,0},{24,8},{1,17},{9,25},{17,1},{25,9},{2,18},{10... | collective-permute-start | bytes 786440 | tf_op jit(solution)/shard_map/ppermute | solution.py:376
  23.7 20.2 %collective-permute-start.6 = (bf16[128,2048]{1,0:T(8,128)(2,1)}, bf16[128,2048]{1,0:T(8,128)(2,1)S(1)}, u32[]{:S(2)}, u32[]{:S(2)}) collective-permute-start(bf16[128,2048]{1,0:T(8,128)(2,1)} %copy-done.7), channel_id=1, source_target_pairs={{0,1},{1,0},{2,3},{3,2},{4,5},{5,4},{6,7},{7,6},{8,9},{9,8},{10,11... | collective-permute-start | bytes 1572872 | tf_op jit(solution)/shard_map/ppermute | solution.py:373
  27.2 5.3 %collective-permute-start.2 = (bf16[64,512]{1,0:T(8,128)(2,1)S(1)}, bf16[64,512]{1,0:T(8,128)(2,1)S(1)}, u32[]{:S(2)}, u32[]{:S(2)}) collective-permute-start(bf16[64,512]{1,0:T(8,128)(2,1)S(1)} %ratio_chunk.1.own_ref.rest_0_), channel_id=1, source_target_pairs={{0,4},{2,6},{4,0},{6,2},{1,5},{3,7},{5,1},{7,3},{8,12},{10,14},{12... | collective-permute-start | bytes 196616 | tf_op jit(solution)/shard_map/ppermute | solution.py:379
  32.5 5.2 %collective-permute-start.3 = (bf16[128,512]{1,0:T(8,128)(2,1)S(1)}, bf16[128,512]{1,0:T(8,128)(2,1)S(1)}, u32[]{:S(2)}, u32[]{:S(2)}) collective-permute-start(bf16[128,512]{1,0:T(8,128)(2,1)S(1)} %join_rows.4.own_ref), channel_id=1, source_target_pairs={{0,2},{2,0},{4,6},{6,4},{1,3},{3,1},{5,7},{7,5},{8,10},{10,8},{12,... | collective-permute-start | bytes 393224 | tf_op jit(solution)/shard_map/ppermute | solution.py:379
  37.9 24.1 %collective-permute-start.18 = (bf16[512,768]{1,0:T(8,128)(2,1)S(1)}, bf16[512,768]{1,0:T(8,128)(2,1)S(1)}, u32[]{:S(2)}, u32[]{:S(2)}) collective-permute-start(bf16[512,768]{1,0:T(8,128)(2,1)S(1)} %hold.3), channel_id=1, source_target_pairs={{0,1},{1,0},{2,3},{3,2},{4,5},{5,4},{6,7},{7,6},{8,9},{9,8},{10,11... | collective-permute-start | bytes 2359304 | tf_op jit(solution)/shard_map/ppermute | solution.py:373
  38.3 2.2 %copy-start.1 = (bf16[512,4096]{1,0:T(8,128)(2,1)S(1)}, bf16[512,4096]{1,0:T(8,128)(2,1)}, u32[]{:S(2)}) copy-start(bf16[512,4096]{1,0:T(8,128)(2,1)} %copy-done) | copy-start | bytes 12582916
  41.0 2.9 %collective-permute-start.9 = (bf16[128,1152]{1,0:T(8,128)(2,1)S(1)}, bf16[128,1152]{1,0:T(8,128)(2,1)S(1)}, u32[]{:S(2)}, u32[]{:S(2)}) collective-permute-start(bf16[128,1152]{1,0:T(8,128)(2,1)S(1)} %get-tuple-element.34), channel_id=1, source_target_pairs={{0,8},{8,0},{16,24},{24,16},{1,9},{9,1},{17,25},{25,17},{2,10},{10... | collective-permute-start | bytes 884744 | tf_op jit(solution)/shard_map/ppermute | solution.py:376
  41.6 7.3 %collective-permute-start.15 = (bf16[128,1152]{1,0:T(8,128)(2,1)S(1)}, bf16[128,1152]{1,0:T(8,128)(2,1)S(1)}, u32[]{:S(2)}, u32[]{:S(2)}) collective-permute-start(bf16[128,1152]{1,0:T(8,128)(2,1)S(1)} %get-tuple-element.42), channel_id=1, source_target_pairs={{0,8},{8,0},{16,24},{24,16},{1,9},{9,1},{17,25},{25,17},{2,10},{10... | collective-permute-start | bytes 884744 | tf_op jit(solution)/shard_map/ppermute | solution.py:376
  42.2 4.3 %collective-permute-start.8 = (bf16[64,512]{1,0:T(8,128)(2,1)S(1)}, bf16[64,512]{1,0:T(8,128)(2,1)S(1)}, u32[]{:S(2)}, u32[]{:S(2)}) collective-permute-start(bf16[64,512]{1,0:T(8,128)(2,1)S(1)} %ratio_chunk.1.own_ref.rest_0_), channel_id=1, source_target_pairs={{0,16},{8,24},{16,0},{24,8},{1,17},{9,25},{17,1},{25,9},{2,18},{10... | collective-permute-start | bytes 196616 | tf_op jit(solution)/shard_map/ppermute | solution.py:376
  43.9 22.4 %collective-permute-start.7 = (bf16[128,2048]{1,0:T(8,128)(2,1)S(1)}, bf16[128,2048]{1,0:T(8,128)(2,1)S(1)}, u32[]{:S(2)}, u32[]{:S(2)}) collective-permute-start(bf16[128,2048]{1,0:T(8,128)(2,1)S(1)} %collective-permute-done.6.refs_2_), channel_id=1, source_target_pairs={{0,8},{8,0},{16,24},{24,16},{1,9},{9,1},{17,25},{25,17},{2,10},{10... | collective-permute-start | bytes 1572872 | tf_op jit(solution)/shard_map/ppermute | solution.py:376
  46.5 5.6 %collective-permute-start.10 = (bf16[64,512]{1,0:T(8,128)(2,1)S(1)}, bf16[64,512]{1,0:T(8,128)(2,1)S(1)}, u32[]{:S(2)}, u32[]{:S(2)}) collective-permute-start(bf16[64,512]{1,0:T(8,128)(2,1)S(1)} %hold.2.own_ref), channel_id=1, source_target_pairs={{0,4},{2,6},{4,0},{6,2},{1,5},{3,7},{5,1},{7,3},{8,12},{10,14},{12... | collective-permute-start | bytes 196616 | tf_op jit(solution)/shard_map/ppermute | solution.py:379
  49.0 11.1 %collective-permute-start.16 = (bf16[128,1152]{1,0:T(8,128)(2,1)S(1)}, bf16[128,1152]{1,0:T(8,128)(2,1)S(1)}, u32[]{:S(2)}, u32[]{:S(2)}) collective-permute-start(bf16[128,1152]{1,0:T(8,128)(2,1)S(1)} %add_pair.10.own_ref), channel_id=1, source_target_pairs={{0,16},{8,24},{16,0},{24,8},{1,17},{9,25},{17,1},{25,9},{2,18},{10... | collective-permute-start | bytes 884744 | tf_op jit(solution)/shard_map/ppermute | solution.py:376
  52.1 5.0 %collective-permute-start.11 = (bf16[128,512]{1,0:T(8,128)(2,1)S(1)}, bf16[128,512]{1,0:T(8,128)(2,1)S(1)}, u32[]{:S(2)}, u32[]{:S(2)}) collective-permute-start(bf16[128,512]{1,0:T(8,128)(2,1)S(1)} %join_rows.6.own_ref), channel_id=1, source_target_pairs={{0,2},{2,0},{4,6},{6,4},{1,3},{3,1},{5,7},{7,5},{8,10},{10,8},{12,... | collective-permute-start | bytes 393224 | tf_op jit(solution)/shard_map/ppermute | solution.py:379
  57.4 2.4 %collective-permute-start.12 = (bf16[128,256]{1,0:T(8,128)(2,1)S(1)}, bf16[128,256]{1,0:T(8,128)(2,1)S(1)}, u32[]{:S(2)}, u32[]{:S(2)}) collective-permute-start(bf16[128,256]{1,0:T(8,128)(2,1)S(1)} %get-tuple-element.36), channel_id=1, source_target_pairs={{0,8},{8,0},{16,24},{24,16},{1,9},{9,1},{17,25},{25,17},{2,10},{10... | collective-permute-start | bytes 196616 | tf_op jit(solution)/shard_map/ppermute | solution.py:376
  57.5 8.7 %collective-permute-start.5 = (bf16[256,512]{1,0:T(8,128)(2,1)S(1)}, bf16[256,512]{1,0:T(8,128)(2,1)S(1)}, u32[]{:S(2)}, u32[]{:S(2)}) collective-permute-start(bf16[256,512]{1,0:T(8,128)(2,1)S(1)} %join_rows.5.refs_0_.ratio_ref), channel_id=1, source_target_pairs={{0,1},{1,0},{2,3},{3,2},{4,5},{5,4},{6,7},{7,6},{8,9},{9,8},{10,11... | collective-permute-start | bytes 786440 | tf_op jit(solution)/shard_map/ppermute | solution.py:373
  59.9 1.9 %collective-permute-start.14 = (bf16[128,768]{1,0:T(8,128)(2,1)S(1)}, bf16[128,768]{1,0:T(8,128)(2,1)S(1)}, u32[]{:S(2)}, u32[]{:S(2)}) collective-permute-start(bf16[128,768]{1,0:T(8,128)(2,1)S(1)} %get-tuple-element.39), channel_id=1, source_target_pairs={{0,8},{8,0},{16,24},{24,16},{1,9},{9,1},{17,25},{25,17},{2,10},{10... | collective-permute-start | bytes 589832 | tf_op jit(solution)/shard_map/ppermute | solution.py:376
  60.1 9.8 %collective-permute-start.17 = (bf16[128,1152]{1,0:T(8,128)(2,1)S(1)}, bf16[128,1152]{1,0:T(8,128)(2,1)S(1)}, u32[]{:S(2)}, u32[]{:S(2)}) collective-permute-start(bf16[128,1152]{1,0:T(8,128)(2,1)S(1)} %add_pair.7.rest_0_.own_ref), channel_id=1, source_target_pairs={{0,16},{8,24},{16,0},{24,8},{1,17},{9,25},{17,1},{25,9},{2,18},{10... | collective-permute-start | bytes 884744 | tf_op jit(solution)/shard_map/ppermute | solution.py:376
  61.8 10.5 %collective-permute-start.20 = (bf16[128,1152]{1,0:T(8,128)(2,1)S(1)}, bf16[128,1152]{1,0:T(8,128)(2,1)S(1)}, u32[]{:S(2)}, u32[]{:S(2)}) collective-permute-start(bf16[128,1152]{1,0:T(8,128)(2,1)S(1)} %add_pair.11.refs_5_), channel_id=1, source_target_pairs={{0,8},{8,0},{16,24},{24,16},{1,9},{9,1},{17,25},{25,17},{2,10},{10... | collective-permute-start | bytes 884744 | tf_op jit(solution)/shard_map/ppermute | solution.py:376
  62.6 8.0 %collective-permute-start.19 = (bf16[128,768]{1,0:T(8,128)(2,1)S(1)}, bf16[128,768]{1,0:T(8,128)(2,1)S(1)}, u32[]{:S(2)}, u32[]{:S(2)}) collective-permute-start(bf16[128,768]{1,0:T(8,128)(2,1)S(1)} %get-tuple-element.45), channel_id=1, source_target_pairs={{0,8},{8,0},{16,24},{24,16},{1,9},{9,1},{17,25},{25,17},{2,10},{10... | collective-permute-start | bytes 589832 | tf_op jit(solution)/shard_map/ppermute | solution.py:376
  70.0 2.3 %collective-permute-start.21 = (bf16[128,1152]{1,0:T(8,128)(2,1)S(1)}, bf16[128,1152]{1,0:T(8,128)(2,1)S(1)}, u32[]{:S(2)}, u32[]{:S(2)}) collective-permute-start(bf16[128,1152]{1,0:T(8,128)(2,1)S(1)} %add_pair.12.refs_6_), channel_id=1, source_target_pairs={{0,8},{8,0},{16,24},{24,16},{1,9},{9,1},{17,25},{25,17},{2,10},{10... | collective-permute-start | bytes 884744 | tf_op jit(solution)/shard_map/ppermute | solution.py:376
  70.1 2.2 %collective-permute-start.23 = (bf16[128,768]{1,0:T(8,128)(2,1)S(1)}, bf16[128,768]{1,0:T(8,128)(2,1)S(1)}, u32[]{:S(2)}, u32[]{:S(2)}) collective-permute-start(bf16[128,768]{1,0:T(8,128)(2,1)S(1)} %add_pair.9.refs_6_.refs_8_), channel_id=1, source_target_pairs={{0,8},{8,0},{16,24},{24,16},{1,9},{9,1},{17,25},{25,17},{2,10},{10... | collective-permute-start | bytes 589832 | tf_op jit(solution)/shard_map/ppermute | solution.py:376
  70.6 1.7 %collective-permute-start.24 = (bf16[128,768]{1,0:T(8,128)(2,1)S(1)}, bf16[128,768]{1,0:T(8,128)(2,1)S(1)}, u32[]{:S(2)}, u32[]{:S(2)}) collective-permute-start(bf16[128,768]{1,0:T(8,128)(2,1)S(1)} %add_pair.13.refs_9_), channel_id=1, source_target_pairs={{0,8},{8,0},{16,24},{24,16},{1,9},{9,1},{17,25},{25,17},{2,10},{10... | collective-permute-start | bytes 589832 | tf_op jit(solution)/shard_map/ppermute | solution.py:376
  70.8 1.5 %collective-permute-start.22 = (bf16[128,256]{1,0:T(8,128)(2,1)S(1)}, bf16[128,256]{1,0:T(8,128)(2,1)S(1)}, u32[]{:S(2)}, u32[]{:S(2)}) collective-permute-start(bf16[128,256]{1,0:T(8,128)(2,1)S(1)} %add_pair.8.refs_5_.refs_7_), channel_id=1, source_target_pairs={{0,8},{8,0},{16,24},{24,16},{1,9},{9,1},{17,25},{25,17},{2,10},{10... | collective-permute-start | bytes 196616 | tf_op jit(solution)/shard_map/ppermute | solution.py:376
  (2 other events, 1.3 us)

commit v5 on v2

v5 whole, which is shorter than its diff:
```python
import functools

import jax
import jax.numpy as jnp
from jax import lax
from jax.experimental import pallas as pl
from jax.experimental.pallas import tpu as pltpu
from jax.sharding import PartitionSpec as P

BF16 = jnp.bfloat16
F32 = jnp.float32
MIB = 1024 * 1024
ANY = pl.BlockSpec(memory_space=pl.ANY)
HBM = pl.BlockSpec(memory_space=pltpu.HBM)
VMEM = pl.BlockSpec(memory_space=pltpu.VMEM)
SMEM = pl.BlockSpec(memory_space=pltpu.SMEM)


def call_params(mib=16):
    return pltpu.CompilerParams(vmem_limit_bytes=mib * MIB)


def cost(flops, bytes_accessed, transcendentals=0):
    return pl.CostEstimate(flops=flops, bytes_accessed=bytes_accessed, transcendentals=transcendentals)


def in_hbm(array):
    return pltpu.with_memory_space_constraint(array, pltpu.HBM)


def window(index, size):
    return pl.ds(pl.multiple_of(index * size, size), size)


class Sizes:
    def __init__(self, mesh):
        self.doc, self.topic, self.vocab = (mesh.shape[axis] for axis in ("doc", "topic", "vocab"))

    def vocab_at(self, here_ref):
        return lax.rem(here_ref[0], self.vocab)

    def topic_at(self, here_ref):
        return lax.rem(lax.div(here_ref[0], self.vocab), self.topic)

    def side(self, here_ref):
        return lax.rem(lax.div(here_ref[0], self.vocab * self.topic), 2)


def rate_partial(sizes, here, doc_topics, word_logits, log_norm):
    docs, width = doc_topics.shape
    words = word_logits.shape[0]
    side_width = width // 2
    span = min(side_width, 1024)
    steps = side_width // span
    count, far = sizes.topic, sizes.vocab - 1
    chunk, half, share = words // count, words // 2, width // sizes.vocab

    def kernel(here_ref, doc_in, logit_in, norm_in, *rest):
        parts, halves = rest[:count], rest[count : count + far]
        own_ref, sibling_ref, prob_ref, norm_ref, logit_ref, acc, sems, norm_sem = rest[count + far :]
        side = sizes.side(here_ref)
        norm_copy = pltpu.make_async_copy(norm_in, norm_ref, norm_sem)
        norm_copy.start()
        blocks = []
        for which, doc_ref in ((1 - side, sibling_ref), (side, own_ref)):
            for j in range(steps):
                at = window(which * steps + j, span)
                i = len(blocks)
                logit_copy = pltpu.make_async_copy(logit_in.at[:, at], logit_ref.at[:, at], sems.at[0, i])
                held = doc_ref.at[:, pl.ds(j * span, span)]
                doc_copy = pltpu.make_async_copy(doc_in.at[:, at], held, sems.at[1, i])
                blocks.append((at, logit_copy, doc_copy, held))
        for _, logit_copy, doc_copy, _ in blocks:
            logit_copy.start()
            doc_copy.start()
        norm_copy.wait()
        for i, (at, logit_copy, doc_copy, held) in enumerate(blocks):
            logit_copy.wait()
            prob = jnp.exp(logit_ref[:, at].astype(F32) - norm_ref[:, at]).astype(BF16)
            prob_ref[:, at] = prob
            doc_copy.wait()
            part = lax.dot_general(
                prob, held[...], (((1,), (1,)), ((), ())), preferred_element_type=F32
            )
            if i == 0:
                acc[...] = part
            else:
                acc[...] += part
        topic_at = sizes.topic_at(here_ref)
        for s in range(count):
            parts[s][...] = acc[window(topic_at ^ s, chunk), :].astype(BF16)
        rows = window(side, half)
        for s in range(far):
            target = lax.rem(sizes.vocab_at(here_ref) + s + 1, sizes.vocab)
            halves[s][...] = logit_ref[rows, window(target, share)]

    out = pl.pallas_call(
        kernel,
        out_shape=[jax.ShapeDtypeStruct((chunk, docs), BF16)] * count
        + [jax.ShapeDtypeStruct((half, share), BF16)] * far
        + [
            jax.ShapeDtypeStruct((docs, side_width), BF16),
            jax.ShapeDtypeStruct((docs, side_width), BF16),
            jax.ShapeDtypeStruct(word_logits.shape, BF16),
            jax.ShapeDtypeStruct(log_norm.shape, F32),
        ],
        in_specs=[SMEM, HBM, HBM, HBM],
        out_specs=[VMEM] * (count + far + 4),
        scratch_shapes=[
            pltpu.VMEM(word_logits.shape, BF16),
            pltpu.VMEM((words, docs), F32),
            pltpu.SemaphoreType.DMA((2, 2 * steps)),
            pltpu.SemaphoreType.DMA,
        ],
        compiler_params=call_params(),
        cost_estimate=cost(2 * words * docs * width, 2 * (words + docs) * width, words * width),
        name="rate_partial",
    )(here, in_hbm(doc_topics), in_hbm(word_logits), in_hbm(log_norm))
    return out[:count], out[count : count + far], *out[count + far :]


def chunk_counts(sizes, here, word_counts, tile_doc, tile_word, docs, words):
    slots, word_tile, doc_tile = word_counts.shape
    chunk = words // sizes.topic

    def kernel(here_ref, doc_at, word_at, count_in, out_ref, held, sem):
        copy = pltpu.make_async_copy(count_in, held, sem)
        copy.start()
        first = sizes.topic_at(here_ref) * chunk
        block = first // word_tile
        row = pl.multiple_of(lax.rem(first, word_tile), chunk)
        out_ref[...] = jnp.zeros_like(out_ref)
        copy.wait()
        for s in range(slots):
            @pl.when(word_at[s] == block)
            def _():
                out_ref[:, window(doc_at[s], doc_tile)] = held[s, pl.ds(row, chunk), :].astype(F32)

    return pl.pallas_call(
        kernel,
        out_shape=jax.ShapeDtypeStruct((chunk, docs), F32),
        in_specs=[SMEM, SMEM, SMEM, HBM],
        out_specs=VMEM,
        scratch_shapes=[pltpu.VMEM(word_counts.shape, jnp.int32), pltpu.SemaphoreType.DMA],
        compiler_params=call_params(),
        cost_estimate=cost(words * docs, 4 * words * docs),
        name="chunk_counts",
    )(here, in_hbm(tile_doc), in_hbm(tile_word), in_hbm(word_counts))


def ratio_chunk(parts, counts, word_tile):
    def kernel(*refs):
        part_refs, count_ref, out_ref = refs[:-2], refs[-2], refs[-1]
        rate = part_refs[0][...].astype(F32)
        for ref in part_refs[1:]:
            rate += ref[...].astype(F32)
        out_ref[...] = (count_ref[...] / (word_tile * rate)).astype(BF16)

    return pl.pallas_call(
        kernel,
        out_shape=jax.ShapeDtypeStruct(counts.shape, BF16),
        in_specs=[VMEM] * (len(parts) + 1),
        out_specs=VMEM,
        compiler_params=call_params(),
        cost_estimate=cost(10 * counts.size, 16 * counts.size),
        name="ratio_chunk",
    )(*parts, counts)


def join_ratio(sizes, here, chunks, after):
    rows, docs = chunks[0].shape
    count = sizes.topic

    def kernel(here_ref, *refs):
        topic_at = sizes.topic_at(here_ref)
        for s in range(count):
            refs[-1][window(topic_at ^ s, rows), :] = refs[s][...]

    return pl.pallas_call(
        kernel,
        out_shape=jax.ShapeDtypeStruct((rows * count, docs), BF16),
        in_specs=[SMEM] + [VMEM] * count + [ANY] * len(after),
        out_specs=VMEM,
        compiler_params=call_params(),
        cost_estimate=cost(0, 4 * rows * docs * count),
        name="join_ratio",
    )(here, *chunks, *after)


def own_product(ratio, docs_held):
    words, docs = ratio.shape
    width = docs_held.shape[1]

    def kernel(ratio_ref, doc_ref, out_ref):
        out_ref[...] = jnp.dot(ratio_ref[...], doc_ref[...], preferred_element_type=F32)

    return pl.pallas_call(
        kernel,
        out_shape=jax.ShapeDtypeStruct((words, width), F32),
        in_specs=[VMEM, VMEM],
        out_specs=VMEM,
        compiler_params=call_params(),
        cost_estimate=cost(2 * words * docs * width, 2 * docs * width + 4 * words * width),
        name="own_product",
    )(ratio, docs_held)


def beta_piece(sizes, here, product, ratio, docs_held, prob_held, start, spans, after):
    words, side_width = product.shape
    docs, width = docs_held.shape[0], sum(spans)

    def kernel(here_ref, product_ref, ratio_ref, doc_ref, prob_ref, *rest):
        side = sizes.side(here_ref)
        begin = start
        for out_ref, span in zip(rest[len(after) :], spans):
            at = pl.ds(begin, span)
            prob_at = pl.ds(pl.multiple_of(side * side_width + begin, 128), span)
            summed = product_ref[:, at] + jnp.dot(ratio_ref[...], doc_ref[:, at], preferred_element_type=F32)
            out_ref[...] = (-prob_ref[:, prob_at].astype(F32) * summed).astype(BF16)
            begin += span

    return pl.pallas_call(
        kernel,
        out_shape=[jax.ShapeDtypeStruct((words, span), BF16) for span in spans],
        in_specs=[SMEM] + [VMEM] * 4 + [ANY] * len(after),
        out_specs=[VMEM] * len(spans),
        compiler_params=call_params(),
        cost_estimate=cost(2 * words * docs * width, 2 * (4 * words + docs) * width),
        name="beta_piece",
    )(here, product, ratio, docs_held, prob_held, *after)


def add_pair(own, other, after=()):
    def kernel(own_ref, other_ref, *rest):
        rest[-1][...] = (own_ref[...].astype(F32) + other_ref[...].astype(F32)).astype(BF16)

    return pl.pallas_call(
        kernel,
        out_shape=jax.ShapeDtypeStruct(own.shape, BF16),
        in_specs=[VMEM, VMEM] + [ANY] * len(after),
        out_specs=VMEM,
        compiler_params=call_params(),
        cost_estimate=cost(own.size, 6 * own.size),
        name="add_pair",
    )(own, other, *after)


def hold(array, after):
    def kernel(in_ref, *rest):
        rest[-1][...] = in_ref[...]

    return pl.pallas_call(
        kernel,
        out_shape=jax.ShapeDtypeStruct(array.shape, array.dtype),
        in_specs=[VMEM] + [ANY] * len(after),
        out_specs=VMEM,
        compiler_params=call_params(),
        cost_estimate=cost(0, 4 * array.size),
        name="hold",
    )(array, *after)


def theta_grad(sizes, here, ratio, far_ratios, prob_held, far_logits, log_norm, after):
    words, docs = ratio.shape
    half = words // 2
    share = far_logits[0].shape[1]
    far = len(far_ratios)
    count = far + 1
    span = min(share, 512)
    blocks = share // span

    def kernel(here_ref, ratio_ref, *refs):
        far_refs, prob_ref = refs[:far], refs[far]
        logit_refs, norm_ref = refs[far + 1 : 3 * far + 1], refs[3 * far + 1]
        out_ref, done_ref, turned = refs[-3:]
        done_ref[...] = jnp.zeros_like(done_ref)
        side = sizes.side(here_ref)

        @pl.when(pl.program_id(0) == 0)
        def _():
            def put(rows, at):
                turned[:, at : at + rows.shape[0]] = (-rows.astype(F32)).T.astype(BF16)

            put(ratio_ref[...], 0)
            for l in range(far):
                for h in range(2):
                    which = side if h == 0 else 1 - side
                    put(far_refs[l][window(which, half), :], (l + 1) * words + h * half)

        prob = jnp.concatenate(
            [prob_ref[...]] + [jnp.exp(ref[...].astype(F32) - norm_ref[...]).astype(BF16) for ref in logit_refs],
            axis=0,
        )
        out_ref[...] = jnp.dot(turned[...], prob, preferred_element_type=F32)

    whole = lambda j, h: (0, 0)
    held = lambda j, h: (0, lax.rem(h[0], sizes.vocab) * blocks + j)
    column = lambda j, h: (0, j)
    return pl.pallas_call(
        kernel,
        out_shape=[jax.ShapeDtypeStruct((docs, share), F32), jax.ShapeDtypeStruct((8, 128), F32)],
        grid_spec=pltpu.PrefetchScalarGridSpec(
            num_scalar_prefetch=1,
            grid=(blocks,),
            in_specs=[pl.BlockSpec((words, docs), whole)] * count
            + [pl.BlockSpec((words, span), held)]
            + [pl.BlockSpec((half, span), column)] * (2 * far)
            + [pl.BlockSpec((1, span), held)]
            + [ANY] * len(after),
            out_specs=[pl.BlockSpec((docs, span), column), pl.BlockSpec((8, 128), whole)],
            scratch_shapes=[pltpu.VMEM((docs, count * words), BF16)],
        ),
        compiler_params=call_params(),
        cost_estimate=cost(
            20 * count * words * docs * share, (40 * docs + 20 * count * words) * share, 10 * count * words * share
        ),
        name="theta_grad",
    )(here, ratio, *far_ratios, prob_held, *far_logits, log_norm, *after)


def place_pieces(sizes, here, own, other, starts, shape, so_far=None):
    pieces = len(own)
    side_width = shape[1] // 2
    before = [] if so_far is None else [so_far]

    def kernel(here_ref, *refs):
        own_refs, other_refs, (out_ref, done_ref, sems) = refs[:pieces], refs[pieces : 2 * pieces], refs[-3:]
        done_ref[...] = jnp.zeros_like(done_ref)
        side = sizes.side(here_ref)
        copies = []
        for p in range(pieces):
            for h, (ref, which) in enumerate(((own_refs[p], side), (other_refs[p], 1 - side))):
                column = pl.multiple_of(which * side_width + starts[p], 128)
                target = out_ref.at[:, pl.ds(column, ref.shape[1])]
                copies.append(pltpu.make_async_copy(ref, target, sems.at[h, p]))
        for copy in copies:
            copy.start()
        for copy in copies:
            copy.wait()

    return pl.pallas_call(
        kernel,
        out_shape=[jax.ShapeDtypeStruct(shape, BF16), jax.ShapeDtypeStruct((8, 128), F32)],
        in_specs=[SMEM] + [VMEM] * (2 * pieces) + [HBM] * len(before),
        out_specs=[HBM, VMEM],
        scratch_shapes=[pltpu.SemaphoreType.DMA((2, pieces))],
        input_output_aliases={2 * pieces + 1: 0} if before else {},
        compiler_params=call_params(),
        cost_estimate=cost(0, 4 * sum(part.size for part in own)),
        name="place_pieces",
    )(here, *own, *other, *before)


def on_device(sizes, doc_topics, word_logits, log_norm, tile_doc, tile_word, word_counts):
    docs, width = doc_topics.shape
    words = word_logits.shape[0]
    word_tile = word_counts.shape[1]
    here = lax.axis_index(("doc", "topic", "vocab")).astype(jnp.int32)[None]

    def shift(array, by):
        return lax.ppermute(array, "vocab", [(i, (i + by) % sizes.vocab) for i in range(sizes.vocab)])

    def swap(array, axis, bits):
        count = {"doc": sizes.doc, "topic": sizes.topic}[axis]
        return lax.ppermute(array, axis, [(i, i ^ bits) for i in range(count)])

    parts, near_logits, docs_held, docs_sent, prob_held, norm_held = rate_partial(
        sizes, here, doc_topics, word_logits, log_norm[None, :]
    )
    near_logits = [shift(part, s) for s, part in enumerate(near_logits, 1)]
    sibling_docs = swap(docs_sent, "doc", 1)
    order = sorted(range(1, sizes.topic), key=lambda s: s < sizes.topic // 2)
    arrived = [swap(parts[s], "topic", s) for s in order]
    counts = chunk_counts(sizes, here, word_counts, tile_doc, tile_word, docs, words)
    own_ratio = ratio_chunk([parts[0]] + arrived, counts, word_tile)
    gathered = {s: swap(own_ratio, "topic", s) for s in order}
    ratio = join_ratio(
        sizes, here, [own_ratio] + [gathered[s] for s in range(1, sizes.topic)], near_logits + [sibling_docs]
    )
    sibling_ratio = swap(ratio, "doc", 1)
    far_ratios = [shift(ratio, s) for s in range(1, sizes.vocab)]

    side_width = width // 2
    spans = [side_width // 4, side_width // 2, side_width // 4]
    starts = [0, spans[0], spans[0] + spans[1]]
    product = own_product(ratio, docs_held)
    sibling = (sibling_ratio, sibling_docs, prob_held)
    sums = list(beta_piece(sizes, here, product, *sibling, 0, spans[:1], []))
    sums += beta_piece(sizes, here, product, *sibling, spans[0], spans[1:], sums)

    far_logits = []
    for part in near_logits:
        part = hold(part, sums[-1:])
        far_logits += [part, swap(part, "doc", 1)]

    bit = 2
    while 2 * bit < sizes.doc:
        sums = [add_pair(part, swap(part, "doc", bit)) for part in sums]
        bit *= 2
    others = [swap(part, "doc", bit) for part in sums]
    first = add_pair(sums[0], others[0], far_ratios)
    theta, theta_done = theta_grad(sizes, here, ratio, far_ratios, prob_held, far_logits, norm_held, [first])
    early = [first, add_pair(sums[1], others[1])]
    out, early_done = place_pieces(
        sizes, here, early, [swap(part, "doc", 1) for part in early], starts[:-1], word_logits.shape
    )
    last = add_pair(sums[-1], others[-1], [theta_done, early_done])
    out, _ = place_pieces(sizes, here, [last], [swap(last, "doc", 1)], starts[-1:], word_logits.shape, out)
    return theta, out


def solution(mesh):
    placed = (
        P("doc", "topic"),
        P("vocab", "topic"),
        P("topic"),
        P(("doc", "vocab")),
        P(("doc", "vocab")),
        P(("doc", "vocab"), None, None),
    )
    return jax.shard_map(
        functools.partial(on_device, Sizes(mesh)),
        mesh=mesh,
        in_specs=placed,
        out_specs=(P("doc", ("topic", "vocab")), P("vocab", "topic")),
        check_vma=False,
    )
```

time: 62.8 us -> 59.9 us (0.954)
  waiting for transfers between devices: 20.9 us -> 27.4 us
  local copies, waits for them, and re-layouts: 4.33 us -> 0 us
  starting transfers between devices: 20.1 us -> 16.8 us
  Pallas kernels: 16.3 us -> 14.8 us
    ppermute x21 -> x17, waiting for transfers between devices: 20.9 us -> 27.4 us  [the longest x15 21.3 us: swap(): return lax.ppermute(array, axis, [(i, i ^ bits) for i in range(count)])]
    ppermute x21 -> x17, starting transfers between devices: 20.1 us -> 16.8 us  [the longest x15 13.6 us: swap(): return lax.ppermute(array, axis, [(i, i ^ bits) for i in range(count)])]
    pallas_call x8 -> x3, Pallas kernels: 3.36 us -> 0.25 us  [add_pair(): pl.pallas_call(kernel, out_shape=jax.ShapeDtypeStruct(own.shape, BF16), i...]
    unnamed x14 -> x0, local copies, waits for them, and re-layouts: 2.39 us -> none
    dynamic_slice x1 -> x0, local copies, waits for them, and re-layouts: 1.94 us -> none  [on_device(): lax.dynamic_slice(word_logits, (side * half, target * share), (half, share))]
    pallas_call x1, Pallas kernels: 5.18 us -> 3.71 us  [theta_grad(): pl.pallas_call(kernel, out_shape=[jax.ShapeDtypeStruct((docs, share), F32...]
    pallas_call x1, Pallas kernels: 3.59 us -> 4.73 us  [rate_partial(): pl.pallas_call(kernel, out_shape=[jax.ShapeDtypeStruct((chunk, docs), BF1...]
    pallas_call x1, Pallas kernels: 0.69 us -> 1.77 us  [chunk_counts(): pl.pallas_call(kernel, out_shape=jax.ShapeDtypeStruct((chunk, docs), F32)...]
  transfers between devices with their start and end apart: 21 -> 17, of which waited for: 9 -> 10; matrix products, arithmetic and copies ran while one was open for 0% -> 0% of each run, Pallas kernels for 24% -> 13%
where the time goes in v5:
time: 59.9 us; the launch traced here: 59.7 us
  waiting for transfers between devices  27.4 us (46%)
  starting transfers between devices  16.8 us (28%)
  Pallas kernels  14.8 us (25%)
  between operations  0.76 us (1%)
    ppermute x15, waiting for transfers between devices, swap(): return lax.ppermute(array, axis, [(i, i ^ bits) for i in range(count)])  21.3 us
    ppermute x15, starting transfers between devices, swap(): return lax.ppermute(array, axis, [(i, i ^ bits) for i in range(count)])  13.6 us
    ppermute x2, waiting for transfers between devices, shift(): lax.ppermute(array, 'vocab', [(i, (i + by) % sizes.vocab) for i in range(...  6.13 us
    pallas_call x1, Pallas kernels, rate_partial(): pl.pallas_call(kernel, out_shape=[jax.ShapeDtypeStruct((chunk, docs), BF1...  4.73 us
    pallas_call x1, Pallas kernels, theta_grad(): pl.pallas_call(kernel, out_shape=[jax.ShapeDtypeStruct((docs, share), F32...  3.71 us
    ppermute x2, starting transfers between devices, shift(): lax.ppermute(array, 'vocab', [(i, (i + by) % sizes.vocab) for i in range(...  3.16 us
    pallas_call x2, Pallas kernels, place_pieces(): pl.pallas_call(kernel, out_shape=[jax.ShapeDtypeStruct(shape, BF16), jax....  2.57 us
    pallas_call x1, Pallas kernels, chunk_counts(): pl.pallas_call(kernel, out_shape=jax.ShapeDtypeStruct((chunk, docs), F32)...  1.77 us
  transfers between devices with their start and end apart: 17, of which 10 were waited for; matrix products, arithmetic and copies ran while one was open for 0% of the time, Pallas kernels for 13%

profile of v5, /device:TPU:0, one launch (start us, length us, event | category | flops | bytes accessed | tf_op | source)
XLA Modules:
  0.0 59.7 jit_solution(3083089769264242018)
XLA Ops:
  0.6 4.7 %rate_partial.1 = (bf16[64,512]{1,0:T(8,128)(2,1)S(1)}, bf16[64,512]{1,0:T(8,128)(2,1)S(1)}, bf16[64,512]{1,0:T(8,128)(2,1)S(1)}, bf16[64,512]{1,0:T(8,128)(2,1)...) custom-call(s32[1]{0:T(128)} %bitcast.here_ref, ...), custom_call_target="tpu_custom_call" | custom-call | flops 1073741824 | bytes 6291456 | tf_op jit(solution)/shard_map/rate_partial/pallas_call | solution.py:97
  5.4 0.5 collective-permute-start.7
  5.9 2.6 %collective-permute-start.6 = (bf16[128,2048]{1,0:T(8,128)(2,1)S(1)}, bf16[128,2048]{1,0:T(8,128)(2,1)S(1)}, u32[]{:S(2)}, u32[]{:S(2)}) collective-permute-start(bf16[128,2048]{1,0:T(8,128)(2,1)S(1)} %get-tuple-element.22), channel_id=1, source_target_pairs={{0,1},{1,0},{2,3},{3,2},{4,5},{5,4},{6,7},{7,6},{8,9},{9,8},{10,11... | collective-permute-start | bytes 1572872 | tf_op jit(solution)/shard_map/ppermute | solution.py:361
  8.5 2.6 %collective-permute-start = (bf16[64,512]{1,0:T(8,128)(2,1)S(1)}, bf16[64,512]{1,0:T(8,128)(2,1)S(1)}, u32[]{:S(2)}, u32[]{:S(2)}) collective-permute-start(bf16[64,512]{1,0:T(8,128)(2,1)S(1)} %get-tuple-element.19), channel_id=1, source_target_pairs={{0,4},{2,6},{4,0},{6,2},{1,5},{3,7},{5,1},{7,3},{8,12},{10,14},{12... | collective-permute-start | bytes 196616 | tf_op jit(solution)/shard_map/ppermute | solution.py:365
  11.1 1.4 %collective-permute-start.1 = (bf16[64,512]{1,0:T(8,128)(2,1)S(1)}, bf16[64,512]{1,0:T(8,128)(2,1)S(1)}, u32[]{:S(2)}, u32[]{:S(2)}) collective-permute-start(bf16[64,512]{1,0:T(8,128)(2,1)S(1)} %get-tuple-element.20), channel_id=1, source_target_pairs={{0,6},{2,4},{4,2},{6,0},{1,7},{3,5},{5,3},{7,1},{8,14},{10,12},{12... | collective-permute-start | bytes 196616 | tf_op jit(solution)/shard_map/ppermute | solution.py:365
  12.4 0.2 collective-permute-start.2
  12.7 1.8 %chunk_counts.1.refs_4_ = f32[64,512]{1,0:T(8,128)S(1)} custom-call(s32[1]{0:T(128)} %bitcast.here_ref, s32[16]{0:T(128)} %doc_at.1, s32[16]{0:T(128)} %word_at.1, s32[16,64,128]{2,1,0:T(8,128)} %count_in.1), custom_call_target="tpu_custom_call" | custom-call | flops 131072 | bytes 524288 | tf_op jit(solution)/shard_map/chunk_counts/pallas_call | solution.py:139
  14.4 1.1 %collective-permute-done.refs_1_ = bf16[64,512]{1,0:T(8,128)(2,1)S(1)} collective-permute-done((bf16[64,512]{1,0:T(8,128)(2,1)S(1)}, bf16[64,512]{1,0:T(8,128)(2,1)S(1)}, u32[]{:S(2)}, u32[]{:S(2)}) %collective-permute-start) | collective-permute-done | bytes 65568 | tf_op jit(solution)/shard_map/ppermute | solution.py:365
  15.5 2.0 %collective-permute-done.1.refs_2_ = bf16[64,512]{1,0:T(8,128)(2,1)S(1)} collective-permute-done((bf16[64,512]{1,0:T(8,128)(2,1)S(1)}, bf16[64,512]{1,0:T(8,128)(2,1)S(1)}, u32[]{:S(2)}, u32[]{:S(2)}) %collective-permute-start.1) | collective-permute-done | bytes 65568 | tf_op jit(solution)/shard_map/ppermute | solution.py:365
  17.5 0.3 collective-permute-done.2.refs_3_
  17.9 0.7 %collective-permute-start.3 = (bf16[64,512]{1,0:T(8,128)(2,1)S(1)}, bf16[64,512]{1,0:T(8,128)(2,1)S(1)}, u32[]{:S(2)}, u32[]{:S(2)}) collective-permute-start(bf16[64,512]{1,0:T(8,128)(2,1)S(1)} %ratio_chunk.1.refs_0_), channel_id=1, source_target_pairs={{0,2},{2,0},{4,6},{6,4},{1,3},{3,1},{5,7},{7,5},{8,10},{10,8},{12,... | collective-permute-start | bytes 196616 | tf_op jit(solution)/shard_map/ppermute | solution.py:365
  18.6 3.1 %collective-permute-start.4 = (bf16[64,512]{1,0:T(8,128)(2,1)S(1)}, bf16[64,512]{1,0:T(8,128)(2,1)S(1)}, u32[]{:S(2)}, u32[]{:S(2)}) collective-permute-start(bf16[64,512]{1,0:T(8,128)(2,1)S(1)} %ratio_chunk.1.refs_0_), channel_id=1, source_target_pairs={{0,4},{2,6},{4,0},{6,2},{1,5},{3,7},{5,1},{7,3},{8,12},{10,14},{12... | collective-permute-start | bytes 196616 | tf_op jit(solution)/shard_map/ppermute | solution.py:365
  21.7 0.6 %collective-permute-start.5 = (bf16[64,512]{1,0:T(8,128)(2,1)S(1)}, bf16[64,512]{1,0:T(8,128)(2,1)S(1)}, u32[]{:S(2)}, u32[]{:S(2)}) collective-permute-start(bf16[64,512]{1,0:T(8,128)(2,1)S(1)} %ratio_chunk.1.refs_0_), channel_id=1, source_target_pairs={{0,6},{2,4},{4,2},{6,0},{1,7},{3,5},{5,3},{7,1},{8,14},{10,12},{12... | collective-permute-start | bytes 196616 | tf_op jit(solution)/shard_map/ppermute | solution.py:365
  22.3 0.6 collective-permute-done.3.refs_1_
  22.9 3.6 %collective-permute-done.4.refs_2_ = bf16[64,512]{1,0:T(8,128)(2,1)S(1)} collective-permute-done((bf16[64,512]{1,0:T(8,128)(2,1)S(1)}, bf16[64,512]{1,0:T(8,128)(2,1)S(1)}, u32[]{:S(2)}, u32[]{:S(2)}) %collective-permute-start.4) | collective-permute-done | bytes 65568 | tf_op jit(solution)/shard_map/ppermute | solution.py:365
  26.5 1.4 %collective-permute-done.5.refs_3_ = bf16[64,512]{1,0:T(8,128)(2,1)S(1)} collective-permute-done((bf16[64,512]{1,0:T(8,128)(2,1)S(1)}, bf16[64,512]{1,0:T(8,128)(2,1)S(1)}, u32[]{:S(2)}, u32[]{:S(2)}) %collective-permute-start.5) | collective-permute-done | bytes 65568 | tf_op jit(solution)/shard_map/ppermute | solution.py:365
  28.0 0.7 %own_product.1.product_ref = f32[256,2048]{1,0:T(8,128)S(1)} custom-call(bf16[256,512]{1,0:T(8,128)(2,1)S(1)} %join_ratio.1.ratio_ref, bf16[512,2048]{1,0:T(8,128)(2,1)S(1)} %get-tuple-element.25.doc_ref), custom_call_target="tpu_custom_call" | custom-call | flops 536870912 | bytes 4194304 | tf_op jit(solution)/shard_map/own_product/pallas_call | solution.py:197
  28.7 0.8 %collective-permute-done.9.ratio_ref = bf16[256,512]{1,0:T(8,128)(2,1)S(1)} collective-permute-done((bf16[256,512]{1,0:T(8,128)(2,1)S(1)}, bf16[256,512]{1,0:T(8,128)(2,1)S(1)}, u32[]{:S(2)}, u32[]{:S(2)}) %collective-permute-start.9) | collective-permute-done | bytes 262176 | tf_op jit(solution)/shard_map/ppermute | solution.py:365
  29.5 0.3 beta_piece.2.rest_0_.own_ref
  29.8 0.6 %beta_piece.3 = (bf16[256,1024]{1,0:T(8,128)(2,1)S(1)}, bf16[256,512]{1,0:T(8,128)(2,1)S(1)}) custom-call(s32[1]{0:T(128)} %bitcast.here_ref, f32[256,2048]{1,0:T(8,128)S(1)} %own_product.1.product_ref, bf16[256,512]{1,0:T(8,128)(2,1)S(1)} %collective-permute-done.9.ratio_ref, bf16[512,2048]{1,0:T(8,128)(2,1)S(1)} %collective-permute-done.7.refs_5_.doc_ref, ...), custom_call_target="tpu_custom_call" | custom-call | flops 402653184 | bytes 4718592 | tf_op jit(solution)/shard_map/beta_piece/pallas_call | solution.py:222
  30.4 1.6 %collective-permute-start.13 = (bf16[256,1024]{1,0:T(8,128)(2,1)S(1)}, bf16[256,1024]{1,0:T(8,128)(2,1)S(1)}, u32[]{:S(2)}, u32[]{:S(2)}) collective-permute-start(bf16[256,1024]{1,0:T(8,128)(2,1)S(1)} %get-tuple-element.30.own_ref), channel_id=1, source_target_pairs={{0,16},{8,24},{16,0},{24,8},{1,17},{9,25},{17,1},{25,9},{2,18},{10... | collective-permute-start | bytes 1572872 | tf_op jit(solution)/shard_map/ppermute | solution.py:365
  32.1 0.6 collective-permute-start.8
  32.7 0.5 collective-permute-start.11
  33.2 1.5 %collective-permute-start.12 = (bf16[256,512]{1,0:T(8,128)(2,1)S(1)}, bf16[256,512]{1,0:T(8,128)(2,1)S(1)}, u32[]{:S(2)}, u32[]{:S(2)}) collective-permute-start(bf16[256,512]{1,0:T(8,128)(2,1)S(1)} %get-tuple-element.26.rest_0_.own_ref), channel_id=1, source_target_pairs={{0,16},{8,24},{16,0},{24,8},{1,17},{9,25},{17,1},{25,9},{2,18},{10... | collective-permute-start | bytes 786440 | tf_op jit(solution)/shard_map/ppermute | solution.py:365
  34.7 6.1 %collective-permute-done.8.rest_0_.refs_0_ = bf16[256,512]{1,0:T(8,128)(2,1)S(1)} collective-permute-done((bf16[256,512]{1,0:T(8,128)(2,1)S(1)}, bf16[256,512]{1,0:T(8,128)(2,1)S(1)}, u32[]{:S(2)}, u32[]{:S(2)}) %collective-permute-start.8) | collective-permute-done | bytes 262176 | tf_op jit(solution)/shard_map/ppermute | solution.py:361
  40.8 10.1 %collective-permute-done.11.other_ref = bf16[256,512]{1,0:T(8,128)(2,1)S(1)} collective-permute-done((bf16[256,512]{1,0:T(8,128)(2,1)S(1)}, bf16[256,512]{1,0:T(8,128)(2,1)S(1)}, u32[]{:S(2)}, u32[]{:S(2)}) %collective-permute-start.11) | collective-permute-done | bytes 262176 | tf_op jit(solution)/shard_map/ppermute | solution.py:365
  51.0 0.1 add_pair.4.refs_1_
  51.2 0.5 collective-permute-start.15
  51.7 3.7 %theta_grad.1 = (f32[512,2048]{1,0:T(8,128)}, f32[8,128]{1,0:T(8,128)S(1)}) custom-call(s32[1]{0:T(128)} %bitcast.here_ref, bf16[256,512]{1,0:T(8,128)(2,1)S(1)} %join_ratio.1.ratio_ref, bf16[256,512]{1,0:T(8,128)(2,1)S(1)} %collective-permute-done.8.rest_0_.refs_0_, bf16[256,4096]{1,0:T(8,128)(2,1)S(1)} %get-tuple-element.24.prob_ref.refs_1_, ...), custom_call_target="tpu_custom_call" | custom-call | flops 10737418240 | bytes 62914560 | tf_op jit(solution)/shard_map/theta_grad/pallas_call | solution.py:299
  55.4 1.2 %place_pieces.2 = (bf16[256,4096]{1,0:T(8,128)(2,1)}, f32[8,128]{1,0:T(8,128)S(1)}) custom-call(s32[1]{0:T(128)} %bitcast.here_ref, bf16[256,512]{1,0:T(8,128)(2,1)S(1)} %add_pair.3.refs_5_.refs_0_, bf16[256,1024]{1,0:T(8,128)(2,1)S(1)} %add_pair.4.refs_1_, bf16[256,512]{1,0:T(8,128)(2,1)S(1)} %collective-permute-done.14.refs_2_, ...), custom_call_target="tpu_custom_call" | custom-call | bytes 1572864 | tf_op jit(solution)/shard_map/place_pieces/pallas_call | solution.py:341
  56.8 1.5 %collective-permute-done.16.refs_1_ = bf16[256,512]{1,0:T(8,128)(2,1)S(1)} collective-permute-done((bf16[256,512]{1,0:T(8,128)(2,1)S(1)}, bf16[256,512]{1,0:T(8,128)(2,1)S(1)}, u32[]{:S(2)}, u32[]{:S(2)}) %collective-permute-start.16) | collective-permute-done | bytes 262176 | tf_op jit(solution)/shard_map/ppermute | solution.py:365
  58.3 1.4 %place_pieces.3 = (bf16[256,4096]{1,0:T(8,128)(2,1)}, f32[8,128]{1,0:T(8,128)}) custom-call(s32[1]{0:T(128)} %bitcast.here_ref, bf16[256,512]{1,0:T(8,128)(2,1)S(1)} %add_pair.5.refs_0_, bf16[256,512]{1,0:T(8,128)(2,1)S(1)} %collective-permute-done.16.refs_1_, bf16[256,4096]{1,0:T(8,128)(2,1)} %get-tuple-element.32.refs_2_), custom_call_target="tpu_custom_call", output_to_operand_aliasing={{0}: (3, {})} | custom-call | bytes 524288 | tf_op jit(solution)/shard_map/place_pieces/pallas_call | solution.py:341
  (16 shorter events, 0.6 us)
Async XLA Ops:
  5.4 22.5 %collective-permute-start.7 = (bf16[512,2048]{1,0:T(8,128)(2,1)S(1)}, bf16[512,2048]{1,0:T(8,128)(2,1)S(1)}, u32[]{:S(2)}, u32[]{:S(2)}) collective-permute-start(bf16[512,2048]{1,0:T(8,128)(2,1)S(1)} %get-tuple-element.23), channel_id=1, source_target_pairs={{0,8},{8,0},{16,24},{24,16},{1,9},{9,1},{17,25},{25,17},{2,10},{10... | collective-permute-start | bytes 6291464 | tf_op jit(solution)/shard_map/ppermute | solution.py:365
  5.9 22.0 %collective-permute-start.6 = (bf16[128,2048]{1,0:T(8,128)(2,1)S(1)}, bf16[128,2048]{1,0:T(8,128)(2,1)S(1)}, u32[]{:S(2)}, u32[]{:S(2)}) collective-permute-start(bf16[128,2048]{1,0:T(8,128)(2,1)S(1)} %get-tuple-element.22), channel_id=1, source_target_pairs={{0,1},{1,0},{2,3},{3,2},{4,5},{5,4},{6,7},{7,6},{8,9},{9,8},{10,11... | collective-permute-start | bytes 1572872 | tf_op jit(solution)/shard_map/ppermute | solution.py:361
  8.5 7.0 %collective-permute-start = (bf16[64,512]{1,0:T(8,128)(2,1)S(1)}, bf16[64,512]{1,0:T(8,128)(2,1)S(1)}, u32[]{:S(2)}, u32[]{:S(2)}) collective-permute-start(bf16[64,512]{1,0:T(8,128)(2,1)S(1)} %get-tuple-element.19), channel_id=1, source_target_pairs={{0,4},{2,6},{4,0},{6,2},{1,5},{3,7},{5,1},{7,3},{8,12},{10,14},{12... | collective-permute-start | bytes 196616 | tf_op jit(solution)/shard_map/ppermute | solution.py:365
  11.1 6.4 %collective-permute-start.1 = (bf16[64,512]{1,0:T(8,128)(2,1)S(1)}, bf16[64,512]{1,0:T(8,128)(2,1)S(1)}, u32[]{:S(2)}, u32[]{:S(2)}) collective-permute-start(bf16[64,512]{1,0:T(8,128)(2,1)S(1)} %get-tuple-element.20), channel_id=1, source_target_pairs={{0,6},{2,4},{4,2},{6,0},{1,7},{3,5},{5,3},{7,1},{8,14},{10,12},{12... | collective-permute-start | bytes 196616 | tf_op jit(solution)/shard_map/ppermute | solution.py:365
  12.4 5.4 %collective-permute-start.2 = (bf16[64,512]{1,0:T(8,128)(2,1)S(1)}, bf16[64,512]{1,0:T(8,128)(2,1)S(1)}, u32[]{:S(2)}, u32[]{:S(2)}) collective-permute-start(bf16[64,512]{1,0:T(8,128)(2,1)S(1)} %get-tuple-element.21), channel_id=1, source_target_pairs={{0,2},{2,0},{4,6},{6,4},{1,3},{3,1},{5,7},{7,5},{8,10},{10,8},{12,... | collective-permute-start | bytes 196616 | tf_op jit(solution)/shard_map/ppermute | solution.py:365
  17.9 5.0 %collective-permute-start.3 = (bf16[64,512]{1,0:T(8,128)(2,1)S(1)}, bf16[64,512]{1,0:T(8,128)(2,1)S(1)}, u32[]{:S(2)}, u32[]{:S(2)}) collective-permute-start(bf16[64,512]{1,0:T(8,128)(2,1)S(1)} %ratio_chunk.1.refs_0_), channel_id=1, source_target_pairs={{0,2},{2,0},{4,6},{6,4},{1,3},{3,1},{5,7},{7,5},{8,10},{10,8},{12,... | collective-permute-start | bytes 196616 | tf_op jit(solution)/shard_map/ppermute | solution.py:365
  18.6 7.9 %collective-permute-start.4 = (bf16[64,512]{1,0:T(8,128)(2,1)S(1)}, bf16[64,512]{1,0:T(8,128)(2,1)S(1)}, u32[]{:S(2)}, u32[]{:S(2)}) collective-permute-start(bf16[64,512]{1,0:T(8,128)(2,1)S(1)} %ratio_chunk.1.refs_0_), channel_id=1, source_target_pairs={{0,4},{2,6},{4,0},{6,2},{1,5},{3,7},{5,1},{7,3},{8,12},{10,14},{12... | collective-permute-start | bytes 196616 | tf_op jit(solution)/shard_map/ppermute | solution.py:365
  21.7 6.2 %collective-permute-start.5 = (bf16[64,512]{1,0:T(8,128)(2,1)S(1)}, bf16[64,512]{1,0:T(8,128)(2,1)S(1)}, u32[]{:S(2)}, u32[]{:S(2)}) collective-permute-start(bf16[64,512]{1,0:T(8,128)(2,1)S(1)} %ratio_chunk.1.refs_0_), channel_id=1, source_target_pairs={{0,6},{2,4},{4,2},{6,0},{1,7},{3,5},{5,3},{7,1},{8,14},{10,12},{12... | collective-permute-start | bytes 196616 | tf_op jit(solution)/shard_map/ppermute | solution.py:365
  27.9 1.6 %collective-permute-start.9 = (bf16[256,512]{1,0:T(8,128)(2,1)S(1)}, bf16[256,512]{1,0:T(8,128)(2,1)S(1)}, u32[]{:S(2)}, u32[]{:S(2)}) collective-permute-start(bf16[256,512]{1,0:T(8,128)(2,1)S(1)} %join_ratio.1.ratio_ref), channel_id=1, source_target_pairs={{0,8},{8,0},{16,24},{24,16},{1,9},{9,1},{17,25},{25,17},{2,10},{10... | collective-permute-start | bytes 786440 | tf_op jit(solution)/shard_map/ppermute | solution.py:365
  30.4 20.6 %collective-permute-start.13 = (bf16[256,1024]{1,0:T(8,128)(2,1)S(1)}, bf16[256,1024]{1,0:T(8,128)(2,1)S(1)}, u32[]{:S(2)}, u32[]{:S(2)}) collective-permute-start(bf16[256,1024]{1,0:T(8,128)(2,1)S(1)} %get-tuple-element.30.own_ref), channel_id=1, source_target_pairs={{0,16},{8,24},{16,0},{24,8},{1,17},{9,25},{17,1},{25,9},{2,18},{10... | collective-permute-start | bytes 1572872 | tf_op jit(solution)/shard_map/ppermute | solution.py:365
  32.0 19.7 %collective-permute-start.10 = (bf16[128,2048]{1,0:T(8,128)(2,1)S(1)}, bf16[128,2048]{1,0:T(8,128)(2,1)S(1)}, u32[]{:S(2)}, u32[]{:S(2)}) collective-permute-start(bf16[128,2048]{1,0:T(8,128)(2,1)S(1)} %hold.1.refs_2_), channel_id=1, source_target_pairs={{0,8},{8,0},{16,24},{24,16},{1,9},{9,1},{17,25},{25,17},{2,10},{10... | collective-permute-start | bytes 1572872 | tf_op jit(solution)/shard_map/ppermute | solution.py:365
  32.1 8.7 %collective-permute-start.8 = (bf16[256,512]{1,0:T(8,128)(2,1)S(1)}, bf16[256,512]{1,0:T(8,128)(2,1)S(1)}, u32[]{:S(2)}, u32[]{:S(2)}) collective-permute-start(bf16[256,512]{1,0:T(8,128)(2,1)S(1)} %join_ratio.1.ratio_ref), channel_id=1, source_target_pairs={{0,1},{1,0},{2,3},{3,2},{4,5},{5,4},{6,7},{7,6},{8,9},{9,8},{10,11... | collective-permute-start | bytes 786440 | tf_op jit(solution)/shard_map/ppermute | solution.py:361
  32.7 18.2 %collective-permute-start.11 = (bf16[256,512]{1,0:T(8,128)(2,1)S(1)}, bf16[256,512]{1,0:T(8,128)(2,1)S(1)}, u32[]{:S(2)}, u32[]{:S(2)}) collective-permute-start(bf16[256,512]{1,0:T(8,128)(2,1)S(1)} %beta_piece.2.rest_0_.own_ref), channel_id=1, source_target_pairs={{0,16},{8,24},{16,0},{24,8},{1,17},{9,25},{17,1},{25,9},{2,18},{10... | collective-permute-start | bytes 786440 | tf_op jit(solution)/shard_map/ppermute | solution.py:365
  33.2 23.4 %collective-permute-start.12 = (bf16[256,512]{1,0:T(8,128)(2,1)S(1)}, bf16[256,512]{1,0:T(8,128)(2,1)S(1)}, u32[]{:S(2)}, u32[]{:S(2)}) collective-permute-start(bf16[256,512]{1,0:T(8,128)(2,1)S(1)} %get-tuple-element.26.rest_0_.own_ref), channel_id=1, source_target_pairs={{0,16},{8,24},{16,0},{24,8},{1,17},{9,25},{17,1},{25,9},{2,18},{10... | collective-permute-start | bytes 786440 | tf_op jit(solution)/shard_map/ppermute | solution.py:365
  51.0 4.5 %collective-permute-start.14 = (bf16[256,512]{1,0:T(8,128)(2,1)S(1)}, bf16[256,512]{1,0:T(8,128)(2,1)S(1)}, u32[]{:S(2)}, u32[]{:S(2)}) collective-permute-start(bf16[256,512]{1,0:T(8,128)(2,1)S(1)} %add_pair.3.refs_5_.refs_0_), channel_id=1, source_target_pairs={{0,8},{8,0},{16,24},{24,16},{1,9},{9,1},{17,25},{25,17},{2,10},{10... | collective-permute-start | bytes 786440 | tf_op jit(solution)/shard_map/ppermute | solution.py:365
  51.2 4.3 %collective-permute-start.15 = (bf16[256,1024]{1,0:T(8,128)(2,1)S(1)}, bf16[256,1024]{1,0:T(8,128)(2,1)S(1)}, u32[]{:S(2)}, u32[]{:S(2)}) collective-permute-start(bf16[256,1024]{1,0:T(8,128)(2,1)S(1)} %add_pair.4.refs_1_), channel_id=1, source_target_pairs={{0,8},{8,0},{16,24},{24,16},{1,9},{9,1},{17,25},{25,17},{2,10},{10... | collective-permute-start | bytes 1572872 | tf_op jit(solution)/shard_map/ppermute | solution.py:365
  56.7 1.6 %collective-permute-start.16 = (bf16[256,512]{1,0:T(8,128)(2,1)S(1)}, bf16[256,512]{1,0:T(8,128)(2,1)S(1)}, u32[]{:S(2)}, u32[]{:S(2)}) collective-permute-start(bf16[256,512]{1,0:T(8,128)(2,1)S(1)} %add_pair.5.refs_0_), channel_id=1, source_target_pairs={{0,8},{8,0},{16,24},{24,16},{1,9},{9,1},{17,25},{25,17},{2,10},{10... | collective-permute-start | bytes 786440 | tf_op jit(solution)/shard_map/ppermute | solution.py:365

commit v6 on v5

--- a/solution.py
+++ b/solution.py
@@ -123,29 +123,25 @@
     slots, word_tile, doc_tile = word_counts.shape
     chunk = words // sizes.topic
 
-    def kernel(here_ref, doc_at, word_at, count_in, out_ref, held, sem):
-        copy = pltpu.make_async_copy(count_in, held, sem)
-        copy.start()
+    def kernel(here_ref, doc_at, word_at, count_ref, out_ref):
         first = sizes.topic_at(here_ref) * chunk
         block = first // word_tile
         row = pl.multiple_of(lax.rem(first, word_tile), chunk)
         out_ref[...] = jnp.zeros_like(out_ref)
-        copy.wait()
         for s in range(slots):
             @pl.when(word_at[s] == block)
             def _():
-                out_ref[:, window(doc_at[s], doc_tile)] = held[s, pl.ds(row, chunk), :].astype(F32)
+                out_ref[:, window(doc_at[s], doc_tile)] = count_ref[s, pl.ds(row, chunk), :].astype(F32)
 
     return pl.pallas_call(
         kernel,
         out_shape=jax.ShapeDtypeStruct((chunk, docs), F32),
-        in_specs=[SMEM, SMEM, SMEM, HBM],
-        out_specs=VMEM,
-        scratch_shapes=[pltpu.VMEM(word_counts.shape, jnp.int32), pltpu.SemaphoreType.DMA],
+        in_specs=[SMEM, SMEM, SMEM, VMEM],
+        out_specs=VMEM,
         compiler_params=call_params(),
         cost_estimate=cost(words * docs, 4 * words * docs),
         name="chunk_counts",
-    )(here, in_hbm(tile_doc), in_hbm(tile_word), in_hbm(word_counts))
+    )(here, in_hbm(tile_doc), in_hbm(tile_word), word_counts)
 
 
 def ratio_chunk(parts, counts, word_tile):
@@ -167,14 +163,14 @@
     )(*parts, counts)
 
 
-def join_ratio(sizes, here, chunks, after):
+def join_ratio(sizes, here, chunks, order, after):
     rows, docs = chunks[0].shape
     count = sizes.topic
 
     def kernel(here_ref, *refs):
         topic_at = sizes.topic_at(here_ref)
-        for s in range(count):
-            refs[-1][window(topic_at ^ s, rows), :] = refs[s][...]
+        for s, ref in zip(order, refs):
+            refs[-1][window(topic_at ^ s, rows), :] = ref[...]
 
     return pl.pallas_call(
         kernel,
@@ -260,7 +256,7 @@
     )(array, *after)
 
 
-def theta_grad(sizes, here, ratio, far_ratios, prob_held, far_logits, log_norm, after):
+def theta_grad(sizes, here, ratio, far_ratios, prob_held, far_logits, log_norm):
     words, docs = ratio.shape
     half = words // 2
     share = far_logits[0].shape[1]
@@ -305,8 +301,7 @@
             in_specs=[pl.BlockSpec((words, docs), whole)] * count
             + [pl.BlockSpec((words, span), held)]
             + [pl.BlockSpec((half, span), column)] * (2 * far)
-            + [pl.BlockSpec((1, span), held)]
-            + [ANY] * len(after),
+            + [pl.BlockSpec((1, span), held)],
             out_specs=[pl.BlockSpec((docs, span), column), pl.BlockSpec((8, 128), whole)],
             scratch_shapes=[pltpu.VMEM((docs, count * words), BF16)],
         ),
@@ -315,17 +310,15 @@
             20 * count * words * docs * share, (40 * docs + 20 * count * words) * share, 10 * count * words * share
         ),
         name="theta_grad",
-    )(here, ratio, *far_ratios, prob_held, *far_logits, log_norm, *after)
-
-
-def place_pieces(sizes, here, own, other, starts, shape, so_far=None):
+    )(here, ratio, *far_ratios, prob_held, *far_logits, log_norm)
+
+
+def place_pieces(sizes, here, own, other, starts, shape):
     pieces = len(own)
     side_width = shape[1] // 2
-    before = [] if so_far is None else [so_far]
 
     def kernel(here_ref, *refs):
-        own_refs, other_refs, (out_ref, done_ref, sems) = refs[:pieces], refs[pieces : 2 * pieces], refs[-3:]
-        done_ref[...] = jnp.zeros_like(done_ref)
+        own_refs, other_refs, (out_ref, sems) = refs[:pieces], refs[pieces : 2 * pieces], refs[-2:]
         side = sizes.side(here_ref)
         copies = []
         for p in range(pieces):
@@ -340,15 +333,14 @@
 
     return pl.pallas_call(
         kernel,
-        out_shape=[jax.ShapeDtypeStruct(shape, BF16), jax.ShapeDtypeStruct((8, 128), F32)],
-        in_specs=[SMEM] + [VMEM] * (2 * pieces) + [HBM] * len(before),
-        out_specs=[HBM, VMEM],
+        out_shape=jax.ShapeDtypeStruct(shape, BF16),
+        in_specs=[SMEM] + [VMEM] * (2 * pieces),
+        out_specs=HBM,
         scratch_shapes=[pltpu.SemaphoreType.DMA((2, pieces))],
-        input_output_aliases={2 * pieces + 1: 0} if before else {},
-        compiler_params=call_params(),
-        cost_estimate=cost(0, 4 * sum(part.size for part in own)),
+        compiler_params=call_params(),
+        cost_estimate=cost(0, 4 * shape[0] * shape[1]),
         name="place_pieces",
-    )(here, *own, *other, *before)
+    )(here, *own, *other)
 
 
 def on_device(sizes, doc_topics, word_logits, log_norm, tile_doc, tile_word, word_counts):
@@ -373,10 +365,8 @@
     arrived = [swap(parts[s], "topic", s) for s in order]
     counts = chunk_counts(sizes, here, word_counts, tile_doc, tile_word, docs, words)
     own_ratio = ratio_chunk([parts[0]] + arrived, counts, word_tile)
-    gathered = {s: swap(own_ratio, "topic", s) for s in order}
-    ratio = join_ratio(
-        sizes, here, [own_ratio] + [gathered[s] for s in range(1, sizes.topic)], near_logits + [sibling_docs]
-    )
+    gathered = [own_ratio] + [swap(own_ratio, "topic", s) for s in order]
+    ratio = join_ratio(sizes, here, gathered, [0] + order, near_logits + [sibling_docs])
     sibling_ratio = swap(ratio, "doc", 1)
     far_ratios = [shift(ratio, s) for s in range(1, sizes.vocab)]
 
@@ -398,14 +388,9 @@
         sums = [add_pair(part, swap(part, "doc", bit)) for part in sums]
         bit *= 2
     others = [swap(part, "doc", bit) for part in sums]
-    first = add_pair(sums[0], others[0], far_ratios)
-    theta, theta_done = theta_grad(sizes, here, ratio, far_ratios, prob_held, far_logits, norm_held, [first])
-    early = [first, add_pair(sums[1], others[1])]
-    out, early_done = place_pieces(
-        sizes, here, early, [swap(part, "doc", 1) for part in early], starts[:-1], word_logits.shape
-    )
-    last = add_pair(sums[-1], others[-1], [theta_done, early_done])
-    out, _ = place_pieces(sizes, here, [last], [swap(last, "doc", 1)], starts[-1:], word_logits.shape, out)
+    theta, theta_done = theta_grad(sizes, here, ratio, far_ratios, prob_held, far_logits, norm_held)
+    sums = [add_pair(*pair, [theta_done]) for pair in zip(sums, others)]
+    out = place_pieces(sizes, here, sums, [swap(part, "doc", 1) for part in sums], starts, word_logits.shape)
     return theta, out
 
 

time: 59.9 us -> 59.8 us (level)
  waiting for transfers between devices: 27.4 us -> 30.1 us
  Pallas kernels: 14.8 us -> 12.7 us
  starting transfers between devices: 16.8 us -> 16.1 us
    ppermute x15, waiting for transfers between devices: 21.3 us -> 25.6 us  [swap(): return lax.ppermute(array, axis, [(i, i ^ bits) for i in range(count)])]
    ppermute x2, waiting for transfers between devices: 6.13 us -> 4.54 us  [shift(): lax.ppermute(array, 'vocab', [(i, (i + by) % sizes.vocab) for i in range(...]
    pallas_call x2 -> x1, Pallas kernels: 2.57 us -> 1.36 us  [place_pieces(): pl.pallas_call(kernel, out_shape=jax.ShapeDtypeStruct(shape, BF16), in_sp...]
    pallas_call x1, Pallas kernels: 1.77 us -> 0.83 us  [chunk_counts(): pl.pallas_call(kernel, out_shape=jax.ShapeDtypeStruct((chunk, docs), F32)...]
  transfers between devices with their start and end apart: 17 -> 17, of which waited for: 10 -> 10; matrix products, arithmetic and copies ran while one was open for 0% -> 0% of each run, Pallas kernels for 13% -> 9%
where the time goes in v6:
time: 59.8 us; the launch traced here: 59.7 us
  waiting for transfers between devices  30.1 us (50%)
  starting transfers between devices  16.1 us (27%)
  Pallas kernels  12.7 us (21%)
  between operations  0.75 us (1%)
    ppermute x15, waiting for transfers between devices, swap(): return lax.ppermute(array, axis, [(i, i ^ bits) for i in range(count)])  25.6 us
    ppermute x15, starting transfers between devices, swap(): return lax.ppermute(array, axis, [(i, i ^ bits) for i in range(count)])  13 us
    pallas_call x1, Pallas kernels, rate_partial(): pl.pallas_call(kernel, out_shape=[jax.ShapeDtypeStruct((chunk, docs), BF1...  4.79 us
    ppermute x2, waiting for transfers between devices, shift(): lax.ppermute(array, 'vocab', [(i, (i + by) % sizes.vocab) for i in range(...  4.54 us
    pallas_call x1, Pallas kernels, theta_grad(): pl.pallas_call(kernel, out_shape=[jax.ShapeDtypeStruct((docs, share), F32...  3.71 us
    ppermute x2, starting transfers between devices, shift(): lax.ppermute(array, 'vocab', [(i, (i + by) % sizes.vocab) for i in range(...  3.11 us
    pallas_call x1, Pallas kernels, place_pieces(): pl.pallas_call(kernel, out_shape=jax.ShapeDtypeStruct(shape, BF16), in_sp...  1.36 us
  transfers between devices with their start and end apart: 17, of which 10 were waited for; matrix products, arithmetic and copies ran while one was open for 0% of the time, Pallas kernels for 9%

profile of v6, /device:TPU:0, one launch (start us, length us, event | category | flops | bytes accessed | tf_op | source)
XLA Modules:
  0.0 59.7 jit_solution(10692156867795708164)
XLA Ops:
  0.6 4.8 %rate_partial.1 = (bf16[64,512]{1,0:T(8,128)(2,1)S(1)}, bf16[64,512]{1,0:T(8,128)(2,1)S(1)}, bf16[64,512]{1,0:T(8,128)(2,1)S(1)}, bf16[64,512]{1,0:T(8,128)(2,1)...) custom-call(s32[1]{0:T(128)} %bitcast.here_ref, ...), custom_call_target="tpu_custom_call" | custom-call | flops 1073741824 | bytes 6291456 | tf_op jit(solution)/shard_map/rate_partial/pallas_call | solution.py:97
  5.4 0.5 collective-permute-start.7
  6.0 2.6 %collective-permute-start.6 = (bf16[128,2048]{1,0:T(8,128)(2,1)S(1)}, bf16[128,2048]{1,0:T(8,128)(2,1)S(1)}, u32[]{:S(2)}, u32[]{:S(2)}) collective-permute-start(bf16[128,2048]{1,0:T(8,128)(2,1)S(1)} %get-tuple-element.19), channel_id=1, source_target_pairs={{0,1},{1,0},{2,3},{3,2},{4,5},{5,4},{6,7},{7,6},{8,9},{9,8},{10,11... | collective-permute-start | bytes 1572872 | tf_op jit(solution)/shard_map/ppermute | solution.py:353
  8.6 2.6 %collective-permute-start = (bf16[64,512]{1,0:T(8,128)(2,1)S(1)}, bf16[64,512]{1,0:T(8,128)(2,1)S(1)}, u32[]{:S(2)}, u32[]{:S(2)}) collective-permute-start(bf16[64,512]{1,0:T(8,128)(2,1)S(1)} %get-tuple-element.16), channel_id=1, source_target_pairs={{0,4},{2,6},{4,0},{6,2},{1,5},{3,7},{5,1},{7,3},{8,12},{10,14},{12... | collective-permute-start | bytes 196616 | tf_op jit(solution)/shard_map/ppermute | solution.py:357
  11.1 1.4 %collective-permute-start.1 = (bf16[64,512]{1,0:T(8,128)(2,1)S(1)}, bf16[64,512]{1,0:T(8,128)(2,1)S(1)}, u32[]{:S(2)}, u32[]{:S(2)}) collective-permute-start(bf16[64,512]{1,0:T(8,128)(2,1)S(1)} %get-tuple-element.17), channel_id=1, source_target_pairs={{0,6},{2,4},{4,2},{6,0},{1,7},{3,5},{5,3},{7,1},{8,14},{10,12},{12... | collective-permute-start | bytes 196616 | tf_op jit(solution)/shard_map/ppermute | solution.py:357
  12.5 0.2 collective-permute-start.2
  12.7 0.8 %chunk_counts.1.refs_4_ = f32[64,512]{1,0:T(8,128)S(1)} custom-call(s32[1]{0:T(128)} %bitcast.here_ref, s32[16]{0:T(128)} %doc_at.1, s32[16]{0:T(128)} %word_at.1, s32[16,64,128]{2,1,0:T(8,128)S(1)} %copy-done), custom_call_target="tpu_custom_call" | custom-call | flops 131072 | bytes 524288 | tf_op jit(solution)/shard_map/chunk_counts/pallas_call | solution.py:136
  13.6 2.0 %collective-permute-done.refs_1_ = bf16[64,512]{1,0:T(8,128)(2,1)S(1)} collective-permute-done((bf16[64,512]{1,0:T(8,128)(2,1)S(1)}, bf16[64,512]{1,0:T(8,128)(2,1)S(1)}, u32[]{:S(2)}, u32[]{:S(2)}) %collective-permute-start) | collective-permute-done | bytes 65568 | tf_op jit(solution)/shard_map/ppermute | solution.py:357
  15.6 2.0 %collective-permute-done.1.refs_2_ = bf16[64,512]{1,0:T(8,128)(2,1)S(1)} collective-permute-done((bf16[64,512]{1,0:T(8,128)(2,1)S(1)}, bf16[64,512]{1,0:T(8,128)(2,1)S(1)}, u32[]{:S(2)}, u32[]{:S(2)}) %collective-permute-start.1) | collective-permute-done | bytes 65568 | tf_op jit(solution)/shard_map/ppermute | solution.py:357
  17.6 0.3 collective-permute-done.2.refs_3_
  17.9 2.6 %collective-permute-start.3 = (bf16[64,512]{1,0:T(8,128)(2,1)S(1)}, bf16[64,512]{1,0:T(8,128)(2,1)S(1)}, u32[]{:S(2)}, u32[]{:S(2)}) collective-permute-start(bf16[64,512]{1,0:T(8,128)(2,1)S(1)} %ratio_chunk.1.refs_0_), channel_id=1, source_target_pairs={{0,4},{2,6},{4,0},{6,2},{1,5},{3,7},{5,1},{7,3},{8,12},{10,14},{12... | collective-permute-start | bytes 196616 | tf_op jit(solution)/shard_map/ppermute | solution.py:357
  20.6 0.7 %collective-permute-start.4 = (bf16[64,512]{1,0:T(8,128)(2,1)S(1)}, bf16[64,512]{1,0:T(8,128)(2,1)S(1)}, u32[]{:S(2)}, u32[]{:S(2)}) collective-permute-start(bf16[64,512]{1,0:T(8,128)(2,1)S(1)} %ratio_chunk.1.refs_0_), channel_id=1, source_target_pairs={{0,6},{2,4},{4,2},{6,0},{1,7},{3,5},{5,3},{7,1},{8,14},{10,12},{12... | collective-permute-start | bytes 196616 | tf_op jit(solution)/shard_map/ppermute | solution.py:357
  21.3 0.5 collective-permute-start.5
  21.8 3.0 %collective-permute-done.3.refs_1_ = bf16[64,512]{1,0:T(8,128)(2,1)S(1)} collective-permute-done((bf16[64,512]{1,0:T(8,128)(2,1)S(1)}, bf16[64,512]{1,0:T(8,128)(2,1)S(1)}, u32[]{:S(2)}, u32[]{:S(2)}) %collective-permute-start.3) | collective-permute-done | bytes 65568 | tf_op jit(solution)/shard_map/ppermute | solution.py:357
  24.8 2.2 %collective-permute-done.4.refs_2_ = bf16[64,512]{1,0:T(8,128)(2,1)S(1)} collective-permute-done((bf16[64,512]{1,0:T(8,128)(2,1)S(1)}, bf16[64,512]{1,0:T(8,128)(2,1)S(1)}, u32[]{:S(2)}, u32[]{:S(2)}) %collective-permute-start.4) | collective-permute-done | bytes 65568 | tf_op jit(solution)/shard_map/ppermute | solution.py:357
  27.1 0.7 %own_product.1.product_ref = f32[256,2048]{1,0:T(8,128)S(1)} custom-call(bf16[256,512]{1,0:T(8,128)(2,1)S(1)} %join_ratio.1.ratio_ref, bf16[512,2048]{1,0:T(8,128)(2,1)S(1)} %get-tuple-element.22.doc_ref), custom_call_target="tpu_custom_call" | custom-call | flops 536870912 | bytes 4194304 | tf_op jit(solution)/shard_map/own_product/pallas_call | solution.py:193
  27.8 0.8 %collective-permute-done.9.ratio_ref = bf16[256,512]{1,0:T(8,128)(2,1)S(1)} collective-permute-done((bf16[256,512]{1,0:T(8,128)(2,1)S(1)}, bf16[256,512]{1,0:T(8,128)(2,1)S(1)}, u32[]{:S(2)}, u32[]{:S(2)}) %collective-permute-start.9) | collective-permute-done | bytes 262176 | tf_op jit(solution)/shard_map/ppermute | solution.py:357
  28.6 0.3 beta_piece.2.rest_0_.own_ref
  28.9 0.6 %beta_piece.3 = (bf16[256,1024]{1,0:T(8,128)(2,1)S(1)}, bf16[256,512]{1,0:T(8,128)(2,1)S(1)}) custom-call(s32[1]{0:T(128)} %bitcast.here_ref, f32[256,2048]{1,0:T(8,128)S(1)} %own_product.1.product_ref, bf16[256,512]{1,0:T(8,128)(2,1)S(1)} %collective-permute-done.9.ratio_ref, bf16[512,2048]{1,0:T(8,128)(2,1)S(1)} %collective-permute-done.7.refs_5_.doc_ref, ...), custom_call_target="tpu_custom_call" | custom-call | flops 402653184 | bytes 4718592 | tf_op jit(solution)/shard_map/beta_piece/pallas_call | solution.py:218
  29.6 0.2 collective-permute-start.10
  29.8 0.5 collective-permute-start.8
  30.3 1.5 %collective-permute-start.13 = (bf16[256,512]{1,0:T(8,128)(2,1)S(1)}, bf16[256,512]{1,0:T(8,128)(2,1)S(1)}, u32[]{:S(2)}, u32[]{:S(2)}) collective-permute-start(bf16[256,512]{1,0:T(8,128)(2,1)S(1)} %get-tuple-element.23.rest_0_.own_ref), channel_id=1, source_target_pairs={{0,16},{8,24},{16,0},{24,8},{1,17},{9,25},{17,1},{25,9},{2,18},{10... | collective-permute-start | bytes 786440 | tf_op jit(solution)/shard_map/ppermute | solution.py:357
  31.8 0.5 collective-permute-start.11
  32.4 1.5 %collective-permute-start.12 = (bf16[256,1024]{1,0:T(8,128)(2,1)S(1)}, bf16[256,1024]{1,0:T(8,128)(2,1)S(1)}, u32[]{:S(2)}, u32[]{:S(2)}) collective-permute-start(bf16[256,1024]{1,0:T(8,128)(2,1)S(1)} %get-tuple-element.27.own_ref), channel_id=1, source_target_pairs={{0,16},{8,24},{16,0},{24,8},{1,17},{9,25},{17,1},{25,9},{2,18},{10... | collective-permute-start | bytes 1572872 | tf_op jit(solution)/shard_map/ppermute | solution.py:357
  33.8 4.5 %collective-permute-done.8.refs_0_ = bf16[256,512]{1,0:T(8,128)(2,1)S(1)} collective-permute-done((bf16[256,512]{1,0:T(8,128)(2,1)S(1)}, bf16[256,512]{1,0:T(8,128)(2,1)S(1)}, u32[]{:S(2)}, u32[]{:S(2)}) %collective-permute-start.8) | collective-permute-done | bytes 262176 | tf_op jit(solution)/shard_map/ppermute | solution.py:353
  38.4 3.7 %theta_grad.1 = (f32[512,2048]{1,0:T(8,128)}, f32[8,128]{1,0:T(8,128)S(1)}) custom-call(s32[1]{0:T(128)} %bitcast.here_ref, bf16[256,512]{1,0:T(8,128)(2,1)S(1)} %join_ratio.1.ratio_ref, bf16[256,512]{1,0:T(8,128)(2,1)S(1)} %collective-permute-done.8.refs_0_, bf16[256,4096]{1,0:T(8,128)(2,1)S(1)} %get-tuple-element.21.prob_ref.refs_1_, ...), custom_call_target="tpu_custom_call" | custom-call | flops 10737418240 | bytes 62914560 | tf_op jit(solution)/shard_map/theta_grad/pallas_call | solution.py:295
  42.1 13.4 %collective-permute-done.12.other_ref = bf16[256,1024]{1,0:T(8,128)(2,1)S(1)} collective-permute-done((bf16[256,1024]{1,0:T(8,128)(2,1)S(1)}, bf16[256,1024]{1,0:T(8,128)(2,1)S(1)}, u32[]{:S(2)}, u32[]{:S(2)}) %collective-permute-start.12) | collective-permute-done | bytes 524320 | tf_op jit(solution)/shard_map/ppermute | solution.py:357
  55.5 0.1 add_pair.4.refs_1_
  55.8 0.5 collective-permute-start.16
  56.5 1.5 %collective-permute-done.16.refs_5_ = bf16[256,512]{1,0:T(8,128)(2,1)S(1)} collective-permute-done((bf16[256,512]{1,0:T(8,128)(2,1)S(1)}, bf16[256,512]{1,0:T(8,128)(2,1)S(1)}, u32[]{:S(2)}, u32[]{:S(2)}) %collective-permute-start.16) | collective-permute-done | bytes 262176 | tf_op jit(solution)/shard_map/ppermute | solution.py:357
  57.9 0.4 collective-permute-done.14.refs_3_
  58.3 1.4 %place_pieces.1 = bf16[256,4096]{1,0:T(8,128)(2,1)} custom-call(s32[1]{0:T(128)} %bitcast.here_ref, bf16[256,512]{1,0:T(8,128)(2,1)S(1)} %add_pair.3.refs_0_, bf16[256,1024]{1,0:T(8,128)(2,1)S(1)} %add_pair.4.refs_1_, bf16[256,512]{1,0:T(8,128)(2,1)S(1)} %add_pair.5.refs_2_, bf16[256,512]{1,0:T(8,128)(2,1)S(1)} %collective-permute-done.14.refs_3_, ...), custom_call_target="tpu_custom_call" | custom-call | bytes 4194304 | tf_op jit(solution)/shard_map/place_pieces/pallas_call | solution.py:334
  (17 shorter events, 0.5 us)
Async XLA Ops:
  0.6 12.1 %copy-start = (s32[16,64,128]{2,1,0:T(8,128)S(1)}, s32[16,64,128]{2,1,0:T(8,128)}, u32[]{:S(2)}) copy-start(s32[16,64,128]{2,1,0:T(8,128)} %count_ref.1) | copy-start | bytes 1572868
  5.4 21.6 %collective-permute-start.7 = (bf16[512,2048]{1,0:T(8,128)(2,1)S(1)}, bf16[512,2048]{1,0:T(8,128)(2,1)S(1)}, u32[]{:S(2)}, u32[]{:S(2)}) collective-permute-start(bf16[512,2048]{1,0:T(8,128)(2,1)S(1)} %get-tuple-element.20), channel_id=1, source_target_pairs={{0,8},{8,0},{16,24},{24,16},{1,9},{9,1},{17,25},{25,17},{2,10},{10... | collective-permute-start | bytes 6291464 | tf_op jit(solution)/shard_map/ppermute | solution.py:357
  6.0 21.0 %collective-permute-start.6 = (bf16[128,2048]{1,0:T(8,128)(2,1)S(1)}, bf16[128,2048]{1,0:T(8,128)(2,1)S(1)}, u32[]{:S(2)}, u32[]{:S(2)}) collective-permute-start(bf16[128,2048]{1,0:T(8,128)(2,1)S(1)} %get-tuple-element.19), channel_id=1, source_target_pairs={{0,1},{1,0},{2,3},{3,2},{4,5},{5,4},{6,7},{7,6},{8,9},{9,8},{10,11... | collective-permute-start | bytes 1572872 | tf_op jit(solution)/shard_map/ppermute | solution.py:353
  8.6 7.0 %collective-permute-start = (bf16[64,512]{1,0:T(8,128)(2,1)S(1)}, bf16[64,512]{1,0:T(8,128)(2,1)S(1)}, u32[]{:S(2)}, u32[]{:S(2)}) collective-permute-start(bf16[64,512]{1,0:T(8,128)(2,1)S(1)} %get-tuple-element.16), channel_id=1, source_target_pairs={{0,4},{2,6},{4,0},{6,2},{1,5},{3,7},{5,1},{7,3},{8,12},{10,14},{12... | collective-permute-start | bytes 196616 | tf_op jit(solution)/shard_map/ppermute | solution.py:357
  11.1 6.4 %collective-permute-start.1 = (bf16[64,512]{1,0:T(8,128)(2,1)S(1)}, bf16[64,512]{1,0:T(8,128)(2,1)S(1)}, u32[]{:S(2)}, u32[]{:S(2)}) collective-permute-start(bf16[64,512]{1,0:T(8,128)(2,1)S(1)} %get-tuple-element.17), channel_id=1, source_target_pairs={{0,6},{2,4},{4,2},{6,0},{1,7},{3,5},{5,3},{7,1},{8,14},{10,12},{12... | collective-permute-start | bytes 196616 | tf_op jit(solution)/shard_map/ppermute | solution.py:357
  12.5 5.4 %collective-permute-start.2 = (bf16[64,512]{1,0:T(8,128)(2,1)S(1)}, bf16[64,512]{1,0:T(8,128)(2,1)S(1)}, u32[]{:S(2)}, u32[]{:S(2)}) collective-permute-start(bf16[64,512]{1,0:T(8,128)(2,1)S(1)} %get-tuple-element.18), channel_id=1, source_target_pairs={{0,2},{2,0},{4,6},{6,4},{1,3},{3,1},{5,7},{7,5},{8,10},{10,8},{12,... | collective-permute-start | bytes 196616 | tf_op jit(solution)/shard_map/ppermute | solution.py:357
  17.9 6.8 %collective-permute-start.3 = (bf16[64,512]{1,0:T(8,128)(2,1)S(1)}, bf16[64,512]{1,0:T(8,128)(2,1)S(1)}, u32[]{:S(2)}, u32[]{:S(2)}) collective-permute-start(bf16[64,512]{1,0:T(8,128)(2,1)S(1)} %ratio_chunk.1.refs_0_), channel_id=1, source_target_pairs={{0,4},{2,6},{4,0},{6,2},{1,5},{3,7},{5,1},{7,3},{8,12},{10,14},{12... | collective-permute-start | bytes 196616 | tf_op jit(solution)/shard_map/ppermute | solution.py:357
  20.6 6.4 %collective-permute-start.4 = (bf16[64,512]{1,0:T(8,128)(2,1)S(1)}, bf16[64,512]{1,0:T(8,128)(2,1)S(1)}, u32[]{:S(2)}, u32[]{:S(2)}) collective-permute-start(bf16[64,512]{1,0:T(8,128)(2,1)S(1)} %ratio_chunk.1.refs_0_), channel_id=1, source_target_pairs={{0,6},{2,4},{4,2},{6,0},{1,7},{3,5},{5,3},{7,1},{8,14},{10,12},{12... | collective-permute-start | bytes 196616 | tf_op jit(solution)/shard_map/ppermute | solution.py:357
  21.3 5.7 %collective-permute-start.5 = (bf16[64,512]{1,0:T(8,128)(2,1)S(1)}, bf16[64,512]{1,0:T(8,128)(2,1)S(1)}, u32[]{:S(2)}, u32[]{:S(2)}) collective-permute-start(bf16[64,512]{1,0:T(8,128)(2,1)S(1)} %ratio_chunk.1.refs_0_), channel_id=1, source_target_pairs={{0,2},{2,0},{4,6},{6,4},{1,3},{3,1},{5,7},{7,5},{8,10},{10,8},{12,... | collective-permute-start | bytes 196616 | tf_op jit(solution)/shard_map/ppermute | solution.py:357
  27.0 1.6 %collective-permute-start.9 = (bf16[256,512]{1,0:T(8,128)(2,1)S(1)}, bf16[256,512]{1,0:T(8,128)(2,1)S(1)}, u32[]{:S(2)}, u32[]{:S(2)}) collective-permute-start(bf16[256,512]{1,0:T(8,128)(2,1)S(1)} %join_ratio.1.ratio_ref), channel_id=1, source_target_pairs={{0,8},{8,0},{16,24},{24,16},{1,9},{9,1},{17,25},{25,17},{2,10},{10... | collective-permute-start | bytes 786440 | tf_op jit(solution)/shard_map/ppermute | solution.py:357
  29.6 8.8 %collective-permute-start.10 = (bf16[128,2048]{1,0:T(8,128)(2,1)S(1)}, bf16[128,2048]{1,0:T(8,128)(2,1)S(1)}, u32[]{:S(2)}, u32[]{:S(2)}) collective-permute-start(bf16[128,2048]{1,0:T(8,128)(2,1)S(1)} %hold.1.refs_2_), channel_id=1, source_target_pairs={{0,8},{8,0},{16,24},{24,16},{1,9},{9,1},{17,25},{25,17},{2,10},{10... | collective-permute-start | bytes 1572872 | tf_op jit(solution)/shard_map/ppermute | solution.py:357
  29.8 8.6 %collective-permute-start.8 = (bf16[256,512]{1,0:T(8,128)(2,1)S(1)}, bf16[256,512]{1,0:T(8,128)(2,1)S(1)}, u32[]{:S(2)}, u32[]{:S(2)}) collective-permute-start(bf16[256,512]{1,0:T(8,128)(2,1)S(1)} %join_ratio.1.ratio_ref), channel_id=1, source_target_pairs={{0,1},{1,0},{2,3},{3,2},{4,5},{5,4},{6,7},{7,6},{8,9},{9,8},{10,11... | collective-permute-start | bytes 786440 | tf_op jit(solution)/shard_map/ppermute | solution.py:353
  30.3 25.3 %collective-permute-start.13 = (bf16[256,512]{1,0:T(8,128)(2,1)S(1)}, bf16[256,512]{1,0:T(8,128)(2,1)S(1)}, u32[]{:S(2)}, u32[]{:S(2)}) collective-permute-start(bf16[256,512]{1,0:T(8,128)(2,1)S(1)} %get-tuple-element.23.rest_0_.own_ref), channel_id=1, source_target_pairs={{0,16},{8,24},{16,0},{24,8},{1,17},{9,25},{17,1},{25,9},{2,18},{10... | collective-permute-start | bytes 786440 | tf_op jit(solution)/shard_map/ppermute | solution.py:357
  31.8 24.5 %collective-permute-start.11 = (bf16[256,512]{1,0:T(8,128)(2,1)S(1)}, bf16[256,512]{1,0:T(8,128)(2,1)S(1)}, u32[]{:S(2)}, u32[]{:S(2)}) collective-permute-start(bf16[256,512]{1,0:T(8,128)(2,1)S(1)} %beta_piece.2.rest_0_.own_ref), channel_id=1, source_target_pairs={{0,16},{8,24},{16,0},{24,8},{1,17},{9,25},{17,1},{25,9},{2,18},{10... | collective-permute-start | bytes 786440 | tf_op jit(solution)/shard_map/ppermute | solution.py:357
  32.4 23.1 %collective-permute-start.12 = (bf16[256,1024]{1,0:T(8,128)(2,1)S(1)}, bf16[256,1024]{1,0:T(8,128)(2,1)S(1)}, u32[]{:S(2)}, u32[]{:S(2)}) collective-permute-start(bf16[256,1024]{1,0:T(8,128)(2,1)S(1)} %get-tuple-element.27.own_ref), channel_id=1, source_target_pairs={{0,16},{8,24},{16,0},{24,8},{1,17},{9,25},{17,1},{25,9},{2,18},{10... | collective-permute-start | bytes 1572872 | tf_op jit(solution)/shard_map/ppermute | solution.py:357
  55.6 2.7 %collective-permute-start.15 = (bf16[256,1024]{1,0:T(8,128)(2,1)S(1)}, bf16[256,1024]{1,0:T(8,128)(2,1)S(1)}, u32[]{:S(2)}, u32[]{:S(2)}) collective-permute-start(bf16[256,1024]{1,0:T(8,128)(2,1)S(1)} %add_pair.4.refs_1_), channel_id=1, source_target_pairs={{0,8},{8,0},{16,24},{24,16},{1,9},{9,1},{17,25},{25,17},{2,10},{10... | collective-permute-start | bytes 1572872 | tf_op jit(solution)/shard_map/ppermute | solution.py:357
  55.8 2.2 %collective-permute-start.16 = (bf16[256,512]{1,0:T(8,128)(2,1)S(1)}, bf16[256,512]{1,0:T(8,128)(2,1)S(1)}, u32[]{:S(2)}, u32[]{:S(2)}) collective-permute-start(bf16[256,512]{1,0:T(8,128)(2,1)S(1)} %add_pair.5.refs_2_), channel_id=1, source_target_pairs={{0,8},{8,0},{16,24},{24,16},{1,9},{9,1},{17,25},{25,17},{2,10},{10... | collective-permute-start | bytes 786440 | tf_op jit(solution)/shard_map/ppermute | solution.py:357
  56.4 1.9 %collective-permute-start.14 = (bf16[256,512]{1,0:T(8,128)(2,1)S(1)}, bf16[256,512]{1,0:T(8,128)(2,1)S(1)}, u32[]{:S(2)}, u32[]{:S(2)}) collective-permute-start(bf16[256,512]{1,0:T(8,128)(2,1)S(1)} %add_pair.3.refs_0_), channel_id=1, source_target_pairs={{0,8},{8,0},{16,24},{24,16},{1,9},{9,1},{17,25},{25,17},{2,10},{10... | collective-permute-start | bytes 786440 | tf_op jit(solution)/shard_map/ppermute | solution.py:357

commit v7 on v6

--- a/solution.py
+++ b/solution.py
@@ -46,13 +46,13 @@
         return lax.rem(lax.div(here_ref[0], self.vocab * self.topic), 2)
 
 
-def rate_partial(sizes, here, doc_topics, word_logits, log_norm):
+def rate_partial(sizes, here, doc_topics, word_logits, log_norm, groups):
     docs, width = doc_topics.shape
     words = word_logits.shape[0]
     side_width = width // 2
     span = min(side_width, 1024)
     steps = side_width // span
-    count, far = sizes.topic, sizes.vocab - 1
+    count, far = groups * sizes.topic, sizes.vocab - 1
     chunk, half, share = words // count, words // 2, width // sizes.vocab
 
     def kernel(here_ref, doc_in, logit_in, norm_in, *rest):
@@ -87,8 +87,9 @@
             else:
                 acc[...] += part
         topic_at = sizes.topic_at(here_ref)
-        for s in range(count):
-            parts[s][...] = acc[window(topic_at ^ s, chunk), :].astype(BF16)
+        for i in range(count):
+            g, s = divmod(i, sizes.topic)
+            parts[i][...] = acc[window(g * sizes.topic + (topic_at ^ s), chunk), :].astype(BF16)
         rows = window(side, half)
         for s in range(far):
             target = lax.rem(sizes.vocab_at(here_ref) + s + 1, sizes.vocab)
@@ -116,37 +117,39 @@
         cost_estimate=cost(2 * words * docs * width, 2 * (words + docs) * width, words * width),
         name="rate_partial",
     )(here, in_hbm(doc_topics), in_hbm(word_logits), in_hbm(log_norm))
-    return out[:count], out[count : count + far], *out[count + far :]
-
-
-def chunk_counts(sizes, here, word_counts, tile_doc, tile_word, docs, words):
+    parts = [out[g * sizes.topic : (g + 1) * sizes.topic] for g in range(groups)]
+    return parts, out[count : count + far], *out[count + far :]
+
+
+def chunk_counts(sizes, here, word_counts, tile_doc, tile_word, docs, words, groups):
     slots, word_tile, doc_tile = word_counts.shape
-    chunk = words // sizes.topic
-
-    def kernel(here_ref, doc_at, word_at, count_ref, out_ref):
-        first = sizes.topic_at(here_ref) * chunk
-        block = first // word_tile
-        row = pl.multiple_of(lax.rem(first, word_tile), chunk)
-        out_ref[...] = jnp.zeros_like(out_ref)
-        for s in range(slots):
-            @pl.when(word_at[s] == block)
-            def _():
-                out_ref[:, window(doc_at[s], doc_tile)] = count_ref[s, pl.ds(row, chunk), :].astype(F32)
-
-    return pl.pallas_call(
-        kernel,
-        out_shape=jax.ShapeDtypeStruct((chunk, docs), F32),
+    chunk = words // (groups * sizes.topic)
+
+    def kernel(here_ref, doc_at, word_at, count_ref, *out_refs):
+        for g, out_ref in enumerate(out_refs):
+            first = (g * sizes.topic + sizes.topic_at(here_ref)) * chunk
+            block = first // word_tile
+            row = pl.multiple_of(lax.rem(first, word_tile), chunk)
+            out_ref[...] = jnp.zeros_like(out_ref)
+            for s in range(slots):
+                @pl.when(word_at[s] == block)
+                def _():
+                    out_ref[:, window(doc_at[s], doc_tile)] = count_ref[s, pl.ds(row, chunk), :].astype(F32)
+
+    return pl.pallas_call(
+        kernel,
+        out_shape=[jax.ShapeDtypeStruct((chunk, docs), F32)] * groups,
         in_specs=[SMEM, SMEM, SMEM, VMEM],
-        out_specs=VMEM,
+        out_specs=[VMEM] * groups,
         compiler_params=call_params(),
         cost_estimate=cost(words * docs, 4 * words * docs),
         name="chunk_counts",
     )(here, in_hbm(tile_doc), in_hbm(tile_word), word_counts)
 
 
-def ratio_chunk(parts, counts, word_tile):
+def ratio_chunk(parts, counts, word_tile, after):
     def kernel(*refs):
-        part_refs, count_ref, out_ref = refs[:-2], refs[-2], refs[-1]
+        part_refs, count_ref, out_ref = refs[: len(parts)], refs[len(parts)], refs[-1]
         rate = part_refs[0][...].astype(F32)
         for ref in part_refs[1:]:
             rate += ref[...].astype(F32)
@@ -155,12 +158,12 @@
     return pl.pallas_call(
         kernel,
         out_shape=jax.ShapeDtypeStruct(counts.shape, BF16),
-        in_specs=[VMEM] * (len(parts) + 1),
+        in_specs=[VMEM] * (len(parts) + 1) + [ANY] * len(after),
         out_specs=VMEM,
         compiler_params=call_params(),
         cost_estimate=cost(10 * counts.size, 16 * counts.size),
         name="ratio_chunk",
-    )(*parts, counts)
+    )(*parts, counts, *after)
 
 
 def join_ratio(sizes, here, chunks, order, after):
@@ -183,6 +186,24 @@
     )(here, *chunks, *after)
 
 
+def stack_rows(groups):
+    rows, docs = groups[0].shape
+
+    def kernel(*refs):
+        for g, ref in enumerate(refs[:-1]):
+            refs[-1][g * rows : (g + 1) * rows, :] = ref[...]
+
+    return pl.pallas_call(
+        kernel,
+        out_shape=jax.ShapeDtypeStruct((len(groups) * rows, docs), BF16),
+        in_specs=[VMEM] * len(groups),
+        out_specs=VMEM,
+        compiler_params=call_params(),
+        cost_estimate=cost(0, 4 * len(groups) * rows * docs),
+        name="stack_rows",
+    )(*groups)
+
+
 def own_product(ratio, docs_held):
     words, docs = ratio.shape
     width = docs_held.shape[1]
@@ -201,18 +222,19 @@
     )(ratio, docs_held)
 
 
-def beta_piece(sizes, here, product, ratio, docs_held, prob_held, start, spans, after):
+def beta_piece(sizes, here, product, ratio, docs_held, prob_held, group, spans, after):
     words, side_width = product.shape
     docs, width = docs_held.shape[0], sum(spans)
+    rows = pl.ds(group * words, words)
 
     def kernel(here_ref, product_ref, ratio_ref, doc_ref, prob_ref, *rest):
         side = sizes.side(here_ref)
-        begin = start
+        begin = 0
         for out_ref, span in zip(rest[len(after) :], spans):
             at = pl.ds(begin, span)
             prob_at = pl.ds(pl.multiple_of(side * side_width + begin, 128), span)
             summed = product_ref[:, at] + jnp.dot(ratio_ref[...], doc_ref[:, at], preferred_element_type=F32)
-            out_ref[...] = (-prob_ref[:, prob_at].astype(F32) * summed).astype(BF16)
+            out_ref[...] = (-prob_ref[rows, prob_at].astype(F32) * summed).astype(BF16)
             begin += span
 
     return pl.pallas_call(
@@ -313,7 +335,7 @@
     )(here, ratio, *far_ratios, prob_held, *far_logits, log_norm)
 
 
-def place_pieces(sizes, here, own, other, starts, shape):
+def place_pieces(sizes, here, own, other, corners, shape):
     pieces = len(own)
     side_width = shape[1] // 2
 
@@ -323,8 +345,9 @@
         copies = []
         for p in range(pieces):
             for h, (ref, which) in enumerate(((own_refs[p], side), (other_refs[p], 1 - side))):
-                column = pl.multiple_of(which * side_width + starts[p], 128)
-                target = out_ref.at[:, pl.ds(column, ref.shape[1])]
+                row, column = corners[p]
+                columns = pl.ds(pl.multiple_of(which * side_width + column, 128), ref.shape[1])
+                target = out_ref.at[pl.ds(row, ref.shape[0]), columns]
                 copies.append(pltpu.make_async_copy(ref, target, sems.at[h, p]))
         for copy in copies:
             copy.start()
@@ -356,41 +379,49 @@
         count = {"doc": sizes.doc, "topic": sizes.topic}[axis]
         return lax.ppermute(array, axis, [(i, i ^ bits) for i in range(count)])
 
+    groups = 2 if words % (32 * sizes.topic) == 0 else 1
     parts, near_logits, docs_held, docs_sent, prob_held, norm_held = rate_partial(
-        sizes, here, doc_topics, word_logits, log_norm[None, :]
+        sizes, here, doc_topics, word_logits, log_norm[None, :], groups
     )
     near_logits = [shift(part, s) for s, part in enumerate(near_logits, 1)]
     sibling_docs = swap(docs_sent, "doc", 1)
     order = sorted(range(1, sizes.topic), key=lambda s: s < sizes.topic // 2)
-    arrived = [swap(parts[s], "topic", s) for s in order]
-    counts = chunk_counts(sizes, here, word_counts, tile_doc, tile_word, docs, words)
-    own_ratio = ratio_chunk([parts[0]] + arrived, counts, word_tile)
-    gathered = [own_ratio] + [swap(own_ratio, "topic", s) for s in order]
-    ratio = join_ratio(sizes, here, gathered, [0] + order, near_logits + [sibling_docs])
-    sibling_ratio = swap(ratio, "doc", 1)
+    counts = chunk_counts(sizes, here, word_counts, tile_doc, tile_word, docs, words, groups)
+    arrived = [[swap(parts[g][s], "topic", s) for s in order] for g in range(groups)]
+    ratios = []
+    for g in range(groups):
+        own_ratio = ratio_chunk([parts[g][0]] + arrived[g], counts[g], word_tile, [sibling_docs])
+        gathered = [own_ratio] + [swap(own_ratio, "topic", s) for s in order]
+        after = sum(arrived[g + 1 :], []) if g < groups - 1 else near_logits
+        ratios.append(join_ratio(sizes, here, gathered, [0] + order, after))
+    ratio = stack_rows(ratios)
     far_ratios = [shift(ratio, s) for s in range(1, sizes.vocab)]
 
     side_width = width // 2
-    spans = [side_width // 4, side_width // 2, side_width // 4]
-    starts = [0, spans[0], spans[0] + spans[1]]
-    product = own_product(ratio, docs_held)
-    sibling = (sibling_ratio, sibling_docs, prob_held)
-    sums = list(beta_piece(sizes, here, product, *sibling, 0, spans[:1], []))
-    sums += beta_piece(sizes, here, product, *sibling, spans[0], spans[1:], sums)
+    far_bits = [1 << b for b in range(1, sizes.doc.bit_length() - 1)]
+    sums, others, corners = [], [], []
+    for g in range(groups):
+        product = own_product(ratios[g], docs_held)
+        spans = [side_width] if g < groups - 1 else [side_width // 2] * 2
+        corners += [(g * words // groups, sum(spans[:i])) for i in range(len(spans))]
+        pieces = beta_piece(
+            sizes, here, product, swap(ratios[g], "doc", 1), sibling_docs, prob_held, g, spans, others[-1:]
+        )
+        for bit in far_bits[:-1]:
+            pieces = [add_pair(part, swap(part, "doc", bit)) for part in pieces]
+        sums += pieces
+        others += [swap(part, "doc", far_bits[-1]) for part in pieces]
 
     far_logits = []
     for part in near_logits:
         part = hold(part, sums[-1:])
         far_logits += [part, swap(part, "doc", 1)]
-
-    bit = 2
-    while 2 * bit < sizes.doc:
-        sums = [add_pair(part, swap(part, "doc", bit)) for part in sums]
-        bit *= 2
-    others = [swap(part, "doc", bit) for part in sums]
     theta, theta_done = theta_grad(sizes, here, ratio, far_ratios, prob_held, far_logits, norm_held)
-    sums = [add_pair(*pair, [theta_done]) for pair in zip(sums, others)]
-    out = place_pieces(sizes, here, sums, [swap(part, "doc", 1) for part in sums], starts, word_logits.shape)
+
+    sums = [
+        add_pair(*pair, [theta_done] if i >= groups - 1 else []) for i, pair in enumerate(zip(sums, others))
+    ]
+    out = place_pieces(sizes, here, sums, [swap(part, "doc", 1) for part in sums], corners, word_logits.shape)
     return theta, out
 
 

time: 59.8 us -> 60.7 us (1.015)
  starting transfers between devices: 16.1 us -> 24.4 us
  waiting for transfers between devices: 30.1 us -> 22.1 us
    ppermute x15 -> x22, waiting for transfers between devices: 25.6 us -> 9.84 us  [swap(): return lax.ppermute(array, axis, [(i, i ^ bits) for i in range(count)])]
    ppermute x15 -> x22, starting transfers between devices: 13 us -> 22 us  [swap(): return lax.ppermute(array, axis, [(i, i ^ bits) for i in range(count)])]
    ppermute x2, waiting for transfers between devices: 4.54 us -> 12.3 us  [shift(): lax.ppermute(array, 'vocab', [(i, (i + by) % sizes.vocab) for i in range(...]
    ppermute x2, starting transfers between devices: 3.11 us -> 2.43 us  [shift(): lax.ppermute(array, 'vocab', [(i, (i + by) % sizes.vocab) for i in range(...]
  transfers between devices with their start and end apart: 17 -> 24, of which waited for: 10 -> 9; matrix products, arithmetic and copies ran while one was open for 0% -> 0% of each run, Pallas kernels for 9% -> 11%
where the time goes in v7:
time: 60.7 us; the launch traced here: 60.6 us
  starting transfers between devices  24.4 us (40%)
  waiting for transfers between devices  22.1 us (36%)
  Pallas kernels  13.2 us (22%)
  between operations  0.85 us (1%)
    ppermute x22, starting transfers between devices, swap(): return lax.ppermute(array, axis, [(i, i ^ bits) for i in range(count)])  22 us
    ppermute x2, waiting for transfers between devices, shift(): lax.ppermute(array, 'vocab', [(i, (i + by) % sizes.vocab) for i in range(...  12.3 us
    ppermute x22, waiting for transfers between devices, swap(): return lax.ppermute(array, axis, [(i, i ^ bits) for i in range(count)])  9.84 us
    pallas_call x1, Pallas kernels, rate_partial(): pl.pallas_call(kernel, out_shape=[jax.ShapeDtypeStruct((chunk, docs), BF1...  4.79 us
    pallas_call x1, Pallas kernels, theta_grad(): pl.pallas_call(kernel, out_shape=[jax.ShapeDtypeStruct((docs, share), F32...  3.71 us
    ppermute x2, starting transfers between devices, shift(): lax.ppermute(array, 'vocab', [(i, (i + by) % sizes.vocab) for i in range(...  2.43 us
    pallas_call x1, Pallas kernels, place_pieces(): pl.pallas_call(kernel, out_shape=jax.ShapeDtypeStruct(shape, BF16), in_sp...  1.36 us
  transfers between devices with their start and end apart: 24, of which 9 were waited for; matrix products, arithmetic and copies ran while one was open for 0% of the time, Pallas kernels for 11%

profile of v7, /device:TPU:0, one launch (start us, length us, event | category | flops | bytes accessed | tf_op | source)
XLA Modules:
  0.0 60.6 jit_solution(14003773533725265388)
XLA Ops:
  0.6 4.8 %rate_partial.1 = (bf16[32,512]{1,0:T(8,128)(2,1)S(1)}, bf16[32,512]{1,0:T(8,128)(2,1)S(1)}, bf16[32,512]{1,0:T(8,128)(2,1)S(1)}, bf16[32,512]{1,0:T(8,128)(2,1)...) custom-call(s32[1]{0:T(128)} %bitcast.here_ref, ...), custom_call_target="tpu_custom_call" | custom-call | flops 1073741824 | bytes 6291456 | tf_op jit(solution)/shard_map/rate_partial/pallas_call | solution.py:98
  5.4 0.5 collective-permute-start.3
  6.0 3.7 %collective-permute-start = (bf16[32,512]{1,0:T(8,128)(2,1)S(1)}, bf16[32,512]{1,0:T(8,128)(2,1)S(1)}, u32[]{:S(2)}, u32[]{:S(2)}) collective-permute-start(bf16[32,512]{1,0:T(8,128)(2,1)S(1)} %get-tuple-element.22), channel_id=1, source_target_pairs={{0,4},{2,6},{4,0},{6,2},{1,5},{3,7},{5,1},{7,3},{8,12},{10,14},{12... | collective-permute-start | bytes 98312 | tf_op jit(solution)/shard_map/ppermute | solution.py:380
  9.6 1.3 %collective-permute-start.1 = (bf16[32,512]{1,0:T(8,128)(2,1)S(1)}, bf16[32,512]{1,0:T(8,128)(2,1)S(1)}, u32[]{:S(2)}, u32[]{:S(2)}) collective-permute-start(bf16[32,512]{1,0:T(8,128)(2,1)S(1)} %get-tuple-element.23), channel_id=1, source_target_pairs={{0,6},{2,4},{4,2},{6,0},{1,7},{3,5},{5,3},{7,1},{8,14},{10,12},{12... | collective-permute-start | bytes 98312 | tf_op jit(solution)/shard_map/ppermute | solution.py:380
  11.0 0.2 collective-permute-start.2
  11.2 2.8 %collective-permute-start.7 = (bf16[32,512]{1,0:T(8,128)(2,1)S(1)}, bf16[32,512]{1,0:T(8,128)(2,1)S(1)}, u32[]{:S(2)}, u32[]{:S(2)}) collective-permute-start(bf16[32,512]{1,0:T(8,128)(2,1)S(1)} %get-tuple-element.27), channel_id=1, source_target_pairs={{0,4},{2,6},{4,0},{6,2},{1,5},{3,7},{5,1},{7,3},{8,12},{10,14},{12... | collective-permute-start | bytes 98312 | tf_op jit(solution)/shard_map/ppermute | solution.py:380
  14.0 1.0 %chunk_counts.1 = (f32[32,512]{1,0:T(8,128)S(1)}, f32[32,512]{1,0:T(8,128)S(1)}) custom-call(s32[1]{0:T(128)} %bitcast.here_ref, s32[16]{0:T(128)} %doc_at.1, s32[16]{0:T(128)} %word_at.1, s32[16,64,128]{2,1,0:T(8,128)S(1)} %copy-done), custom_call_target="tpu_custom_call" | custom-call | flops 131072 | bytes 524288 | tf_op jit(solution)/shard_map/chunk_counts/pallas_call | solution.py:139
  15.0 1.4 %collective-permute-start.8 = (bf16[32,512]{1,0:T(8,128)(2,1)S(1)}, bf16[32,512]{1,0:T(8,128)(2,1)S(1)}, u32[]{:S(2)}, u32[]{:S(2)}) collective-permute-start(bf16[32,512]{1,0:T(8,128)(2,1)S(1)} %get-tuple-element.28), channel_id=1, source_target_pairs={{0,6},{2,4},{4,2},{6,0},{1,7},{3,5},{5,3},{7,1},{8,14},{10,12},{12... | collective-permute-start | bytes 98312 | tf_op jit(solution)/shard_map/ppermute | solution.py:380
  16.5 3.1 %collective-permute-start.4 = (bf16[32,512]{1,0:T(8,128)(2,1)S(1)}, bf16[32,512]{1,0:T(8,128)(2,1)S(1)}, u32[]{:S(2)}, u32[]{:S(2)}) collective-permute-start(bf16[32,512]{1,0:T(8,128)(2,1)S(1)} %ratio_chunk.2.refs_0_), channel_id=1, source_target_pairs={{0,4},{2,6},{4,0},{6,2},{1,5},{3,7},{5,1},{7,3},{8,12},{10,14},{12... | collective-permute-start | bytes 98312 | tf_op jit(solution)/shard_map/ppermute | solution.py:380
  19.6 1.3 %collective-permute-start.5 = (bf16[32,512]{1,0:T(8,128)(2,1)S(1)}, bf16[32,512]{1,0:T(8,128)(2,1)S(1)}, u32[]{:S(2)}, u32[]{:S(2)}) collective-permute-start(bf16[32,512]{1,0:T(8,128)(2,1)S(1)} %ratio_chunk.2.refs_0_), channel_id=1, source_target_pairs={{0,6},{2,4},{4,2},{6,0},{1,7},{3,5},{5,3},{7,1},{8,14},{10,12},{12... | collective-permute-start | bytes 98312 | tf_op jit(solution)/shard_map/ppermute | solution.py:380
  21.0 0.8 %collective-permute-done.4.refs_1_ = bf16[32,512]{1,0:T(8,128)(2,1)S(1)} collective-permute-done((bf16[32,512]{1,0:T(8,128)(2,1)S(1)}, bf16[32,512]{1,0:T(8,128)(2,1)S(1)}, u32[]{:S(2)}, u32[]{:S(2)}) %collective-permute-start.4) | collective-permute-done | bytes 32800 | tf_op jit(solution)/shard_map/ppermute | solution.py:380
  21.8 3.5 %collective-permute-done.5.refs_2_ = bf16[32,512]{1,0:T(8,128)(2,1)S(1)} collective-permute-done((bf16[32,512]{1,0:T(8,128)(2,1)S(1)}, bf16[32,512]{1,0:T(8,128)(2,1)S(1)}, u32[]{:S(2)}, u32[]{:S(2)}) %collective-permute-start.5) | collective-permute-done | bytes 32800 | tf_op jit(solution)/shard_map/ppermute | solution.py:380
  25.4 1.6 %collective-permute-start.13 = (bf16[128,2048]{1,0:T(8,128)(2,1)S(1)}, bf16[128,2048]{1,0:T(8,128)(2,1)S(1)}, u32[]{:S(2)}, u32[]{:S(2)}) collective-permute-start(bf16[128,2048]{1,0:T(8,128)(2,1)S(1)} %get-tuple-element.32), channel_id=1, source_target_pairs={{0,1},{1,0},{2,3},{3,2},{4,5},{5,4},{6,7},{7,6},{8,9},{9,8},{10,11... | collective-permute-start | bytes 1572872 | tf_op jit(solution)/shard_map/ppermute | solution.py:376
  27.0 0.5 own_product.3.product_ref
  27.5 0.5 beta_piece.2.own_ref
  28.0 1.5 %collective-permute-start.17 = (bf16[128,2048]{1,0:T(8,128)(2,1)S(1)}, bf16[128,2048]{1,0:T(8,128)(2,1)S(1)}, u32[]{:S(2)}, u32[]{:S(2)}) collective-permute-start(bf16[128,2048]{1,0:T(8,128)(2,1)S(1)} %beta_piece.2.own_ref), channel_id=1, source_target_pairs={{0,16},{8,24},{16,0},{24,8},{1,17},{9,25},{17,1},{25,9},{2,18},{10... | collective-permute-start | bytes 1572872 | tf_op jit(solution)/shard_map/ppermute | solution.py:380
  29.6 1.0 %collective-permute-start.10 = (bf16[32,512]{1,0:T(8,128)(2,1)S(1)}, bf16[32,512]{1,0:T(8,128)(2,1)S(1)}, u32[]{:S(2)}, u32[]{:S(2)}) collective-permute-start(bf16[32,512]{1,0:T(8,128)(2,1)S(1)} %ratio_chunk.3.refs_0_), channel_id=1, source_target_pairs={{0,4},{2,6},{4,0},{6,2},{1,5},{3,7},{5,1},{7,3},{8,12},{10,14},{12... | collective-permute-start | bytes 98312 | tf_op jit(solution)/shard_map/ppermute | solution.py:380
  30.6 1.3 %collective-permute-start.11 = (bf16[32,512]{1,0:T(8,128)(2,1)S(1)}, bf16[32,512]{1,0:T(8,128)(2,1)S(1)}, u32[]{:S(2)}, u32[]{:S(2)}) collective-permute-start(bf16[32,512]{1,0:T(8,128)(2,1)S(1)} %ratio_chunk.3.refs_0_), channel_id=1, source_target_pairs={{0,6},{2,4},{4,2},{6,0},{1,7},{3,5},{5,3},{7,1},{8,14},{10,12},{12... | collective-permute-start | bytes 98312 | tf_op jit(solution)/shard_map/ppermute | solution.py:380
  31.9 1.2 %collective-permute-start.12 = (bf16[32,512]{1,0:T(8,128)(2,1)S(1)}, bf16[32,512]{1,0:T(8,128)(2,1)S(1)}, u32[]{:S(2)}, u32[]{:S(2)}) collective-permute-start(bf16[32,512]{1,0:T(8,128)(2,1)S(1)} %ratio_chunk.3.refs_0_), channel_id=1, source_target_pairs={{0,2},{2,0},{4,6},{6,4},{1,3},{3,1},{5,7},{7,5},{8,10},{10,8},{12,... | collective-permute-start | bytes 98312 | tf_op jit(solution)/shard_map/ppermute | solution.py:380
  33.1 6.6 %collective-permute-done.13.refs_4_.in_ref = bf16[128,2048]{1,0:T(8,128)(2,1)S(1)} collective-permute-done((bf16[128,2048]{1,0:T(8,128)(2,1)S(1)}, bf16[128,2048]{1,0:T(8,128)(2,1)S(1)}, u32[]{:S(2)}, u32[]{:S(2)}) %collective-permute-start.13) | collective-permute-done | bytes 524320 | tf_op jit(solution)/shard_map/ppermute | solution.py:376
  39.9 0.5 own_product.2.product_ref
  40.3 0.9 %collective-permute-done.15.ratio_ref = bf16[128,512]{1,0:T(8,128)(2,1)S(1)} collective-permute-done((bf16[128,512]{1,0:T(8,128)(2,1)S(1)}, bf16[128,512]{1,0:T(8,128)(2,1)S(1)}, u32[]{:S(2)}, u32[]{:S(2)}) %collective-permute-start.15) | collective-permute-done | bytes 131104 | tf_op jit(solution)/shard_map/ppermute | solution.py:380
  41.2 0.9 %collective-permute-done.17.rest_0_.other_ref = bf16[128,2048]{1,0:T(8,128)(2,1)S(1)} collective-permute-done((bf16[128,2048]{1,0:T(8,128)(2,1)S(1)}, bf16[128,2048]{1,0:T(8,128)(2,1)S(1)}, u32[]{:S(2)}, u32[]{:S(2)}) %collective-permute-start.17) | collective-permute-done | bytes 524320 | tf_op jit(solution)/shard_map/ppermute | solution.py:380
  42.1 0.5 beta_piece.3
  42.7 0.9 %collective-permute-start.14 = (bf16[256,512]{1,0:T(8,128)(2,1)S(1)}, bf16[256,512]{1,0:T(8,128)(2,1)S(1)}, u32[]{:S(2)}, u32[]{:S(2)}) collective-permute-start(bf16[256,512]{1,0:T(8,128)(2,1)S(1)} %stack_rows.1.ratio_ref), channel_id=1, source_target_pairs={{0,1},{1,0},{2,3},{3,2},{4,5},{5,4},{6,7},{7,6},{8,9},{9,8},{10,11... | collective-permute-start | bytes 786440 | tf_op jit(solution)/shard_map/ppermute | solution.py:376
  43.6 1.5 %collective-permute-start.20 = (bf16[128,1024]{1,0:T(8,128)(2,1)S(1)}, bf16[128,1024]{1,0:T(8,128)(2,1)S(1)}, u32[]{:S(2)}, u32[]{:S(2)}) collective-permute-start(bf16[128,1024]{1,0:T(8,128)(2,1)S(1)} %get-tuple-element.35.rest_0_.own_ref), channel_id=1, source_target_pairs={{0,16},{8,24},{16,0},{24,8},{1,17},{9,25},{17,1},{25,9},{2,18},{10... | collective-permute-start | bytes 786440 | tf_op jit(solution)/shard_map/ppermute | solution.py:380
  45.1 0.5 collective-permute-start.19
  45.8 5.7 %collective-permute-done.14.refs_0_ = bf16[256,512]{1,0:T(8,128)(2,1)S(1)} collective-permute-done((bf16[256,512]{1,0:T(8,128)(2,1)S(1)}, bf16[256,512]{1,0:T(8,128)(2,1)S(1)}, u32[]{:S(2)}, u32[]{:S(2)}) %collective-permute-start.14) | collective-permute-done | bytes 262176 | tf_op jit(solution)/shard_map/ppermute | solution.py:376
  51.5 3.7 %theta_grad.1 = (f32[512,2048]{1,0:T(8,128)}, f32[8,128]{1,0:T(8,128)S(1)}) custom-call(s32[1]{0:T(128)} %bitcast.here_ref, bf16[256,512]{1,0:T(8,128)(2,1)S(1)} %stack_rows.1.ratio_ref, bf16[256,512]{1,0:T(8,128)(2,1)S(1)} %collective-permute-done.14.refs_0_, bf16[256,4096]{1,0:T(8,128)(2,1)S(1)} %get-tuple-element.33.prob_ref.refs_1_, ...), custom_call_target="tpu_custom_call" | custom-call | flops 10737418240 | bytes 62914560 | tf_op jit(solution)/shard_map/theta_grad/pallas_call | solution.py:317
  55.3 2.2 %collective-permute-done.19.other_ref = bf16[128,1024]{1,0:T(8,128)(2,1)S(1)} collective-permute-done((bf16[128,1024]{1,0:T(8,128)(2,1)S(1)}, bf16[128,1024]{1,0:T(8,128)(2,1)S(1)}, u32[]{:S(2)}, u32[]{:S(2)}) %collective-permute-start.19) | collective-permute-done | bytes 262176 | tf_op jit(solution)/shard_map/ppermute | solution.py:380
  57.7 1.5 %collective-permute-done.22.refs_4_ = bf16[128,1024]{1,0:T(8,128)(2,1)S(1)} collective-permute-done((bf16[128,1024]{1,0:T(8,128)(2,1)S(1)}, bf16[128,1024]{1,0:T(8,128)(2,1)S(1)}, u32[]{:S(2)}, u32[]{:S(2)}) %collective-permute-start.22) | collective-permute-done | bytes 262176 | tf_op jit(solution)/shard_map/ppermute | solution.py:380
  59.2 1.4 %place_pieces.1 = bf16[256,4096]{1,0:T(8,128)(2,1)} custom-call(s32[1]{0:T(128)} %bitcast.here_ref, bf16[128,2048]{1,0:T(8,128)(2,1)S(1)} %add_pair.3.refs_0_, bf16[128,1024]{1,0:T(8,128)(2,1)S(1)} %add_pair.4.refs_1_, bf16[128,1024]{1,0:T(8,128)(2,1)S(1)} %add_pair.5.refs_2_, bf16[128,2048]{1,0:T(8,128)(2,1)S(1)} %collective-permute-done.21.refs_3_, ...), custom_call_target="tpu_custom_call" | custom-call | bytes 4194304 | tf_op jit(solution)/shard_map/place_pieces/pallas_call | solution.py:357
  (35 shorter events, 1.0 us)
Async XLA Ops:
  0.6 13.4 %copy-start = (s32[16,64,128]{2,1,0:T(8,128)S(1)}, s32[16,64,128]{2,1,0:T(8,128)}, u32[]{:S(2)}) copy-start(s32[16,64,128]{2,1,0:T(8,128)} %count_ref.1) | copy-start | bytes 1572868
  5.4 11.0 %collective-permute-start.3 = (bf16[512,2048]{1,0:T(8,128)(2,1)S(1)}, bf16[512,2048]{1,0:T(8,128)(2,1)S(1)}, u32[]{:S(2)}, u32[]{:S(2)}) collective-permute-start(bf16[512,2048]{1,0:T(8,128)(2,1)S(1)} %get-tuple-element.26), channel_id=1, source_target_pairs={{0,8},{8,0},{16,24},{24,16},{1,9},{9,1},{17,25},{25,17},{2,10},{10... | collective-permute-start | bytes 6291464 | tf_op jit(solution)/shard_map/ppermute | solution.py:380
  6.0 9.0 %collective-permute-start = (bf16[32,512]{1,0:T(8,128)(2,1)S(1)}, bf16[32,512]{1,0:T(8,128)(2,1)S(1)}, u32[]{:S(2)}, u32[]{:S(2)}) collective-permute-start(bf16[32,512]{1,0:T(8,128)(2,1)S(1)} %get-tuple-element.22), channel_id=1, source_target_pairs={{0,4},{2,6},{4,0},{6,2},{1,5},{3,7},{5,1},{7,3},{8,12},{10,14},{12... | collective-permute-start | bytes 98312 | tf_op jit(solution)/shard_map/ppermute | solution.py:380
  9.6 6.8 %collective-permute-start.1 = (bf16[32,512]{1,0:T(8,128)(2,1)S(1)}, bf16[32,512]{1,0:T(8,128)(2,1)S(1)}, u32[]{:S(2)}, u32[]{:S(2)}) collective-permute-start(bf16[32,512]{1,0:T(8,128)(2,1)S(1)} %get-tuple-element.23), channel_id=1, source_target_pairs={{0,6},{2,4},{4,2},{6,0},{1,7},{3,5},{5,3},{7,1},{8,14},{10,12},{12... | collective-permute-start | bytes 98312 | tf_op jit(solution)/shard_map/ppermute | solution.py:380
  11.0 5.5 %collective-permute-start.2 = (bf16[32,512]{1,0:T(8,128)(2,1)S(1)}, bf16[32,512]{1,0:T(8,128)(2,1)S(1)}, u32[]{:S(2)}, u32[]{:S(2)}) collective-permute-start(bf16[32,512]{1,0:T(8,128)(2,1)S(1)} %get-tuple-element.24), channel_id=1, source_target_pairs={{0,2},{2,0},{4,6},{6,4},{1,3},{3,1},{5,7},{7,5},{8,10},{10,8},{12,... | collective-permute-start | bytes 98312 | tf_op jit(solution)/shard_map/ppermute | solution.py:380
  11.2 9.7 %collective-permute-start.7 = (bf16[32,512]{1,0:T(8,128)(2,1)S(1)}, bf16[32,512]{1,0:T(8,128)(2,1)S(1)}, u32[]{:S(2)}, u32[]{:S(2)}) collective-permute-start(bf16[32,512]{1,0:T(8,128)(2,1)S(1)} %get-tuple-element.27), channel_id=1, source_target_pairs={{0,4},{2,6},{4,0},{6,2},{1,5},{3,7},{5,1},{7,3},{8,12},{10,14},{12... | collective-permute-start | bytes 98312 | tf_op jit(solution)/shard_map/ppermute | solution.py:380
  15.0 6.0 %collective-permute-start.8 = (bf16[32,512]{1,0:T(8,128)(2,1)S(1)}, bf16[32,512]{1,0:T(8,128)(2,1)S(1)}, u32[]{:S(2)}, u32[]{:S(2)}) collective-permute-start(bf16[32,512]{1,0:T(8,128)(2,1)S(1)} %get-tuple-element.28), channel_id=1, source_target_pairs={{0,6},{2,4},{4,2},{6,0},{1,7},{3,5},{5,3},{7,1},{8,14},{10,12},{12... | collective-permute-start | bytes 98312 | tf_op jit(solution)/shard_map/ppermute | solution.py:380
  16.4 4.6 %collective-permute-start.9 = (bf16[32,512]{1,0:T(8,128)(2,1)S(1)}, bf16[32,512]{1,0:T(8,128)(2,1)S(1)}, u32[]{:S(2)}, u32[]{:S(2)}) collective-permute-start(bf16[32,512]{1,0:T(8,128)(2,1)S(1)} %get-tuple-element.29), channel_id=1, source_target_pairs={{0,2},{2,0},{4,6},{6,4},{1,3},{3,1},{5,7},{7,5},{8,10},{10,8},{12,... | collective-permute-start | bytes 98312 | tf_op jit(solution)/shard_map/ppermute | solution.py:380
  16.5 5.3 %collective-permute-start.4 = (bf16[32,512]{1,0:T(8,128)(2,1)S(1)}, bf16[32,512]{1,0:T(8,128)(2,1)S(1)}, u32[]{:S(2)}, u32[]{:S(2)}) collective-permute-start(bf16[32,512]{1,0:T(8,128)(2,1)S(1)} %ratio_chunk.2.refs_0_), channel_id=1, source_target_pairs={{0,4},{2,6},{4,0},{6,2},{1,5},{3,7},{5,1},{7,3},{8,12},{10,14},{12... | collective-permute-start | bytes 98312 | tf_op jit(solution)/shard_map/ppermute | solution.py:380
  19.6 5.7 %collective-permute-start.5 = (bf16[32,512]{1,0:T(8,128)(2,1)S(1)}, bf16[32,512]{1,0:T(8,128)(2,1)S(1)}, u32[]{:S(2)}, u32[]{:S(2)}) collective-permute-start(bf16[32,512]{1,0:T(8,128)(2,1)S(1)} %ratio_chunk.2.refs_0_), channel_id=1, source_target_pairs={{0,6},{2,4},{4,2},{6,0},{1,7},{3,5},{5,3},{7,1},{8,14},{10,12},{12... | collective-permute-start | bytes 98312 | tf_op jit(solution)/shard_map/ppermute | solution.py:380
  20.9 4.4 %collective-permute-start.6 = (bf16[32,512]{1,0:T(8,128)(2,1)S(1)}, bf16[32,512]{1,0:T(8,128)(2,1)S(1)}, u32[]{:S(2)}, u32[]{:S(2)}) collective-permute-start(bf16[32,512]{1,0:T(8,128)(2,1)S(1)} %ratio_chunk.2.refs_0_), channel_id=1, source_target_pairs={{0,2},{2,0},{4,6},{6,4},{1,3},{3,1},{5,7},{7,5},{8,10},{10,8},{12,... | collective-permute-start | bytes 98312 | tf_op jit(solution)/shard_map/ppermute | solution.py:380
  25.3 2.2 %collective-permute-start.16 = (bf16[128,512]{1,0:T(8,128)(2,1)S(1)}, bf16[128,512]{1,0:T(8,128)(2,1)S(1)}, u32[]{:S(2)}, u32[]{:S(2)}) collective-permute-start(bf16[128,512]{1,0:T(8,128)(2,1)S(1)} %join_ratio.2.refs_0_.ratio_ref), channel_id=1, source_target_pairs={{0,8},{8,0},{16,24},{24,16},{1,9},{9,1},{17,25},{25,17},{2,10},{10... | collective-permute-start | bytes 393224 | tf_op jit(solution)/shard_map/ppermute | solution.py:380
  25.4 14.3 %collective-permute-start.13 = (bf16[128,2048]{1,0:T(8,128)(2,1)S(1)}, bf16[128,2048]{1,0:T(8,128)(2,1)S(1)}, u32[]{:S(2)}, u32[]{:S(2)}) collective-permute-start(bf16[128,2048]{1,0:T(8,128)(2,1)S(1)} %get-tuple-element.32), channel_id=1, source_target_pairs={{0,1},{1,0},{2,3},{3,2},{4,5},{5,4},{6,7},{7,6},{8,9},{9,8},{10,11... | collective-permute-start | bytes 1572872 | tf_op jit(solution)/shard_map/ppermute | solution.py:376
  28.0 14.0 %collective-permute-start.17 = (bf16[128,2048]{1,0:T(8,128)(2,1)S(1)}, bf16[128,2048]{1,0:T(8,128)(2,1)S(1)}, u32[]{:S(2)}, u32[]{:S(2)}) collective-permute-start(bf16[128,2048]{1,0:T(8,128)(2,1)S(1)} %beta_piece.2.own_ref), channel_id=1, source_target_pairs={{0,16},{8,24},{16,0},{24,8},{1,17},{9,25},{17,1},{25,9},{2,18},{10... | collective-permute-start | bytes 1572872 | tf_op jit(solution)/shard_map/ppermute | solution.py:380
  29.6 10.2 %collective-permute-start.10 = (bf16[32,512]{1,0:T(8,128)(2,1)S(1)}, bf16[32,512]{1,0:T(8,128)(2,1)S(1)}, u32[]{:S(2)}, u32[]{:S(2)}) collective-permute-start(bf16[32,512]{1,0:T(8,128)(2,1)S(1)} %ratio_chunk.3.refs_0_), channel_id=1, source_target_pairs={{0,4},{2,6},{4,0},{6,2},{1,5},{3,7},{5,1},{7,3},{8,12},{10,14},{12... | collective-permute-start | bytes 98312 | tf_op jit(solution)/shard_map/ppermute | solution.py:380
  30.6 9.2 %collective-permute-start.11 = (bf16[32,512]{1,0:T(8,128)(2,1)S(1)}, bf16[32,512]{1,0:T(8,128)(2,1)S(1)}, u32[]{:S(2)}, u32[]{:S(2)}) collective-permute-start(bf16[32,512]{1,0:T(8,128)(2,1)S(1)} %ratio_chunk.3.refs_0_), channel_id=1, source_target_pairs={{0,6},{2,4},{4,2},{6,0},{1,7},{3,5},{5,3},{7,1},{8,14},{10,12},{12... | collective-permute-start | bytes 98312 | tf_op jit(solution)/shard_map/ppermute | solution.py:380
  31.9 7.8 %collective-permute-start.12 = (bf16[32,512]{1,0:T(8,128)(2,1)S(1)}, bf16[32,512]{1,0:T(8,128)(2,1)S(1)}, u32[]{:S(2)}, u32[]{:S(2)}) collective-permute-start(bf16[32,512]{1,0:T(8,128)(2,1)S(1)} %ratio_chunk.3.refs_0_), channel_id=1, source_target_pairs={{0,2},{2,0},{4,6},{6,4},{1,3},{3,1},{5,7},{7,5},{8,10},{10,8},{12,... | collective-permute-start | bytes 98312 | tf_op jit(solution)/shard_map/ppermute | solution.py:380
  39.8 1.4 %collective-permute-start.15 = (bf16[128,512]{1,0:T(8,128)(2,1)S(1)}, bf16[128,512]{1,0:T(8,128)(2,1)S(1)}, u32[]{:S(2)}, u32[]{:S(2)}) collective-permute-start(bf16[128,512]{1,0:T(8,128)(2,1)S(1)} %join_ratio.3.refs_1_.ratio_ref), channel_id=1, source_target_pairs={{0,8},{8,0},{16,24},{24,16},{1,9},{9,1},{17,25},{25,17},{2,10},{10... | collective-permute-start | bytes 393224 | tf_op jit(solution)/shard_map/ppermute | solution.py:380
  42.6 8.9 %collective-permute-start.18 = (bf16[128,2048]{1,0:T(8,128)(2,1)S(1)}, bf16[128,2048]{1,0:T(8,128)(2,1)S(1)}, u32[]{:S(2)}, u32[]{:S(2)}) collective-permute-start(bf16[128,2048]{1,0:T(8,128)(2,1)S(1)} %hold.1.refs_2_), channel_id=1, source_target_pairs={{0,8},{8,0},{16,24},{24,16},{1,9},{9,1},{17,25},{25,17},{2,10},{10... | collective-permute-start | bytes 1572872 | tf_op jit(solution)/shard_map/ppermute | solution.py:380
  42.7 8.8 %collective-permute-start.14 = (bf16[256,512]{1,0:T(8,128)(2,1)S(1)}, bf16[256,512]{1,0:T(8,128)(2,1)S(1)}, u32[]{:S(2)}, u32[]{:S(2)}) collective-permute-start(bf16[256,512]{1,0:T(8,128)(2,1)S(1)} %stack_rows.1.ratio_ref), channel_id=1, source_target_pairs={{0,1},{1,0},{2,3},{3,2},{4,5},{5,4},{6,7},{7,6},{8,9},{9,8},{10,11... | collective-permute-start | bytes 786440 | tf_op jit(solution)/shard_map/ppermute | solution.py:376
  43.6 11.6 %collective-permute-start.20 = (bf16[128,1024]{1,0:T(8,128)(2,1)S(1)}, bf16[128,1024]{1,0:T(8,128)(2,1)S(1)}, u32[]{:S(2)}, u32[]{:S(2)}) collective-permute-start(bf16[128,1024]{1,0:T(8,128)(2,1)S(1)} %get-tuple-element.35.rest_0_.own_ref), channel_id=1, source_target_pairs={{0,16},{8,24},{16,0},{24,8},{1,17},{9,25},{17,1},{25,9},{2,18},{10... | collective-permute-start | bytes 786440 | tf_op jit(solution)/shard_map/ppermute | solution.py:380
  45.1 12.5 %collective-permute-start.19 = (bf16[128,1024]{1,0:T(8,128)(2,1)S(1)}, bf16[128,1024]{1,0:T(8,128)(2,1)S(1)}, u32[]{:S(2)}, u32[]{:S(2)}) collective-permute-start(bf16[128,1024]{1,0:T(8,128)(2,1)S(1)} %get-tuple-element.38.own_ref), channel_id=1, source_target_pairs={{0,16},{8,24},{16,0},{24,8},{1,17},{9,25},{17,1},{25,9},{2,18},{10... | collective-permute-start | bytes 786440 | tf_op jit(solution)/shard_map/ppermute | solution.py:380
  45.7 12.0 %collective-permute-start.21 = (bf16[128,2048]{1,0:T(8,128)(2,1)S(1)}, bf16[128,2048]{1,0:T(8,128)(2,1)S(1)}, u32[]{:S(2)}, u32[]{:S(2)}) collective-permute-start(bf16[128,2048]{1,0:T(8,128)(2,1)S(1)} %add_pair.3.refs_0_), channel_id=1, source_target_pairs={{0,8},{8,0},{16,24},{24,16},{1,9},{9,1},{17,25},{25,17},{2,10},{10... | collective-permute-start | bytes 1572872 | tf_op jit(solution)/shard_map/ppermute | solution.py:380
  55.3 2.5 %collective-permute-start.23 = (bf16[128,1024]{1,0:T(8,128)(2,1)S(1)}, bf16[128,1024]{1,0:T(8,128)(2,1)S(1)}, u32[]{:S(2)}, u32[]{:S(2)}) collective-permute-start(bf16[128,1024]{1,0:T(8,128)(2,1)S(1)} %add_pair.5.refs_2_), channel_id=1, source_target_pairs={{0,8},{8,0},{16,24},{24,16},{1,9},{9,1},{17,25},{25,17},{2,10},{10... | collective-permute-start | bytes 786440 | tf_op jit(solution)/shard_map/ppermute | solution.py:380
  57.6 1.6 %collective-permute-start.22 = (bf16[128,1024]{1,0:T(8,128)(2,1)S(1)}, bf16[128,1024]{1,0:T(8,128)(2,1)S(1)}, u32[]{:S(2)}, u32[]{:S(2)}) collective-permute-start(bf16[128,1024]{1,0:T(8,128)(2,1)S(1)} %add_pair.4.refs_1_), channel_id=1, source_target_pairs={{0,8},{8,0},{16,24},{24,16},{1,9},{9,1},{17,25},{25,17},{2,10},{10... | collective-permute-start | bytes 786440 | tf_op jit(solution)/shard_map/ppermute | solution.py:380

commit v8 on v6

--- a/solution.py
+++ b/solution.py
@@ -201,29 +201,46 @@
     )(ratio, docs_held)
 
 
-def beta_piece(sizes, here, product, ratio, docs_held, prob_held, start, spans, after):
+def beta_pieces(sizes, here, product, ratio, docs_held, prob_held, flips, after):
     words, side_width = product.shape
-    docs, width = docs_held.shape[0], sum(spans)
+    docs = docs_held.shape[0]
+    rows = words // len(flips)
 
     def kernel(here_ref, product_ref, ratio_ref, doc_ref, prob_ref, *rest):
-        side = sizes.side(here_ref)
-        begin = start
-        for out_ref, span in zip(rest[len(after) :], spans):
-            at = pl.ds(begin, span)
-            prob_at = pl.ds(pl.multiple_of(side * side_width + begin, 128), span)
-            summed = product_ref[:, at] + jnp.dot(ratio_ref[...], doc_ref[:, at], preferred_element_type=F32)
-            out_ref[...] = (-prob_ref[:, prob_at].astype(F32) * summed).astype(BF16)
-            begin += span
-
-    return pl.pallas_call(
-        kernel,
-        out_shape=[jax.ShapeDtypeStruct((words, span), BF16) for span in spans],
+        columns = window(sizes.side(here_ref), side_width)
+        topic_at = sizes.topic_at(here_ref)
+        summed = product_ref[...] + jnp.dot(ratio_ref[...], doc_ref[...], preferred_element_type=F32)
+        for i, (flip, out_ref) in enumerate(zip(flips, rest[len(after) :])):
+            prob = prob_ref[window(topic_at ^ flip, rows), columns].astype(F32)
+            out_ref[...] = (-prob * summed[i * rows : (i + 1) * rows, :]).astype(BF16)
+
+    return pl.pallas_call(
+        kernel,
+        out_shape=[jax.ShapeDtypeStruct((rows, side_width), BF16)] * len(flips),
         in_specs=[SMEM] + [VMEM] * 4 + [ANY] * len(after),
-        out_specs=[VMEM] * len(spans),
-        compiler_params=call_params(),
-        cost_estimate=cost(2 * words * docs * width, 2 * (4 * words + docs) * width),
-        name="beta_piece",
+        out_specs=[VMEM] * len(flips),
+        compiler_params=call_params(),
+        cost_estimate=cost(2 * words * docs * side_width, 2 * (4 * words + docs) * side_width),
+        name="beta_pieces",
     )(here, product, ratio, docs_held, prob_held, *after)
+
+
+def stack_rows(parts, after):
+    rows, docs = parts[0].shape
+
+    def kernel(*refs):
+        for i, ref in enumerate(refs[: len(parts)]):
+            refs[-1][i * rows : (i + 1) * rows, :] = ref[...]
+
+    return pl.pallas_call(
+        kernel,
+        out_shape=jax.ShapeDtypeStruct((len(parts) * rows, docs), BF16),
+        in_specs=[VMEM] * len(parts) + [ANY] * len(after),
+        out_specs=VMEM,
+        compiler_params=call_params(),
+        cost_estimate=cost(0, 4 * len(parts) * rows * docs),
+        name="stack_rows",
+    )(*parts, *after)
 
 
 def add_pair(own, other, after=()):
@@ -313,18 +330,17 @@
     )(here, ratio, *far_ratios, prob_held, *far_logits, log_norm)
 
 
-def place_pieces(sizes, here, own, other, starts, shape):
+def place_pieces(sizes, here, own, other, flips, shape):
     pieces = len(own)
     side_width = shape[1] // 2
 
     def kernel(here_ref, *refs):
         own_refs, other_refs, (out_ref, sems) = refs[:pieces], refs[pieces : 2 * pieces], refs[-2:]
-        side = sizes.side(here_ref)
+        side, topic_at = sizes.side(here_ref), sizes.topic_at(here_ref)
         copies = []
-        for p in range(pieces):
+        for p, flip in enumerate(flips):
             for h, (ref, which) in enumerate(((own_refs[p], side), (other_refs[p], 1 - side))):
-                column = pl.multiple_of(which * side_width + starts[p], 128)
-                target = out_ref.at[:, pl.ds(column, ref.shape[1])]
+                target = out_ref.at[window(topic_at ^ flip, ref.shape[0]), window(which, side_width)]
                 copies.append(pltpu.make_async_copy(ref, target, sems.at[h, p]))
         for copy in copies:
             copy.start()
@@ -365,32 +381,30 @@
     arrived = [swap(parts[s], "topic", s) for s in order]
     counts = chunk_counts(sizes, here, word_counts, tile_doc, tile_word, docs, words)
     own_ratio = ratio_chunk([parts[0]] + arrived, counts, word_tile)
-    gathered = [own_ratio] + [swap(own_ratio, "topic", s) for s in order]
-    ratio = join_ratio(sizes, here, gathered, [0] + order, near_logits + [sibling_docs])
-    sibling_ratio = swap(ratio, "doc", 1)
+    gathered = [swap(own_ratio, "topic", s) for s in order]
+    far_bits = [1 << b for b in range(1, sizes.doc.bit_length() - 1)]
+
+    def beta(ratio, flips, after):
+        pieces = beta_pieces(
+            sizes, here, own_product(ratio, docs_held), swap(ratio, "doc", 1), sibling_docs, prob_held, flips, after
+        )
+        for bit in far_bits[:-1]:
+            pieces = [add_pair(part, swap(part, "doc", bit)) for part in pieces]
+        return [(part, swap(part, "doc", far_bits[-1])) for part in pieces]
+
+    own_pair = beta(own_ratio, [0], [])
+    pairs = own_pair + beta(stack_rows(gathered, near_logits), order, [own_pair[0][1]])
+    ratio = join_ratio(sizes, here, [own_ratio] + gathered, [0] + order, [pairs[1][0]])
     far_ratios = [shift(ratio, s) for s in range(1, sizes.vocab)]
-
-    side_width = width // 2
-    spans = [side_width // 4, side_width // 2, side_width // 4]
-    starts = [0, spans[0], spans[0] + spans[1]]
-    product = own_product(ratio, docs_held)
-    sibling = (sibling_ratio, sibling_docs, prob_held)
-    sums = list(beta_piece(sizes, here, product, *sibling, 0, spans[:1], []))
-    sums += beta_piece(sizes, here, product, *sibling, spans[0], spans[1:], sums)
 
     far_logits = []
     for part in near_logits:
-        part = hold(part, sums[-1:])
+        part = hold(part, [pairs[-1][0]])
         far_logits += [part, swap(part, "doc", 1)]
-
-    bit = 2
-    while 2 * bit < sizes.doc:
-        sums = [add_pair(part, swap(part, "doc", bit)) for part in sums]
-        bit *= 2
-    others = [swap(part, "doc", bit) for part in sums]
     theta, theta_done = theta_grad(sizes, here, ratio, far_ratios, prob_held, far_logits, norm_held)
-    sums = [add_pair(*pair, [theta_done]) for pair in zip(sums, others)]
-    out = place_pieces(sizes, here, sums, [swap(part, "doc", 1) for part in sums], starts, word_logits.shape)
+
+    sums = [add_pair(*pair, [theta_done] if p else []) for p, pair in enumerate(pairs)]
+    out = place_pieces(sizes, here, sums, [swap(part, "doc", 1) for part in sums], [0] + order, word_logits.shape)
     return theta, out
 
 

time: 59.8 us -> 55.7 us (0.931)
  waiting for transfers between devices: 30.1 us -> 23.2 us
  starting transfers between devices: 16.1 us -> 18.2 us
  Pallas kernels: 12.7 us -> 13.3 us
    ppermute x15 -> x18, waiting for transfers between devices: 25.6 us -> 18.6 us  [swap(): return lax.ppermute(array, axis, [(i, i ^ bits) for i in range(count)])]
    ppermute x15 -> x18, starting transfers between devices: 13 us -> 15 us  [swap(): return lax.ppermute(array, axis, [(i, i ^ bits) for i in range(count)])]
  transfers between devices with their start and end apart: 17 -> 20, of which waited for: 10 -> 12; matrix products, arithmetic and copies ran while one was open for 0% -> 0% of each run, Pallas kernels for 9% -> 12%
where the time goes in v8:
time: 55.7 us; the launch traced here: 55.5 us
  waiting for transfers between devices  23.2 us (42%)
  starting transfers between devices  18.2 us (33%)
  Pallas kernels  13.3 us (24%)
  between operations  0.79 us (1%)
    ppermute x18, waiting for transfers between devices, swap(): return lax.ppermute(array, axis, [(i, i ^ bits) for i in range(count)])  18.6 us
    ppermute x18, starting transfers between devices, swap(): return lax.ppermute(array, axis, [(i, i ^ bits) for i in range(count)])  15 us
    pallas_call x1, Pallas kernels, rate_partial(): pl.pallas_call(kernel, out_shape=[jax.ShapeDtypeStruct((chunk, docs), BF1...  4.78 us
    ppermute x2, waiting for transfers between devices, shift(): lax.ppermute(array, 'vocab', [(i, (i + by) % sizes.vocab) for i in range(...  4.61 us
    pallas_call x1, Pallas kernels, theta_grad(): pl.pallas_call(kernel, out_shape=[jax.ShapeDtypeStruct((docs, share), F32...  3.73 us
    ppermute x2, starting transfers between devices, shift(): lax.ppermute(array, 'vocab', [(i, (i + by) % sizes.vocab) for i in range(...  3.16 us
    pallas_call x1, Pallas kernels, place_pieces(): pl.pallas_call(kernel, out_shape=jax.ShapeDtypeStruct(shape, BF16), in_sp...  1.37 us
  transfers between devices with their start and end apart: 20, of which 12 were waited for; matrix products, arithmetic and copies ran while one was open for 0% of the time, Pallas kernels for 12%

profile of v8, /device:TPU:0, one launch (start us, length us, event | category | flops | bytes accessed | tf_op | source)
XLA Modules:
  0.0 55.5 jit_solution(1661273244920301881)
XLA Ops:
  0.6 4.8 %rate_partial.1 = (bf16[64,512]{1,0:T(8,128)(2,1)S(1)}, bf16[64,512]{1,0:T(8,128)(2,1)S(1)}, bf16[64,512]{1,0:T(8,128)(2,1)S(1)}, bf16[64,512]{1,0:T(8,128)(2,1)...) custom-call(s32[1]{0:T(128)} %bitcast.here_ref, ...), custom_call_target="tpu_custom_call" | custom-call | flops 1073741824 | bytes 6291456 | tf_op jit(solution)/shard_map/rate_partial/pallas_call | solution.py:97
  5.4 0.5 collective-permute-start.8
  6.0 2.6 %collective-permute-start.6 = (bf16[128,2048]{1,0:T(8,128)(2,1)S(1)}, bf16[128,2048]{1,0:T(8,128)(2,1)S(1)}, u32[]{:S(2)}, u32[]{:S(2)}) collective-permute-start(bf16[128,2048]{1,0:T(8,128)(2,1)S(1)} %get-tuple-element.20), channel_id=1, source_target_pairs={{0,1},{1,0},{2,3},{3,2},{4,5},{5,4},{6,7},{7,6},{8,9},{9,8},{10,11... | collective-permute-start | bytes 1572872 | tf_op jit(solution)/shard_map/ppermute | solution.py:369
  8.6 2.6 %collective-permute-start = (bf16[64,512]{1,0:T(8,128)(2,1)S(1)}, bf16[64,512]{1,0:T(8,128)(2,1)S(1)}, u32[]{:S(2)}, u32[]{:S(2)}) collective-permute-start(bf16[64,512]{1,0:T(8,128)(2,1)S(1)} %get-tuple-element.17), channel_id=1, source_target_pairs={{0,4},{2,6},{4,0},{6,2},{1,5},{3,7},{5,1},{7,3},{8,12},{10,14},{12... | collective-permute-start | bytes 196616 | tf_op jit(solution)/shard_map/ppermute | solution.py:373
  11.1 1.3 %collective-permute-start.1 = (bf16[64,512]{1,0:T(8,128)(2,1)S(1)}, bf16[64,512]{1,0:T(8,128)(2,1)S(1)}, u32[]{:S(2)}, u32[]{:S(2)}) collective-permute-start(bf16[64,512]{1,0:T(8,128)(2,1)S(1)} %get-tuple-element.18), channel_id=1, source_target_pairs={{0,6},{2,4},{4,2},{6,0},{1,7},{3,5},{5,3},{7,1},{8,14},{10,12},{12... | collective-permute-start | bytes 196616 | tf_op jit(solution)/shard_map/ppermute | solution.py:373
  12.7 0.8 %chunk_counts.1.refs_4_ = f32[64,512]{1,0:T(8,128)S(1)} custom-call(s32[1]{0:T(128)} %bitcast.here_ref, s32[16]{0:T(128)} %doc_at.1, s32[16]{0:T(128)} %word_at.1, s32[16,64,128]{2,1,0:T(8,128)S(1)} %copy-done), custom_call_target="tpu_custom_call" | custom-call | flops 131072 | bytes 524288 | tf_op jit(solution)/shard_map/chunk_counts/pallas_call | solution.py:136
  13.6 2.0 %collective-permute-done.refs_1_ = bf16[64,512]{1,0:T(8,128)(2,1)S(1)} collective-permute-done((bf16[64,512]{1,0:T(8,128)(2,1)S(1)}, bf16[64,512]{1,0:T(8,128)(2,1)S(1)}, u32[]{:S(2)}, u32[]{:S(2)}) %collective-permute-start) | collective-permute-done | bytes 65568 | tf_op jit(solution)/shard_map/ppermute | solution.py:373
  15.6 2.0 %collective-permute-done.1.refs_2_ = bf16[64,512]{1,0:T(8,128)(2,1)S(1)} collective-permute-done((bf16[64,512]{1,0:T(8,128)(2,1)S(1)}, bf16[64,512]{1,0:T(8,128)(2,1)S(1)}, u32[]{:S(2)}, u32[]{:S(2)}) %collective-permute-start.1) | collective-permute-done | bytes 65568 | tf_op jit(solution)/shard_map/ppermute | solution.py:373
  18.0 2.6 %collective-permute-start.3 = (bf16[64,512]{1,0:T(8,128)(2,1)S(1)}, bf16[64,512]{1,0:T(8,128)(2,1)S(1)}, u32[]{:S(2)}, u32[]{:S(2)}) collective-permute-start(bf16[64,512]{1,0:T(8,128)(2,1)S(1)} %ratio_chunk.1.ratio_ref.refs_0_), channel_id=1, source_target_pairs={{0,4},{2,6},{4,0},{6,2},{1,5},{3,7},{5,1},{7,3},{8,12},{10,14},{12... | collective-permute-start | bytes 196616 | tf_op jit(solution)/shard_map/ppermute | solution.py:373
  20.7 0.7 %collective-permute-start.4 = (bf16[64,512]{1,0:T(8,128)(2,1)S(1)}, bf16[64,512]{1,0:T(8,128)(2,1)S(1)}, u32[]{:S(2)}, u32[]{:S(2)}) collective-permute-start(bf16[64,512]{1,0:T(8,128)(2,1)S(1)} %ratio_chunk.1.ratio_ref.refs_0_), channel_id=1, source_target_pairs={{0,6},{2,4},{4,2},{6,0},{1,7},{3,5},{5,3},{7,1},{8,14},{10,12},{12... | collective-permute-start | bytes 196616 | tf_op jit(solution)/shard_map/ppermute | solution.py:373
  21.4 0.5 own_product.3.product_ref
  21.9 0.6 collective-permute-start.5
  22.4 0.5 beta_pieces.2.own_ref
  22.9 1.6 %collective-permute-start.10 = (bf16[64,2048]{1,0:T(8,128)(2,1)S(1)}, bf16[64,2048]{1,0:T(8,128)(2,1)S(1)}, u32[]{:S(2)}, u32[]{:S(2)}) collective-permute-start(bf16[64,2048]{1,0:T(8,128)(2,1)S(1)} %beta_pieces.2.own_ref), channel_id=1, source_target_pairs={{0,16},{8,24},{16,0},{24,8},{1,17},{9,25},{17,1},{25,9},{2,18},{10... | collective-permute-start | bytes 786440 | tf_op jit(solution)/shard_map/ppermute | solution.py:373
  24.5 0.9 %collective-permute-done.3.refs_0_.refs_1_ = bf16[64,512]{1,0:T(8,128)(2,1)S(1)} collective-permute-done((bf16[64,512]{1,0:T(8,128)(2,1)S(1)}, bf16[64,512]{1,0:T(8,128)(2,1)S(1)}, u32[]{:S(2)}, u32[]{:S(2)}) %collective-permute-start.3) | collective-permute-done | bytes 65568 | tf_op jit(solution)/shard_map/ppermute | solution.py:373
  25.4 2.0 %collective-permute-done.4.refs_1_.refs_2_ = bf16[64,512]{1,0:T(8,128)(2,1)S(1)} collective-permute-done((bf16[64,512]{1,0:T(8,128)(2,1)S(1)}, bf16[64,512]{1,0:T(8,128)(2,1)S(1)}, u32[]{:S(2)}, u32[]{:S(2)}) %collective-permute-start.4) | collective-permute-done | bytes 65568 | tf_op jit(solution)/shard_map/ppermute | solution.py:373
  27.3 0.4 collective-permute-done.5.refs_2_.refs_3_
  27.8 0.6 %own_product.2.product_ref = f32[192,2048]{1,0:T(8,128)S(1)} custom-call(bf16[192,512]{1,0:T(8,128)(2,1)S(1)} %stack_rows.1.ratio_ref, bf16[512,2048]{1,0:T(8,128)(2,1)S(1)} %get-tuple-element.21.doc_ref), custom_call_target="tpu_custom_call" | custom-call | flops 402653184 | bytes 3670016 | tf_op jit(solution)/shard_map/own_product/pallas_call | solution.py:193
  28.4 0.8 %collective-permute-done.7.ratio_ref = bf16[192,512]{1,0:T(8,128)(2,1)S(1)} collective-permute-done((bf16[192,512]{1,0:T(8,128)(2,1)S(1)}, bf16[192,512]{1,0:T(8,128)(2,1)S(1)}, u32[]{:S(2)}, u32[]{:S(2)}) %collective-permute-start.7) | collective-permute-done | bytes 196640 | tf_op jit(solution)/shard_map/ppermute | solution.py:373
  29.3 1.8 %collective-permute-done.10.rest_0_.other_ref = bf16[64,2048]{1,0:T(8,128)(2,1)S(1)} collective-permute-done((bf16[64,2048]{1,0:T(8,128)(2,1)S(1)}, bf16[64,2048]{1,0:T(8,128)(2,1)S(1)}, u32[]{:S(2)}, u32[]{:S(2)}) %collective-permute-start.10) | collective-permute-done | bytes 262176 | tf_op jit(solution)/shard_map/ppermute | solution.py:373
  31.1 0.6 %beta_pieces.3 = (bf16[64,2048]{1,0:T(8,128)(2,1)S(1)}, bf16[64,2048]{1,0:T(8,128)(2,1)S(1)}, bf16[64,2048]{1,0:T(8,128)(2,1)S(1)}) custom-call(s32[1]{0:T(128)} %bitcast.here_ref, f32[192,2048]{1,0:T(8,128)S(1)} %own_product.2.product_ref, bf16[192,512]{1,0:T(8,128)(2,1)S(1)} %collective-permute-done.7.ratio_ref, ...), custom_call_target="tpu_custom_call" | custom-call | flops 402653184 | bytes 5242880 | tf_op jit(solution)/shard_map/beta_pieces/pallas_call | solution.py:217
  31.9 0.6 %collective-permute-start.11 = (bf16[256,512]{1,0:T(8,128)(2,1)S(1)}, bf16[256,512]{1,0:T(8,128)(2,1)S(1)}, u32[]{:S(2)}, u32[]{:S(2)}) collective-permute-start(bf16[256,512]{1,0:T(8,128)(2,1)S(1)} %join_ratio.1.ratio_ref), channel_id=1, source_target_pairs={{0,1},{1,0},{2,3},{3,2},{4,5},{5,4},{6,7},{7,6},{8,9},{9,8},{10,11... | collective-permute-start | bytes 786440 | tf_op jit(solution)/shard_map/ppermute | solution.py:369
  32.4 1.5 %collective-permute-start.15 = (bf16[64,2048]{1,0:T(8,128)(2,1)S(1)}, bf16[64,2048]{1,0:T(8,128)(2,1)S(1)}, u32[]{:S(2)}, u32[]{:S(2)}) collective-permute-start(bf16[64,2048]{1,0:T(8,128)(2,1)S(1)} %get-tuple-element.25.rest_0_.own_ref), channel_id=1, source_target_pairs={{0,16},{8,24},{16,0},{24,8},{1,17},{9,25},{17,1},{25,9},{2,18},{10... | collective-permute-start | bytes 786440 | tf_op jit(solution)/shard_map/ppermute | solution.py:373
  33.9 0.5 collective-permute-start.13
  34.5 1.5 %collective-permute-start.14 = (bf16[64,2048]{1,0:T(8,128)(2,1)S(1)}, bf16[64,2048]{1,0:T(8,128)(2,1)S(1)}, u32[]{:S(2)}, u32[]{:S(2)}) collective-permute-start(bf16[64,2048]{1,0:T(8,128)(2,1)S(1)} %get-tuple-element.29.own_ref), channel_id=1, source_target_pairs={{0,16},{8,24},{16,0},{24,8},{1,17},{9,25},{17,1},{25,9},{2,18},{10... | collective-permute-start | bytes 786440 | tf_op jit(solution)/shard_map/ppermute | solution.py:373
  36.0 4.6 %collective-permute-done.11.refs_0_ = bf16[256,512]{1,0:T(8,128)(2,1)S(1)} collective-permute-done((bf16[256,512]{1,0:T(8,128)(2,1)S(1)}, bf16[256,512]{1,0:T(8,128)(2,1)S(1)}, u32[]{:S(2)}, u32[]{:S(2)}) %collective-permute-start.11) | collective-permute-done | bytes 262176 | tf_op jit(solution)/shard_map/ppermute | solution.py:369
  40.6 3.7 %theta_grad.1 = (f32[512,2048]{1,0:T(8,128)}, f32[8,128]{1,0:T(8,128)S(1)}) custom-call(s32[1]{0:T(128)} %bitcast.here_ref, bf16[256,512]{1,0:T(8,128)(2,1)S(1)} %join_ratio.1.ratio_ref, bf16[256,512]{1,0:T(8,128)(2,1)S(1)} %collective-permute-done.11.refs_0_, bf16[256,4096]{1,0:T(8,128)(2,1)S(1)} %get-tuple-element.23.prob_ref.refs_1_, ...), custom_call_target="tpu_custom_call" | custom-call | flops 10737418240 | bytes 62914560 | tf_op jit(solution)/shard_map/theta_grad/pallas_call | solution.py:312
  44.4 0.6 collective-permute-start.19
  45.0 7.1 %collective-permute-done.14.other_ref = bf16[64,2048]{1,0:T(8,128)(2,1)S(1)} collective-permute-done((bf16[64,2048]{1,0:T(8,128)(2,1)S(1)}, bf16[64,2048]{1,0:T(8,128)(2,1)S(1)}, u32[]{:S(2)}, u32[]{:S(2)}) %collective-permute-start.14) | collective-permute-done | bytes 262176 | tf_op jit(solution)/shard_map/ppermute | solution.py:373
  52.3 0.5 collective-permute-start.17
  52.9 0.9 %collective-permute-done.18.refs_6_ = bf16[64,2048]{1,0:T(8,128)(2,1)S(1)} collective-permute-done((bf16[64,2048]{1,0:T(8,128)(2,1)S(1)}, bf16[64,2048]{1,0:T(8,128)(2,1)S(1)}, u32[]{:S(2)}, u32[]{:S(2)}) %collective-permute-start.18) | collective-permute-done | bytes 262176 | tf_op jit(solution)/shard_map/ppermute | solution.py:373
  54.1 1.4 %place_pieces.1 = bf16[256,4096]{1,0:T(8,128)(2,1)} custom-call(s32[1]{0:T(128)} %bitcast.here_ref, bf16[64,2048]{1,0:T(8,128)(2,1)S(1)} %add_pair.4.refs_0_, bf16[64,2048]{1,0:T(8,128)(2,1)S(1)} %add_pair.5.refs_1_, bf16[64,2048]{1,0:T(8,128)(2,1)S(1)} %add_pair.6.refs_2_, bf16[64,2048]{1,0:T(8,128)(2,1)S(1)} %add_pair.7.refs_3_, ...), custom_call_target="tpu_custom_call" | custom-call | bytes 4194304 | tf_op jit(solution)/shard_map/place_pieces/pallas_call | solution.py:350
  (26 shorter events, 1.6 us)
Async XLA Ops:
  0.6 12.1 %copy-start = (s32[16,64,128]{2,1,0:T(8,128)S(1)}, s32[16,64,128]{2,1,0:T(8,128)}, u32[]{:S(2)}) copy-start(s32[16,64,128]{2,1,0:T(8,128)} %count_ref.1) | copy-start | bytes 1572868
  5.4 17.0 %collective-permute-start.8 = (bf16[512,2048]{1,0:T(8,128)(2,1)S(1)}, bf16[512,2048]{1,0:T(8,128)(2,1)S(1)}, u32[]{:S(2)}, u32[]{:S(2)}) collective-permute-start(bf16[512,2048]{1,0:T(8,128)(2,1)S(1)} %get-tuple-element.22), channel_id=1, source_target_pairs={{0,8},{8,0},{16,24},{24,16},{1,9},{9,1},{17,25},{25,17},{2,10},{10... | collective-permute-start | bytes 6291464 | tf_op jit(solution)/shard_map/ppermute | solution.py:373
  6.0 21.8 %collective-permute-start.6 = (bf16[128,2048]{1,0:T(8,128)(2,1)S(1)}, bf16[128,2048]{1,0:T(8,128)(2,1)S(1)}, u32[]{:S(2)}, u32[]{:S(2)}) collective-permute-start(bf16[128,2048]{1,0:T(8,128)(2,1)S(1)} %get-tuple-element.20), channel_id=1, source_target_pairs={{0,1},{1,0},{2,3},{3,2},{4,5},{5,4},{6,7},{7,6},{8,9},{9,8},{10,11... | collective-permute-start | bytes 1572872 | tf_op jit(solution)/shard_map/ppermute | solution.py:369
  8.6 7.0 %collective-permute-start = (bf16[64,512]{1,0:T(8,128)(2,1)S(1)}, bf16[64,512]{1,0:T(8,128)(2,1)S(1)}, u32[]{:S(2)}, u32[]{:S(2)}) collective-permute-start(bf16[64,512]{1,0:T(8,128)(2,1)S(1)} %get-tuple-element.17), channel_id=1, source_target_pairs={{0,4},{2,6},{4,0},{6,2},{1,5},{3,7},{5,1},{7,3},{8,12},{10,14},{12... | collective-permute-start | bytes 196616 | tf_op jit(solution)/shard_map/ppermute | solution.py:373
  11.1 6.4 %collective-permute-start.1 = (bf16[64,512]{1,0:T(8,128)(2,1)S(1)}, bf16[64,512]{1,0:T(8,128)(2,1)S(1)}, u32[]{:S(2)}, u32[]{:S(2)}) collective-permute-start(bf16[64,512]{1,0:T(8,128)(2,1)S(1)} %get-tuple-element.18), channel_id=1, source_target_pairs={{0,6},{2,4},{4,2},{6,0},{1,7},{3,5},{5,3},{7,1},{8,14},{10,12},{12... | collective-permute-start | bytes 196616 | tf_op jit(solution)/shard_map/ppermute | solution.py:373
  12.5 5.4 %collective-permute-start.2 = (bf16[64,512]{1,0:T(8,128)(2,1)S(1)}, bf16[64,512]{1,0:T(8,128)(2,1)S(1)}, u32[]{:S(2)}, u32[]{:S(2)}) collective-permute-start(bf16[64,512]{1,0:T(8,128)(2,1)S(1)} %get-tuple-element.19), channel_id=1, source_target_pairs={{0,2},{2,0},{4,6},{6,4},{1,3},{3,1},{5,7},{7,5},{8,10},{10,8},{12,... | collective-permute-start | bytes 196616 | tf_op jit(solution)/shard_map/ppermute | solution.py:373
  17.9 3.9 %collective-permute-start.9 = (bf16[64,512]{1,0:T(8,128)(2,1)S(1)}, bf16[64,512]{1,0:T(8,128)(2,1)S(1)}, u32[]{:S(2)}, u32[]{:S(2)}) collective-permute-start(bf16[64,512]{1,0:T(8,128)(2,1)S(1)} %ratio_chunk.1.ratio_ref.refs_0_), channel_id=1, source_target_pairs={{0,8},{8,0},{16,24},{24,16},{1,9},{9,1},{17,25},{25,17},{2,10},{10... | collective-permute-start | bytes 196616 | tf_op jit(solution)/shard_map/ppermute | solution.py:373
  18.0 7.3 %collective-permute-start.3 = (bf16[64,512]{1,0:T(8,128)(2,1)S(1)}, bf16[64,512]{1,0:T(8,128)(2,1)S(1)}, u32[]{:S(2)}, u32[]{:S(2)}) collective-permute-start(bf16[64,512]{1,0:T(8,128)(2,1)S(1)} %ratio_chunk.1.ratio_ref.refs_0_), channel_id=1, source_target_pairs={{0,4},{2,6},{4,0},{6,2},{1,5},{3,7},{5,1},{7,3},{8,12},{10,14},{12... | collective-permute-start | bytes 196616 | tf_op jit(solution)/shard_map/ppermute | solution.py:373
  20.7 6.7 %collective-permute-start.4 = (bf16[64,512]{1,0:T(8,128)(2,1)S(1)}, bf16[64,512]{1,0:T(8,128)(2,1)S(1)}, u32[]{:S(2)}, u32[]{:S(2)}) collective-permute-start(bf16[64,512]{1,0:T(8,128)(2,1)S(1)} %ratio_chunk.1.ratio_ref.refs_0_), channel_id=1, source_target_pairs={{0,6},{2,4},{4,2},{6,0},{1,7},{3,5},{5,3},{7,1},{8,14},{10,12},{12... | collective-permute-start | bytes 196616 | tf_op jit(solution)/shard_map/ppermute | solution.py:373
  21.9 5.9 %collective-permute-start.5 = (bf16[64,512]{1,0:T(8,128)(2,1)S(1)}, bf16[64,512]{1,0:T(8,128)(2,1)S(1)}, u32[]{:S(2)}, u32[]{:S(2)}) collective-permute-start(bf16[64,512]{1,0:T(8,128)(2,1)S(1)} %ratio_chunk.1.ratio_ref.refs_0_), channel_id=1, source_target_pairs={{0,2},{2,0},{4,6},{6,4},{1,3},{3,1},{5,7},{7,5},{8,10},{10,8},{12,... | collective-permute-start | bytes 196616 | tf_op jit(solution)/shard_map/ppermute | solution.py:373
  22.9 8.2 %collective-permute-start.10 = (bf16[64,2048]{1,0:T(8,128)(2,1)S(1)}, bf16[64,2048]{1,0:T(8,128)(2,1)S(1)}, u32[]{:S(2)}, u32[]{:S(2)}) collective-permute-start(bf16[64,2048]{1,0:T(8,128)(2,1)S(1)} %beta_pieces.2.own_ref), channel_id=1, source_target_pairs={{0,16},{8,24},{16,0},{24,8},{1,17},{9,25},{17,1},{25,9},{2,18},{10... | collective-permute-start | bytes 786440 | tf_op jit(solution)/shard_map/ppermute | solution.py:373
  27.8 1.5 %collective-permute-start.7 = (bf16[192,512]{1,0:T(8,128)(2,1)S(1)}, bf16[192,512]{1,0:T(8,128)(2,1)S(1)}, u32[]{:S(2)}, u32[]{:S(2)}) collective-permute-start(bf16[192,512]{1,0:T(8,128)(2,1)S(1)} %stack_rows.1.ratio_ref), channel_id=1, source_target_pairs={{0,8},{8,0},{16,24},{24,16},{1,9},{9,1},{17,25},{25,17},{2,10},{10... | collective-permute-start | bytes 589832 | tf_op jit(solution)/shard_map/ppermute | solution.py:373
  31.7 8.9 %collective-permute-start.12 = (bf16[128,2048]{1,0:T(8,128)(2,1)S(1)}, bf16[128,2048]{1,0:T(8,128)(2,1)S(1)}, u32[]{:S(2)}, u32[]{:S(2)}) collective-permute-start(bf16[128,2048]{1,0:T(8,128)(2,1)S(1)} %hold.1.refs_2_), channel_id=1, source_target_pairs={{0,8},{8,0},{16,24},{24,16},{1,9},{9,1},{17,25},{25,17},{2,10},{10... | collective-permute-start | bytes 1572872 | tf_op jit(solution)/shard_map/ppermute | solution.py:373
  31.9 8.8 %collective-permute-start.11 = (bf16[256,512]{1,0:T(8,128)(2,1)S(1)}, bf16[256,512]{1,0:T(8,128)(2,1)S(1)}, u32[]{:S(2)}, u32[]{:S(2)}) collective-permute-start(bf16[256,512]{1,0:T(8,128)(2,1)S(1)} %join_ratio.1.ratio_ref), channel_id=1, source_target_pairs={{0,1},{1,0},{2,3},{3,2},{4,5},{5,4},{6,7},{7,6},{8,9},{9,8},{10,11... | collective-permute-start | bytes 786440 | tf_op jit(solution)/shard_map/ppermute | solution.py:369
  32.4 11.9 %collective-permute-start.15 = (bf16[64,2048]{1,0:T(8,128)(2,1)S(1)}, bf16[64,2048]{1,0:T(8,128)(2,1)S(1)}, u32[]{:S(2)}, u32[]{:S(2)}) collective-permute-start(bf16[64,2048]{1,0:T(8,128)(2,1)S(1)} %get-tuple-element.25.rest_0_.own_ref), channel_id=1, source_target_pairs={{0,16},{8,24},{16,0},{24,8},{1,17},{9,25},{17,1},{25,9},{2,18},{10... | collective-permute-start | bytes 786440 | tf_op jit(solution)/shard_map/ppermute | solution.py:373
  33.9 18.3 %collective-permute-start.13 = (bf16[64,2048]{1,0:T(8,128)(2,1)S(1)}, bf16[64,2048]{1,0:T(8,128)(2,1)S(1)}, u32[]{:S(2)}, u32[]{:S(2)}) collective-permute-start(bf16[64,2048]{1,0:T(8,128)(2,1)S(1)} %get-tuple-element.24.refs_4_.own_ref), channel_id=1, source_target_pairs={{0,16},{8,24},{16,0},{24,8},{1,17},{9,25},{17,1},{25,9},{2,18},{10... | collective-permute-start | bytes 786440 | tf_op jit(solution)/shard_map/ppermute | solution.py:373
  34.5 17.6 %collective-permute-start.14 = (bf16[64,2048]{1,0:T(8,128)(2,1)S(1)}, bf16[64,2048]{1,0:T(8,128)(2,1)S(1)}, u32[]{:S(2)}, u32[]{:S(2)}) collective-permute-start(bf16[64,2048]{1,0:T(8,128)(2,1)S(1)} %get-tuple-element.29.own_ref), channel_id=1, source_target_pairs={{0,16},{8,24},{16,0},{24,8},{1,17},{9,25},{17,1},{25,9},{2,18},{10... | collective-permute-start | bytes 786440 | tf_op jit(solution)/shard_map/ppermute | solution.py:373
  40.6 12.2 %collective-permute-start.16 = (bf16[64,2048]{1,0:T(8,128)(2,1)S(1)}, bf16[64,2048]{1,0:T(8,128)(2,1)S(1)}, u32[]{:S(2)}, u32[]{:S(2)}) collective-permute-start(bf16[64,2048]{1,0:T(8,128)(2,1)S(1)} %add_pair.4.refs_0_), channel_id=1, source_target_pairs={{0,8},{8,0},{16,24},{24,16},{1,9},{9,1},{17,25},{25,17},{2,10},{10... | collective-permute-start | bytes 786440 | tf_op jit(solution)/shard_map/ppermute | solution.py:373
  44.4 8.4 %collective-permute-start.19 = (bf16[64,2048]{1,0:T(8,128)(2,1)S(1)}, bf16[64,2048]{1,0:T(8,128)(2,1)S(1)}, u32[]{:S(2)}, u32[]{:S(2)}) collective-permute-start(bf16[64,2048]{1,0:T(8,128)(2,1)S(1)} %add_pair.7.refs_3_), channel_id=1, source_target_pairs={{0,8},{8,0},{16,24},{24,16},{1,9},{9,1},{17,25},{25,17},{2,10},{10... | collective-permute-start | bytes 786440 | tf_op jit(solution)/shard_map/ppermute | solution.py:373
  52.2 1.6 %collective-permute-start.18 = (bf16[64,2048]{1,0:T(8,128)(2,1)S(1)}, bf16[64,2048]{1,0:T(8,128)(2,1)S(1)}, u32[]{:S(2)}, u32[]{:S(2)}) collective-permute-start(bf16[64,2048]{1,0:T(8,128)(2,1)S(1)} %add_pair.6.refs_2_), channel_id=1, source_target_pairs={{0,8},{8,0},{16,24},{24,16},{1,9},{9,1},{17,25},{25,17},{2,10},{10... | collective-permute-start | bytes 786440 | tf_op jit(solution)/shard_map/ppermute | solution.py:373
  52.3 1.8 %collective-permute-start.17 = (bf16[64,2048]{1,0:T(8,128)(2,1)S(1)}, bf16[64,2048]{1,0:T(8,128)(2,1)S(1)}, u32[]{:S(2)}, u32[]{:S(2)}) collective-permute-start(bf16[64,2048]{1,0:T(8,128)(2,1)S(1)} %add_pair.5.refs_1_), channel_id=1, source_target_pairs={{0,8},{8,0},{16,24},{24,16},{1,9},{9,1},{17,25},{25,17},{2,10},{10... | collective-permute-start | bytes 786440 | tf_op jit(solution)/shard_map/ppermute | solution.py:373

commit v9 on v8

--- a/solution.py
+++ b/solution.py
@@ -50,7 +50,7 @@
     docs, width = doc_topics.shape
     words = word_logits.shape[0]
     side_width = width // 2
-    span = min(side_width, 1024)
+    span = min(side_width, 512)
     steps = side_width // span
     count, far = sizes.topic, sizes.vocab - 1
     chunk, half, share = words // count, words // 2, width // sizes.vocab
@@ -60,7 +60,6 @@
         own_ref, sibling_ref, prob_ref, norm_ref, logit_ref, acc, sems, norm_sem = rest[count + far :]
         side = sizes.side(here_ref)
         norm_copy = pltpu.make_async_copy(norm_in, norm_ref, norm_sem)
-        norm_copy.start()
         blocks = []
         for which, doc_ref in ((1 - side, sibling_ref), (side, own_ref)):
             for j in range(steps):
@@ -70,8 +69,10 @@
                 held = doc_ref.at[:, pl.ds(j * span, span)]
                 doc_copy = pltpu.make_async_copy(doc_in.at[:, at], held, sems.at[1, i])
                 blocks.append((at, logit_copy, doc_copy, held))
-        for _, logit_copy, doc_copy, _ in blocks:
+        for i, (_, logit_copy, doc_copy, _) in enumerate(blocks):
             logit_copy.start()
+            if i == 0:
+                norm_copy.start()
             doc_copy.start()
         norm_copy.wait()
         for i, (at, logit_copy, doc_copy, held) in enumerate(blocks):
@@ -201,28 +202,31 @@
     )(ratio, docs_held)
 
 
-def beta_pieces(sizes, here, product, ratio, docs_held, prob_held, flips, after):
-    words, side_width = product.shape
+def beta_piece(sizes, here, product, ratio, docs_held, prob_held, flips, chosen):
+    side_width = product.shape[1]
     docs = docs_held.shape[0]
-    rows = words // len(flips)
-
-    def kernel(here_ref, product_ref, ratio_ref, doc_ref, prob_ref, *rest):
+    rows = product.shape[0] // len(flips)
+    words = rows * len(chosen)
+
+    def kernel(here_ref, product_ref, ratio_ref, doc_ref, prob_ref, out_ref):
         columns = window(sizes.side(here_ref), side_width)
         topic_at = sizes.topic_at(here_ref)
-        summed = product_ref[...] + jnp.dot(ratio_ref[...], doc_ref[...], preferred_element_type=F32)
-        for i, (flip, out_ref) in enumerate(zip(flips, rest[len(after) :])):
-            prob = prob_ref[window(topic_at ^ flip, rows), columns].astype(F32)
-            out_ref[...] = (-prob * summed[i * rows : (i + 1) * rows, :]).astype(BF16)
-
-    return pl.pallas_call(
-        kernel,
-        out_shape=[jax.ShapeDtypeStruct((rows, side_width), BF16)] * len(flips),
-        in_specs=[SMEM] + [VMEM] * 4 + [ANY] * len(after),
-        out_specs=[VMEM] * len(flips),
+        at = pl.ds(chosen[0] * rows, words)
+        summed = product_ref[at, :] + jnp.dot(ratio_ref[at, :], doc_ref[...], preferred_element_type=F32)
+        for i, c in enumerate(chosen):
+            at = pl.ds(i * rows, rows)
+            prob = prob_ref[window(topic_at ^ flips[c], rows), columns].astype(F32)
+            out_ref[at, :] = (-prob * summed[i * rows : (i + 1) * rows, :]).astype(BF16)
+
+    return pl.pallas_call(
+        kernel,
+        out_shape=jax.ShapeDtypeStruct((words, side_width), BF16),
+        in_specs=[SMEM] + [VMEM] * 4,
+        out_specs=VMEM,
         compiler_params=call_params(),
         cost_estimate=cost(2 * words * docs * side_width, 2 * (4 * words + docs) * side_width),
-        name="beta_pieces",
-    )(here, product, ratio, docs_held, prob_held, *after)
+        name="beta_piece",
+    )(here, product, ratio, docs_held, prob_held)
 
 
 def stack_rows(parts, after):
@@ -323,9 +327,7 @@
             scratch_shapes=[pltpu.VMEM((docs, count * words), BF16)],
         ),
         compiler_params=call_params(),
-        cost_estimate=cost(
-            20 * count * words * docs * share, (40 * docs + 20 * count * words) * share, 10 * count * words * share
-        ),
+        cost_estimate=cost(1, 1),
         name="theta_grad",
     )(here, ratio, *far_ratios, prob_held, *far_logits, log_norm)
 
@@ -338,10 +340,13 @@
         own_refs, other_refs, (out_ref, sems) = refs[:pieces], refs[pieces : 2 * pieces], refs[-2:]
         side, topic_at = sizes.side(here_ref), sizes.topic_at(here_ref)
         copies = []
-        for p, flip in enumerate(flips):
+        for p in range(pieces):
+            rows = own_refs[p].shape[0] // len(flips[p])
             for h, (ref, which) in enumerate(((own_refs[p], side), (other_refs[p], 1 - side))):
-                target = out_ref.at[window(topic_at ^ flip, ref.shape[0]), window(which, side_width)]
-                copies.append(pltpu.make_async_copy(ref, target, sems.at[h, p]))
+                for i, flip in enumerate(flips[p]):
+                    part = ref.at[pl.ds(i * rows, rows), :]
+                    target = out_ref.at[window(topic_at ^ flip, rows), window(which, side_width)]
+                    copies.append(pltpu.make_async_copy(part, target, sems.at[len(copies)]))
         for copy in copies:
             copy.start()
         for copy in copies:
@@ -352,7 +357,7 @@
         out_shape=jax.ShapeDtypeStruct(shape, BF16),
         in_specs=[SMEM] + [VMEM] * (2 * pieces),
         out_specs=HBM,
-        scratch_shapes=[pltpu.SemaphoreType.DMA((2, pieces))],
+        scratch_shapes=[pltpu.SemaphoreType.DMA((2 * sum(map(len, flips)),))],
         compiler_params=call_params(),
         cost_estimate=cost(0, 4 * shape[0] * shape[1]),
         name="place_pieces",
@@ -384,27 +389,31 @@
     gathered = [swap(own_ratio, "topic", s) for s in order]
     far_bits = [1 << b for b in range(1, sizes.doc.bit_length() - 1)]
 
-    def beta(ratio, flips, after):
-        pieces = beta_pieces(
-            sizes, here, own_product(ratio, docs_held), swap(ratio, "doc", 1), sibling_docs, prob_held, flips, after
-        )
+    def beta(ratio, flips, groups):
+        product, sibling_ratio = own_product(ratio, docs_held), swap(ratio, "doc", 1)
+        pieces = [
+            beta_piece(sizes, here, product, sibling_ratio, sibling_docs, prob_held, flips, chosen) for chosen in groups
+        ]
         for bit in far_bits[:-1]:
             pieces = [add_pair(part, swap(part, "doc", bit)) for part in pieces]
         return [(part, swap(part, "doc", far_bits[-1])) for part in pieces]
 
-    own_pair = beta(own_ratio, [0], [])
-    pairs = own_pair + beta(stack_rows(gathered, near_logits), order, [own_pair[0][1]])
-    ratio = join_ratio(sizes, here, [own_ratio] + gathered, [0] + order, [pairs[1][0]])
+    first = add_pair(*beta(own_ratio, [0], [[0]])[0])
+    last = len(order) - 1
+    groups = [list(range(last)), [last]] if last else [[0]]
+    pairs = beta(stack_rows(gathered, near_logits), order, groups)
+
+    ratio = join_ratio(sizes, here, [own_ratio] + gathered, [0] + order, [first])
     far_ratios = [shift(ratio, s) for s in range(1, sizes.vocab)]
-
     far_logits = []
     for part in near_logits:
-        part = hold(part, [pairs[-1][0]])
+        part = hold(part, [pairs[0][0]])
         far_logits += [part, swap(part, "doc", 1)]
     theta, theta_done = theta_grad(sizes, here, ratio, far_ratios, prob_held, far_logits, norm_held)
 
-    sums = [add_pair(*pair, [theta_done] if p else []) for p, pair in enumerate(pairs)]
-    out = place_pieces(sizes, here, sums, [swap(part, "doc", 1) for part in sums], [0] + order, word_logits.shape)
+    sums = [first] + [add_pair(*pair, [theta_done]) for pair in pairs]
+    flips = [[0]] + [[order[c] for c in chosen] for chosen in groups]
+    out = place_pieces(sizes, here, sums, [swap(part, "doc", 1) for part in sums], flips, word_logits.shape)
     return theta, out
 
 

time: 55.7 us -> 59.6 us (1.070)
  waiting for transfers between devices: 23.2 us -> 27.4 us
  starting transfers between devices: 18.2 us -> 17 us
  Pallas kernels: 13.3 us -> 14.3 us
    ppermute x18 -> x16, waiting for transfers between devices: 18.6 us -> 23.2 us  [swap(): return lax.ppermute(array, axis, [(i, i ^ bits) for i in range(count)])]
    ppermute x18 -> x16, starting transfers between devices: 15 us -> 13.8 us  [swap(): return lax.ppermute(array, axis, [(i, i ^ bits) for i in range(count)])]
    pallas_call x1, Pallas kernels: 4.78 us -> 5.41 us  [rate_partial(): pl.pallas_call(kernel, out_shape=[jax.ShapeDtypeStruct((chunk, docs), BF1...]
    pallas_call x2 -> x3, Pallas kernels: 1.11 us -> 1.51 us  [beta_piece(): pl.pallas_call(kernel, out_shape=jax.ShapeDtypeStruct((words, side_width)...]
  transfers between devices with their start and end apart: 20 -> 18, of which waited for: 12 -> 11; matrix products, arithmetic and copies ran while one was open for 0% -> 0% of each run, Pallas kernels for 12% -> 13%
where the time goes in v9:
time: 59.6 us; the launch traced here: 59.4 us
  waiting for transfers between devices  27.4 us (46%)
  starting transfers between devices  17 us (29%)
  Pallas kernels  14.3 us (24%)
  between operations  0.78 us (1%)
    ppermute x16, waiting for transfers between devices, swap(): return lax.ppermute(array, axis, [(i, i ^ bits) for i in range(count)])  23.2 us
    ppermute x16, starting transfers between devices, swap(): return lax.ppermute(array, axis, [(i, i ^ bits) for i in range(count)])  13.8 us
    pallas_call x1, Pallas kernels, rate_partial(): pl.pallas_call(kernel, out_shape=[jax.ShapeDtypeStruct((chunk, docs), BF1...  5.41 us
    ppermute x2, waiting for transfers between devices, shift(): lax.ppermute(array, 'vocab', [(i, (i + by) % sizes.vocab) for i in range(...  4.19 us
    pallas_call x1, Pallas kernels, theta_grad(): pl.pallas_call(kernel, out_shape=[jax.ShapeDtypeStruct((docs, share), F32...  3.71 us
    ppermute x2, starting transfers between devices, shift(): lax.ppermute(array, 'vocab', [(i, (i + by) % sizes.vocab) for i in range(...  3.16 us
    pallas_call x3, Pallas kernels, beta_piece(): pl.pallas_call(kernel, out_shape=jax.ShapeDtypeStruct((words, side_width)...  1.51 us
    pallas_call x1, Pallas kernels, place_pieces(): pl.pallas_call(kernel, out_shape=jax.ShapeDtypeStruct(shape, BF16), in_sp...  1.37 us
  transfers between devices with their start and end apart: 18, of which 11 were waited for; matrix products, arithmetic and copies ran while one was open for 0% of the time, Pallas kernels for 13%

profile of v9, /device:TPU:0, one launch (start us, length us, event | category | flops | bytes accessed | tf_op | source)
XLA Modules:
  0.0 59.4 jit_solution(15359854491426983107)
XLA Ops:
  0.6 5.4 %rate_partial.1 = (bf16[64,512]{1,0:T(8,128)(2,1)S(1)}, bf16[64,512]{1,0:T(8,128)(2,1)S(1)}, bf16[64,512]{1,0:T(8,128)(2,1)S(1)}, bf16[64,512]{1,0:T(8,128)(2,1)...) custom-call(s32[1]{0:T(128)} %bitcast.here_ref, ...), custom_call_target="tpu_custom_call" | custom-call | flops 1073741824 | bytes 6291456 | tf_op jit(solution)/shard_map/rate_partial/pallas_call | solution.py:98
  6.1 0.5 collective-permute-start.7
  6.6 2.6 %collective-permute-start.10 = (bf16[128,2048]{1,0:T(8,128)(2,1)S(1)}, bf16[128,2048]{1,0:T(8,128)(2,1)S(1)}, u32[]{:S(2)}, u32[]{:S(2)}) collective-permute-start(bf16[128,2048]{1,0:T(8,128)(2,1)S(1)} %get-tuple-element.20), channel_id=1, source_target_pairs={{0,1},{1,0},{2,3},{3,2},{4,5},{5,4},{6,7},{7,6},{8,9},{9,8},{10,11... | collective-permute-start | bytes 1572872 | tf_op jit(solution)/shard_map/ppermute | solution.py:374
  9.2 2.6 %collective-permute-start = (bf16[64,512]{1,0:T(8,128)(2,1)S(1)}, bf16[64,512]{1,0:T(8,128)(2,1)S(1)}, u32[]{:S(2)}, u32[]{:S(2)}) collective-permute-start(bf16[64,512]{1,0:T(8,128)(2,1)S(1)} %get-tuple-element.14), channel_id=1, source_target_pairs={{0,4},{2,6},{4,0},{6,2},{1,5},{3,7},{5,1},{7,3},{8,12},{10,14},{12... | collective-permute-start | bytes 196616 | tf_op jit(solution)/shard_map/ppermute | solution.py:378
  11.8 1.3 %collective-permute-start.1 = (bf16[64,512]{1,0:T(8,128)(2,1)S(1)}, bf16[64,512]{1,0:T(8,128)(2,1)S(1)}, u32[]{:S(2)}, u32[]{:S(2)}) collective-permute-start(bf16[64,512]{1,0:T(8,128)(2,1)S(1)} %get-tuple-element.15), channel_id=1, source_target_pairs={{0,6},{2,4},{4,2},{6,0},{1,7},{3,5},{5,3},{7,1},{8,14},{10,12},{12... | collective-permute-start | bytes 196616 | tf_op jit(solution)/shard_map/ppermute | solution.py:378
  13.1 0.2 collective-permute-start.2
  13.3 0.8 %chunk_counts.1.refs_4_ = f32[64,512]{1,0:T(8,128)S(1)} custom-call(s32[1]{0:T(128)} %bitcast.here_ref, s32[16]{0:T(128)} %doc_at.1, s32[16]{0:T(128)} %word_at.1, s32[16,64,128]{2,1,0:T(8,128)S(1)} %copy-done), custom_call_target="tpu_custom_call" | custom-call | flops 131072 | bytes 524288 | tf_op jit(solution)/shard_map/chunk_counts/pallas_call | solution.py:137
  14.2 2.0 %collective-permute-done.refs_1_ = bf16[64,512]{1,0:T(8,128)(2,1)S(1)} collective-permute-done((bf16[64,512]{1,0:T(8,128)(2,1)S(1)}, bf16[64,512]{1,0:T(8,128)(2,1)S(1)}, u32[]{:S(2)}, u32[]{:S(2)}) %collective-permute-start) | collective-permute-done | bytes 65568 | tf_op jit(solution)/shard_map/ppermute | solution.py:378
  16.2 2.0 %collective-permute-done.1.refs_2_ = bf16[64,512]{1,0:T(8,128)(2,1)S(1)} collective-permute-done((bf16[64,512]{1,0:T(8,128)(2,1)S(1)}, bf16[64,512]{1,0:T(8,128)(2,1)S(1)}, u32[]{:S(2)}, u32[]{:S(2)}) %collective-permute-start.1) | collective-permute-done | bytes 65568 | tf_op jit(solution)/shard_map/ppermute | solution.py:378
  18.2 0.3 collective-permute-done.2.refs_3_
  18.6 0.7 %collective-permute-start.5 = (bf16[64,512]{1,0:T(8,128)(2,1)S(1)}, bf16[64,512]{1,0:T(8,128)(2,1)S(1)}, u32[]{:S(2)}, u32[]{:S(2)}) collective-permute-start(bf16[64,512]{1,0:T(8,128)(2,1)S(1)} %ratio_chunk.1.ratio_ref.refs_0_), channel_id=1, source_target_pairs={{0,2},{2,0},{4,6},{6,4},{1,3},{3,1},{5,7},{7,5},{8,10},{10,8},{12,... | collective-permute-start | bytes 196616 | tf_op jit(solution)/shard_map/ppermute | solution.py:378
  19.3 3.4 %collective-permute-start.4 = (bf16[64,512]{1,0:T(8,128)(2,1)S(1)}, bf16[64,512]{1,0:T(8,128)(2,1)S(1)}, u32[]{:S(2)}, u32[]{:S(2)}) collective-permute-start(bf16[64,512]{1,0:T(8,128)(2,1)S(1)} %ratio_chunk.1.ratio_ref.refs_0_), channel_id=1, source_target_pairs={{0,6},{2,4},{4,2},{6,0},{1,7},{3,5},{5,3},{7,1},{8,14},{10,12},{12... | collective-permute-start | bytes 196616 | tf_op jit(solution)/shard_map/ppermute | solution.py:378
  22.9 3.9 %collective-permute-done.4.refs_2_.refs_1_ = bf16[64,512]{1,0:T(8,128)(2,1)S(1)} collective-permute-done((bf16[64,512]{1,0:T(8,128)(2,1)S(1)}, bf16[64,512]{1,0:T(8,128)(2,1)S(1)}, u32[]{:S(2)}, u32[]{:S(2)}) %collective-permute-start.4) | collective-permute-done | bytes 65568 | tf_op jit(solution)/shard_map/ppermute | solution.py:378
  26.8 2.1 %collective-permute-done.3.refs_1_.refs_0_ = bf16[64,512]{1,0:T(8,128)(2,1)S(1)} collective-permute-done((bf16[64,512]{1,0:T(8,128)(2,1)S(1)}, bf16[64,512]{1,0:T(8,128)(2,1)S(1)}, u32[]{:S(2)}, u32[]{:S(2)}) %collective-permute-start.3) | collective-permute-done | bytes 65568 | tf_op jit(solution)/shard_map/ppermute | solution.py:378
  29.0 0.5 collective-permute-start.6
  29.5 0.5 own_product.2.product_ref
  30.0 0.6 own_product.3.product_ref
  30.6 0.5 beta_piece.3.own_ref
  31.1 1.6 %collective-permute-start.8 = (bf16[64,2048]{1,0:T(8,128)(2,1)S(1)}, bf16[64,2048]{1,0:T(8,128)(2,1)S(1)}, u32[]{:S(2)}, u32[]{:S(2)}) collective-permute-start(bf16[64,2048]{1,0:T(8,128)(2,1)S(1)} %beta_piece.3.own_ref), channel_id=1, source_target_pairs={{0,16},{8,24},{16,0},{24,8},{1,17},{9,25},{17,1},{25,9},{2,18},{10... | collective-permute-start | bytes 786440 | tf_op jit(solution)/shard_map/ppermute | solution.py:378
  32.6 0.5 beta_piece.4.rest_0_.own_ref
  33.3 0.6 %collective-permute-start.13 = (bf16[128,2048]{1,0:T(8,128)(2,1)S(1)}, bf16[128,2048]{1,0:T(8,128)(2,1)S(1)}, u32[]{:S(2)}, u32[]{:S(2)}) collective-permute-start(bf16[128,2048]{1,0:T(8,128)(2,1)S(1)} %beta_piece.4.rest_0_.own_ref), channel_id=1, source_target_pairs={{0,16},{8,24},{16,0},{24,8},{1,17},{9,25},{17,1},{25,9},{2,18},{10... | collective-permute-start | bytes 1572872 | tf_op jit(solution)/shard_map/ppermute | solution.py:378
  33.9 6.4 %collective-permute-done.8.other_ref = bf16[64,2048]{1,0:T(8,128)(2,1)S(1)} collective-permute-done((bf16[64,2048]{1,0:T(8,128)(2,1)S(1)}, bf16[64,2048]{1,0:T(8,128)(2,1)S(1)}, u32[]{:S(2)}, u32[]{:S(2)}) %collective-permute-start.8) | collective-permute-done | bytes 262176 | tf_op jit(solution)/shard_map/ppermute | solution.py:378
  40.4 0.6 collective-permute-start.9
  41.0 0.5 beta_piece.5.own_ref
  41.5 1.6 %collective-permute-start.14 = (bf16[64,2048]{1,0:T(8,128)(2,1)S(1)}, bf16[64,2048]{1,0:T(8,128)(2,1)S(1)}, u32[]{:S(2)}, u32[]{:S(2)}) collective-permute-start(bf16[64,2048]{1,0:T(8,128)(2,1)S(1)} %beta_piece.5.own_ref), channel_id=1, source_target_pairs={{0,16},{8,24},{16,0},{24,8},{1,17},{9,25},{17,1},{25,9},{2,18},{10... | collective-permute-start | bytes 786440 | tf_op jit(solution)/shard_map/ppermute | solution.py:378
  43.0 4.2 %collective-permute-done.9.refs_0_ = bf16[256,512]{1,0:T(8,128)(2,1)S(1)} collective-permute-done((bf16[256,512]{1,0:T(8,128)(2,1)S(1)}, bf16[256,512]{1,0:T(8,128)(2,1)S(1)}, u32[]{:S(2)}, u32[]{:S(2)}) %collective-permute-start.9) | collective-permute-done | bytes 262176 | tf_op jit(solution)/shard_map/ppermute | solution.py:374
  47.2 3.7 %theta_grad.1 = (f32[512,2048]{1,0:T(8,128)}, f32[8,128]{1,0:T(8,128)S(1)}) custom-call(s32[1]{0:T(128)} %bitcast.here_ref, bf16[256,512]{1,0:T(8,128)(2,1)S(1)} %join_ratio.1.ratio_ref, bf16[256,512]{1,0:T(8,128)(2,1)S(1)} %collective-permute-done.9.refs_0_, bf16[256,4096]{1,0:T(8,128)(2,1)S(1)} %get-tuple-element.19.prob_ref.refs_1_, ...), custom_call_target="tpu_custom_call" | custom-call | flops 1 | bytes 1 | tf_op jit(solution)/shard_map/theta_grad/pallas_call | solution.py:316
  50.9 0.6 collective-permute-done.13.other_ref
  51.7 0.5 collective-permute-start.15
  52.2 4.1 %collective-permute-done.14.other_ref = bf16[64,2048]{1,0:T(8,128)(2,1)S(1)} collective-permute-done((bf16[64,2048]{1,0:T(8,128)(2,1)S(1)}, bf16[64,2048]{1,0:T(8,128)(2,1)S(1)}, u32[]{:S(2)}, u32[]{:S(2)}) %collective-permute-start.14) | collective-permute-done | bytes 262176 | tf_op jit(solution)/shard_map/ppermute | solution.py:378
  56.5 1.5 %collective-permute-done.17.refs_5_ = bf16[64,2048]{1,0:T(8,128)(2,1)S(1)} collective-permute-done((bf16[64,2048]{1,0:T(8,128)(2,1)S(1)}, bf16[64,2048]{1,0:T(8,128)(2,1)S(1)}, u32[]{:S(2)}, u32[]{:S(2)}) %collective-permute-start.17) | collective-permute-done | bytes 262176 | tf_op jit(solution)/shard_map/ppermute | solution.py:378
  58.0 1.4 %place_pieces.1 = bf16[256,4096]{1,0:T(8,128)(2,1)} custom-call(s32[1]{0:T(128)} %bitcast.here_ref, bf16[64,2048]{1,0:T(8,128)(2,1)S(1)} %add_pair.3.refs_4_.refs_0_, bf16[128,2048]{1,0:T(8,128)(2,1)S(1)} %add_pair.4.refs_1_, bf16[64,2048]{1,0:T(8,128)(2,1)S(1)} %add_pair.5.refs_2_, bf16[64,2048]{1,0:T(8,128)(2,1)S(1)} %collective-permute-done.15.refs_3_, ...), custom_call_target="tpu_custom_call" | custom-call | bytes 4194304 | tf_op jit(solution)/shard_map/place_pieces/pallas_call | solution.py:355
  (22 shorter events, 0.9 us)
Async XLA Ops:
  0.6 12.7 %copy-start = (s32[16,64,128]{2,1,0:T(8,128)S(1)}, s32[16,64,128]{2,1,0:T(8,128)}, u32[]{:S(2)}) copy-start(s32[16,64,128]{2,1,0:T(8,128)} %count_ref.1) | copy-start | bytes 1572868
  6.1 24.5 %collective-permute-start.7 = (bf16[512,2048]{1,0:T(8,128)(2,1)S(1)}, bf16[512,2048]{1,0:T(8,128)(2,1)S(1)}, u32[]{:S(2)}, u32[]{:S(2)}) collective-permute-start(bf16[512,2048]{1,0:T(8,128)(2,1)S(1)} %get-tuple-element.18), channel_id=1, source_target_pairs={{0,8},{8,0},{16,24},{24,16},{1,9},{9,1},{17,25},{25,17},{2,10},{10... | collective-permute-start | bytes 6291464 | tf_op jit(solution)/shard_map/ppermute | solution.py:378
  6.6 22.3 %collective-permute-start.10 = (bf16[128,2048]{1,0:T(8,128)(2,1)S(1)}, bf16[128,2048]{1,0:T(8,128)(2,1)S(1)}, u32[]{:S(2)}, u32[]{:S(2)}) collective-permute-start(bf16[128,2048]{1,0:T(8,128)(2,1)S(1)} %get-tuple-element.20), channel_id=1, source_target_pairs={{0,1},{1,0},{2,3},{3,2},{4,5},{5,4},{6,7},{7,6},{8,9},{9,8},{10,11... | collective-permute-start | bytes 1572872 | tf_op jit(solution)/shard_map/ppermute | solution.py:374
  9.2 7.0 %collective-permute-start = (bf16[64,512]{1,0:T(8,128)(2,1)S(1)}, bf16[64,512]{1,0:T(8,128)(2,1)S(1)}, u32[]{:S(2)}, u32[]{:S(2)}) collective-permute-start(bf16[64,512]{1,0:T(8,128)(2,1)S(1)} %get-tuple-element.14), channel_id=1, source_target_pairs={{0,4},{2,6},{4,0},{6,2},{1,5},{3,7},{5,1},{7,3},{8,12},{10,14},{12... | collective-permute-start | bytes 196616 | tf_op jit(solution)/shard_map/ppermute | solution.py:378
  11.8 6.4 %collective-permute-start.1 = (bf16[64,512]{1,0:T(8,128)(2,1)S(1)}, bf16[64,512]{1,0:T(8,128)(2,1)S(1)}, u32[]{:S(2)}, u32[]{:S(2)}) collective-permute-start(bf16[64,512]{1,0:T(8,128)(2,1)S(1)} %get-tuple-element.15), channel_id=1, source_target_pairs={{0,6},{2,4},{4,2},{6,0},{1,7},{3,5},{5,3},{7,1},{8,14},{10,12},{12... | collective-permute-start | bytes 196616 | tf_op jit(solution)/shard_map/ppermute | solution.py:378
  13.1 5.4 %collective-permute-start.2 = (bf16[64,512]{1,0:T(8,128)(2,1)S(1)}, bf16[64,512]{1,0:T(8,128)(2,1)S(1)}, u32[]{:S(2)}, u32[]{:S(2)}) collective-permute-start(bf16[64,512]{1,0:T(8,128)(2,1)S(1)} %get-tuple-element.16), channel_id=1, source_target_pairs={{0,2},{2,0},{4,6},{6,4},{1,3},{3,1},{5,7},{7,5},{8,10},{10,8},{12,... | collective-permute-start | bytes 196616 | tf_op jit(solution)/shard_map/ppermute | solution.py:378
  18.6 4.3 %collective-permute-start.5 = (bf16[64,512]{1,0:T(8,128)(2,1)S(1)}, bf16[64,512]{1,0:T(8,128)(2,1)S(1)}, u32[]{:S(2)}, u32[]{:S(2)}) collective-permute-start(bf16[64,512]{1,0:T(8,128)(2,1)S(1)} %ratio_chunk.1.ratio_ref.refs_0_), channel_id=1, source_target_pairs={{0,2},{2,0},{4,6},{6,4},{1,3},{3,1},{5,7},{7,5},{8,10},{10,8},{12,... | collective-permute-start | bytes 196616 | tf_op jit(solution)/shard_map/ppermute | solution.py:378
  19.3 7.5 %collective-permute-start.4 = (bf16[64,512]{1,0:T(8,128)(2,1)S(1)}, bf16[64,512]{1,0:T(8,128)(2,1)S(1)}, u32[]{:S(2)}, u32[]{:S(2)}) collective-permute-start(bf16[64,512]{1,0:T(8,128)(2,1)S(1)} %ratio_chunk.1.ratio_ref.refs_0_), channel_id=1, source_target_pairs={{0,6},{2,4},{4,2},{6,0},{1,7},{3,5},{5,3},{7,1},{8,14},{10,12},{12... | collective-permute-start | bytes 196616 | tf_op jit(solution)/shard_map/ppermute | solution.py:378
  22.7 6.2 %collective-permute-start.3 = (bf16[64,512]{1,0:T(8,128)(2,1)S(1)}, bf16[64,512]{1,0:T(8,128)(2,1)S(1)}, u32[]{:S(2)}, u32[]{:S(2)}) collective-permute-start(bf16[64,512]{1,0:T(8,128)(2,1)S(1)} %ratio_chunk.1.ratio_ref.refs_0_), channel_id=1, source_target_pairs={{0,4},{2,6},{4,0},{6,2},{1,5},{3,7},{5,1},{7,3},{8,12},{10,14},{12... | collective-permute-start | bytes 196616 | tf_op jit(solution)/shard_map/ppermute | solution.py:378
  28.9 3.7 %collective-permute-start.11 = (bf16[192,512]{1,0:T(8,128)(2,1)S(1)}, bf16[192,512]{1,0:T(8,128)(2,1)S(1)}, u32[]{:S(2)}, u32[]{:S(2)}) collective-permute-start(bf16[192,512]{1,0:T(8,128)(2,1)S(1)} %stack_rows.1.ratio_ref), channel_id=1, source_target_pairs={{0,8},{8,0},{16,24},{24,16},{1,9},{9,1},{17,25},{25,17},{2,10},{10... | collective-permute-start | bytes 589832 | tf_op jit(solution)/shard_map/ppermute | solution.py:378
  29.0 1.6 %collective-permute-start.6 = (bf16[64,512]{1,0:T(8,128)(2,1)S(1)}, bf16[64,512]{1,0:T(8,128)(2,1)S(1)}, u32[]{:S(2)}, u32[]{:S(2)}) collective-permute-start(bf16[64,512]{1,0:T(8,128)(2,1)S(1)} %ratio_chunk.1.ratio_ref.refs_0_), channel_id=1, source_target_pairs={{0,8},{8,0},{16,24},{24,16},{1,9},{9,1},{17,25},{25,17},{2,10},{10... | collective-permute-start | bytes 196616 | tf_op jit(solution)/shard_map/ppermute | solution.py:378
  31.1 9.2 %collective-permute-start.8 = (bf16[64,2048]{1,0:T(8,128)(2,1)S(1)}, bf16[64,2048]{1,0:T(8,128)(2,1)S(1)}, u32[]{:S(2)}, u32[]{:S(2)}) collective-permute-start(bf16[64,2048]{1,0:T(8,128)(2,1)S(1)} %beta_piece.3.own_ref), channel_id=1, source_target_pairs={{0,16},{8,24},{16,0},{24,8},{1,17},{9,25},{17,1},{25,9},{2,18},{10... | collective-permute-start | bytes 786440 | tf_op jit(solution)/shard_map/ppermute | solution.py:378
  33.2 14.0 %collective-permute-start.12 = (bf16[128,2048]{1,0:T(8,128)(2,1)S(1)}, bf16[128,2048]{1,0:T(8,128)(2,1)S(1)}, u32[]{:S(2)}, u32[]{:S(2)}) collective-permute-start(bf16[128,2048]{1,0:T(8,128)(2,1)S(1)} %hold.1.refs_2_), channel_id=1, source_target_pairs={{0,8},{8,0},{16,24},{24,16},{1,9},{9,1},{17,25},{25,17},{2,10},{10... | collective-permute-start | bytes 1572872 | tf_op jit(solution)/shard_map/ppermute | solution.py:378
  33.3 18.3 %collective-permute-start.13 = (bf16[128,2048]{1,0:T(8,128)(2,1)S(1)}, bf16[128,2048]{1,0:T(8,128)(2,1)S(1)}, u32[]{:S(2)}, u32[]{:S(2)}) collective-permute-start(bf16[128,2048]{1,0:T(8,128)(2,1)S(1)} %beta_piece.4.rest_0_.own_ref), channel_id=1, source_target_pairs={{0,16},{8,24},{16,0},{24,8},{1,17},{9,25},{17,1},{25,9},{2,18},{10... | collective-permute-start | bytes 1572872 | tf_op jit(solution)/shard_map/ppermute | solution.py:378
  40.4 6.8 %collective-permute-start.9 = (bf16[256,512]{1,0:T(8,128)(2,1)S(1)}, bf16[256,512]{1,0:T(8,128)(2,1)S(1)}, u32[]{:S(2)}, u32[]{:S(2)}) collective-permute-start(bf16[256,512]{1,0:T(8,128)(2,1)S(1)} %join_ratio.1.ratio_ref), channel_id=1, source_target_pairs={{0,1},{1,0},{2,3},{3,2},{4,5},{5,4},{6,7},{7,6},{8,9},{9,8},{10,11... | collective-permute-start | bytes 786440 | tf_op jit(solution)/shard_map/ppermute | solution.py:374
  41.5 14.9 %collective-permute-start.14 = (bf16[64,2048]{1,0:T(8,128)(2,1)S(1)}, bf16[64,2048]{1,0:T(8,128)(2,1)S(1)}, u32[]{:S(2)}, u32[]{:S(2)}) collective-permute-start(bf16[64,2048]{1,0:T(8,128)(2,1)S(1)} %beta_piece.5.own_ref), channel_id=1, source_target_pairs={{0,16},{8,24},{16,0},{24,8},{1,17},{9,25},{17,1},{25,9},{2,18},{10... | collective-permute-start | bytes 786440 | tf_op jit(solution)/shard_map/ppermute | solution.py:378
  51.6 6.4 %collective-permute-start.16 = (bf16[128,2048]{1,0:T(8,128)(2,1)S(1)}, bf16[128,2048]{1,0:T(8,128)(2,1)S(1)}, u32[]{:S(2)}, u32[]{:S(2)}) collective-permute-start(bf16[128,2048]{1,0:T(8,128)(2,1)S(1)} %add_pair.4.refs_1_), channel_id=1, source_target_pairs={{0,8},{8,0},{16,24},{24,16},{1,9},{9,1},{17,25},{25,17},{2,10},{10... | collective-permute-start | bytes 1572872 | tf_op jit(solution)/shard_map/ppermute | solution.py:378
  51.7 4.8 %collective-permute-start.15 = (bf16[64,2048]{1,0:T(8,128)(2,1)S(1)}, bf16[64,2048]{1,0:T(8,128)(2,1)S(1)}, u32[]{:S(2)}, u32[]{:S(2)}) collective-permute-start(bf16[64,2048]{1,0:T(8,128)(2,1)S(1)} %add_pair.3.refs_4_.refs_0_), channel_id=1, source_target_pairs={{0,8},{8,0},{16,24},{24,16},{1,9},{9,1},{17,25},{25,17},{2,10},{10... | collective-permute-start | bytes 786440 | tf_op jit(solution)/shard_map/ppermute | solution.py:378
  56.4 1.6 %collective-permute-start.17 = (bf16[64,2048]{1,0:T(8,128)(2,1)S(1)}, bf16[64,2048]{1,0:T(8,128)(2,1)S(1)}, u32[]{:S(2)}, u32[]{:S(2)}) collective-permute-start(bf16[64,2048]{1,0:T(8,128)(2,1)S(1)} %add_pair.5.refs_2_), channel_id=1, source_target_pairs={{0,8},{8,0},{16,24},{24,16},{1,9},{9,1},{17,25},{25,17},{2,10},{10... | collective-permute-start | bytes 786440 | tf_op jit(solution)/shard_map/ppermute | solution.py:378

commit v10 on v8

--- a/solution.py
+++ b/solution.py
@@ -204,19 +204,24 @@
 def beta_pieces(sizes, here, product, ratio, docs_held, prob_held, flips, after):
     words, side_width = product.shape
     docs = docs_held.shape[0]
-    rows = words // len(flips)
+    rows = words // sum(map(len, flips))
 
     def kernel(here_ref, product_ref, ratio_ref, doc_ref, prob_ref, *rest):
         columns = window(sizes.side(here_ref), side_width)
         topic_at = sizes.topic_at(here_ref)
         summed = product_ref[...] + jnp.dot(ratio_ref[...], doc_ref[...], preferred_element_type=F32)
-        for i, (flip, out_ref) in enumerate(zip(flips, rest[len(after) :])):
-            prob = prob_ref[window(topic_at ^ flip, rows), columns].astype(F32)
-            out_ref[...] = (-prob * summed[i * rows : (i + 1) * rows, :]).astype(BF16)
-
-    return pl.pallas_call(
-        kernel,
-        out_shape=[jax.ShapeDtypeStruct((rows, side_width), BF16)] * len(flips),
+        chunk = 0
+        for piece, out_ref in zip(flips, rest[len(after) :]):
+            for i, flip in enumerate(piece):
+                prob = prob_ref[window(topic_at ^ flip, rows), columns].astype(F32)
+                out_ref[i * rows : (i + 1) * rows, :] = (
+                    -prob * summed[chunk * rows : (chunk + 1) * rows, :]
+                ).astype(BF16)
+                chunk += 1
+
+    return pl.pallas_call(
+        kernel,
+        out_shape=[jax.ShapeDtypeStruct((rows * len(piece), side_width), BF16) for piece in flips],
         in_specs=[SMEM] + [VMEM] * 4 + [ANY] * len(after),
         out_specs=[VMEM] * len(flips),
         compiler_params=call_params(),
@@ -323,9 +328,7 @@
             scratch_shapes=[pltpu.VMEM((docs, count * words), BF16)],
         ),
         compiler_params=call_params(),
-        cost_estimate=cost(
-            20 * count * words * docs * share, (40 * docs + 20 * count * words) * share, 10 * count * words * share
-        ),
+        cost_estimate=cost(1, 1),
         name="theta_grad",
     )(here, ratio, *far_ratios, prob_held, *far_logits, log_norm)
 
@@ -338,10 +341,13 @@
         own_refs, other_refs, (out_ref, sems) = refs[:pieces], refs[pieces : 2 * pieces], refs[-2:]
         side, topic_at = sizes.side(here_ref), sizes.topic_at(here_ref)
         copies = []
-        for p, flip in enumerate(flips):
+        for p in range(pieces):
+            rows = own_refs[p].shape[0] // len(flips[p])
             for h, (ref, which) in enumerate(((own_refs[p], side), (other_refs[p], 1 - side))):
-                target = out_ref.at[window(topic_at ^ flip, ref.shape[0]), window(which, side_width)]
-                copies.append(pltpu.make_async_copy(ref, target, sems.at[h, p]))
+                for i, flip in enumerate(flips[p]):
+                    part = ref.at[pl.ds(i * rows, rows), :]
+                    target = out_ref.at[window(topic_at ^ flip, rows), window(which, side_width)]
+                    copies.append(pltpu.make_async_copy(part, target, sems.at[len(copies)]))
         for copy in copies:
             copy.start()
         for copy in copies:
@@ -352,7 +358,7 @@
         out_shape=jax.ShapeDtypeStruct(shape, BF16),
         in_specs=[SMEM] + [VMEM] * (2 * pieces),
         out_specs=HBM,
-        scratch_shapes=[pltpu.SemaphoreType.DMA((2, pieces))],
+        scratch_shapes=[pltpu.SemaphoreType.DMA((2 * sum(map(len, flips)),))],
         compiler_params=call_params(),
         cost_estimate=cost(0, 4 * shape[0] * shape[1]),
         name="place_pieces",
@@ -375,13 +381,13 @@
     parts, near_logits, docs_held, docs_sent, prob_held, norm_held = rate_partial(
         sizes, here, doc_topics, word_logits, log_norm[None, :]
     )
-    near_logits = [shift(part, s) for s, part in enumerate(near_logits, 1)]
     sibling_docs = swap(docs_sent, "doc", 1)
     order = sorted(range(1, sizes.topic), key=lambda s: s < sizes.topic // 2)
     arrived = [swap(parts[s], "topic", s) for s in order]
     counts = chunk_counts(sizes, here, word_counts, tile_doc, tile_word, docs, words)
     own_ratio = ratio_chunk([parts[0]] + arrived, counts, word_tile)
     gathered = [swap(own_ratio, "topic", s) for s in order]
+    near_logits = [shift(hold(part, gathered[:1]), s) for s, part in enumerate(near_logits, 1)]
     far_bits = [1 << b for b in range(1, sizes.doc.bit_length() - 1)]
 
     def beta(ratio, flips, after):
@@ -392,19 +398,20 @@
             pieces = [add_pair(part, swap(part, "doc", bit)) for part in pieces]
         return [(part, swap(part, "doc", far_bits[-1])) for part in pieces]
 
-    own_pair = beta(own_ratio, [0], [])
-    pairs = own_pair + beta(stack_rows(gathered, near_logits), order, [own_pair[0][1]])
+    flips = [[0], order]
+    pairs = beta(own_ratio, flips[:1], [])
+    pairs += beta(stack_rows(gathered, []), flips[1:], [pairs[0][1]])
+
     ratio = join_ratio(sizes, here, [own_ratio] + gathered, [0] + order, [pairs[1][0]])
     far_ratios = [shift(ratio, s) for s in range(1, sizes.vocab)]
-
     far_logits = []
     for part in near_logits:
-        part = hold(part, [pairs[-1][0]])
+        part = hold(part, [pairs[1][0]])
         far_logits += [part, swap(part, "doc", 1)]
     theta, theta_done = theta_grad(sizes, here, ratio, far_ratios, prob_held, far_logits, norm_held)
 
     sums = [add_pair(*pair, [theta_done] if p else []) for p, pair in enumerate(pairs)]
-    out = place_pieces(sizes, here, sums, [swap(part, "doc", 1) for part in sums], [0] + order, word_logits.shape)
+    out = place_pieces(sizes, here, sums, [swap(part, "doc", 1) for part in sums], flips, word_logits.shape)
     return theta, out
 
 

time: 55.7 us -> 54.3 us (0.975)
  starting transfers between devices: 18.2 us -> 17.3 us
    ppermute x18 -> x14, waiting for transfers between devices: 18.6 us -> 10.5 us  [swap(): return lax.ppermute(array, axis, [(i, i ^ bits) for i in range(count)])]
    ppermute x2, waiting for transfers between devices: 4.61 us -> 12.2 us  [shift(): lax.ppermute(array, 'vocab', [(i, (i + by) % sizes.vocab) for i in range(...]
    ppermute x18 -> x14, starting transfers between devices: 15 us -> 14.2 us  [swap(): return lax.ppermute(array, axis, [(i, i ^ bits) for i in range(count)])]
  transfers between devices with their start and end apart: 20 -> 16, of which waited for: 12 -> 9; matrix products, arithmetic and copies ran while one was open for 0% -> 0% of each run, Pallas kernels for 12% -> 13%
where the time goes in v10:
time: 54.3 us; the launch traced here: 54.2 us
  waiting for transfers between devices  22.7 us (42%)
  starting transfers between devices  17.3 us (32%)
  Pallas kernels  13.3 us (24%)
  between operations  0.77 us (1%)
    ppermute x14, starting transfers between devices, swap(): return lax.ppermute(array, axis, [(i, i ^ bits) for i in range(count)])  14.2 us
    ppermute x2, waiting for transfers between devices, shift(): lax.ppermute(array, 'vocab', [(i, (i + by) % sizes.vocab) for i in range(...  12.2 us
    ppermute x14, waiting for transfers between devices, swap(): return lax.ppermute(array, axis, [(i, i ^ bits) for i in range(count)])  10.5 us
    pallas_call x1, Pallas kernels, rate_partial(): pl.pallas_call(kernel, out_shape=[jax.ShapeDtypeStruct((chunk, docs), BF1...  4.79 us
    pallas_call x1, Pallas kernels, theta_grad(): pl.pallas_call(kernel, out_shape=[jax.ShapeDtypeStruct((docs, share), F32...  3.71 us
    ppermute x2, starting transfers between devices, shift(): lax.ppermute(array, 'vocab', [(i, (i + by) % sizes.vocab) for i in range(...  3.09 us
    pallas_call x1, Pallas kernels, place_pieces(): pl.pallas_call(kernel, out_shape=jax.ShapeDtypeStruct(shape, BF16), in_sp...  1.37 us
    pallas_call x2, Pallas kernels, beta_pieces(): pl.pallas_call(kernel, out_shape=[jax.ShapeDtypeStruct((rows * len(piece)...  1.14 us
  transfers between devices with their start and end apart: 16, of which 9 were waited for; matrix products, arithmetic and copies ran while one was open for 0% of the time, Pallas kernels for 13%

profile of v10, /device:TPU:0, one launch (start us, length us, event | category | flops | bytes accessed | tf_op | source)
XLA Modules:
  0.0 54.2 jit_solution(6956981152309456690)
XLA Ops:
  0.6 4.8 %rate_partial.1 = (bf16[64,512]{1,0:T(8,128)(2,1)S(1)}, bf16[64,512]{1,0:T(8,128)(2,1)S(1)}, bf16[64,512]{1,0:T(8,128)(2,1)S(1)}, bf16[64,512]{1,0:T(8,128)(2,1)...) custom-call(s32[1]{0:T(128)} %bitcast.here_ref, ...), custom_call_target="tpu_custom_call" | custom-call | flops 1073741824 | bytes 6291456 | tf_op jit(solution)/shard_map/rate_partial/pallas_call | solution.py:97
  5.4 0.5 collective-permute-start.7
  6.0 3.7 %collective-permute-start = (bf16[64,512]{1,0:T(8,128)(2,1)S(1)}, bf16[64,512]{1,0:T(8,128)(2,1)S(1)}, u32[]{:S(2)}, u32[]{:S(2)}) collective-permute-start(bf16[64,512]{1,0:T(8,128)(2,1)S(1)} %get-tuple-element.14), channel_id=1, source_target_pairs={{0,4},{2,6},{4,0},{6,2},{1,5},{3,7},{5,1},{7,3},{8,12},{10,14},{12... | collective-permute-start | bytes 196616 | tf_op jit(solution)/shard_map/ppermute | solution.py:379
  9.6 1.3 %collective-permute-start.1 = (bf16[64,512]{1,0:T(8,128)(2,1)S(1)}, bf16[64,512]{1,0:T(8,128)(2,1)S(1)}, u32[]{:S(2)}, u32[]{:S(2)}) collective-permute-start(bf16[64,512]{1,0:T(8,128)(2,1)S(1)} %get-tuple-element.15), channel_id=1, source_target_pairs={{0,6},{2,4},{4,2},{6,0},{1,7},{3,5},{5,3},{7,1},{8,14},{10,12},{12... | collective-permute-start | bytes 196616 | tf_op jit(solution)/shard_map/ppermute | solution.py:379
  11.0 0.2 collective-permute-start.2
  11.2 0.8 %chunk_counts.1.refs_4_ = f32[64,512]{1,0:T(8,128)S(1)} custom-call(s32[1]{0:T(128)} %bitcast.here_ref, s32[16]{0:T(128)} %doc_at.1, s32[16]{0:T(128)} %word_at.1, s32[16,64,128]{2,1,0:T(8,128)S(1)} %copy-done), custom_call_target="tpu_custom_call" | custom-call | flops 131072 | bytes 524288 | tf_op jit(solution)/shard_map/chunk_counts/pallas_call | solution.py:136
  12.0 1.8 %collective-permute-done.refs_1_ = bf16[64,512]{1,0:T(8,128)(2,1)S(1)} collective-permute-done((bf16[64,512]{1,0:T(8,128)(2,1)S(1)}, bf16[64,512]{1,0:T(8,128)(2,1)S(1)}, u32[]{:S(2)}, u32[]{:S(2)}) %collective-permute-start) | collective-permute-done | bytes 65568 | tf_op jit(solution)/shard_map/ppermute | solution.py:379
  13.9 2.4 %collective-permute-done.1.refs_2_ = bf16[64,512]{1,0:T(8,128)(2,1)S(1)} collective-permute-done((bf16[64,512]{1,0:T(8,128)(2,1)S(1)}, bf16[64,512]{1,0:T(8,128)(2,1)S(1)}, u32[]{:S(2)}, u32[]{:S(2)}) %collective-permute-start.1) | collective-permute-done | bytes 65568 | tf_op jit(solution)/shard_map/ppermute | solution.py:379
  16.3 0.2 collective-permute-done.2.refs_3_
  16.6 2.8 %collective-permute-start.3 = (bf16[64,512]{1,0:T(8,128)(2,1)S(1)}, bf16[64,512]{1,0:T(8,128)(2,1)S(1)}, u32[]{:S(2)}, u32[]{:S(2)}) collective-permute-start(bf16[64,512]{1,0:T(8,128)(2,1)S(1)} %ratio_chunk.1.ratio_ref.refs_0_), channel_id=1, source_target_pairs={{0,4},{2,6},{4,0},{6,2},{1,5},{3,7},{5,1},{7,3},{8,12},{10,14},{12... | collective-permute-start | bytes 196616 | tf_op jit(solution)/shard_map/ppermute | solution.py:379
  19.4 1.2 %collective-permute-start.5 = (bf16[64,512]{1,0:T(8,128)(2,1)S(1)}, bf16[64,512]{1,0:T(8,128)(2,1)S(1)}, u32[]{:S(2)}, u32[]{:S(2)}) collective-permute-start(bf16[64,512]{1,0:T(8,128)(2,1)S(1)} %ratio_chunk.1.ratio_ref.refs_0_), channel_id=1, source_target_pairs={{0,2},{2,0},{4,6},{6,4},{1,3},{3,1},{5,7},{7,5},{8,10},{10,8},{12,... | collective-permute-start | bytes 196616 | tf_op jit(solution)/shard_map/ppermute | solution.py:379
  20.6 0.4 collective-permute-start.4
  21.1 0.5 own_product.3.product_ref
  21.6 0.5 beta_pieces.2.own_ref
  22.1 1.6 %collective-permute-start.9 = (bf16[64,2048]{1,0:T(8,128)(2,1)S(1)}, bf16[64,2048]{1,0:T(8,128)(2,1)S(1)}, u32[]{:S(2)}, u32[]{:S(2)}) collective-permute-start(bf16[64,2048]{1,0:T(8,128)(2,1)S(1)} %beta_pieces.2.own_ref), channel_id=1, source_target_pairs={{0,16},{8,24},{16,0},{24,8},{1,17},{9,25},{17,1},{25,9},{2,18},{10... | collective-permute-start | bytes 786440 | tf_op jit(solution)/shard_map/ppermute | solution.py:379
  23.7 1.6 %collective-permute-start.11 = (bf16[128,2048]{1,0:T(8,128)(2,1)S(1)}, bf16[128,2048]{1,0:T(8,128)(2,1)S(1)}, u32[]{:S(2)}, u32[]{:S(2)}) collective-permute-start(bf16[128,2048]{1,0:T(8,128)(2,1)S(1)} %hold.2), channel_id=1, source_target_pairs={{0,1},{1,0},{2,3},{3,2},{4,5},{5,4},{6,7},{7,6},{8,9},{9,8},{10,11... | collective-permute-start | bytes 1572872 | tf_op jit(solution)/shard_map/ppermute | solution.py:375
  25.3 1.4 %collective-permute-done.4.refs_1_.refs_2_ = bf16[64,512]{1,0:T(8,128)(2,1)S(1)} collective-permute-done((bf16[64,512]{1,0:T(8,128)(2,1)S(1)}, bf16[64,512]{1,0:T(8,128)(2,1)S(1)}, u32[]{:S(2)}, u32[]{:S(2)}) %collective-permute-start.4) | collective-permute-done | bytes 65568 | tf_op jit(solution)/shard_map/ppermute | solution.py:379
  26.7 0.1 collective-permute-start.6
  26.8 0.6 %own_product.2.product_ref = f32[192,2048]{1,0:T(8,128)S(1)} custom-call(bf16[192,512]{1,0:T(8,128)(2,1)S(1)} %stack_rows.1.ratio_ref, bf16[512,2048]{1,0:T(8,128)(2,1)S(1)} %get-tuple-element.17.doc_ref), custom_call_target="tpu_custom_call" | custom-call | flops 402653184 | bytes 3670016 | tf_op jit(solution)/shard_map/own_product/pallas_call | solution.py:193
  27.4 0.8 %collective-permute-done.6.ratio_ref = bf16[192,512]{1,0:T(8,128)(2,1)S(1)} collective-permute-done((bf16[192,512]{1,0:T(8,128)(2,1)S(1)}, bf16[192,512]{1,0:T(8,128)(2,1)S(1)}, u32[]{:S(2)}, u32[]{:S(2)}) %collective-permute-start.6) | collective-permute-done | bytes 196640 | tf_op jit(solution)/shard_map/ppermute | solution.py:379
  28.2 1.8 %collective-permute-done.9.rest_0_.other_ref = bf16[64,2048]{1,0:T(8,128)(2,1)S(1)} collective-permute-done((bf16[64,2048]{1,0:T(8,128)(2,1)S(1)}, bf16[64,2048]{1,0:T(8,128)(2,1)S(1)}, u32[]{:S(2)}, u32[]{:S(2)}) %collective-permute-start.9) | collective-permute-done | bytes 262176 | tf_op jit(solution)/shard_map/ppermute | solution.py:379
  30.0 0.7 %beta_pieces.3.refs_4_.rest_0_.own_ref = bf16[192,2048]{1,0:T(8,128)(2,1)S(1)} custom-call(s32[1]{0:T(128)} %bitcast.here_ref, f32[192,2048]{1,0:T(8,128)S(1)} %own_product.2.product_ref, bf16[192,512]{1,0:T(8,128)(2,1)S(1)} %collective-permute-done.6.ratio_ref, bf16[512,2048]{1,0:T(8,128)(2,1)S(1)} %collective-permute-done.7.doc_ref, ...), custom_call_target="tpu_custom_call" | custom-call | flops 402653184 | bytes 5242880 | tf_op jit(solution)/shard_map/beta_pieces/pallas_call | solution.py:222
  30.7 1.6 %collective-permute-start.13 = (bf16[192,2048]{1,0:T(8,128)(2,1)S(1)}, bf16[192,2048]{1,0:T(8,128)(2,1)S(1)}, u32[]{:S(2)}, u32[]{:S(2)}) collective-permute-start(bf16[192,2048]{1,0:T(8,128)(2,1)S(1)} %beta_pieces.3.refs_4_.rest_0_.own_ref), channel_id=1, source_target_pairs={{0,16},{8,24},{16,0},{24,8},{1,17},{9,25},{17,1},{25,9},{2,18},{10... | collective-permute-start | bytes 2359304 | tf_op jit(solution)/shard_map/ppermute | solution.py:379
  32.3 4.9 %collective-permute-done.11.in_ref = bf16[128,2048]{1,0:T(8,128)(2,1)S(1)} collective-permute-done((bf16[128,2048]{1,0:T(8,128)(2,1)S(1)}, bf16[128,2048]{1,0:T(8,128)(2,1)S(1)}, u32[]{:S(2)}, u32[]{:S(2)}) %collective-permute-start.11) | collective-permute-done | bytes 524320 | tf_op jit(solution)/shard_map/ppermute | solution.py:375
  37.4 1.5 %collective-permute-start.10 = (bf16[256,512]{1,0:T(8,128)(2,1)S(1)}, bf16[256,512]{1,0:T(8,128)(2,1)S(1)}, u32[]{:S(2)}, u32[]{:S(2)}) collective-permute-start(bf16[256,512]{1,0:T(8,128)(2,1)S(1)} %join_ratio.1.ratio_ref), channel_id=1, source_target_pairs={{0,1},{1,0},{2,3},{3,2},{4,5},{5,4},{6,7},{7,6},{8,9},{9,8},{10,11... | collective-permute-start | bytes 786440 | tf_op jit(solution)/shard_map/ppermute | solution.py:375
  38.9 7.3 %collective-permute-done.10.refs_0_ = bf16[256,512]{1,0:T(8,128)(2,1)S(1)} collective-permute-done((bf16[256,512]{1,0:T(8,128)(2,1)S(1)}, bf16[256,512]{1,0:T(8,128)(2,1)S(1)}, u32[]{:S(2)}, u32[]{:S(2)}) %collective-permute-start.10) | collective-permute-done | bytes 262176 | tf_op jit(solution)/shard_map/ppermute | solution.py:375
  46.1 3.7 %theta_grad.1 = (f32[512,2048]{1,0:T(8,128)}, f32[8,128]{1,0:T(8,128)S(1)}) custom-call(s32[1]{0:T(128)} %bitcast.here_ref, bf16[256,512]{1,0:T(8,128)(2,1)S(1)} %join_ratio.1.ratio_ref, bf16[256,512]{1,0:T(8,128)(2,1)S(1)} %collective-permute-done.10.refs_0_, bf16[256,4096]{1,0:T(8,128)(2,1)S(1)} %get-tuple-element.19.prob_ref.refs_1_, ...), custom_call_target="tpu_custom_call" | custom-call | flops 1 | bytes 1 | tf_op jit(solution)/shard_map/theta_grad/pallas_call | solution.py:317
  49.8 0.2 add_pair.3.refs_1_
  50.1 0.1 collective-permute-start.15
  50.2 0.6 %collective-permute-start.14 = (bf16[64,2048]{1,0:T(8,128)(2,1)S(1)}, bf16[64,2048]{1,0:T(8,128)(2,1)S(1)}, u32[]{:S(2)}, u32[]{:S(2)}) collective-permute-start(bf16[64,2048]{1,0:T(8,128)(2,1)S(1)} %add_pair.2.refs_0_), channel_id=1, source_target_pairs={{0,8},{8,0},{16,24},{24,16},{1,9},{9,1},{17,25},{25,17},{2,10},{10... | collective-permute-start | bytes 786440 | tf_op jit(solution)/shard_map/ppermute | solution.py:379
  50.8 2.0 %collective-permute-done.14.refs_2_ = bf16[64,2048]{1,0:T(8,128)(2,1)S(1)} collective-permute-done((bf16[64,2048]{1,0:T(8,128)(2,1)S(1)}, bf16[64,2048]{1,0:T(8,128)(2,1)S(1)}, u32[]{:S(2)}, u32[]{:S(2)}) %collective-permute-start.14) | collective-permute-done | bytes 262176 | tf_op jit(solution)/shard_map/ppermute | solution.py:379
  52.8 1.4 %place_pieces.1 = bf16[256,4096]{1,0:T(8,128)(2,1)} custom-call(s32[1]{0:T(128)} %bitcast.here_ref, bf16[64,2048]{1,0:T(8,128)(2,1)S(1)} %add_pair.2.refs_0_, bf16[192,2048]{1,0:T(8,128)(2,1)S(1)} %add_pair.3.refs_1_, bf16[64,2048]{1,0:T(8,128)(2,1)S(1)} %collective-permute-done.14.refs_2_, bf16[192,2048]{1,0:T(8,128)(2,1)S(1)} %collective-permute-done.15.refs_3_), custom_call_target="tpu_custom_call" | custom-call | bytes 4194304 | tf_op jit(solution)/shard_map/place_pieces/pallas_call | solution.py:356
  (17 shorter events, 0.4 us)
Async XLA Ops:
  0.6 10.6 %copy-start = (s32[16,64,128]{2,1,0:T(8,128)S(1)}, s32[16,64,128]{2,1,0:T(8,128)}, u32[]{:S(2)}) copy-start(s32[16,64,128]{2,1,0:T(8,128)} %count_ref.1) | copy-start | bytes 1572868
  5.4 16.1 %collective-permute-start.7 = (bf16[512,2048]{1,0:T(8,128)(2,1)S(1)}, bf16[512,2048]{1,0:T(8,128)(2,1)S(1)}, u32[]{:S(2)}, u32[]{:S(2)}) collective-permute-start(bf16[512,2048]{1,0:T(8,128)(2,1)S(1)} %get-tuple-element.18), channel_id=1, source_target_pairs={{0,8},{8,0},{16,24},{24,16},{1,9},{9,1},{17,25},{25,17},{2,10},{10... | collective-permute-start | bytes 6291464 | tf_op jit(solution)/shard_map/ppermute | solution.py:379
  6.0 7.9 %collective-permute-start = (bf16[64,512]{1,0:T(8,128)(2,1)S(1)}, bf16[64,512]{1,0:T(8,128)(2,1)S(1)}, u32[]{:S(2)}, u32[]{:S(2)}) collective-permute-start(bf16[64,512]{1,0:T(8,128)(2,1)S(1)} %get-tuple-element.14), channel_id=1, source_target_pairs={{0,4},{2,6},{4,0},{6,2},{1,5},{3,7},{5,1},{7,3},{8,12},{10,14},{12... | collective-permute-start | bytes 196616 | tf_op jit(solution)/shard_map/ppermute | solution.py:379
  9.6 6.7 %collective-permute-start.1 = (bf16[64,512]{1,0:T(8,128)(2,1)S(1)}, bf16[64,512]{1,0:T(8,128)(2,1)S(1)}, u32[]{:S(2)}, u32[]{:S(2)}) collective-permute-start(bf16[64,512]{1,0:T(8,128)(2,1)S(1)} %get-tuple-element.15), channel_id=1, source_target_pairs={{0,6},{2,4},{4,2},{6,0},{1,7},{3,5},{5,3},{7,1},{8,14},{10,12},{12... | collective-permute-start | bytes 196616 | tf_op jit(solution)/shard_map/ppermute | solution.py:379
  11.0 5.5 %collective-permute-start.2 = (bf16[64,512]{1,0:T(8,128)(2,1)S(1)}, bf16[64,512]{1,0:T(8,128)(2,1)S(1)}, u32[]{:S(2)}, u32[]{:S(2)}) collective-permute-start(bf16[64,512]{1,0:T(8,128)(2,1)S(1)} %get-tuple-element.16), channel_id=1, source_target_pairs={{0,2},{2,0},{4,6},{6,4},{1,3},{3,1},{5,7},{7,5},{8,10},{10,8},{12,... | collective-permute-start | bytes 196616 | tf_op jit(solution)/shard_map/ppermute | solution.py:379
  16.5 5.0 %collective-permute-start.8 = (bf16[64,512]{1,0:T(8,128)(2,1)S(1)}, bf16[64,512]{1,0:T(8,128)(2,1)S(1)}, u32[]{:S(2)}, u32[]{:S(2)}) collective-permute-start(bf16[64,512]{1,0:T(8,128)(2,1)S(1)} %ratio_chunk.1.ratio_ref.refs_0_), channel_id=1, source_target_pairs={{0,8},{8,0},{16,24},{24,16},{1,9},{9,1},{17,25},{25,17},{2,10},{10... | collective-permute-start | bytes 196616 | tf_op jit(solution)/shard_map/ppermute | solution.py:379
  16.6 7.1 %collective-permute-start.3 = (bf16[64,512]{1,0:T(8,128)(2,1)S(1)}, bf16[64,512]{1,0:T(8,128)(2,1)S(1)}, u32[]{:S(2)}, u32[]{:S(2)}) collective-permute-start(bf16[64,512]{1,0:T(8,128)(2,1)S(1)} %ratio_chunk.1.ratio_ref.refs_0_), channel_id=1, source_target_pairs={{0,4},{2,6},{4,0},{6,2},{1,5},{3,7},{5,1},{7,3},{8,12},{10,14},{12... | collective-permute-start | bytes 196616 | tf_op jit(solution)/shard_map/ppermute | solution.py:379
  19.4 5.9 %collective-permute-start.5 = (bf16[64,512]{1,0:T(8,128)(2,1)S(1)}, bf16[64,512]{1,0:T(8,128)(2,1)S(1)}, u32[]{:S(2)}, u32[]{:S(2)}) collective-permute-start(bf16[64,512]{1,0:T(8,128)(2,1)S(1)} %ratio_chunk.1.ratio_ref.refs_0_), channel_id=1, source_target_pairs={{0,2},{2,0},{4,6},{6,4},{1,3},{3,1},{5,7},{7,5},{8,10},{10,8},{12,... | collective-permute-start | bytes 196616 | tf_op jit(solution)/shard_map/ppermute | solution.py:379
  20.6 6.1 %collective-permute-start.4 = (bf16[64,512]{1,0:T(8,128)(2,1)S(1)}, bf16[64,512]{1,0:T(8,128)(2,1)S(1)}, u32[]{:S(2)}, u32[]{:S(2)}) collective-permute-start(bf16[64,512]{1,0:T(8,128)(2,1)S(1)} %ratio_chunk.1.ratio_ref.refs_0_), channel_id=1, source_target_pairs={{0,6},{2,4},{4,2},{6,0},{1,7},{3,5},{5,3},{7,1},{8,14},{10,12},{12... | collective-permute-start | bytes 196616 | tf_op jit(solution)/shard_map/ppermute | solution.py:379
  22.1 8.0 %collective-permute-start.9 = (bf16[64,2048]{1,0:T(8,128)(2,1)S(1)}, bf16[64,2048]{1,0:T(8,128)(2,1)S(1)}, u32[]{:S(2)}, u32[]{:S(2)}) collective-permute-start(bf16[64,2048]{1,0:T(8,128)(2,1)S(1)} %beta_pieces.2.own_ref), channel_id=1, source_target_pairs={{0,16},{8,24},{16,0},{24,8},{1,17},{9,25},{17,1},{25,9},{2,18},{10... | collective-permute-start | bytes 786440 | tf_op jit(solution)/shard_map/ppermute | solution.py:379
  23.7 13.5 %collective-permute-start.11 = (bf16[128,2048]{1,0:T(8,128)(2,1)S(1)}, bf16[128,2048]{1,0:T(8,128)(2,1)S(1)}, u32[]{:S(2)}, u32[]{:S(2)}) collective-permute-start(bf16[128,2048]{1,0:T(8,128)(2,1)S(1)} %hold.2), channel_id=1, source_target_pairs={{0,1},{1,0},{2,3},{3,2},{4,5},{5,4},{6,7},{7,6},{8,9},{9,8},{10,11... | collective-permute-start | bytes 1572872 | tf_op jit(solution)/shard_map/ppermute | solution.py:375
  26.7 1.5 %collective-permute-start.6 = (bf16[192,512]{1,0:T(8,128)(2,1)S(1)}, bf16[192,512]{1,0:T(8,128)(2,1)S(1)}, u32[]{:S(2)}, u32[]{:S(2)}) collective-permute-start(bf16[192,512]{1,0:T(8,128)(2,1)S(1)} %stack_rows.1.ratio_ref), channel_id=1, source_target_pairs={{0,8},{8,0},{16,24},{24,16},{1,9},{9,1},{17,25},{25,17},{2,10},{10... | collective-permute-start | bytes 589832 | tf_op jit(solution)/shard_map/ppermute | solution.py:379
  30.7 19.1 %collective-permute-start.13 = (bf16[192,2048]{1,0:T(8,128)(2,1)S(1)}, bf16[192,2048]{1,0:T(8,128)(2,1)S(1)}, u32[]{:S(2)}, u32[]{:S(2)}) collective-permute-start(bf16[192,2048]{1,0:T(8,128)(2,1)S(1)} %beta_pieces.3.refs_4_.rest_0_.own_ref), channel_id=1, source_target_pairs={{0,16},{8,24},{16,0},{24,8},{1,17},{9,25},{17,1},{25,9},{2,18},{10... | collective-permute-start | bytes 2359304 | tf_op jit(solution)/shard_map/ppermute | solution.py:379
  37.2 8.9 %collective-permute-start.12 = (bf16[128,2048]{1,0:T(8,128)(2,1)S(1)}, bf16[128,2048]{1,0:T(8,128)(2,1)S(1)}, u32[]{:S(2)}, u32[]{:S(2)}) collective-permute-start(bf16[128,2048]{1,0:T(8,128)(2,1)S(1)} %hold.3.refs_2_), channel_id=1, source_target_pairs={{0,8},{8,0},{16,24},{24,16},{1,9},{9,1},{17,25},{25,17},{2,10},{10... | collective-permute-start | bytes 1572872 | tf_op jit(solution)/shard_map/ppermute | solution.py:379
  37.4 8.8 %collective-permute-start.10 = (bf16[256,512]{1,0:T(8,128)(2,1)S(1)}, bf16[256,512]{1,0:T(8,128)(2,1)S(1)}, u32[]{:S(2)}, u32[]{:S(2)}) collective-permute-start(bf16[256,512]{1,0:T(8,128)(2,1)S(1)} %join_ratio.1.ratio_ref), channel_id=1, source_target_pairs={{0,1},{1,0},{2,3},{3,2},{4,5},{5,4},{6,7},{7,6},{8,9},{9,8},{10,11... | collective-permute-start | bytes 786440 | tf_op jit(solution)/shard_map/ppermute | solution.py:375
  50.1 2.7 %collective-permute-start.15 = (bf16[192,2048]{1,0:T(8,128)(2,1)S(1)}, bf16[192,2048]{1,0:T(8,128)(2,1)S(1)}, u32[]{:S(2)}, u32[]{:S(2)}) collective-permute-start(bf16[192,2048]{1,0:T(8,128)(2,1)S(1)} %add_pair.3.refs_1_), channel_id=1, source_target_pairs={{0,8},{8,0},{16,24},{24,16},{1,9},{9,1},{17,25},{25,17},{2,10},{10... | collective-permute-start | bytes 2359304 | tf_op jit(solution)/shard_map/ppermute | solution.py:379
  50.2 2.6 %collective-permute-start.14 = (bf16[64,2048]{1,0:T(8,128)(2,1)S(1)}, bf16[64,2048]{1,0:T(8,128)(2,1)S(1)}, u32[]{:S(2)}, u32[]{:S(2)}) collective-permute-start(bf16[64,2048]{1,0:T(8,128)(2,1)S(1)} %add_pair.2.refs_0_), channel_id=1, source_target_pairs={{0,8},{8,0},{16,24},{24,16},{1,9},{9,1},{17,25},{25,17},{2,10},{10... | collective-permute-start | bytes 786440 | tf_op jit(solution)/shard_map/ppermute | solution.py:379

commit v11 on v10

--- a/solution.py
+++ b/solution.py
@@ -10,6 +10,8 @@
 BF16 = jnp.bfloat16
 F32 = jnp.float32
 MIB = 1024 * 1024
+HOLD_COST = 5 * 10**8
+TURN_COST = 4 * 10**9
 ANY = pl.BlockSpec(memory_space=pl.ANY)
 HBM = pl.BlockSpec(memory_space=pltpu.HBM)
 VMEM = pl.BlockSpec(memory_space=pltpu.VMEM)
@@ -201,33 +203,29 @@
     )(ratio, docs_held)
 
 
-def beta_pieces(sizes, here, product, ratio, docs_held, prob_held, flips, after):
+def beta_piece(sizes, here, product, ratio, docs_held, prob_held, flips):
     words, side_width = product.shape
     docs = docs_held.shape[0]
-    rows = words // sum(map(len, flips))
-
-    def kernel(here_ref, product_ref, ratio_ref, doc_ref, prob_ref, *rest):
+    rows = words // len(flips)
+
+    def kernel(here_ref, product_ref, ratio_ref, doc_ref, prob_ref, out_ref):
         columns = window(sizes.side(here_ref), side_width)
         topic_at = sizes.topic_at(here_ref)
         summed = product_ref[...] + jnp.dot(ratio_ref[...], doc_ref[...], preferred_element_type=F32)
-        chunk = 0
-        for piece, out_ref in zip(flips, rest[len(after) :]):
-            for i, flip in enumerate(piece):
-                prob = prob_ref[window(topic_at ^ flip, rows), columns].astype(F32)
-                out_ref[i * rows : (i + 1) * rows, :] = (
-                    -prob * summed[chunk * rows : (chunk + 1) * rows, :]
-                ).astype(BF16)
-                chunk += 1
-
-    return pl.pallas_call(
-        kernel,
-        out_shape=[jax.ShapeDtypeStruct((rows * len(piece), side_width), BF16) for piece in flips],
-        in_specs=[SMEM] + [VMEM] * 4 + [ANY] * len(after),
-        out_specs=[VMEM] * len(flips),
-        compiler_params=call_params(),
-        cost_estimate=cost(2 * words * docs * side_width, 2 * (4 * words + docs) * side_width),
-        name="beta_pieces",
-    )(here, product, ratio, docs_held, prob_held, *after)
+        for i, flip in enumerate(flips):
+            at = slice(i * rows, (i + 1) * rows)
+            prob = prob_ref[window(topic_at ^ flip, rows), columns].astype(F32)
+            out_ref[at, :] = (-prob * summed[at, :]).astype(BF16)
+
+    return pl.pallas_call(
+        kernel,
+        out_shape=jax.ShapeDtypeStruct((words, side_width), BF16),
+        in_specs=[SMEM] + [VMEM] * 4,
+        out_specs=VMEM,
+        compiler_params=call_params(),
+        cost_estimate=cost(1, 1) if len(flips) > 1 else cost(2 * words * docs * side_width, 2 * (4 * words + docs) * side_width),
+        name="beta_piece",
+    )(here, product, ratio, docs_held, prob_held)
 
 
 def stack_rows(parts, after):
@@ -263,7 +261,7 @@
     )(own, other, *after)
 
 
-def hold(array, after):
+def hold(array, after, flops=1):
     def kernel(in_ref, *rest):
         rest[-1][...] = in_ref[...]
 
@@ -273,43 +271,53 @@
         in_specs=[VMEM] + [ANY] * len(after),
         out_specs=VMEM,
         compiler_params=call_params(),
-        cost_estimate=cost(0, 4 * array.size),
+        cost_estimate=cost(flops, 4 * array.size),
         name="hold",
     )(array, *after)
 
 
-def theta_grad(sizes, here, ratio, far_ratios, prob_held, far_logits, log_norm):
+def turn_ratios(sizes, here, ratio, far_ratios):
     words, docs = ratio.shape
     half = words // 2
+    count = 1 + len(far_ratios)
+
+    def kernel(here_ref, *refs):
+        side = sizes.side(here_ref)
+        for l, (ref, out_ref) in enumerate(zip(refs[:count], refs[count:])):
+            for h, which in enumerate((side, 1 - side) if l else (0, 1)):
+                rows = ref[window(which, half), :].astype(F32)
+                out_ref[:, h * half : (h + 1) * half] = (-rows).T.astype(BF16)
+
+    return pl.pallas_call(
+        kernel,
+        out_shape=[jax.ShapeDtypeStruct((docs, words), BF16)] * count,
+        in_specs=[SMEM] + [VMEM] * count,
+        out_specs=[VMEM] * count,
+        compiler_params=call_params(),
+        cost_estimate=cost(TURN_COST, 1),
+        name="turn_ratios",
+    )(here, ratio, *far_ratios)
+
+
+def theta_grad(sizes, here, turned, prob_held, far_logits, log_norm):
+    docs, words = turned[0].shape
+    half = words // 2
     share = far_logits[0].shape[1]
-    far = len(far_ratios)
-    count = far + 1
+    count = len(turned)
     span = min(share, 512)
     blocks = share // span
 
-    def kernel(here_ref, ratio_ref, *refs):
-        far_refs, prob_ref = refs[:far], refs[far]
-        logit_refs, norm_ref = refs[far + 1 : 3 * far + 1], refs[3 * far + 1]
-        out_ref, done_ref, turned = refs[-3:]
+    def kernel(here_ref, *refs):
+        turned_refs, prob_ref = refs[:count], refs[count]
+        logit_refs, norm_ref = refs[count + 1 : 3 * count - 1], refs[3 * count - 1]
+        out_ref, done_ref = refs[-2:]
         done_ref[...] = jnp.zeros_like(done_ref)
-        side = sizes.side(here_ref)
-
-        @pl.when(pl.program_id(0) == 0)
-        def _():
-            def put(rows, at):
-                turned[:, at : at + rows.shape[0]] = (-rows.astype(F32)).T.astype(BF16)
-
-            put(ratio_ref[...], 0)
-            for l in range(far):
-                for h in range(2):
-                    which = side if h == 0 else 1 - side
-                    put(far_refs[l][window(which, half), :], (l + 1) * words + h * half)
-
-        prob = jnp.concatenate(
-            [prob_ref[...]] + [jnp.exp(ref[...].astype(F32) - norm_ref[...]).astype(BF16) for ref in logit_refs],
-            axis=0,
-        )
-        out_ref[...] = jnp.dot(turned[...], prob, preferred_element_type=F32)
+        summed = jnp.dot(turned_refs[0][...], prob_ref[...], preferred_element_type=F32)
+        for l in range(count - 1):
+            pair = logit_refs[2 * l : 2 * l + 2]
+            prob = jnp.concatenate([jnp.exp(ref[...].astype(F32) - norm_ref[...]).astype(BF16) for ref in pair], axis=0)
+            summed += jnp.dot(turned_refs[l + 1][...], prob, preferred_element_type=F32)
+        out_ref[...] = summed
 
     whole = lambda j, h: (0, 0)
     held = lambda j, h: (0, lax.rem(h[0], sizes.vocab) * blocks + j)
@@ -320,17 +328,16 @@
         grid_spec=pltpu.PrefetchScalarGridSpec(
             num_scalar_prefetch=1,
             grid=(blocks,),
-            in_specs=[pl.BlockSpec((words, docs), whole)] * count
+            in_specs=[pl.BlockSpec((docs, words), whole)] * count
             + [pl.BlockSpec((words, span), held)]
-            + [pl.BlockSpec((half, span), column)] * (2 * far)
+            + [pl.BlockSpec((half, span), column)] * (2 * count - 2)
             + [pl.BlockSpec((1, span), held)],
             out_specs=[pl.BlockSpec((docs, span), column), pl.BlockSpec((8, 128), whole)],
-            scratch_shapes=[pltpu.VMEM((docs, count * words), BF16)],
         ),
-        compiler_params=call_params(),
+        compiler_params=call_params(16),
         cost_estimate=cost(1, 1),
         name="theta_grad",
-    )(here, ratio, *far_ratios, prob_held, *far_logits, log_norm)
+    )(here, *turned, prob_held, *far_logits, log_norm)
 
 
 def place_pieces(sizes, here, own, other, flips, shape):
@@ -387,20 +394,18 @@
     counts = chunk_counts(sizes, here, word_counts, tile_doc, tile_word, docs, words)
     own_ratio = ratio_chunk([parts[0]] + arrived, counts, word_tile)
     gathered = [swap(own_ratio, "topic", s) for s in order]
+    far_bits = [1 << b for b in range(1, sizes.doc.bit_length() - 1)]
+
+    def beta(ratio, flips, after):
+        part = beta_piece(sizes, here, own_product(ratio, docs_held), swap(ratio, "doc", 1), sibling_docs, prob_held, flips)
+        for bit in far_bits[:-1]:
+            part = add_pair(part, swap(part, "doc", bit))
+        return part, swap(hold(part, after, HOLD_COST) if after else part, "doc", far_bits[-1])
+
+    flips = [[0], order]
+    pairs = [beta(own_ratio, flips[0], [])]
     near_logits = [shift(hold(part, gathered[:1]), s) for s, part in enumerate(near_logits, 1)]
-    far_bits = [1 << b for b in range(1, sizes.doc.bit_length() - 1)]
-
-    def beta(ratio, flips, after):
-        pieces = beta_pieces(
-            sizes, here, own_product(ratio, docs_held), swap(ratio, "doc", 1), sibling_docs, prob_held, flips, after
-        )
-        for bit in far_bits[:-1]:
-            pieces = [add_pair(part, swap(part, "doc", bit)) for part in pieces]
-        return [(part, swap(part, "doc", far_bits[-1])) for part in pieces]
-
-    flips = [[0], order]
-    pairs = beta(own_ratio, flips[:1], [])
-    pairs += beta(stack_rows(gathered, []), flips[1:], [pairs[0][1]])
+    pairs.append(beta(stack_rows(gathered, []), flips[1], [pairs[0][1]]))
 
     ratio = join_ratio(sizes, here, [own_ratio] + gathered, [0] + order, [pairs[1][0]])
     far_ratios = [shift(ratio, s) for s in range(1, sizes.vocab)]
@@ -408,7 +413,8 @@
     for part in near_logits:
         part = hold(part, [pairs[1][0]])
         far_logits += [part, swap(part, "doc", 1)]
-    theta, theta_done = theta_grad(sizes, here, ratio, far_ratios, prob_held, far_logits, norm_held)
+    turned = turn_ratios(sizes, here, ratio, far_ratios)
+    theta, theta_done = theta_grad(sizes, here, turned, prob_held, far_logits, norm_held)
 
     sums = [add_pair(*pair, [theta_done] if p else []) for p, pair in enumerate(pairs)]
     out = place_pieces(sizes, here, sums, [swap(part, "doc", 1) for part in sums], flips, word_logits.shape)

time: 54.3 us -> 55.5 us (1.022)
  waiting for transfers between devices: 22.7 us -> 24.9 us
  starting transfers between devices: 17.3 us -> 16.2 us
    ppermute x2, waiting for transfers between devices: 12.2 us -> 13.4 us  [shift(): lax.ppermute(array, 'vocab', [(i, (i + by) % sizes.vocab) for i in range(...]
    ppermute x14, waiting for transfers between devices: 10.5 us -> 11.4 us  [swap(): return lax.ppermute(array, axis, [(i, i ^ bits) for i in range(count)])]
    ppermute x2, starting transfers between devices: 3.09 us -> 2.17 us  [shift(): lax.ppermute(array, 'vocab', [(i, (i + by) % sizes.vocab) for i in range(...]
    pallas_call x2 -> x3, Pallas kernels: 1.14 us -> 1.34 us  [the longest x2 1.13 us: beta_piece(): pl.pallas_call(kernel, out_shape=jax.ShapeDtypeStruct((words, side_width)...]
where the time goes in v11:
time: 55.5 us; the launch traced here: 55.3 us
  waiting for transfers between devices  24.9 us (45%)
  starting transfers between devices  16.2 us (29%)
  Pallas kernels  13.5 us (24%)
  between operations  0.8 us (1%)
    ppermute x14, starting transfers between devices, swap(): return lax.ppermute(array, axis, [(i, i ^ bits) for i in range(count)])  14 us
    ppermute x2, waiting for transfers between devices, shift(): lax.ppermute(array, 'vocab', [(i, (i + by) % sizes.vocab) for i in range(...  13.4 us
    ppermute x14, waiting for transfers between devices, swap(): return lax.ppermute(array, axis, [(i, i ^ bits) for i in range(count)])  11.4 us
    pallas_call x1, Pallas kernels, rate_partial(): pl.pallas_call(kernel, out_shape=[jax.ShapeDtypeStruct((chunk, docs), BF1...  4.79 us
    pallas_call x1, Pallas kernels, theta_grad(): pl.pallas_call(kernel, out_shape=[jax.ShapeDtypeStruct((docs, share), F32...  3.64 us
    ppermute x2, starting transfers between devices, shift(): lax.ppermute(array, 'vocab', [(i, (i + by) % sizes.vocab) for i in range(...  2.17 us
    pallas_call x1, Pallas kernels, place_pieces(): pl.pallas_call(kernel, out_shape=jax.ShapeDtypeStruct(shape, BF16), in_sp...  1.37 us
    pallas_call x2, Pallas kernels, beta_piece(): pl.pallas_call(kernel, out_shape=jax.ShapeDtypeStruct((words, side_width)...  1.13 us
  transfers between devices with their start and end apart: 16, of which 9 were waited for; matrix products, arithmetic and copies ran while one was open for 0% of the time, Pallas kernels for 13%

profile of v11, /device:TPU:0, one launch (start us, length us, event | category | flops | bytes accessed | tf_op | source)
XLA Modules:
  0.0 55.3 jit_solution(8097478369395886062)
XLA Ops:
  0.6 4.8 %rate_partial.1 = (bf16[64,512]{1,0:T(8,128)(2,1)S(1)}, bf16[64,512]{1,0:T(8,128)(2,1)S(1)}, bf16[64,512]{1,0:T(8,128)(2,1)S(1)}, bf16[64,512]{1,0:T(8,128)(2,1)...) custom-call(s32[1]{0:T(128)} %bitcast.here_ref, ...), custom_call_target="tpu_custom_call" | custom-call | flops 1073741824 | bytes 6291456 | tf_op jit(solution)/shard_map/rate_partial/pallas_call | solution.py:99
  5.4 0.5 collective-permute-start.7
  6.0 3.7 %collective-permute-start = (bf16[64,512]{1,0:T(8,128)(2,1)S(1)}, bf16[64,512]{1,0:T(8,128)(2,1)S(1)}, u32[]{:S(2)}, u32[]{:S(2)}) collective-permute-start(bf16[64,512]{1,0:T(8,128)(2,1)S(1)} %get-tuple-element.16), channel_id=1, source_target_pairs={{0,4},{2,6},{4,0},{6,2},{1,5},{3,7},{5,1},{7,3},{8,12},{10,14},{12... | collective-permute-start | bytes 196616 | tf_op jit(solution)/shard_map/ppermute | solution.py:386
  9.6 1.3 %collective-permute-start.1 = (bf16[64,512]{1,0:T(8,128)(2,1)S(1)}, bf16[64,512]{1,0:T(8,128)(2,1)S(1)}, u32[]{:S(2)}, u32[]{:S(2)}) collective-permute-start(bf16[64,512]{1,0:T(8,128)(2,1)S(1)} %get-tuple-element.17), channel_id=1, source_target_pairs={{0,6},{2,4},{4,2},{6,0},{1,7},{3,5},{5,3},{7,1},{8,14},{10,12},{12... | collective-permute-start | bytes 196616 | tf_op jit(solution)/shard_map/ppermute | solution.py:386
  11.0 0.2 collective-permute-start.2
  11.2 0.8 %chunk_counts.1.refs_4_ = f32[64,512]{1,0:T(8,128)S(1)} custom-call(s32[1]{0:T(128)} %bitcast.here_ref, s32[16]{0:T(128)} %doc_at.1, s32[16]{0:T(128)} %word_at.1, s32[16,64,128]{2,1,0:T(8,128)S(1)} %copy-done), custom_call_target="tpu_custom_call" | custom-call | flops 131072 | bytes 524288 | tf_op jit(solution)/shard_map/chunk_counts/pallas_call | solution.py:138
  12.0 1.8 %collective-permute-done.refs_1_ = bf16[64,512]{1,0:T(8,128)(2,1)S(1)} collective-permute-done((bf16[64,512]{1,0:T(8,128)(2,1)S(1)}, bf16[64,512]{1,0:T(8,128)(2,1)S(1)}, u32[]{:S(2)}, u32[]{:S(2)}) %collective-permute-start) | collective-permute-done | bytes 65568 | tf_op jit(solution)/shard_map/ppermute | solution.py:386
  13.9 2.4 %collective-permute-done.1.refs_2_ = bf16[64,512]{1,0:T(8,128)(2,1)S(1)} collective-permute-done((bf16[64,512]{1,0:T(8,128)(2,1)S(1)}, bf16[64,512]{1,0:T(8,128)(2,1)S(1)}, u32[]{:S(2)}, u32[]{:S(2)}) %collective-permute-start.1) | collective-permute-done | bytes 65568 | tf_op jit(solution)/shard_map/ppermute | solution.py:386
  16.3 0.2 collective-permute-done.2.refs_3_
  16.6 0.9 %collective-permute-start.5 = (bf16[64,512]{1,0:T(8,128)(2,1)S(1)}, bf16[64,512]{1,0:T(8,128)(2,1)S(1)}, u32[]{:S(2)}, u32[]{:S(2)}) collective-permute-start(bf16[64,512]{1,0:T(8,128)(2,1)S(1)} %ratio_chunk.1.refs_0_.ratio_ref), channel_id=1, source_target_pairs={{0,2},{2,0},{4,6},{6,4},{1,3},{3,1},{5,7},{7,5},{8,10},{10,8},{12,... | collective-permute-start | bytes 196616 | tf_op jit(solution)/shard_map/ppermute | solution.py:386
  17.5 3.4 %collective-permute-start.4 = (bf16[64,512]{1,0:T(8,128)(2,1)S(1)}, bf16[64,512]{1,0:T(8,128)(2,1)S(1)}, u32[]{:S(2)}, u32[]{:S(2)}) collective-permute-start(bf16[64,512]{1,0:T(8,128)(2,1)S(1)} %ratio_chunk.1.refs_0_.ratio_ref), channel_id=1, source_target_pairs={{0,6},{2,4},{4,2},{6,0},{1,7},{3,5},{5,3},{7,1},{8,14},{10,12},{12... | collective-permute-start | bytes 196616 | tf_op jit(solution)/shard_map/ppermute | solution.py:386
  20.9 0.5 own_product.3.product_ref
  21.4 0.5 beta_piece.3.own_ref
  21.9 1.6 %collective-permute-start.12 = (bf16[64,2048]{1,0:T(8,128)(2,1)S(1)}, bf16[64,2048]{1,0:T(8,128)(2,1)S(1)}, u32[]{:S(2)}, u32[]{:S(2)}) collective-permute-start(bf16[64,2048]{1,0:T(8,128)(2,1)S(1)} %beta_piece.3.own_ref), channel_id=1, source_target_pairs={{0,16},{8,24},{16,0},{24,8},{1,17},{9,25},{17,1},{25,9},{2,18},{10... | collective-permute-start | bytes 786440 | tf_op jit(solution)/shard_map/ppermute | solution.py:386
  23.5 4.0 %collective-permute-done.3.refs_0_.refs_1_.rest_0_ = bf16[64,512]{1,0:T(8,128)(2,1)S(1)} collective-permute-done((bf16[64,512]{1,0:T(8,128)(2,1)S(1)}, bf16[64,512]{1,0:T(8,128)(2,1)S(1)}, u32[]{:S(2)}, u32[]{:S(2)}) %collective-permute-start.3) | collective-permute-done | bytes 65568 | tf_op jit(solution)/shard_map/ppermute | solution.py:386
  27.6 1.6 %collective-permute-start.9 = (bf16[128,2048]{1,0:T(8,128)(2,1)S(1)}, bf16[128,2048]{1,0:T(8,128)(2,1)S(1)}, u32[]{:S(2)}, u32[]{:S(2)}) collective-permute-start(bf16[128,2048]{1,0:T(8,128)(2,1)S(1)} %hold.3), channel_id=1, source_target_pairs={{0,1},{1,0},{2,3},{3,2},{4,5},{5,4},{6,7},{7,6},{8,9},{9,8},{10,11... | collective-permute-start | bytes 1572872 | tf_op jit(solution)/shard_map/ppermute | solution.py:382
  29.2 0.1 collective-permute-start.6
  29.2 0.6 %own_product.2.product_ref = f32[192,2048]{1,0:T(8,128)S(1)} custom-call(bf16[192,512]{1,0:T(8,128)(2,1)S(1)} %stack_rows.1.ratio_ref, bf16[512,2048]{1,0:T(8,128)(2,1)S(1)} %get-tuple-element.19.doc_ref), custom_call_target="tpu_custom_call" | custom-call | flops 402653184 | bytes 3670016 | tf_op jit(solution)/shard_map/own_product/pallas_call | solution.py:195
  29.8 0.8 %collective-permute-done.6.ratio_ref = bf16[192,512]{1,0:T(8,128)(2,1)S(1)} collective-permute-done((bf16[192,512]{1,0:T(8,128)(2,1)S(1)}, bf16[192,512]{1,0:T(8,128)(2,1)S(1)}, u32[]{:S(2)}, u32[]{:S(2)}) %collective-permute-start.6) | collective-permute-done | bytes 196640 | tf_op jit(solution)/shard_map/ppermute | solution.py:386
  30.7 0.6 %beta_piece.2.refs_4_.rest_0_.in_ref.own_ref = bf16[192,2048]{1,0:T(8,128)(2,1)S(1)} custom-call(s32[1]{0:T(128)} %bitcast.here_ref, f32[192,2048]{1,0:T(8,128)S(1)} %own_product.2.product_ref, bf16[192,512]{1,0:T(8,128)(2,1)S(1)} %collective-permute-done.6.ratio_ref, bf16[512,2048]{1,0:T(8,128)(2,1)S(1)} %collective-permute-done.7.doc_ref, ...), custom_call_target="tpu_custom_call" | custom-call | flops 1 | bytes 1 | tf_op jit(solution)/shard_map/beta_piece/pallas_call | solution.py:220
  31.4 1.6 %collective-permute-start.13 = (bf16[192,2048]{1,0:T(8,128)(2,1)S(1)}, bf16[192,2048]{1,0:T(8,128)(2,1)S(1)}, u32[]{:S(2)}, u32[]{:S(2)}) collective-permute-start(bf16[192,2048]{1,0:T(8,128)(2,1)S(1)} %hold.5), channel_id=1, source_target_pairs={{0,16},{8,24},{16,0},{24,8},{1,17},{9,25},{17,1},{25,9},{2,18},{10... | collective-permute-start | bytes 2359304 | tf_op jit(solution)/shard_map/ppermute | solution.py:386
  33.0 0.6 %collective-permute-start.8 = (bf16[256,512]{1,0:T(8,128)(2,1)S(1)}, bf16[256,512]{1,0:T(8,128)(2,1)S(1)}, u32[]{:S(2)}, u32[]{:S(2)}) collective-permute-start(bf16[256,512]{1,0:T(8,128)(2,1)S(1)} %join_ratio.1.refs_0_), channel_id=1, source_target_pairs={{0,1},{1,0},{2,3},{3,2},{4,5},{5,4},{6,7},{7,6},{8,9},{9,8},{10,11... | collective-permute-start | bytes 786440 | tf_op jit(solution)/shard_map/ppermute | solution.py:382
  33.5 8.9 %collective-permute-done.9.in_ref = bf16[128,2048]{1,0:T(8,128)(2,1)S(1)} collective-permute-done((bf16[128,2048]{1,0:T(8,128)(2,1)S(1)}, bf16[128,2048]{1,0:T(8,128)(2,1)S(1)}, u32[]{:S(2)}, u32[]{:S(2)}) %collective-permute-start.9) | collective-permute-done | bytes 524320 | tf_op jit(solution)/shard_map/ppermute | solution.py:382
  42.4 0.1 collective-permute-start.10
  42.5 4.6 %collective-permute-done.8.refs_1_ = bf16[256,512]{1,0:T(8,128)(2,1)S(1)} collective-permute-done((bf16[256,512]{1,0:T(8,128)(2,1)S(1)}, bf16[256,512]{1,0:T(8,128)(2,1)S(1)}, u32[]{:S(2)}, u32[]{:S(2)}) %collective-permute-start.8) | collective-permute-done | bytes 262176 | tf_op jit(solution)/shard_map/ppermute | solution.py:382
  47.1 0.2 turn_ratios.1
  47.3 3.6 %theta_grad.1 = (f32[512,2048]{1,0:T(8,128)}, f32[8,128]{1,0:T(8,128)S(1)}) custom-call(s32[1]{0:T(128)} %bitcast.here_ref, bf16[512,256]{1,0:T(8,128)(2,1)S(1)} %get-tuple-element.22.refs_0_, bf16[512,256]{1,0:T(8,128)(2,1)S(1)} %get-tuple-element.23.refs_1_, bf16[256,4096]{1,0:T(8,128)(2,1)S(1)} %get-tuple-element.21.prob_ref.refs_2_, ...), custom_call_target="tpu_custom_call" | custom-call | flops 1 | bytes 1 | tf_op jit(solution)/shard_map/theta_grad/pallas_call | solution.py:325
  51.0 0.1 collective-permute-done.13.other_ref
  51.0 0.2 add_pair.3.refs_1_
  51.4 0.6 %collective-permute-start.14 = (bf16[64,2048]{1,0:T(8,128)(2,1)S(1)}, bf16[64,2048]{1,0:T(8,128)(2,1)S(1)}, u32[]{:S(2)}, u32[]{:S(2)}) collective-permute-start(bf16[64,2048]{1,0:T(8,128)(2,1)S(1)} %add_pair.2.refs_0_), channel_id=1, source_target_pairs={{0,8},{8,0},{16,24},{24,16},{1,9},{9,1},{17,25},{25,17},{2,10},{10... | collective-permute-start | bytes 786440 | tf_op jit(solution)/shard_map/ppermute | solution.py:386
  51.9 2.0 %collective-permute-done.14.refs_2_ = bf16[64,2048]{1,0:T(8,128)(2,1)S(1)} collective-permute-done((bf16[64,2048]{1,0:T(8,128)(2,1)S(1)}, bf16[64,2048]{1,0:T(8,128)(2,1)S(1)}, u32[]{:S(2)}, u32[]{:S(2)}) %collective-permute-start.14) | collective-permute-done | bytes 262176 | tf_op jit(solution)/shard_map/ppermute | solution.py:386
  54.0 1.4 %place_pieces.1 = bf16[256,4096]{1,0:T(8,128)(2,1)} custom-call(s32[1]{0:T(128)} %bitcast.here_ref, bf16[64,2048]{1,0:T(8,128)(2,1)S(1)} %add_pair.2.refs_0_, bf16[192,2048]{1,0:T(8,128)(2,1)S(1)} %add_pair.3.refs_1_, bf16[64,2048]{1,0:T(8,128)(2,1)S(1)} %collective-permute-done.14.refs_2_, bf16[192,2048]{1,0:T(8,128)(2,1)S(1)} %collective-permute-done.15.refs_3_), custom_call_target="tpu_custom_call" | custom-call | bytes 4194304 | tf_op jit(solution)/shard_map/place_pieces/pallas_call | solution.py:363
  (19 shorter events, 0.4 us)
Async XLA Ops:
  0.6 10.6 %copy-start = (s32[16,64,128]{2,1,0:T(8,128)S(1)}, s32[16,64,128]{2,1,0:T(8,128)}, u32[]{:S(2)}) copy-start(s32[16,64,128]{2,1,0:T(8,128)} %count_ref.1) | copy-start | bytes 1572868
  5.4 15.9 %collective-permute-start.7 = (bf16[512,2048]{1,0:T(8,128)(2,1)S(1)}, bf16[512,2048]{1,0:T(8,128)(2,1)S(1)}, u32[]{:S(2)}, u32[]{:S(2)}) collective-permute-start(bf16[512,2048]{1,0:T(8,128)(2,1)S(1)} %get-tuple-element.20), channel_id=1, source_target_pairs={{0,8},{8,0},{16,24},{24,16},{1,9},{9,1},{17,25},{25,17},{2,10},{10... | collective-permute-start | bytes 6291464 | tf_op jit(solution)/shard_map/ppermute | solution.py:386
  6.0 7.9 %collective-permute-start = (bf16[64,512]{1,0:T(8,128)(2,1)S(1)}, bf16[64,512]{1,0:T(8,128)(2,1)S(1)}, u32[]{:S(2)}, u32[]{:S(2)}) collective-permute-start(bf16[64,512]{1,0:T(8,128)(2,1)S(1)} %get-tuple-element.16), channel_id=1, source_target_pairs={{0,4},{2,6},{4,0},{6,2},{1,5},{3,7},{5,1},{7,3},{8,12},{10,14},{12... | collective-permute-start | bytes 196616 | tf_op jit(solution)/shard_map/ppermute | solution.py:386
  9.6 6.7 %collective-permute-start.1 = (bf16[64,512]{1,0:T(8,128)(2,1)S(1)}, bf16[64,512]{1,0:T(8,128)(2,1)S(1)}, u32[]{:S(2)}, u32[]{:S(2)}) collective-permute-start(bf16[64,512]{1,0:T(8,128)(2,1)S(1)} %get-tuple-element.17), channel_id=1, source_target_pairs={{0,6},{2,4},{4,2},{6,0},{1,7},{3,5},{5,3},{7,1},{8,14},{10,12},{12... | collective-permute-start | bytes 196616 | tf_op jit(solution)/shard_map/ppermute | solution.py:386
  11.0 5.5 %collective-permute-start.2 = (bf16[64,512]{1,0:T(8,128)(2,1)S(1)}, bf16[64,512]{1,0:T(8,128)(2,1)S(1)}, u32[]{:S(2)}, u32[]{:S(2)}) collective-permute-start(bf16[64,512]{1,0:T(8,128)(2,1)S(1)} %get-tuple-element.18), channel_id=1, source_target_pairs={{0,2},{2,0},{4,6},{6,4},{1,3},{3,1},{5,7},{7,5},{8,10},{10,8},{12,... | collective-permute-start | bytes 196616 | tf_op jit(solution)/shard_map/ppermute | solution.py:386
  16.5 4.8 %collective-permute-start.11 = (bf16[64,512]{1,0:T(8,128)(2,1)S(1)}, bf16[64,512]{1,0:T(8,128)(2,1)S(1)}, u32[]{:S(2)}, u32[]{:S(2)}) collective-permute-start(bf16[64,512]{1,0:T(8,128)(2,1)S(1)} %ratio_chunk.1.refs_0_.ratio_ref), channel_id=1, source_target_pairs={{0,8},{8,0},{16,24},{24,16},{1,9},{9,1},{17,25},{25,17},{2,10},{10... | collective-permute-start | bytes 196616 | tf_op jit(solution)/shard_map/ppermute | solution.py:386
  16.6 12.5 %collective-permute-start.5 = (bf16[64,512]{1,0:T(8,128)(2,1)S(1)}, bf16[64,512]{1,0:T(8,128)(2,1)S(1)}, u32[]{:S(2)}, u32[]{:S(2)}) collective-permute-start(bf16[64,512]{1,0:T(8,128)(2,1)S(1)} %ratio_chunk.1.refs_0_.ratio_ref), channel_id=1, source_target_pairs={{0,2},{2,0},{4,6},{6,4},{1,3},{3,1},{5,7},{7,5},{8,10},{10,8},{12,... | collective-permute-start | bytes 196616 | tf_op jit(solution)/shard_map/ppermute | solution.py:386
  17.5 11.6 %collective-permute-start.4 = (bf16[64,512]{1,0:T(8,128)(2,1)S(1)}, bf16[64,512]{1,0:T(8,128)(2,1)S(1)}, u32[]{:S(2)}, u32[]{:S(2)}) collective-permute-start(bf16[64,512]{1,0:T(8,128)(2,1)S(1)} %ratio_chunk.1.refs_0_.ratio_ref), channel_id=1, source_target_pairs={{0,6},{2,4},{4,2},{6,0},{1,7},{3,5},{5,3},{7,1},{8,14},{10,12},{12... | collective-permute-start | bytes 196616 | tf_op jit(solution)/shard_map/ppermute | solution.py:386
  20.9 6.6 %collective-permute-start.3 = (bf16[64,512]{1,0:T(8,128)(2,1)S(1)}, bf16[64,512]{1,0:T(8,128)(2,1)S(1)}, u32[]{:S(2)}, u32[]{:S(2)}) collective-permute-start(bf16[64,512]{1,0:T(8,128)(2,1)S(1)} %ratio_chunk.1.refs_0_.ratio_ref), channel_id=1, source_target_pairs={{0,4},{2,6},{4,0},{6,2},{1,5},{3,7},{5,1},{7,3},{8,12},{10,14},{12... | collective-permute-start | bytes 196616 | tf_op jit(solution)/shard_map/ppermute | solution.py:386
  21.9 9.4 %collective-permute-start.12 = (bf16[64,2048]{1,0:T(8,128)(2,1)S(1)}, bf16[64,2048]{1,0:T(8,128)(2,1)S(1)}, u32[]{:S(2)}, u32[]{:S(2)}) collective-permute-start(bf16[64,2048]{1,0:T(8,128)(2,1)S(1)} %beta_piece.3.own_ref), channel_id=1, source_target_pairs={{0,16},{8,24},{16,0},{24,8},{1,17},{9,25},{17,1},{25,9},{2,18},{10... | collective-permute-start | bytes 786440 | tf_op jit(solution)/shard_map/ppermute | solution.py:386
  27.6 14.8 %collective-permute-start.9 = (bf16[128,2048]{1,0:T(8,128)(2,1)S(1)}, bf16[128,2048]{1,0:T(8,128)(2,1)S(1)}, u32[]{:S(2)}, u32[]{:S(2)}) collective-permute-start(bf16[128,2048]{1,0:T(8,128)(2,1)S(1)} %hold.3), channel_id=1, source_target_pairs={{0,1},{1,0},{2,3},{3,2},{4,5},{5,4},{6,7},{7,6},{8,9},{9,8},{10,11... | collective-permute-start | bytes 1572872 | tf_op jit(solution)/shard_map/ppermute | solution.py:382
  29.2 1.5 %collective-permute-start.6 = (bf16[192,512]{1,0:T(8,128)(2,1)S(1)}, bf16[192,512]{1,0:T(8,128)(2,1)S(1)}, u32[]{:S(2)}, u32[]{:S(2)}) collective-permute-start(bf16[192,512]{1,0:T(8,128)(2,1)S(1)} %stack_rows.1.ratio_ref), channel_id=1, source_target_pairs={{0,8},{8,0},{16,24},{24,16},{1,9},{9,1},{17,25},{25,17},{2,10},{10... | collective-permute-start | bytes 589832 | tf_op jit(solution)/shard_map/ppermute | solution.py:386
  31.4 19.7 %collective-permute-start.13 = (bf16[192,2048]{1,0:T(8,128)(2,1)S(1)}, bf16[192,2048]{1,0:T(8,128)(2,1)S(1)}, u32[]{:S(2)}, u32[]{:S(2)}) collective-permute-start(bf16[192,2048]{1,0:T(8,128)(2,1)S(1)} %hold.5), channel_id=1, source_target_pairs={{0,16},{8,24},{16,0},{24,8},{1,17},{9,25},{17,1},{25,9},{2,18},{10... | collective-permute-start | bytes 2359304 | tf_op jit(solution)/shard_map/ppermute | solution.py:386
  33.0 14.1 %collective-permute-start.8 = (bf16[256,512]{1,0:T(8,128)(2,1)S(1)}, bf16[256,512]{1,0:T(8,128)(2,1)S(1)}, u32[]{:S(2)}, u32[]{:S(2)}) collective-permute-start(bf16[256,512]{1,0:T(8,128)(2,1)S(1)} %join_ratio.1.refs_0_), channel_id=1, source_target_pairs={{0,1},{1,0},{2,3},{3,2},{4,5},{5,4},{6,7},{7,6},{8,9},{9,8},{10,11... | collective-permute-start | bytes 786440 | tf_op jit(solution)/shard_map/ppermute | solution.py:382
  42.4 4.9 %collective-permute-start.10 = (bf16[128,2048]{1,0:T(8,128)(2,1)S(1)}, bf16[128,2048]{1,0:T(8,128)(2,1)S(1)}, u32[]{:S(2)}, u32[]{:S(2)}) collective-permute-start(bf16[128,2048]{1,0:T(8,128)(2,1)S(1)} %hold.4.refs_3_), channel_id=1, source_target_pairs={{0,8},{8,0},{16,24},{24,16},{1,9},{9,1},{17,25},{25,17},{2,10},{10... | collective-permute-start | bytes 1572872 | tf_op jit(solution)/shard_map/ppermute | solution.py:386
  51.2 2.7 %collective-permute-start.15 = (bf16[192,2048]{1,0:T(8,128)(2,1)S(1)}, bf16[192,2048]{1,0:T(8,128)(2,1)S(1)}, u32[]{:S(2)}, u32[]{:S(2)}) collective-permute-start(bf16[192,2048]{1,0:T(8,128)(2,1)S(1)} %add_pair.3.refs_1_), channel_id=1, source_target_pairs={{0,8},{8,0},{16,24},{24,16},{1,9},{9,1},{17,25},{25,17},{2,10},{10... | collective-permute-start | bytes 2359304 | tf_op jit(solution)/shard_map/ppermute | solution.py:386
  51.4 2.6 %collective-permute-start.14 = (bf16[64,2048]{1,0:T(8,128)(2,1)S(1)}, bf16[64,2048]{1,0:T(8,128)(2,1)S(1)}, u32[]{:S(2)}, u32[]{:S(2)}) collective-permute-start(bf16[64,2048]{1,0:T(8,128)(2,1)S(1)} %add_pair.2.refs_0_), channel_id=1, source_target_pairs={{0,8},{8,0},{16,24},{24,16},{1,9},{9,1},{17,25},{25,17},{2,10},{10... | collective-permute-start | bytes 786440 | tf_op jit(solution)/shard_map/ppermute | solution.py:386

commit v12 on v11

--- a/solution.py
+++ b/solution.py
@@ -10,8 +10,8 @@
 BF16 = jnp.bfloat16
 F32 = jnp.float32
 MIB = 1024 * 1024
-HOLD_COST = 5 * 10**8
-TURN_COST = 4 * 10**9
+HOLD_COST = 15 * 10**7
+TURN_COST = 10**9
 ANY = pl.BlockSpec(memory_space=pl.ANY)
 HBM = pl.BlockSpec(memory_space=pltpu.HBM)
 VMEM = pl.BlockSpec(memory_space=pltpu.VMEM)
@@ -203,28 +203,31 @@
     )(ratio, docs_held)
 
 
-def beta_piece(sizes, here, product, ratio, docs_held, prob_held, flips):
+def beta_pieces(sizes, here, product, ratio, docs_held, prob_held, flips):
     words, side_width = product.shape
     docs = docs_held.shape[0]
-    rows = words // len(flips)
-
-    def kernel(here_ref, product_ref, ratio_ref, doc_ref, prob_ref, out_ref):
+    rows = words // sum(map(len, flips))
+
+    def kernel(here_ref, product_ref, ratio_ref, doc_ref, prob_ref, *out_refs):
         columns = window(sizes.side(here_ref), side_width)
         topic_at = sizes.topic_at(here_ref)
         summed = product_ref[...] + jnp.dot(ratio_ref[...], doc_ref[...], preferred_element_type=F32)
-        for i, flip in enumerate(flips):
-            at = slice(i * rows, (i + 1) * rows)
-            prob = prob_ref[window(topic_at ^ flip, rows), columns].astype(F32)
-            out_ref[at, :] = (-prob * summed[at, :]).astype(BF16)
-
-    return pl.pallas_call(
-        kernel,
-        out_shape=jax.ShapeDtypeStruct((words, side_width), BF16),
+        chunk = 0
+        for piece, out_ref in zip(flips, out_refs):
+            for i, flip in enumerate(piece):
+                prob = prob_ref[window(topic_at ^ flip, rows), columns].astype(F32)
+                part = summed[chunk * rows : (chunk + 1) * rows, :]
+                out_ref[i * rows : (i + 1) * rows, :] = (-prob * part).astype(BF16)
+                chunk += 1
+
+    return pl.pallas_call(
+        kernel,
+        out_shape=[jax.ShapeDtypeStruct((rows * len(piece), side_width), BF16) for piece in flips],
         in_specs=[SMEM] + [VMEM] * 4,
-        out_specs=VMEM,
-        compiler_params=call_params(),
-        cost_estimate=cost(1, 1) if len(flips) > 1 else cost(2 * words * docs * side_width, 2 * (4 * words + docs) * side_width),
-        name="beta_piece",
+        out_specs=[VMEM] * len(flips),
+        compiler_params=call_params(),
+        cost_estimate=cost(2 * words * docs * side_width, 2 * (4 * words + docs) * side_width),
+        name="beta_pieces",
     )(here, product, ratio, docs_held, prob_held)
 
 
@@ -244,6 +247,24 @@
         cost_estimate=cost(0, 4 * len(parts) * rows * docs),
         name="stack_rows",
     )(*parts, *after)
+
+
+def cut_rows(array, count, after):
+    rows, width = array.shape[0] // count, array.shape[1]
+
+    def kernel(in_ref, *rest):
+        for i, out_ref in enumerate(rest[len(after) :]):
+            out_ref[...] = in_ref[i * rows : (i + 1) * rows, :]
+
+    return pl.pallas_call(
+        kernel,
+        out_shape=[jax.ShapeDtypeStruct((rows, width), array.dtype)] * count,
+        in_specs=[VMEM] + [ANY] * len(after),
+        out_specs=[VMEM] * count,
+        compiler_params=call_params(),
+        cost_estimate=cost(0, 4 * array.size),
+        name="cut_rows",
+    )(array, *after)
 
 
 def add_pair(own, other, after=()):
@@ -301,21 +322,21 @@
 
 def theta_grad(sizes, here, turned, prob_held, far_logits, log_norm):
     docs, words = turned[0].shape
-    half = words // 2
-    share = far_logits[0].shape[1]
+    cuts = len(far_logits[0])
+    rows, share = far_logits[0][0].shape
     count = len(turned)
     span = min(share, 512)
     blocks = share // span
 
     def kernel(here_ref, *refs):
         turned_refs, prob_ref = refs[:count], refs[count]
-        logit_refs, norm_ref = refs[count + 1 : 3 * count - 1], refs[3 * count - 1]
+        logit_refs, norm_ref = refs[count + 1 : -3], refs[-3]
         out_ref, done_ref = refs[-2:]
         done_ref[...] = jnp.zeros_like(done_ref)
         summed = jnp.dot(turned_refs[0][...], prob_ref[...], preferred_element_type=F32)
         for l in range(count - 1):
-            pair = logit_refs[2 * l : 2 * l + 2]
-            prob = jnp.concatenate([jnp.exp(ref[...].astype(F32) - norm_ref[...]).astype(BF16) for ref in pair], axis=0)
+            part = logit_refs[cuts * l : cuts * (l + 1)]
+            prob = jnp.concatenate([jnp.exp(ref[...].astype(F32) - norm_ref[...]).astype(BF16) for ref in part], axis=0)
             summed += jnp.dot(turned_refs[l + 1][...], prob, preferred_element_type=F32)
         out_ref[...] = summed
 
@@ -330,14 +351,14 @@
             grid=(blocks,),
             in_specs=[pl.BlockSpec((docs, words), whole)] * count
             + [pl.BlockSpec((words, span), held)]
-            + [pl.BlockSpec((half, span), column)] * (2 * count - 2)
+            + [pl.BlockSpec((rows, span), column)] * (cuts * (count - 1))
             + [pl.BlockSpec((1, span), held)],
             out_specs=[pl.BlockSpec((docs, span), column), pl.BlockSpec((8, 128), whole)],
         ),
         compiler_params=call_params(16),
         cost_estimate=cost(1, 1),
         name="theta_grad",
-    )(here, *turned, prob_held, *far_logits, log_norm)
+    )(here, *turned, prob_held, *sum(far_logits, []), log_norm)
 
 
 def place_pieces(sizes, here, own, other, flips, shape):
@@ -393,26 +414,30 @@
     arrived = [swap(parts[s], "topic", s) for s in order]
     counts = chunk_counts(sizes, here, word_counts, tile_doc, tile_word, docs, words)
     own_ratio = ratio_chunk([parts[0]] + arrived, counts, word_tile)
+    order.reverse()
     gathered = [swap(own_ratio, "topic", s) for s in order]
     far_bits = [1 << b for b in range(1, sizes.doc.bit_length() - 1)]
 
     def beta(ratio, flips, after):
-        part = beta_piece(sizes, here, own_product(ratio, docs_held), swap(ratio, "doc", 1), sibling_docs, prob_held, flips)
+        pieces = beta_pieces(
+            sizes, here, own_product(ratio, docs_held), swap(ratio, "doc", 1), sibling_docs, prob_held, flips
+        )
         for bit in far_bits[:-1]:
-            part = add_pair(part, swap(part, "doc", bit))
-        return part, swap(hold(part, after, HOLD_COST) if after else part, "doc", far_bits[-1])
-
-    flips = [[0], order]
-    pairs = [beta(own_ratio, flips[0], [])]
-    near_logits = [shift(hold(part, gathered[:1]), s) for s, part in enumerate(near_logits, 1)]
-    pairs.append(beta(stack_rows(gathered, []), flips[1], [pairs[0][1]]))
+            pieces = [add_pair(part, swap(part, "doc", bit)) for part in pieces]
+        sent = [hold(pieces[0], after, HOLD_COST) if after else pieces[0], *pieces[1:]]
+        return [(part, swap(copy, "doc", far_bits[-1])) for part, copy in zip(pieces, sent)]
+
+    flips = [[0]] + [piece for piece in (order[:-1], order[-1:]) if piece]
+    pairs = beta(own_ratio, flips[:1], [])
+    near_logits = [shift(hold(part, gathered[-1:]), s) for s, part in enumerate(near_logits, 1)]
+    pairs += beta(stack_rows(gathered, []), flips[1:], [pairs[0][1]])
 
     ratio = join_ratio(sizes, here, [own_ratio] + gathered, [0] + order, [pairs[1][0]])
     far_ratios = [shift(ratio, s) for s in range(1, sizes.vocab)]
     far_logits = []
     for part in near_logits:
-        part = hold(part, [pairs[1][0]])
-        far_logits += [part, swap(part, "doc", 1)]
+        pieces = list(cut_rows(part, 2, [pairs[1][0]]))
+        far_logits.append(pieces + [swap(piece, "doc", 1) for piece in pieces])
     turned = turn_ratios(sizes, here, ratio, far_ratios)
     theta, theta_done = theta_grad(sizes, here, turned, prob_held, far_logits, norm_held)
 

time: 55.5 us -> 51.6 us (0.930)
  waiting for transfers between devices: 24.9 us -> 18 us
  starting transfers between devices: 16.2 us -> 19.1 us
    ppermute x2, waiting for transfers between devices: 13.4 us -> 7.63 us  [shift(): lax.ppermute(array, 'vocab', [(i, (i + by) % sizes.vocab) for i in range(...]
    ppermute x14 -> x17, starting transfers between devices: 14 us -> 15.9 us  [swap(): return lax.ppermute(array, axis, [(i, i ^ bits) for i in range(count)])]
    ppermute x2, starting transfers between devices: 2.17 us -> 3.24 us  [shift(): lax.ppermute(array, 'vocab', [(i, (i + by) % sizes.vocab) for i in range(...]
    ppermute x14 -> x17, waiting for transfers between devices: 11.4 us -> 10.4 us  [swap(): return lax.ppermute(array, axis, [(i, i ^ bits) for i in range(count)])]
    pallas_call x2 -> x3, Pallas kernels: 1.13 us -> 1.15 us  [the longest x2 1.11 us: beta_pieces(): pl.pallas_call(kernel, out_shape=[jax.ShapeDtypeStruct((rows * len(piece)...]
  transfers between devices with their start and end apart: 16 -> 19, of which waited for: 9 -> 13; matrix products, arithmetic and copies ran while one was open for 0% -> 0% of each run, Pallas kernels for 13% -> 14%
where the time goes in v12:
time: 51.6 us; the launch traced here: 51.4 us
  starting transfers between devices  19.1 us (37%)
  waiting for transfers between devices  18 us (35%)
  Pallas kernels  13.5 us (26%)
  between operations  0.81 us (2%)
    ppermute x17, starting transfers between devices, swap(): return lax.ppermute(array, axis, [(i, i ^ bits) for i in range(count)])  15.9 us
    ppermute x17, waiting for transfers between devices, swap(): return lax.ppermute(array, axis, [(i, i ^ bits) for i in range(count)])  10.4 us
    ppermute x2, waiting for transfers between devices, shift(): lax.ppermute(array, 'vocab', [(i, (i + by) % sizes.vocab) for i in range(...  7.63 us
    pallas_call x1, Pallas kernels, rate_partial(): pl.pallas_call(kernel, out_shape=[jax.ShapeDtypeStruct((chunk, docs), BF1...  4.79 us
    pallas_call x1, Pallas kernels, theta_grad(): pl.pallas_call(kernel, out_shape=[jax.ShapeDtypeStruct((docs, share), F32...  3.65 us
    ppermute x2, starting transfers between devices, shift(): lax.ppermute(array, 'vocab', [(i, (i + by) % sizes.vocab) for i in range(...  3.24 us
    pallas_call x1, Pallas kernels, place_pieces(): pl.pallas_call(kernel, out_shape=jax.ShapeDtypeStruct(shape, BF16), in_sp...  1.37 us
    pallas_call x2, Pallas kernels, beta_pieces(): pl.pallas_call(kernel, out_shape=[jax.ShapeDtypeStruct((rows * len(piece)...  1.11 us
  transfers between devices with their start and end apart: 19, of which 13 were waited for; matrix products, arithmetic and copies ran while one was open for 0% of the time, Pallas kernels for 14%

profile of v12, /device:TPU:0, one launch (start us, length us, event | category | flops | bytes accessed | tf_op | source)
XLA Modules:
  0.0 51.4 jit_solution(14894417046893652371)
XLA Ops:
  0.6 4.8 %rate_partial.1 = (bf16[64,512]{1,0:T(8,128)(2,1)S(1)}, bf16[64,512]{1,0:T(8,128)(2,1)S(1)}, bf16[64,512]{1,0:T(8,128)(2,1)S(1)}, bf16[64,512]{1,0:T(8,128)(2,1)...) custom-call(s32[1]{0:T(128)} %bitcast.here_ref, ...), custom_call_target="tpu_custom_call" | custom-call | flops 1073741824 | bytes 6291456 | tf_op jit(solution)/shard_map/rate_partial/pallas_call | solution.py:99
  5.4 0.5 %collective-permute-start.7 = (bf16[512,2048]{1,0:T(8,128)(2,1)S(1)}, bf16[512,2048]{1,0:T(8,128)(2,1)S(1)}, u32[]{:S(2)}, u32[]{:S(2)}) collective-permute-start(bf16[512,2048]{1,0:T(8,128)(2,1)S(1)} %get-tuple-element.24), channel_id=1, source_target_pairs={{0,8},{8,0},{16,24},{24,16},{1,9},{9,1},{17,25},{25,17},{2,10},{10... | collective-permute-start | bytes 6291464 | tf_op jit(solution)/shard_map/ppermute | solution.py:407
  6.0 3.7 %collective-permute-start = (bf16[64,512]{1,0:T(8,128)(2,1)S(1)}, bf16[64,512]{1,0:T(8,128)(2,1)S(1)}, u32[]{:S(2)}, u32[]{:S(2)}) collective-permute-start(bf16[64,512]{1,0:T(8,128)(2,1)S(1)} %get-tuple-element.20), channel_id=1, source_target_pairs={{0,4},{2,6},{4,0},{6,2},{1,5},{3,7},{5,1},{7,3},{8,12},{10,14},{12... | collective-permute-start | bytes 196616 | tf_op jit(solution)/shard_map/ppermute | solution.py:407
  9.6 1.3 %collective-permute-start.1 = (bf16[64,512]{1,0:T(8,128)(2,1)S(1)}, bf16[64,512]{1,0:T(8,128)(2,1)S(1)}, u32[]{:S(2)}, u32[]{:S(2)}) collective-permute-start(bf16[64,512]{1,0:T(8,128)(2,1)S(1)} %get-tuple-element.21), channel_id=1, source_target_pairs={{0,6},{2,4},{4,2},{6,0},{1,7},{3,5},{5,3},{7,1},{8,14},{10,12},{12... | collective-permute-start | bytes 196616 | tf_op jit(solution)/shard_map/ppermute | solution.py:407
  11.2 0.8 %chunk_counts.1.refs_4_ = f32[64,512]{1,0:T(8,128)S(1)} custom-call(s32[1]{0:T(128)} %bitcast.here_ref, s32[16]{0:T(128)} %doc_at.1, s32[16]{0:T(128)} %word_at.1, s32[16,64,128]{2,1,0:T(8,128)S(1)} %copy-done), custom_call_target="tpu_custom_call" | custom-call | flops 131072 | bytes 524288 | tf_op jit(solution)/shard_map/chunk_counts/pallas_call | solution.py:138
  12.0 1.8 %collective-permute-done.refs_1_ = bf16[64,512]{1,0:T(8,128)(2,1)S(1)} collective-permute-done((bf16[64,512]{1,0:T(8,128)(2,1)S(1)}, bf16[64,512]{1,0:T(8,128)(2,1)S(1)}, u32[]{:S(2)}, u32[]{:S(2)}) %collective-permute-start) | collective-permute-done | bytes 65568 | tf_op jit(solution)/shard_map/ppermute | solution.py:407
  13.9 2.4 %collective-permute-done.1.refs_2_ = bf16[64,512]{1,0:T(8,128)(2,1)S(1)} collective-permute-done((bf16[64,512]{1,0:T(8,128)(2,1)S(1)}, bf16[64,512]{1,0:T(8,128)(2,1)S(1)}, u32[]{:S(2)}, u32[]{:S(2)}) %collective-permute-start.1) | collective-permute-done | bytes 65568 | tf_op jit(solution)/shard_map/ppermute | solution.py:407
  16.6 2.8 %collective-permute-start.5 = (bf16[64,512]{1,0:T(8,128)(2,1)S(1)}, bf16[64,512]{1,0:T(8,128)(2,1)S(1)}, u32[]{:S(2)}, u32[]{:S(2)}) collective-permute-start(bf16[64,512]{1,0:T(8,128)(2,1)S(1)} %ratio_chunk.1.refs_0_.ratio_ref), channel_id=1, source_target_pairs={{0,4},{2,6},{4,0},{6,2},{1,5},{3,7},{5,1},{7,3},{8,12},{10,14},{12... | collective-permute-start | bytes 196616 | tf_op jit(solution)/shard_map/ppermute | solution.py:407
  19.4 0.7 %collective-permute-start.4 = (bf16[64,512]{1,0:T(8,128)(2,1)S(1)}, bf16[64,512]{1,0:T(8,128)(2,1)S(1)}, u32[]{:S(2)}, u32[]{:S(2)}) collective-permute-start(bf16[64,512]{1,0:T(8,128)(2,1)S(1)} %ratio_chunk.1.refs_0_.ratio_ref), channel_id=1, source_target_pairs={{0,6},{2,4},{4,2},{6,0},{1,7},{3,5},{5,3},{7,1},{8,14},{10,12},{12... | collective-permute-start | bytes 196616 | tf_op jit(solution)/shard_map/ppermute | solution.py:407
  20.1 0.5 collective-permute-start.3
  20.6 0.5 own_product.3.product_ref
  21.1 0.5 beta_pieces.3.own_ref
  21.6 1.6 %collective-permute-start.13 = (bf16[64,2048]{1,0:T(8,128)(2,1)S(1)}, bf16[64,2048]{1,0:T(8,128)(2,1)S(1)}, u32[]{:S(2)}, u32[]{:S(2)}) collective-permute-start(bf16[64,2048]{1,0:T(8,128)(2,1)S(1)} %beta_pieces.3.own_ref), channel_id=1, source_target_pairs={{0,16},{8,24},{16,0},{24,8},{1,17},{9,25},{17,1},{25,9},{2,18},{10... | collective-permute-start | bytes 786440 | tf_op jit(solution)/shard_map/ppermute | solution.py:407
  23.2 0.7 %collective-permute-done.5.refs_2_.refs_3_.rest_0_ = bf16[64,512]{1,0:T(8,128)(2,1)S(1)} collective-permute-done((bf16[64,512]{1,0:T(8,128)(2,1)S(1)}, bf16[64,512]{1,0:T(8,128)(2,1)S(1)}, u32[]{:S(2)}, u32[]{:S(2)}) %collective-permute-start.5) | collective-permute-done | bytes 65568 | tf_op jit(solution)/shard_map/ppermute | solution.py:407
  23.9 1.7 %collective-permute-start.9 = (bf16[128,2048]{1,0:T(8,128)(2,1)S(1)}, bf16[128,2048]{1,0:T(8,128)(2,1)S(1)}, u32[]{:S(2)}, u32[]{:S(2)}) collective-permute-start(bf16[128,2048]{1,0:T(8,128)(2,1)S(1)} %hold.2), channel_id=1, source_target_pairs={{0,1},{1,0},{2,3},{3,2},{4,5},{5,4},{6,7},{7,6},{8,9},{9,8},{10,11... | collective-permute-start | bytes 1572872 | tf_op jit(solution)/shard_map/ppermute | solution.py:403
  25.6 0.5 %collective-permute-done.4.refs_1_.refs_2_ = bf16[64,512]{1,0:T(8,128)(2,1)S(1)} collective-permute-done((bf16[64,512]{1,0:T(8,128)(2,1)S(1)}, bf16[64,512]{1,0:T(8,128)(2,1)S(1)}, u32[]{:S(2)}, u32[]{:S(2)}) %collective-permute-start.4) | collective-permute-done | bytes 65568 | tf_op jit(solution)/shard_map/ppermute | solution.py:407
  26.4 0.6 %own_product.2.product_ref = f32[192,2048]{1,0:T(8,128)S(1)} custom-call(bf16[192,512]{1,0:T(8,128)(2,1)S(1)} %stack_rows.1.ratio_ref, bf16[512,2048]{1,0:T(8,128)(2,1)S(1)} %get-tuple-element.23.doc_ref), custom_call_target="tpu_custom_call" | custom-call | flops 402653184 | bytes 3670016 | tf_op jit(solution)/shard_map/own_product/pallas_call | solution.py:195
  27.0 0.8 %collective-permute-done.6.ratio_ref = bf16[192,512]{1,0:T(8,128)(2,1)S(1)} collective-permute-done((bf16[192,512]{1,0:T(8,128)(2,1)S(1)}, bf16[192,512]{1,0:T(8,128)(2,1)S(1)}, u32[]{:S(2)}, u32[]{:S(2)}) %collective-permute-start.6) | collective-permute-done | bytes 196640 | tf_op jit(solution)/shard_map/ppermute | solution.py:407
  27.8 0.6 %beta_pieces.2 = (bf16[128,2048]{1,0:T(8,128)(2,1)S(1)}, bf16[64,2048]{1,0:T(8,128)(2,1)S(1)}) custom-call(s32[1]{0:T(128)} %bitcast.here_ref, f32[192,2048]{1,0:T(8,128)S(1)} %own_product.2.product_ref, bf16[192,512]{1,0:T(8,128)(2,1)S(1)} %collective-permute-done.6.ratio_ref, bf16[512,2048]{1,0:T(8,128)(2,1)S(1)} %collective-permute-done.7.doc_ref, ...), custom_call_target="tpu_custom_call" | custom-call | flops 402653184 | bytes 5242880 | tf_op jit(solution)/shard_map/beta_pieces/pallas_call | solution.py:223
  28.4 1.3 %collective-permute-done.13.other_ref.rest_0_ = bf16[64,2048]{1,0:T(8,128)(2,1)S(1)} collective-permute-done((bf16[64,2048]{1,0:T(8,128)(2,1)S(1)}, bf16[64,2048]{1,0:T(8,128)(2,1)S(1)}, u32[]{:S(2)}, u32[]{:S(2)}) %collective-permute-start.13) | collective-permute-done | bytes 262176 | tf_op jit(solution)/shard_map/ppermute | solution.py:407
  29.8 1.6 %collective-permute-start.14 = (bf16[128,2048]{1,0:T(8,128)(2,1)S(1)}, bf16[128,2048]{1,0:T(8,128)(2,1)S(1)}, u32[]{:S(2)}, u32[]{:S(2)}) collective-permute-start(bf16[128,2048]{1,0:T(8,128)(2,1)S(1)} %hold.3), channel_id=1, source_target_pairs={{0,16},{8,24},{16,0},{24,8},{1,17},{9,25},{17,1},{25,9},{2,18},{10... | collective-permute-start | bytes 1572872 | tf_op jit(solution)/shard_map/ppermute | solution.py:407
  31.4 1.6 %collective-permute-start.8 = (bf16[256,512]{1,0:T(8,128)(2,1)S(1)}, bf16[256,512]{1,0:T(8,128)(2,1)S(1)}, u32[]{:S(2)}, u32[]{:S(2)}) collective-permute-start(bf16[256,512]{1,0:T(8,128)(2,1)S(1)} %join_ratio.1.refs_0_), channel_id=1, source_target_pairs={{0,1},{1,0},{2,3},{3,2},{4,5},{5,4},{6,7},{7,6},{8,9},{9,8},{10,11... | collective-permute-start | bytes 786440 | tf_op jit(solution)/shard_map/ppermute | solution.py:403
  33.0 5.8 %collective-permute-done.9.in_ref = bf16[128,2048]{1,0:T(8,128)(2,1)S(1)} collective-permute-done((bf16[128,2048]{1,0:T(8,128)(2,1)S(1)}, bf16[128,2048]{1,0:T(8,128)(2,1)S(1)}, u32[]{:S(2)}, u32[]{:S(2)}) %collective-permute-start.9) | collective-permute-done | bytes 524320 | tf_op jit(solution)/shard_map/ppermute | solution.py:403
  39.0 0.5 collective-permute-start.11
  39.5 1.6 %collective-permute-start.15 = (bf16[64,2048]{1,0:T(8,128)(2,1)S(1)}, bf16[64,2048]{1,0:T(8,128)(2,1)S(1)}, u32[]{:S(2)}, u32[]{:S(2)}) collective-permute-start(bf16[64,2048]{1,0:T(8,128)(2,1)S(1)} %get-tuple-element.35.own_ref), channel_id=1, source_target_pairs={{0,16},{8,24},{16,0},{24,8},{1,17},{9,25},{17,1},{25,9},{2,18},{10... | collective-permute-start | bytes 786440 | tf_op jit(solution)/shard_map/ppermute | solution.py:407
  41.0 1.8 %collective-permute-done.8.refs_1_ = bf16[256,512]{1,0:T(8,128)(2,1)S(1)} collective-permute-done((bf16[256,512]{1,0:T(8,128)(2,1)S(1)}, bf16[256,512]{1,0:T(8,128)(2,1)S(1)}, u32[]{:S(2)}, u32[]{:S(2)}) %collective-permute-start.8) | collective-permute-done | bytes 262176 | tf_op jit(solution)/shard_map/ppermute | solution.py:403
  43.1 3.7 %theta_grad.1 = (f32[512,2048]{1,0:T(8,128)}, f32[8,128]{1,0:T(8,128)S(1)}) custom-call(s32[1]{0:T(128)} %bitcast.here_ref, bf16[512,256]{1,0:T(8,128)(2,1)S(1)} %get-tuple-element.27.refs_0_, bf16[512,256]{1,0:T(8,128)(2,1)S(1)} %get-tuple-element.28.refs_1_, bf16[256,4096]{1,0:T(8,128)(2,1)S(1)} %get-tuple-element.25.prob_ref.refs_2_, ...), custom_call_target="tpu_custom_call" | custom-call | flops 1 | bytes 1 | tf_op jit(solution)/shard_map/theta_grad/pallas_call | solution.py:346
  47.0 0.6 %collective-permute-start.16 = (bf16[64,2048]{1,0:T(8,128)(2,1)S(1)}, bf16[64,2048]{1,0:T(8,128)(2,1)S(1)}, u32[]{:S(2)}, u32[]{:S(2)}) collective-permute-start(bf16[64,2048]{1,0:T(8,128)(2,1)S(1)} %add_pair.3.refs_0_), channel_id=1, source_target_pairs={{0,8},{8,0},{16,24},{24,16},{1,9},{9,1},{17,25},{25,17},{2,10},{10... | collective-permute-start | bytes 786440 | tf_op jit(solution)/shard_map/ppermute | solution.py:407
  47.5 0.8 %collective-permute-done.15.other_ref = bf16[64,2048]{1,0:T(8,128)(2,1)S(1)} collective-permute-done((bf16[64,2048]{1,0:T(8,128)(2,1)S(1)}, bf16[64,2048]{1,0:T(8,128)(2,1)S(1)}, u32[]{:S(2)}, u32[]{:S(2)}) %collective-permute-start.15) | collective-permute-done | bytes 262176 | tf_op jit(solution)/shard_map/ppermute | solution.py:407
  48.5 0.7 %collective-permute-done.16.refs_3_ = bf16[64,2048]{1,0:T(8,128)(2,1)S(1)} collective-permute-done((bf16[64,2048]{1,0:T(8,128)(2,1)S(1)}, bf16[64,2048]{1,0:T(8,128)(2,1)S(1)}, u32[]{:S(2)}, u32[]{:S(2)}) %collective-permute-start.16) | collective-permute-done | bytes 262176 | tf_op jit(solution)/shard_map/ppermute | solution.py:407
  49.2 0.8 %collective-permute-done.18.refs_5_ = bf16[64,2048]{1,0:T(8,128)(2,1)S(1)} collective-permute-done((bf16[64,2048]{1,0:T(8,128)(2,1)S(1)}, bf16[64,2048]{1,0:T(8,128)(2,1)S(1)}, u32[]{:S(2)}, u32[]{:S(2)}) %collective-permute-start.18) | collective-permute-done | bytes 262176 | tf_op jit(solution)/shard_map/ppermute | solution.py:407
  50.0 1.4 %place_pieces.1 = bf16[256,4096]{1,0:T(8,128)(2,1)} custom-call(s32[1]{0:T(128)} %bitcast.here_ref, bf16[64,2048]{1,0:T(8,128)(2,1)S(1)} %add_pair.3.refs_0_, bf16[128,2048]{1,0:T(8,128)(2,1)S(1)} %add_pair.4.refs_1_, bf16[64,2048]{1,0:T(8,128)(2,1)S(1)} %add_pair.5.refs_2_, bf16[64,2048]{1,0:T(8,128)(2,1)S(1)} %collective-permute-done.16.refs_3_, ...), custom_call_target="tpu_custom_call" | custom-call | bytes 4194304 | tf_op jit(solution)/shard_map/place_pieces/pallas_call | solution.py:384
  (26 shorter events, 1.6 us)
Async XLA Ops:
  0.6 10.6 %copy-start = (s32[16,64,128]{2,1,0:T(8,128)S(1)}, s32[16,64,128]{2,1,0:T(8,128)}, u32[]{:S(2)}) copy-start(s32[16,64,128]{2,1,0:T(8,128)} %count_ref.1) | copy-start | bytes 1572868
  5.4 15.7 %collective-permute-start.7 = (bf16[512,2048]{1,0:T(8,128)(2,1)S(1)}, bf16[512,2048]{1,0:T(8,128)(2,1)S(1)}, u32[]{:S(2)}, u32[]{:S(2)}) collective-permute-start(bf16[512,2048]{1,0:T(8,128)(2,1)S(1)} %get-tuple-element.24), channel_id=1, source_target_pairs={{0,8},{8,0},{16,24},{24,16},{1,9},{9,1},{17,25},{25,17},{2,10},{10... | collective-permute-start | bytes 6291464 | tf_op jit(solution)/shard_map/ppermute | solution.py:407
  6.0 7.9 %collective-permute-start = (bf16[64,512]{1,0:T(8,128)(2,1)S(1)}, bf16[64,512]{1,0:T(8,128)(2,1)S(1)}, u32[]{:S(2)}, u32[]{:S(2)}) collective-permute-start(bf16[64,512]{1,0:T(8,128)(2,1)S(1)} %get-tuple-element.20), channel_id=1, source_target_pairs={{0,4},{2,6},{4,0},{6,2},{1,5},{3,7},{5,1},{7,3},{8,12},{10,14},{12... | collective-permute-start | bytes 196616 | tf_op jit(solution)/shard_map/ppermute | solution.py:407
  9.6 6.7 %collective-permute-start.1 = (bf16[64,512]{1,0:T(8,128)(2,1)S(1)}, bf16[64,512]{1,0:T(8,128)(2,1)S(1)}, u32[]{:S(2)}, u32[]{:S(2)}) collective-permute-start(bf16[64,512]{1,0:T(8,128)(2,1)S(1)} %get-tuple-element.21), channel_id=1, source_target_pairs={{0,6},{2,4},{4,2},{6,0},{1,7},{3,5},{5,3},{7,1},{8,14},{10,12},{12... | collective-permute-start | bytes 196616 | tf_op jit(solution)/shard_map/ppermute | solution.py:407
  11.0 5.5 %collective-permute-start.2 = (bf16[64,512]{1,0:T(8,128)(2,1)S(1)}, bf16[64,512]{1,0:T(8,128)(2,1)S(1)}, u32[]{:S(2)}, u32[]{:S(2)}) collective-permute-start(bf16[64,512]{1,0:T(8,128)(2,1)S(1)} %get-tuple-element.22), channel_id=1, source_target_pairs={{0,2},{2,0},{4,6},{6,4},{1,3},{3,1},{5,7},{7,5},{8,10},{10,8},{12,... | collective-permute-start | bytes 196616 | tf_op jit(solution)/shard_map/ppermute | solution.py:407
  16.5 4.6 %collective-permute-start.12 = (bf16[64,512]{1,0:T(8,128)(2,1)S(1)}, bf16[64,512]{1,0:T(8,128)(2,1)S(1)}, u32[]{:S(2)}, u32[]{:S(2)}) collective-permute-start(bf16[64,512]{1,0:T(8,128)(2,1)S(1)} %ratio_chunk.1.refs_0_.ratio_ref), channel_id=1, source_target_pairs={{0,8},{8,0},{16,24},{24,16},{1,9},{9,1},{17,25},{25,17},{2,10},{10... | collective-permute-start | bytes 196616 | tf_op jit(solution)/shard_map/ppermute | solution.py:407
  16.6 7.3 %collective-permute-start.5 = (bf16[64,512]{1,0:T(8,128)(2,1)S(1)}, bf16[64,512]{1,0:T(8,128)(2,1)S(1)}, u32[]{:S(2)}, u32[]{:S(2)}) collective-permute-start(bf16[64,512]{1,0:T(8,128)(2,1)S(1)} %ratio_chunk.1.refs_0_.ratio_ref), channel_id=1, source_target_pairs={{0,4},{2,6},{4,0},{6,2},{1,5},{3,7},{5,1},{7,3},{8,12},{10,14},{12... | collective-permute-start | bytes 196616 | tf_op jit(solution)/shard_map/ppermute | solution.py:407
  19.4 6.7 %collective-permute-start.4 = (bf16[64,512]{1,0:T(8,128)(2,1)S(1)}, bf16[64,512]{1,0:T(8,128)(2,1)S(1)}, u32[]{:S(2)}, u32[]{:S(2)}) collective-permute-start(bf16[64,512]{1,0:T(8,128)(2,1)S(1)} %ratio_chunk.1.refs_0_.ratio_ref), channel_id=1, source_target_pairs={{0,6},{2,4},{4,2},{6,0},{1,7},{3,5},{5,3},{7,1},{8,14},{10,12},{12... | collective-permute-start | bytes 196616 | tf_op jit(solution)/shard_map/ppermute | solution.py:407
  20.1 6.1 %collective-permute-start.3 = (bf16[64,512]{1,0:T(8,128)(2,1)S(1)}, bf16[64,512]{1,0:T(8,128)(2,1)S(1)}, u32[]{:S(2)}, u32[]{:S(2)}) collective-permute-start(bf16[64,512]{1,0:T(8,128)(2,1)S(1)} %ratio_chunk.1.refs_0_.ratio_ref), channel_id=1, source_target_pairs={{0,2},{2,0},{4,6},{6,4},{1,3},{3,1},{5,7},{7,5},{8,10},{10,8},{12,... | collective-permute-start | bytes 196616 | tf_op jit(solution)/shard_map/ppermute | solution.py:407
  21.6 8.2 %collective-permute-start.13 = (bf16[64,2048]{1,0:T(8,128)(2,1)S(1)}, bf16[64,2048]{1,0:T(8,128)(2,1)S(1)}, u32[]{:S(2)}, u32[]{:S(2)}) collective-permute-start(bf16[64,2048]{1,0:T(8,128)(2,1)S(1)} %beta_pieces.3.own_ref), channel_id=1, source_target_pairs={{0,16},{8,24},{16,0},{24,8},{1,17},{9,25},{17,1},{25,9},{2,18},{10... | collective-permute-start | bytes 786440 | tf_op jit(solution)/shard_map/ppermute | solution.py:407
  23.9 14.9 %collective-permute-start.9 = (bf16[128,2048]{1,0:T(8,128)(2,1)S(1)}, bf16[128,2048]{1,0:T(8,128)(2,1)S(1)}, u32[]{:S(2)}, u32[]{:S(2)}) collective-permute-start(bf16[128,2048]{1,0:T(8,128)(2,1)S(1)} %hold.2), channel_id=1, source_target_pairs={{0,1},{1,0},{2,3},{3,2},{4,5},{5,4},{6,7},{7,6},{8,9},{9,8},{10,11... | collective-permute-start | bytes 1572872 | tf_op jit(solution)/shard_map/ppermute | solution.py:403
  26.3 1.5 %collective-permute-start.6 = (bf16[192,512]{1,0:T(8,128)(2,1)S(1)}, bf16[192,512]{1,0:T(8,128)(2,1)S(1)}, u32[]{:S(2)}, u32[]{:S(2)}) collective-permute-start(bf16[192,512]{1,0:T(8,128)(2,1)S(1)} %stack_rows.1.ratio_ref), channel_id=1, source_target_pairs={{0,8},{8,0},{16,24},{24,16},{1,9},{9,1},{17,25},{25,17},{2,10},{10... | collective-permute-start | bytes 589832 | tf_op jit(solution)/shard_map/ppermute | solution.py:407
  29.8 16.9 %collective-permute-start.14 = (bf16[128,2048]{1,0:T(8,128)(2,1)S(1)}, bf16[128,2048]{1,0:T(8,128)(2,1)S(1)}, u32[]{:S(2)}, u32[]{:S(2)}) collective-permute-start(bf16[128,2048]{1,0:T(8,128)(2,1)S(1)} %hold.3), channel_id=1, source_target_pairs={{0,16},{8,24},{16,0},{24,8},{1,17},{9,25},{17,1},{25,9},{2,18},{10... | collective-permute-start | bytes 1572872 | tf_op jit(solution)/shard_map/ppermute | solution.py:407
  31.4 11.4 %collective-permute-start.8 = (bf16[256,512]{1,0:T(8,128)(2,1)S(1)}, bf16[256,512]{1,0:T(8,128)(2,1)S(1)}, u32[]{:S(2)}, u32[]{:S(2)}) collective-permute-start(bf16[256,512]{1,0:T(8,128)(2,1)S(1)} %join_ratio.1.refs_0_), channel_id=1, source_target_pairs={{0,1},{1,0},{2,3},{3,2},{4,5},{5,4},{6,7},{7,6},{8,9},{9,8},{10,11... | collective-permute-start | bytes 786440 | tf_op jit(solution)/shard_map/ppermute | solution.py:403
  38.9 4.2 %collective-permute-start.10 = (bf16[64,2048]{1,0:T(8,128)(2,1)S(1)}, bf16[64,2048]{1,0:T(8,128)(2,1)S(1)}, u32[]{:S(2)}, u32[]{:S(2)}) collective-permute-start(bf16[64,2048]{1,0:T(8,128)(2,1)S(1)} %get-tuple-element.30.refs_3_), channel_id=1, source_target_pairs={{0,8},{8,0},{16,24},{24,16},{1,9},{9,1},{17,25},{25,17},{2,10},{10... | collective-permute-start | bytes 786440 | tf_op jit(solution)/shard_map/ppermute | solution.py:407
  39.0 4.1 %collective-permute-start.11 = (bf16[64,2048]{1,0:T(8,128)(2,1)S(1)}, bf16[64,2048]{1,0:T(8,128)(2,1)S(1)}, u32[]{:S(2)}, u32[]{:S(2)}) collective-permute-start(bf16[64,2048]{1,0:T(8,128)(2,1)S(1)} %get-tuple-element.31.refs_4_), channel_id=1, source_target_pairs={{0,8},{8,0},{16,24},{24,16},{1,9},{9,1},{17,25},{25,17},{2,10},{10... | collective-permute-start | bytes 786440 | tf_op jit(solution)/shard_map/ppermute | solution.py:407
  39.5 8.9 %collective-permute-start.15 = (bf16[64,2048]{1,0:T(8,128)(2,1)S(1)}, bf16[64,2048]{1,0:T(8,128)(2,1)S(1)}, u32[]{:S(2)}, u32[]{:S(2)}) collective-permute-start(bf16[64,2048]{1,0:T(8,128)(2,1)S(1)} %get-tuple-element.35.own_ref), channel_id=1, source_target_pairs={{0,16},{8,24},{16,0},{24,8},{1,17},{9,25},{17,1},{25,9},{2,18},{10... | collective-permute-start | bytes 786440 | tf_op jit(solution)/shard_map/ppermute | solution.py:407
  46.8 3.2 %collective-permute-start.17 = (bf16[128,2048]{1,0:T(8,128)(2,1)S(1)}, bf16[128,2048]{1,0:T(8,128)(2,1)S(1)}, u32[]{:S(2)}, u32[]{:S(2)}) collective-permute-start(bf16[128,2048]{1,0:T(8,128)(2,1)S(1)} %add_pair.4.refs_1_), channel_id=1, source_target_pairs={{0,8},{8,0},{16,24},{24,16},{1,9},{9,1},{17,25},{25,17},{2,10},{10... | collective-permute-start | bytes 1572872 | tf_op jit(solution)/shard_map/ppermute | solution.py:407
  47.0 2.2 %collective-permute-start.16 = (bf16[64,2048]{1,0:T(8,128)(2,1)S(1)}, bf16[64,2048]{1,0:T(8,128)(2,1)S(1)}, u32[]{:S(2)}, u32[]{:S(2)}) collective-permute-start(bf16[64,2048]{1,0:T(8,128)(2,1)S(1)} %add_pair.3.refs_0_), channel_id=1, source_target_pairs={{0,8},{8,0},{16,24},{24,16},{1,9},{9,1},{17,25},{25,17},{2,10},{10... | collective-permute-start | bytes 786440 | tf_op jit(solution)/shard_map/ppermute | solution.py:407
  48.4 1.6 %collective-permute-start.18 = (bf16[64,2048]{1,0:T(8,128)(2,1)S(1)}, bf16[64,2048]{1,0:T(8,128)(2,1)S(1)}, u32[]{:S(2)}, u32[]{:S(2)}) collective-permute-start(bf16[64,2048]{1,0:T(8,128)(2,1)S(1)} %add_pair.5.refs_2_), channel_id=1, source_target_pairs={{0,8},{8,0},{16,24},{24,16},{1,9},{9,1},{17,25},{25,17},{2,10},{10... | collective-permute-start | bytes 786440 | tf_op jit(solution)/shard_map/ppermute | solution.py:407

commit v13 on v12

--- a/solution.py
+++ b/solution.py
@@ -52,7 +52,7 @@
     docs, width = doc_topics.shape
     words = word_logits.shape[0]
     side_width = width // 2
-    span = min(side_width, 1024)
+    span = min(side_width, 512)
     steps = side_width // span
     count, far = sizes.topic, sizes.vocab - 1
     chunk, half, share = words // count, words // 2, width // sizes.vocab
@@ -63,31 +63,35 @@
         side = sizes.side(here_ref)
         norm_copy = pltpu.make_async_copy(norm_in, norm_ref, norm_sem)
         norm_copy.start()
-        blocks = []
-        for which, doc_ref in ((1 - side, sibling_ref), (side, own_ref)):
-            for j in range(steps):
-                at = window(which * steps + j, span)
-                i = len(blocks)
-                logit_copy = pltpu.make_async_copy(logit_in.at[:, at], logit_ref.at[:, at], sems.at[0, i])
-                held = doc_ref.at[:, pl.ds(j * span, span)]
-                doc_copy = pltpu.make_async_copy(doc_in.at[:, at], held, sems.at[1, i])
-                blocks.append((at, logit_copy, doc_copy, held))
-        for _, logit_copy, doc_copy, _ in blocks:
-            logit_copy.start()
-            doc_copy.start()
+
+        def block(which, doc_ref, h, j):
+            at = window(which * steps + j, span)
+            held = doc_ref.at[:, window(j, span)]
+            logit_copy = pltpu.make_async_copy(logit_in.at[:, at], logit_ref.at[:, at], sems.at[0, h * steps + j])
+            return at, held, logit_copy, pltpu.make_async_copy(doc_in.at[:, at], held, sems.at[1, h * steps + j])
+
+        sides = ((1 - side, sibling_ref), (side, own_ref))
+        for h, (which, doc_ref) in enumerate(sides):
+            @pl.loop(0, steps)
+            def _(j):
+                _, _, logit_copy, doc_copy = block(which, doc_ref, h, j)
+                logit_copy.start()
+                doc_copy.start()
+
+        acc[...] = jnp.zeros_like(acc)
         norm_copy.wait()
-        for i, (at, logit_copy, doc_copy, held) in enumerate(blocks):
-            logit_copy.wait()
-            prob = jnp.exp(logit_ref[:, at].astype(F32) - norm_ref[:, at]).astype(BF16)
-            prob_ref[:, at] = prob
-            doc_copy.wait()
-            part = lax.dot_general(
-                prob, held[...], (((1,), (1,)), ((), ())), preferred_element_type=F32
-            )
-            if i == 0:
-                acc[...] = part
-            else:
-                acc[...] += part
+        for h, (which, doc_ref) in enumerate(sides):
+            @pl.loop(0, steps)
+            def _(j):
+                at, held, logit_copy, doc_copy = block(which, doc_ref, h, j)
+                logit_copy.wait()
+                prob = jnp.exp(logit_ref[:, at].astype(F32) - norm_ref[:, at]).astype(BF16)
+                prob_ref[:, at] = prob
+                doc_copy.wait()
+                acc[...] += lax.dot_general(
+                    prob, held[...], (((1,), (1,)), ((), ())), preferred_element_type=F32
+                )
+
         topic_at = sizes.topic_at(here_ref)
         for s in range(count):
             parts[s][...] = acc[window(topic_at ^ s, chunk), :].astype(BF16)

time: 51.6 us -> 51.6 us (level)
  no operation moved by 1% of the time
where the time goes in v13:
time: 51.6 us; the launch traced here: 51.4 us
  starting transfers between devices  19.1 us (37%)
  waiting for transfers between devices  18 us (35%)
  Pallas kernels  13.5 us (26%)
  between operations  0.81 us (2%)
    ppermute x17, starting transfers between devices, swap(): return lax.ppermute(array, axis, [(i, i ^ bits) for i in range(count)])  15.8 us
    ppermute x17, waiting for transfers between devices, swap(): return lax.ppermute(array, axis, [(i, i ^ bits) for i in range(count)])  10.4 us
    ppermute x2, waiting for transfers between devices, shift(): lax.ppermute(array, 'vocab', [(i, (i + by) % sizes.vocab) for i in range(...  7.64 us
    pallas_call x1, Pallas kernels, rate_partial(): pl.pallas_call(kernel, out_shape=[jax.ShapeDtypeStruct((chunk, docs), BF1...  4.78 us
    pallas_call x1, Pallas kernels, theta_grad(): pl.pallas_call(kernel, out_shape=[jax.ShapeDtypeStruct((docs, share), F32...  3.65 us
    ppermute x2, starting transfers between devices, shift(): lax.ppermute(array, 'vocab', [(i, (i + by) % sizes.vocab) for i in range(...  3.25 us
    pallas_call x1, Pallas kernels, place_pieces(): pl.pallas_call(kernel, out_shape=jax.ShapeDtypeStruct(shape, BF16), in_sp...  1.37 us
    pallas_call x2, Pallas kernels, beta_pieces(): pl.pallas_call(kernel, out_shape=[jax.ShapeDtypeStruct((rows * len(piece)...  1.11 us
  transfers between devices with their start and end apart: 19, of which 13 were waited for; matrix products, arithmetic and copies ran while one was open for 0% of the time, Pallas kernels for 14%

profile of v13, /device:TPU:0, one launch (start us, length us, event | category | flops | bytes accessed | tf_op | source)
XLA Modules:
  0.0 51.4 jit_solution(16264215732081744927)
XLA Ops:
  0.6 4.8 %rate_partial.1 = (bf16[64,512]{1,0:T(8,128)(2,1)S(1)}, bf16[64,512]{1,0:T(8,128)(2,1)S(1)}, bf16[64,512]{1,0:T(8,128)(2,1)S(1)}, bf16[64,512]{1,0:T(8,128)(2,1)...) custom-call(s32[1]{0:T(128)} %bitcast.here_ref, ...), custom_call_target="tpu_custom_call" | custom-call | flops 1073741824 | bytes 6291456 | tf_op jit(solution)/shard_map/rate_partial/pallas_call | solution.py:103
  5.4 0.5 %collective-permute-start.7 = (bf16[512,2048]{1,0:T(8,128)(2,1)S(1)}, bf16[512,2048]{1,0:T(8,128)(2,1)S(1)}, u32[]{:S(2)}, u32[]{:S(2)}) collective-permute-start(bf16[512,2048]{1,0:T(8,128)(2,1)S(1)} %get-tuple-element.24), channel_id=1, source_target_pairs={{0,8},{8,0},{16,24},{24,16},{1,9},{9,1},{17,25},{25,17},{2,10},{10... | collective-permute-start | bytes 6291464 | tf_op jit(solution)/shard_map/ppermute | solution.py:411
  6.0 3.7 %collective-permute-start = (bf16[64,512]{1,0:T(8,128)(2,1)S(1)}, bf16[64,512]{1,0:T(8,128)(2,1)S(1)}, u32[]{:S(2)}, u32[]{:S(2)}) collective-permute-start(bf16[64,512]{1,0:T(8,128)(2,1)S(1)} %get-tuple-element.20), channel_id=1, source_target_pairs={{0,4},{2,6},{4,0},{6,2},{1,5},{3,7},{5,1},{7,3},{8,12},{10,14},{12... | collective-permute-start | bytes 196616 | tf_op jit(solution)/shard_map/ppermute | solution.py:411
  9.6 1.3 %collective-permute-start.1 = (bf16[64,512]{1,0:T(8,128)(2,1)S(1)}, bf16[64,512]{1,0:T(8,128)(2,1)S(1)}, u32[]{:S(2)}, u32[]{:S(2)}) collective-permute-start(bf16[64,512]{1,0:T(8,128)(2,1)S(1)} %get-tuple-element.21), channel_id=1, source_target_pairs={{0,6},{2,4},{4,2},{6,0},{1,7},{3,5},{5,3},{7,1},{8,14},{10,12},{12... | collective-permute-start | bytes 196616 | tf_op jit(solution)/shard_map/ppermute | solution.py:411
  11.2 0.8 %chunk_counts.1.refs_4_ = f32[64,512]{1,0:T(8,128)S(1)} custom-call(s32[1]{0:T(128)} %bitcast.here_ref, s32[16]{0:T(128)} %doc_at.1, s32[16]{0:T(128)} %word_at.1, s32[16,64,128]{2,1,0:T(8,128)S(1)} %copy-done), custom_call_target="tpu_custom_call" | custom-call | flops 131072 | bytes 524288 | tf_op jit(solution)/shard_map/chunk_counts/pallas_call | solution.py:142
  12.0 1.8 %collective-permute-done.refs_1_ = bf16[64,512]{1,0:T(8,128)(2,1)S(1)} collective-permute-done((bf16[64,512]{1,0:T(8,128)(2,1)S(1)}, bf16[64,512]{1,0:T(8,128)(2,1)S(1)}, u32[]{:S(2)}, u32[]{:S(2)}) %collective-permute-start) | collective-permute-done | bytes 65568 | tf_op jit(solution)/shard_map/ppermute | solution.py:411
  13.9 2.4 %collective-permute-done.1.refs_2_ = bf16[64,512]{1,0:T(8,128)(2,1)S(1)} collective-permute-done((bf16[64,512]{1,0:T(8,128)(2,1)S(1)}, bf16[64,512]{1,0:T(8,128)(2,1)S(1)}, u32[]{:S(2)}, u32[]{:S(2)}) %collective-permute-start.1) | collective-permute-done | bytes 65568 | tf_op jit(solution)/shard_map/ppermute | solution.py:411
  16.6 2.8 %collective-permute-start.5 = (bf16[64,512]{1,0:T(8,128)(2,1)S(1)}, bf16[64,512]{1,0:T(8,128)(2,1)S(1)}, u32[]{:S(2)}, u32[]{:S(2)}) collective-permute-start(bf16[64,512]{1,0:T(8,128)(2,1)S(1)} %ratio_chunk.1.refs_0_.ratio_ref), channel_id=1, source_target_pairs={{0,4},{2,6},{4,0},{6,2},{1,5},{3,7},{5,1},{7,3},{8,12},{10,14},{12... | collective-permute-start | bytes 196616 | tf_op jit(solution)/shard_map/ppermute | solution.py:411
  19.4 0.7 %collective-permute-start.4 = (bf16[64,512]{1,0:T(8,128)(2,1)S(1)}, bf16[64,512]{1,0:T(8,128)(2,1)S(1)}, u32[]{:S(2)}, u32[]{:S(2)}) collective-permute-start(bf16[64,512]{1,0:T(8,128)(2,1)S(1)} %ratio_chunk.1.refs_0_.ratio_ref), channel_id=1, source_target_pairs={{0,6},{2,4},{4,2},{6,0},{1,7},{3,5},{5,3},{7,1},{8,14},{10,12},{12... | collective-permute-start | bytes 196616 | tf_op jit(solution)/shard_map/ppermute | solution.py:411
  20.1 0.5 collective-permute-start.3
  20.6 0.5 own_product.3.product_ref
  21.1 0.5 beta_pieces.3.own_ref
  21.6 1.6 %collective-permute-start.13 = (bf16[64,2048]{1,0:T(8,128)(2,1)S(1)}, bf16[64,2048]{1,0:T(8,128)(2,1)S(1)}, u32[]{:S(2)}, u32[]{:S(2)}) collective-permute-start(bf16[64,2048]{1,0:T(8,128)(2,1)S(1)} %beta_pieces.3.own_ref), channel_id=1, source_target_pairs={{0,16},{8,24},{16,0},{24,8},{1,17},{9,25},{17,1},{25,9},{2,18},{10... | collective-permute-start | bytes 786440 | tf_op jit(solution)/shard_map/ppermute | solution.py:411
  23.2 0.7 %collective-permute-done.5.refs_2_.refs_3_.rest_0_ = bf16[64,512]{1,0:T(8,128)(2,1)S(1)} collective-permute-done((bf16[64,512]{1,0:T(8,128)(2,1)S(1)}, bf16[64,512]{1,0:T(8,128)(2,1)S(1)}, u32[]{:S(2)}, u32[]{:S(2)}) %collective-permute-start.5) | collective-permute-done | bytes 65568 | tf_op jit(solution)/shard_map/ppermute | solution.py:411
  23.9 1.7 %collective-permute-start.9 = (bf16[128,2048]{1,0:T(8,128)(2,1)S(1)}, bf16[128,2048]{1,0:T(8,128)(2,1)S(1)}, u32[]{:S(2)}, u32[]{:S(2)}) collective-permute-start(bf16[128,2048]{1,0:T(8,128)(2,1)S(1)} %hold.2), channel_id=1, source_target_pairs={{0,1},{1,0},{2,3},{3,2},{4,5},{5,4},{6,7},{7,6},{8,9},{9,8},{10,11... | collective-permute-start | bytes 1572872 | tf_op jit(solution)/shard_map/ppermute | solution.py:407
  25.6 0.5 %collective-permute-done.4.refs_1_.refs_2_ = bf16[64,512]{1,0:T(8,128)(2,1)S(1)} collective-permute-done((bf16[64,512]{1,0:T(8,128)(2,1)S(1)}, bf16[64,512]{1,0:T(8,128)(2,1)S(1)}, u32[]{:S(2)}, u32[]{:S(2)}) %collective-permute-start.4) | collective-permute-done | bytes 65568 | tf_op jit(solution)/shard_map/ppermute | solution.py:411
  26.4 0.6 %own_product.2.product_ref = f32[192,2048]{1,0:T(8,128)S(1)} custom-call(bf16[192,512]{1,0:T(8,128)(2,1)S(1)} %stack_rows.1.ratio_ref, bf16[512,2048]{1,0:T(8,128)(2,1)S(1)} %get-tuple-element.23.doc_ref), custom_call_target="tpu_custom_call" | custom-call | flops 402653184 | bytes 3670016 | tf_op jit(solution)/shard_map/own_product/pallas_call | solution.py:199
  27.0 0.8 %collective-permute-done.6.ratio_ref = bf16[192,512]{1,0:T(8,128)(2,1)S(1)} collective-permute-done((bf16[192,512]{1,0:T(8,128)(2,1)S(1)}, bf16[192,512]{1,0:T(8,128)(2,1)S(1)}, u32[]{:S(2)}, u32[]{:S(2)}) %collective-permute-start.6) | collective-permute-done | bytes 196640 | tf_op jit(solution)/shard_map/ppermute | solution.py:411
  27.8 0.6 %beta_pieces.2 = (bf16[128,2048]{1,0:T(8,128)(2,1)S(1)}, bf16[64,2048]{1,0:T(8,128)(2,1)S(1)}) custom-call(s32[1]{0:T(128)} %bitcast.here_ref, f32[192,2048]{1,0:T(8,128)S(1)} %own_product.2.product_ref, bf16[192,512]{1,0:T(8,128)(2,1)S(1)} %collective-permute-done.6.ratio_ref, bf16[512,2048]{1,0:T(8,128)(2,1)S(1)} %collective-permute-done.7.doc_ref, ...), custom_call_target="tpu_custom_call" | custom-call | flops 402653184 | bytes 5242880 | tf_op jit(solution)/shard_map/beta_pieces/pallas_call | solution.py:227
  28.4 1.3 %collective-permute-done.13.other_ref.rest_0_ = bf16[64,2048]{1,0:T(8,128)(2,1)S(1)} collective-permute-done((bf16[64,2048]{1,0:T(8,128)(2,1)S(1)}, bf16[64,2048]{1,0:T(8,128)(2,1)S(1)}, u32[]{:S(2)}, u32[]{:S(2)}) %collective-permute-start.13) | collective-permute-done | bytes 262176 | tf_op jit(solution)/shard_map/ppermute | solution.py:411
  29.8 1.6 %collective-permute-start.14 = (bf16[128,2048]{1,0:T(8,128)(2,1)S(1)}, bf16[128,2048]{1,0:T(8,128)(2,1)S(1)}, u32[]{:S(2)}, u32[]{:S(2)}) collective-permute-start(bf16[128,2048]{1,0:T(8,128)(2,1)S(1)} %hold.3), channel_id=1, source_target_pairs={{0,16},{8,24},{16,0},{24,8},{1,17},{9,25},{17,1},{25,9},{2,18},{10... | collective-permute-start | bytes 1572872 | tf_op jit(solution)/shard_map/ppermute | solution.py:411
  31.4 1.6 %collective-permute-start.8 = (bf16[256,512]{1,0:T(8,128)(2,1)S(1)}, bf16[256,512]{1,0:T(8,128)(2,1)S(1)}, u32[]{:S(2)}, u32[]{:S(2)}) collective-permute-start(bf16[256,512]{1,0:T(8,128)(2,1)S(1)} %join_ratio.1.refs_0_), channel_id=1, source_target_pairs={{0,1},{1,0},{2,3},{3,2},{4,5},{5,4},{6,7},{7,6},{8,9},{9,8},{10,11... | collective-permute-start | bytes 786440 | tf_op jit(solution)/shard_map/ppermute | solution.py:407
  33.0 5.8 %collective-permute-done.9.in_ref = bf16[128,2048]{1,0:T(8,128)(2,1)S(1)} collective-permute-done((bf16[128,2048]{1,0:T(8,128)(2,1)S(1)}, bf16[128,2048]{1,0:T(8,128)(2,1)S(1)}, u32[]{:S(2)}, u32[]{:S(2)}) %collective-permute-start.9) | collective-permute-done | bytes 524320 | tf_op jit(solution)/shard_map/ppermute | solution.py:407
  39.0 0.5 collective-permute-start.11
  39.5 1.6 %collective-permute-start.15 = (bf16[64,2048]{1,0:T(8,128)(2,1)S(1)}, bf16[64,2048]{1,0:T(8,128)(2,1)S(1)}, u32[]{:S(2)}, u32[]{:S(2)}) collective-permute-start(bf16[64,2048]{1,0:T(8,128)(2,1)S(1)} %get-tuple-element.35.own_ref), channel_id=1, source_target_pairs={{0,16},{8,24},{16,0},{24,8},{1,17},{9,25},{17,1},{25,9},{2,18},{10... | collective-permute-start | bytes 786440 | tf_op jit(solution)/shard_map/ppermute | solution.py:411
  41.0 1.8 %collective-permute-done.8.refs_1_ = bf16[256,512]{1,0:T(8,128)(2,1)S(1)} collective-permute-done((bf16[256,512]{1,0:T(8,128)(2,1)S(1)}, bf16[256,512]{1,0:T(8,128)(2,1)S(1)}, u32[]{:S(2)}, u32[]{:S(2)}) %collective-permute-start.8) | collective-permute-done | bytes 262176 | tf_op jit(solution)/shard_map/ppermute | solution.py:407
  43.1 3.6 %theta_grad.1 = (f32[512,2048]{1,0:T(8,128)}, f32[8,128]{1,0:T(8,128)S(1)}) custom-call(s32[1]{0:T(128)} %bitcast.here_ref, bf16[512,256]{1,0:T(8,128)(2,1)S(1)} %get-tuple-element.27.refs_0_, bf16[512,256]{1,0:T(8,128)(2,1)S(1)} %get-tuple-element.28.refs_1_, bf16[256,4096]{1,0:T(8,128)(2,1)S(1)} %get-tuple-element.25.prob_ref.refs_2_, ...), custom_call_target="tpu_custom_call" | custom-call | flops 1 | bytes 1 | tf_op jit(solution)/shard_map/theta_grad/pallas_call | solution.py:350
  47.0 0.6 %collective-permute-start.16 = (bf16[64,2048]{1,0:T(8,128)(2,1)S(1)}, bf16[64,2048]{1,0:T(8,128)(2,1)S(1)}, u32[]{:S(2)}, u32[]{:S(2)}) collective-permute-start(bf16[64,2048]{1,0:T(8,128)(2,1)S(1)} %add_pair.3.refs_0_), channel_id=1, source_target_pairs={{0,8},{8,0},{16,24},{24,16},{1,9},{9,1},{17,25},{25,17},{2,10},{10... | collective-permute-start | bytes 786440 | tf_op jit(solution)/shard_map/ppermute | solution.py:411
  47.5 0.8 %collective-permute-done.15.other_ref = bf16[64,2048]{1,0:T(8,128)(2,1)S(1)} collective-permute-done((bf16[64,2048]{1,0:T(8,128)(2,1)S(1)}, bf16[64,2048]{1,0:T(8,128)(2,1)S(1)}, u32[]{:S(2)}, u32[]{:S(2)}) %collective-permute-start.15) | collective-permute-done | bytes 262176 | tf_op jit(solution)/shard_map/ppermute | solution.py:411
  48.5 0.7 %collective-permute-done.16.refs_3_ = bf16[64,2048]{1,0:T(8,128)(2,1)S(1)} collective-permute-done((bf16[64,2048]{1,0:T(8,128)(2,1)S(1)}, bf16[64,2048]{1,0:T(8,128)(2,1)S(1)}, u32[]{:S(2)}, u32[]{:S(2)}) %collective-permute-start.16) | collective-permute-done | bytes 262176 | tf_op jit(solution)/shard_map/ppermute | solution.py:411
  49.2 0.8 %collective-permute-done.18.refs_5_ = bf16[64,2048]{1,0:T(8,128)(2,1)S(1)} collective-permute-done((bf16[64,2048]{1,0:T(8,128)(2,1)S(1)}, bf16[64,2048]{1,0:T(8,128)(2,1)S(1)}, u32[]{:S(2)}, u32[]{:S(2)}) %collective-permute-start.18) | collective-permute-done | bytes 262176 | tf_op jit(solution)/shard_map/ppermute | solution.py:411
  50.0 1.4 %place_pieces.1 = bf16[256,4096]{1,0:T(8,128)(2,1)} custom-call(s32[1]{0:T(128)} %bitcast.here_ref, bf16[64,2048]{1,0:T(8,128)(2,1)S(1)} %add_pair.3.refs_0_, bf16[128,2048]{1,0:T(8,128)(2,1)S(1)} %add_pair.4.refs_1_, bf16[64,2048]{1,0:T(8,128)(2,1)S(1)} %add_pair.5.refs_2_, bf16[64,2048]{1,0:T(8,128)(2,1)S(1)} %collective-permute-done.16.refs_3_, ...), custom_call_target="tpu_custom_call" | custom-call | bytes 4194304 | tf_op jit(solution)/shard_map/place_pieces/pallas_call | solution.py:388
  (26 shorter events, 1.6 us)
Async XLA Ops:
  0.6 10.6 %copy-start = (s32[16,64,128]{2,1,0:T(8,128)S(1)}, s32[16,64,128]{2,1,0:T(8,128)}, u32[]{:S(2)}) copy-start(s32[16,64,128]{2,1,0:T(8,128)} %count_ref.1) | copy-start | bytes 1572868
  5.4 15.7 %collective-permute-start.7 = (bf16[512,2048]{1,0:T(8,128)(2,1)S(1)}, bf16[512,2048]{1,0:T(8,128)(2,1)S(1)}, u32[]{:S(2)}, u32[]{:S(2)}) collective-permute-start(bf16[512,2048]{1,0:T(8,128)(2,1)S(1)} %get-tuple-element.24), channel_id=1, source_target_pairs={{0,8},{8,0},{16,24},{24,16},{1,9},{9,1},{17,25},{25,17},{2,10},{10... | collective-permute-start | bytes 6291464 | tf_op jit(solution)/shard_map/ppermute | solution.py:411
  6.0 7.9 %collective-permute-start = (bf16[64,512]{1,0:T(8,128)(2,1)S(1)}, bf16[64,512]{1,0:T(8,128)(2,1)S(1)}, u32[]{:S(2)}, u32[]{:S(2)}) collective-permute-start(bf16[64,512]{1,0:T(8,128)(2,1)S(1)} %get-tuple-element.20), channel_id=1, source_target_pairs={{0,4},{2,6},{4,0},{6,2},{1,5},{3,7},{5,1},{7,3},{8,12},{10,14},{12... | collective-permute-start | bytes 196616 | tf_op jit(solution)/shard_map/ppermute | solution.py:411
  9.6 6.7 %collective-permute-start.1 = (bf16[64,512]{1,0:T(8,128)(2,1)S(1)}, bf16[64,512]{1,0:T(8,128)(2,1)S(1)}, u32[]{:S(2)}, u32[]{:S(2)}) collective-permute-start(bf16[64,512]{1,0:T(8,128)(2,1)S(1)} %get-tuple-element.21), channel_id=1, source_target_pairs={{0,6},{2,4},{4,2},{6,0},{1,7},{3,5},{5,3},{7,1},{8,14},{10,12},{12... | collective-permute-start | bytes 196616 | tf_op jit(solution)/shard_map/ppermute | solution.py:411
  11.0 5.5 %collective-permute-start.2 = (bf16[64,512]{1,0:T(8,128)(2,1)S(1)}, bf16[64,512]{1,0:T(8,128)(2,1)S(1)}, u32[]{:S(2)}, u32[]{:S(2)}) collective-permute-start(bf16[64,512]{1,0:T(8,128)(2,1)S(1)} %get-tuple-element.22), channel_id=1, source_target_pairs={{0,2},{2,0},{4,6},{6,4},{1,3},{3,1},{5,7},{7,5},{8,10},{10,8},{12,... | collective-permute-start | bytes 196616 | tf_op jit(solution)/shard_map/ppermute | solution.py:411
  16.5 4.6 %collective-permute-start.12 = (bf16[64,512]{1,0:T(8,128)(2,1)S(1)}, bf16[64,512]{1,0:T(8,128)(2,1)S(1)}, u32[]{:S(2)}, u32[]{:S(2)}) collective-permute-start(bf16[64,512]{1,0:T(8,128)(2,1)S(1)} %ratio_chunk.1.refs_0_.ratio_ref), channel_id=1, source_target_pairs={{0,8},{8,0},{16,24},{24,16},{1,9},{9,1},{17,25},{25,17},{2,10},{10... | collective-permute-start | bytes 196616 | tf_op jit(solution)/shard_map/ppermute | solution.py:411
  16.6 7.3 %collective-permute-start.5 = (bf16[64,512]{1,0:T(8,128)(2,1)S(1)}, bf16[64,512]{1,0:T(8,128)(2,1)S(1)}, u32[]{:S(2)}, u32[]{:S(2)}) collective-permute-start(bf16[64,512]{1,0:T(8,128)(2,1)S(1)} %ratio_chunk.1.refs_0_.ratio_ref), channel_id=1, source_target_pairs={{0,4},{2,6},{4,0},{6,2},{1,5},{3,7},{5,1},{7,3},{8,12},{10,14},{12... | collective-permute-start | bytes 196616 | tf_op jit(solution)/shard_map/ppermute | solution.py:411
  19.4 6.7 %collective-permute-start.4 = (bf16[64,512]{1,0:T(8,128)(2,1)S(1)}, bf16[64,512]{1,0:T(8,128)(2,1)S(1)}, u32[]{:S(2)}, u32[]{:S(2)}) collective-permute-start(bf16[64,512]{1,0:T(8,128)(2,1)S(1)} %ratio_chunk.1.refs_0_.ratio_ref), channel_id=1, source_target_pairs={{0,6},{2,4},{4,2},{6,0},{1,7},{3,5},{5,3},{7,1},{8,14},{10,12},{12... | collective-permute-start | bytes 196616 | tf_op jit(solution)/shard_map/ppermute | solution.py:411
  20.1 6.1 %collective-permute-start.3 = (bf16[64,512]{1,0:T(8,128)(2,1)S(1)}, bf16[64,512]{1,0:T(8,128)(2,1)S(1)}, u32[]{:S(2)}, u32[]{:S(2)}) collective-permute-start(bf16[64,512]{1,0:T(8,128)(2,1)S(1)} %ratio_chunk.1.refs_0_.ratio_ref), channel_id=1, source_target_pairs={{0,2},{2,0},{4,6},{6,4},{1,3},{3,1},{5,7},{7,5},{8,10},{10,8},{12,... | collective-permute-start | bytes 196616 | tf_op jit(solution)/shard_map/ppermute | solution.py:411
  21.6 8.2 %collective-permute-start.13 = (bf16[64,2048]{1,0:T(8,128)(2,1)S(1)}, bf16[64,2048]{1,0:T(8,128)(2,1)S(1)}, u32[]{:S(2)}, u32[]{:S(2)}) collective-permute-start(bf16[64,2048]{1,0:T(8,128)(2,1)S(1)} %beta_pieces.3.own_ref), channel_id=1, source_target_pairs={{0,16},{8,24},{16,0},{24,8},{1,17},{9,25},{17,1},{25,9},{2,18},{10... | collective-permute-start | bytes 786440 | tf_op jit(solution)/shard_map/ppermute | solution.py:411
  23.9 14.9 %collective-permute-start.9 = (bf16[128,2048]{1,0:T(8,128)(2,1)S(1)}, bf16[128,2048]{1,0:T(8,128)(2,1)S(1)}, u32[]{:S(2)}, u32[]{:S(2)}) collective-permute-start(bf16[128,2048]{1,0:T(8,128)(2,1)S(1)} %hold.2), channel_id=1, source_target_pairs={{0,1},{1,0},{2,3},{3,2},{4,5},{5,4},{6,7},{7,6},{8,9},{9,8},{10,11... | collective-permute-start | bytes 1572872 | tf_op jit(solution)/shard_map/ppermute | solution.py:407
  26.3 1.5 %collective-permute-start.6 = (bf16[192,512]{1,0:T(8,128)(2,1)S(1)}, bf16[192,512]{1,0:T(8,128)(2,1)S(1)}, u32[]{:S(2)}, u32[]{:S(2)}) collective-permute-start(bf16[192,512]{1,0:T(8,128)(2,1)S(1)} %stack_rows.1.ratio_ref), channel_id=1, source_target_pairs={{0,8},{8,0},{16,24},{24,16},{1,9},{9,1},{17,25},{25,17},{2,10},{10... | collective-permute-start | bytes 589832 | tf_op jit(solution)/shard_map/ppermute | solution.py:411
  29.8 16.9 %collective-permute-start.14 = (bf16[128,2048]{1,0:T(8,128)(2,1)S(1)}, bf16[128,2048]{1,0:T(8,128)(2,1)S(1)}, u32[]{:S(2)}, u32[]{:S(2)}) collective-permute-start(bf16[128,2048]{1,0:T(8,128)(2,1)S(1)} %hold.3), channel_id=1, source_target_pairs={{0,16},{8,24},{16,0},{24,8},{1,17},{9,25},{17,1},{25,9},{2,18},{10... | collective-permute-start | bytes 1572872 | tf_op jit(solution)/shard_map/ppermute | solution.py:411
  31.4 11.4 %collective-permute-start.8 = (bf16[256,512]{1,0:T(8,128)(2,1)S(1)}, bf16[256,512]{1,0:T(8,128)(2,1)S(1)}, u32[]{:S(2)}, u32[]{:S(2)}) collective-permute-start(bf16[256,512]{1,0:T(8,128)(2,1)S(1)} %join_ratio.1.refs_0_), channel_id=1, source_target_pairs={{0,1},{1,0},{2,3},{3,2},{4,5},{5,4},{6,7},{7,6},{8,9},{9,8},{10,11... | collective-permute-start | bytes 786440 | tf_op jit(solution)/shard_map/ppermute | solution.py:407
  38.9 4.2 %collective-permute-start.10 = (bf16[64,2048]{1,0:T(8,128)(2,1)S(1)}, bf16[64,2048]{1,0:T(8,128)(2,1)S(1)}, u32[]{:S(2)}, u32[]{:S(2)}) collective-permute-start(bf16[64,2048]{1,0:T(8,128)(2,1)S(1)} %get-tuple-element.30.refs_3_), channel_id=1, source_target_pairs={{0,8},{8,0},{16,24},{24,16},{1,9},{9,1},{17,25},{25,17},{2,10},{10... | collective-permute-start | bytes 786440 | tf_op jit(solution)/shard_map/ppermute | solution.py:411
  39.0 4.1 %collective-permute-start.11 = (bf16[64,2048]{1,0:T(8,128)(2,1)S(1)}, bf16[64,2048]{1,0:T(8,128)(2,1)S(1)}, u32[]{:S(2)}, u32[]{:S(2)}) collective-permute-start(bf16[64,2048]{1,0:T(8,128)(2,1)S(1)} %get-tuple-element.31.refs_4_), channel_id=1, source_target_pairs={{0,8},{8,0},{16,24},{24,16},{1,9},{9,1},{17,25},{25,17},{2,10},{10... | collective-permute-start | bytes 786440 | tf_op jit(solution)/shard_map/ppermute | solution.py:411
  39.5 8.9 %collective-permute-start.15 = (bf16[64,2048]{1,0:T(8,128)(2,1)S(1)}, bf16[64,2048]{1,0:T(8,128)(2,1)S(1)}, u32[]{:S(2)}, u32[]{:S(2)}) collective-permute-start(bf16[64,2048]{1,0:T(8,128)(2,1)S(1)} %get-tuple-element.35.own_ref), channel_id=1, source_target_pairs={{0,16},{8,24},{16,0},{24,8},{1,17},{9,25},{17,1},{25,9},{2,18},{10... | collective-permute-start | bytes 786440 | tf_op jit(solution)/shard_map/ppermute | solution.py:411
  46.8 3.2 %collective-permute-start.17 = (bf16[128,2048]{1,0:T(8,128)(2,1)S(1)}, bf16[128,2048]{1,0:T(8,128)(2,1)S(1)}, u32[]{:S(2)}, u32[]{:S(2)}) collective-permute-start(bf16[128,2048]{1,0:T(8,128)(2,1)S(1)} %add_pair.4.refs_1_), channel_id=1, source_target_pairs={{0,8},{8,0},{16,24},{24,16},{1,9},{9,1},{17,25},{25,17},{2,10},{10... | collective-permute-start | bytes 1572872 | tf_op jit(solution)/shard_map/ppermute | solution.py:411
  47.0 2.2 %collective-permute-start.16 = (bf16[64,2048]{1,0:T(8,128)(2,1)S(1)}, bf16[64,2048]{1,0:T(8,128)(2,1)S(1)}, u32[]{:S(2)}, u32[]{:S(2)}) collective-permute-start(bf16[64,2048]{1,0:T(8,128)(2,1)S(1)} %add_pair.3.refs_0_), channel_id=1, source_target_pairs={{0,8},{8,0},{16,24},{24,16},{1,9},{9,1},{17,25},{25,17},{2,10},{10... | collective-permute-start | bytes 786440 | tf_op jit(solution)/shard_map/ppermute | solution.py:411
  48.4 1.6 %collective-permute-start.18 = (bf16[64,2048]{1,0:T(8,128)(2,1)S(1)}, bf16[64,2048]{1,0:T(8,128)(2,1)S(1)}, u32[]{:S(2)}, u32[]{:S(2)}) collective-permute-start(bf16[64,2048]{1,0:T(8,128)(2,1)S(1)} %add_pair.5.refs_2_), channel_id=1, source_target_pairs={{0,8},{8,0},{16,24},{24,16},{1,9},{9,1},{17,25},{25,17},{2,10},{10... | collective-permute-start | bytes 786440 | tf_op jit(solution)/shard_map/ppermute | solution.py:411

commit v14 on v12

--- a/solution.py
+++ b/solution.py
@@ -52,43 +52,59 @@
     docs, width = doc_topics.shape
     words = word_logits.shape[0]
     side_width = width // 2
-    span = min(side_width, 1024)
-    steps = side_width // span
+    word_rows, doc_rows = words // 4, min(docs, 256)
+    steps = docs // doc_rows
     count, far = sizes.topic, sizes.vocab - 1
     chunk, half, share = words // count, words // 2, width // sizes.vocab
 
     def kernel(here_ref, doc_in, logit_in, norm_in, *rest):
         parts, halves = rest[:count], rest[count : count + far]
-        own_ref, sibling_ref, prob_ref, norm_ref, logit_ref, acc, sems, norm_sem = rest[count + far :]
+        own_ref, sibling_ref, prob_ref, norm_ref, logit_ref, acc, logit_sems, doc_sems, norm_sem = rest[count + far :]
         side = sizes.side(here_ref)
+        sides = ((0, 1 - side, sibling_ref), (1, side, own_ref))
+
+        def logit_copy(i):
+            at = window(i, word_rows)
+            return pltpu.make_async_copy(logit_in.at[at, :], logit_ref.at[at, :], logit_sems.at[i])
+
+        def doc_copy(h, which, doc_ref, i):
+            at = window(i, doc_rows)
+            return pltpu.make_async_copy(
+                doc_in.at[at, window(which, side_width)], doc_ref.at[at, :], doc_sems.at[h, i]
+            )
+
         norm_copy = pltpu.make_async_copy(norm_in, norm_ref, norm_sem)
         norm_copy.start()
-        blocks = []
-        for which, doc_ref in ((1 - side, sibling_ref), (side, own_ref)):
-            for j in range(steps):
-                at = window(which * steps + j, span)
-                i = len(blocks)
-                logit_copy = pltpu.make_async_copy(logit_in.at[:, at], logit_ref.at[:, at], sems.at[0, i])
-                held = doc_ref.at[:, pl.ds(j * span, span)]
-                doc_copy = pltpu.make_async_copy(doc_in.at[:, at], held, sems.at[1, i])
-                blocks.append((at, logit_copy, doc_copy, held))
-        for _, logit_copy, doc_copy, _ in blocks:
-            logit_copy.start()
-            doc_copy.start()
+        for i in range(words // word_rows):
+            logit_copy(i).start()
+        for i in range(steps):
+            for h, which, doc_ref in sides:
+                doc_copy(h, which, doc_ref, i).start()
         norm_copy.wait()
-        for i, (at, logit_copy, doc_copy, held) in enumerate(blocks):
-            logit_copy.wait()
-            prob = jnp.exp(logit_ref[:, at].astype(F32) - norm_ref[:, at]).astype(BF16)
-            prob_ref[:, at] = prob
-            doc_copy.wait()
-            part = lax.dot_general(
-                prob, held[...], (((1,), (1,)), ((), ())), preferred_element_type=F32
-            )
-            if i == 0:
-                acc[...] = part
-            else:
-                acc[...] += part
+
+        @pl.loop(0, words // word_rows)
+        def _(i):
+            logit_copy(i).wait()
+            at = window(i, word_rows)
+            prob_ref[at, :] = jnp.exp(logit_ref[at, :].astype(F32) - norm_ref[...]).astype(BF16)
+
         topic_at = sizes.topic_at(here_ref)
+
+        @pl.loop(0, steps)
+        def _(i):
+            at = window(i, doc_rows)
+            rate = None
+            for h, which, doc_ref in sides:
+                doc_copy(h, which, doc_ref, i).wait()
+                part = lax.dot_general(
+                    prob_ref[:, window(which, side_width)],
+                    doc_ref[at, :],
+                    (((1,), (1,)), ((), ())),
+                    preferred_element_type=F32,
+                )
+                rate = part if rate is None else rate + part
+            acc[:, at] = rate
+
         for s in range(count):
             parts[s][...] = acc[window(topic_at ^ s, chunk), :].astype(BF16)
         rows = window(side, half)
@@ -111,7 +127,8 @@
         scratch_shapes=[
             pltpu.VMEM(word_logits.shape, BF16),
             pltpu.VMEM((words, docs), F32),
-            pltpu.SemaphoreType.DMA((2, 2 * steps)),
+            pltpu.SemaphoreType.DMA((words // word_rows,)),
+            pltpu.SemaphoreType.DMA((2, steps)),
             pltpu.SemaphoreType.DMA,
         ],
         compiler_params=call_params(),

time: 51.6 us -> 51.5 us (level)
  no operation moved by 1% of the time
where the time goes in v14:
time: 51.5 us; the launch traced here: 51.4 us
  starting transfers between devices  19.1 us (37%)
  waiting for transfers between devices  18 us (35%)
  Pallas kernels  13.4 us (26%)
  between operations  0.81 us (2%)
    ppermute x17, starting transfers between devices, swap(): return lax.ppermute(array, axis, [(i, i ^ bits) for i in range(count)])  15.9 us
    ppermute x17, waiting for transfers between devices, swap(): return lax.ppermute(array, axis, [(i, i ^ bits) for i in range(count)])  10.4 us
    ppermute x2, waiting for transfers between devices, shift(): lax.ppermute(array, 'vocab', [(i, (i + by) % sizes.vocab) for i in range(...  7.64 us
    pallas_call x1, Pallas kernels, rate_partial(): pl.pallas_call(kernel, out_shape=[jax.ShapeDtypeStruct((chunk, docs), BF1...  4.75 us
    pallas_call x1, Pallas kernels, theta_grad(): pl.pallas_call(kernel, out_shape=[jax.ShapeDtypeStruct((docs, share), F32...  3.65 us
    ppermute x2, starting transfers between devices, shift(): lax.ppermute(array, 'vocab', [(i, (i + by) % sizes.vocab) for i in range(...  3.25 us
    pallas_call x1, Pallas kernels, place_pieces(): pl.pallas_call(kernel, out_shape=jax.ShapeDtypeStruct(shape, BF16), in_sp...  1.37 us
    pallas_call x2, Pallas kernels, beta_pieces(): pl.pallas_call(kernel, out_shape=[jax.ShapeDtypeStruct((rows * len(piece)...  1.11 us
  transfers between devices with their start and end apart: 19, of which 13 were waited for; matrix products, arithmetic and copies ran while one was open for 0% of the time, Pallas kernels for 14%

profile of v14, /device:TPU:0, one launch (start us, length us, event | category | flops | bytes accessed | tf_op | source)
XLA Modules:
  0.0 51.4 jit_solution(5516326824335784549)
XLA Ops:
  0.6 4.7 %rate_partial.1 = (bf16[64,512]{1,0:T(8,128)(2,1)S(1)}, bf16[64,512]{1,0:T(8,128)(2,1)S(1)}, bf16[64,512]{1,0:T(8,128)(2,1)S(1)}, bf16[64,512]{1,0:T(8,128)(2,1)...) custom-call(s32[1]{0:T(128)} %bitcast.here_ref, ...), custom_call_target="tpu_custom_call" | custom-call | flops 1073741824 | bytes 6291456 | tf_op jit(solution)/shard_map/rate_partial/pallas_call | solution.py:115
  5.4 0.5 %collective-permute-start.7 = (bf16[512,2048]{1,0:T(8,128)(2,1)S(1)}, bf16[512,2048]{1,0:T(8,128)(2,1)S(1)}, u32[]{:S(2)}, u32[]{:S(2)}) collective-permute-start(bf16[512,2048]{1,0:T(8,128)(2,1)S(1)} %get-tuple-element.24), channel_id=1, source_target_pairs={{0,8},{8,0},{16,24},{24,16},{1,9},{9,1},{17,25},{25,17},{2,10},{10... | collective-permute-start | bytes 6291464 | tf_op jit(solution)/shard_map/ppermute | solution.py:424
  6.0 3.6 %collective-permute-start = (bf16[64,512]{1,0:T(8,128)(2,1)S(1)}, bf16[64,512]{1,0:T(8,128)(2,1)S(1)}, u32[]{:S(2)}, u32[]{:S(2)}) collective-permute-start(bf16[64,512]{1,0:T(8,128)(2,1)S(1)} %get-tuple-element.20), channel_id=1, source_target_pairs={{0,4},{2,6},{4,0},{6,2},{1,5},{3,7},{5,1},{7,3},{8,12},{10,14},{12... | collective-permute-start | bytes 196616 | tf_op jit(solution)/shard_map/ppermute | solution.py:424
  9.6 1.3 %collective-permute-start.1 = (bf16[64,512]{1,0:T(8,128)(2,1)S(1)}, bf16[64,512]{1,0:T(8,128)(2,1)S(1)}, u32[]{:S(2)}, u32[]{:S(2)}) collective-permute-start(bf16[64,512]{1,0:T(8,128)(2,1)S(1)} %get-tuple-element.21), channel_id=1, source_target_pairs={{0,6},{2,4},{4,2},{6,0},{1,7},{3,5},{5,3},{7,1},{8,14},{10,12},{12... | collective-permute-start | bytes 196616 | tf_op jit(solution)/shard_map/ppermute | solution.py:424
  11.2 0.8 %chunk_counts.1.refs_4_ = f32[64,512]{1,0:T(8,128)S(1)} custom-call(s32[1]{0:T(128)} %bitcast.here_ref, s32[16]{0:T(128)} %doc_at.1, s32[16]{0:T(128)} %word_at.1, s32[16,64,128]{2,1,0:T(8,128)S(1)} %copy-done), custom_call_target="tpu_custom_call" | custom-call | flops 131072 | bytes 524288 | tf_op jit(solution)/shard_map/chunk_counts/pallas_call | solution.py:155
  12.0 1.8 %collective-permute-done.refs_1_ = bf16[64,512]{1,0:T(8,128)(2,1)S(1)} collective-permute-done((bf16[64,512]{1,0:T(8,128)(2,1)S(1)}, bf16[64,512]{1,0:T(8,128)(2,1)S(1)}, u32[]{:S(2)}, u32[]{:S(2)}) %collective-permute-start) | collective-permute-done | bytes 65568 | tf_op jit(solution)/shard_map/ppermute | solution.py:424
  13.8 2.4 %collective-permute-done.1.refs_2_ = bf16[64,512]{1,0:T(8,128)(2,1)S(1)} collective-permute-done((bf16[64,512]{1,0:T(8,128)(2,1)S(1)}, bf16[64,512]{1,0:T(8,128)(2,1)S(1)}, u32[]{:S(2)}, u32[]{:S(2)}) %collective-permute-start.1) | collective-permute-done | bytes 65568 | tf_op jit(solution)/shard_map/ppermute | solution.py:424
  16.6 2.8 %collective-permute-start.5 = (bf16[64,512]{1,0:T(8,128)(2,1)S(1)}, bf16[64,512]{1,0:T(8,128)(2,1)S(1)}, u32[]{:S(2)}, u32[]{:S(2)}) collective-permute-start(bf16[64,512]{1,0:T(8,128)(2,1)S(1)} %ratio_chunk.1.refs_0_.ratio_ref), channel_id=1, source_target_pairs={{0,4},{2,6},{4,0},{6,2},{1,5},{3,7},{5,1},{7,3},{8,12},{10,14},{12... | collective-permute-start | bytes 196616 | tf_op jit(solution)/shard_map/ppermute | solution.py:424
  19.4 0.7 %collective-permute-start.4 = (bf16[64,512]{1,0:T(8,128)(2,1)S(1)}, bf16[64,512]{1,0:T(8,128)(2,1)S(1)}, u32[]{:S(2)}, u32[]{:S(2)}) collective-permute-start(bf16[64,512]{1,0:T(8,128)(2,1)S(1)} %ratio_chunk.1.refs_0_.ratio_ref), channel_id=1, source_target_pairs={{0,6},{2,4},{4,2},{6,0},{1,7},{3,5},{5,3},{7,1},{8,14},{10,12},{12... | collective-permute-start | bytes 196616 | tf_op jit(solution)/shard_map/ppermute | solution.py:424
  20.1 0.5 collective-permute-start.3
  20.6 0.5 own_product.3.product_ref
  21.1 0.5 beta_pieces.3.own_ref
  21.6 1.6 %collective-permute-start.13 = (bf16[64,2048]{1,0:T(8,128)(2,1)S(1)}, bf16[64,2048]{1,0:T(8,128)(2,1)S(1)}, u32[]{:S(2)}, u32[]{:S(2)}) collective-permute-start(bf16[64,2048]{1,0:T(8,128)(2,1)S(1)} %beta_pieces.3.own_ref), channel_id=1, source_target_pairs={{0,16},{8,24},{16,0},{24,8},{1,17},{9,25},{17,1},{25,9},{2,18},{10... | collective-permute-start | bytes 786440 | tf_op jit(solution)/shard_map/ppermute | solution.py:424
  23.1 0.7 %collective-permute-done.5.refs_2_.refs_3_.rest_0_ = bf16[64,512]{1,0:T(8,128)(2,1)S(1)} collective-permute-done((bf16[64,512]{1,0:T(8,128)(2,1)S(1)}, bf16[64,512]{1,0:T(8,128)(2,1)S(1)}, u32[]{:S(2)}, u32[]{:S(2)}) %collective-permute-start.5) | collective-permute-done | bytes 65568 | tf_op jit(solution)/shard_map/ppermute | solution.py:424
  23.9 1.7 %collective-permute-start.9 = (bf16[128,2048]{1,0:T(8,128)(2,1)S(1)}, bf16[128,2048]{1,0:T(8,128)(2,1)S(1)}, u32[]{:S(2)}, u32[]{:S(2)}) collective-permute-start(bf16[128,2048]{1,0:T(8,128)(2,1)S(1)} %hold.2), channel_id=1, source_target_pairs={{0,1},{1,0},{2,3},{3,2},{4,5},{5,4},{6,7},{7,6},{8,9},{9,8},{10,11... | collective-permute-start | bytes 1572872 | tf_op jit(solution)/shard_map/ppermute | solution.py:420
  25.5 0.5 %collective-permute-done.4.refs_1_.refs_2_ = bf16[64,512]{1,0:T(8,128)(2,1)S(1)} collective-permute-done((bf16[64,512]{1,0:T(8,128)(2,1)S(1)}, bf16[64,512]{1,0:T(8,128)(2,1)S(1)}, u32[]{:S(2)}, u32[]{:S(2)}) %collective-permute-start.4) | collective-permute-done | bytes 65568 | tf_op jit(solution)/shard_map/ppermute | solution.py:424
  26.3 0.6 %own_product.2.product_ref = f32[192,2048]{1,0:T(8,128)S(1)} custom-call(bf16[192,512]{1,0:T(8,128)(2,1)S(1)} %stack_rows.1.ratio_ref, bf16[512,2048]{1,0:T(8,128)(2,1)S(1)} %get-tuple-element.23.doc_ref), custom_call_target="tpu_custom_call" | custom-call | flops 402653184 | bytes 3670016 | tf_op jit(solution)/shard_map/own_product/pallas_call | solution.py:212
  26.9 0.8 %collective-permute-done.6.ratio_ref = bf16[192,512]{1,0:T(8,128)(2,1)S(1)} collective-permute-done((bf16[192,512]{1,0:T(8,128)(2,1)S(1)}, bf16[192,512]{1,0:T(8,128)(2,1)S(1)}, u32[]{:S(2)}, u32[]{:S(2)}) %collective-permute-start.6) | collective-permute-done | bytes 196640 | tf_op jit(solution)/shard_map/ppermute | solution.py:424
  27.8 0.6 %beta_pieces.2 = (bf16[128,2048]{1,0:T(8,128)(2,1)S(1)}, bf16[64,2048]{1,0:T(8,128)(2,1)S(1)}) custom-call(s32[1]{0:T(128)} %bitcast.here_ref, f32[192,2048]{1,0:T(8,128)S(1)} %own_product.2.product_ref, bf16[192,512]{1,0:T(8,128)(2,1)S(1)} %collective-permute-done.6.ratio_ref, bf16[512,2048]{1,0:T(8,128)(2,1)S(1)} %collective-permute-done.7.doc_ref, ...), custom_call_target="tpu_custom_call" | custom-call | flops 402653184 | bytes 5242880 | tf_op jit(solution)/shard_map/beta_pieces/pallas_call | solution.py:240
  28.4 1.3 %collective-permute-done.13.other_ref.rest_0_ = bf16[64,2048]{1,0:T(8,128)(2,1)S(1)} collective-permute-done((bf16[64,2048]{1,0:T(8,128)(2,1)S(1)}, bf16[64,2048]{1,0:T(8,128)(2,1)S(1)}, u32[]{:S(2)}, u32[]{:S(2)}) %collective-permute-start.13) | collective-permute-done | bytes 262176 | tf_op jit(solution)/shard_map/ppermute | solution.py:424
  29.8 1.6 %collective-permute-start.14 = (bf16[128,2048]{1,0:T(8,128)(2,1)S(1)}, bf16[128,2048]{1,0:T(8,128)(2,1)S(1)}, u32[]{:S(2)}, u32[]{:S(2)}) collective-permute-start(bf16[128,2048]{1,0:T(8,128)(2,1)S(1)} %hold.3), channel_id=1, source_target_pairs={{0,16},{8,24},{16,0},{24,8},{1,17},{9,25},{17,1},{25,9},{2,18},{10... | collective-permute-start | bytes 1572872 | tf_op jit(solution)/shard_map/ppermute | solution.py:424
  31.4 1.6 %collective-permute-start.8 = (bf16[256,512]{1,0:T(8,128)(2,1)S(1)}, bf16[256,512]{1,0:T(8,128)(2,1)S(1)}, u32[]{:S(2)}, u32[]{:S(2)}) collective-permute-start(bf16[256,512]{1,0:T(8,128)(2,1)S(1)} %join_ratio.1.refs_0_), channel_id=1, source_target_pairs={{0,1},{1,0},{2,3},{3,2},{4,5},{5,4},{6,7},{7,6},{8,9},{9,8},{10,11... | collective-permute-start | bytes 786440 | tf_op jit(solution)/shard_map/ppermute | solution.py:420
  33.0 5.8 %collective-permute-done.9.in_ref = bf16[128,2048]{1,0:T(8,128)(2,1)S(1)} collective-permute-done((bf16[128,2048]{1,0:T(8,128)(2,1)S(1)}, bf16[128,2048]{1,0:T(8,128)(2,1)S(1)}, u32[]{:S(2)}, u32[]{:S(2)}) %collective-permute-start.9) | collective-permute-done | bytes 524320 | tf_op jit(solution)/shard_map/ppermute | solution.py:420
  38.9 0.5 collective-permute-start.11
  39.4 1.6 %collective-permute-start.15 = (bf16[64,2048]{1,0:T(8,128)(2,1)S(1)}, bf16[64,2048]{1,0:T(8,128)(2,1)S(1)}, u32[]{:S(2)}, u32[]{:S(2)}) collective-permute-start(bf16[64,2048]{1,0:T(8,128)(2,1)S(1)} %get-tuple-element.35.own_ref), channel_id=1, source_target_pairs={{0,16},{8,24},{16,0},{24,8},{1,17},{9,25},{17,1},{25,9},{2,18},{10... | collective-permute-start | bytes 786440 | tf_op jit(solution)/shard_map/ppermute | solution.py:424
  41.0 1.8 %collective-permute-done.8.refs_1_ = bf16[256,512]{1,0:T(8,128)(2,1)S(1)} collective-permute-done((bf16[256,512]{1,0:T(8,128)(2,1)S(1)}, bf16[256,512]{1,0:T(8,128)(2,1)S(1)}, u32[]{:S(2)}, u32[]{:S(2)}) %collective-permute-start.8) | collective-permute-done | bytes 262176 | tf_op jit(solution)/shard_map/ppermute | solution.py:420
  43.0 3.7 %theta_grad.1 = (f32[512,2048]{1,0:T(8,128)}, f32[8,128]{1,0:T(8,128)S(1)}) custom-call(s32[1]{0:T(128)} %bitcast.here_ref, bf16[512,256]{1,0:T(8,128)(2,1)S(1)} %get-tuple-element.27.refs_0_, bf16[512,256]{1,0:T(8,128)(2,1)S(1)} %get-tuple-element.28.refs_1_, bf16[256,4096]{1,0:T(8,128)(2,1)S(1)} %get-tuple-element.25.prob_ref.refs_2_, ...), custom_call_target="tpu_custom_call" | custom-call | flops 1 | bytes 1 | tf_op jit(solution)/shard_map/theta_grad/pallas_call | solution.py:363
  46.9 0.6 %collective-permute-start.16 = (bf16[64,2048]{1,0:T(8,128)(2,1)S(1)}, bf16[64,2048]{1,0:T(8,128)(2,1)S(1)}, u32[]{:S(2)}, u32[]{:S(2)}) collective-permute-start(bf16[64,2048]{1,0:T(8,128)(2,1)S(1)} %add_pair.3.refs_0_), channel_id=1, source_target_pairs={{0,8},{8,0},{16,24},{24,16},{1,9},{9,1},{17,25},{25,17},{2,10},{10... | collective-permute-start | bytes 786440 | tf_op jit(solution)/shard_map/ppermute | solution.py:424
  47.5 0.8 %collective-permute-done.15.other_ref = bf16[64,2048]{1,0:T(8,128)(2,1)S(1)} collective-permute-done((bf16[64,2048]{1,0:T(8,128)(2,1)S(1)}, bf16[64,2048]{1,0:T(8,128)(2,1)S(1)}, u32[]{:S(2)}, u32[]{:S(2)}) %collective-permute-start.15) | collective-permute-done | bytes 262176 | tf_op jit(solution)/shard_map/ppermute | solution.py:424
  48.5 0.7 %collective-permute-done.16.refs_3_ = bf16[64,2048]{1,0:T(8,128)(2,1)S(1)} collective-permute-done((bf16[64,2048]{1,0:T(8,128)(2,1)S(1)}, bf16[64,2048]{1,0:T(8,128)(2,1)S(1)}, u32[]{:S(2)}, u32[]{:S(2)}) %collective-permute-start.16) | collective-permute-done | bytes 262176 | tf_op jit(solution)/shard_map/ppermute | solution.py:424
  49.1 0.8 %collective-permute-done.18.refs_5_ = bf16[64,2048]{1,0:T(8,128)(2,1)S(1)} collective-permute-done((bf16[64,2048]{1,0:T(8,128)(2,1)S(1)}, bf16[64,2048]{1,0:T(8,128)(2,1)S(1)}, u32[]{:S(2)}, u32[]{:S(2)}) %collective-permute-start.18) | collective-permute-done | bytes 262176 | tf_op jit(solution)/shard_map/ppermute | solution.py:424
  50.0 1.4 %place_pieces.1 = bf16[256,4096]{1,0:T(8,128)(2,1)} custom-call(s32[1]{0:T(128)} %bitcast.here_ref, bf16[64,2048]{1,0:T(8,128)(2,1)S(1)} %add_pair.3.refs_0_, bf16[128,2048]{1,0:T(8,128)(2,1)S(1)} %add_pair.4.refs_1_, bf16[64,2048]{1,0:T(8,128)(2,1)S(1)} %add_pair.5.refs_2_, bf16[64,2048]{1,0:T(8,128)(2,1)S(1)} %collective-permute-done.16.refs_3_, ...), custom_call_target="tpu_custom_call" | custom-call | bytes 4194304 | tf_op jit(solution)/shard_map/place_pieces/pallas_call | solution.py:401
  (26 shorter events, 1.6 us)
Async XLA Ops:
  0.6 10.5 %copy-start = (s32[16,64,128]{2,1,0:T(8,128)S(1)}, s32[16,64,128]{2,1,0:T(8,128)}, u32[]{:S(2)}) copy-start(s32[16,64,128]{2,1,0:T(8,128)} %count_ref.1) | copy-start | bytes 1572868
  5.4 15.7 %collective-permute-start.7 = (bf16[512,2048]{1,0:T(8,128)(2,1)S(1)}, bf16[512,2048]{1,0:T(8,128)(2,1)S(1)}, u32[]{:S(2)}, u32[]{:S(2)}) collective-permute-start(bf16[512,2048]{1,0:T(8,128)(2,1)S(1)} %get-tuple-element.24), channel_id=1, source_target_pairs={{0,8},{8,0},{16,24},{24,16},{1,9},{9,1},{17,25},{25,17},{2,10},{10... | collective-permute-start | bytes 6291464 | tf_op jit(solution)/shard_map/ppermute | solution.py:424
  6.0 7.9 %collective-permute-start = (bf16[64,512]{1,0:T(8,128)(2,1)S(1)}, bf16[64,512]{1,0:T(8,128)(2,1)S(1)}, u32[]{:S(2)}, u32[]{:S(2)}) collective-permute-start(bf16[64,512]{1,0:T(8,128)(2,1)S(1)} %get-tuple-element.20), channel_id=1, source_target_pairs={{0,4},{2,6},{4,0},{6,2},{1,5},{3,7},{5,1},{7,3},{8,12},{10,14},{12... | collective-permute-start | bytes 196616 | tf_op jit(solution)/shard_map/ppermute | solution.py:424
  9.6 6.7 %collective-permute-start.1 = (bf16[64,512]{1,0:T(8,128)(2,1)S(1)}, bf16[64,512]{1,0:T(8,128)(2,1)S(1)}, u32[]{:S(2)}, u32[]{:S(2)}) collective-permute-start(bf16[64,512]{1,0:T(8,128)(2,1)S(1)} %get-tuple-element.21), channel_id=1, source_target_pairs={{0,6},{2,4},{4,2},{6,0},{1,7},{3,5},{5,3},{7,1},{8,14},{10,12},{12... | collective-permute-start | bytes 196616 | tf_op jit(solution)/shard_map/ppermute | solution.py:424
  10.9 5.5 %collective-permute-start.2 = (bf16[64,512]{1,0:T(8,128)(2,1)S(1)}, bf16[64,512]{1,0:T(8,128)(2,1)S(1)}, u32[]{:S(2)}, u32[]{:S(2)}) collective-permute-start(bf16[64,512]{1,0:T(8,128)(2,1)S(1)} %get-tuple-element.22), channel_id=1, source_target_pairs={{0,2},{2,0},{4,6},{6,4},{1,3},{3,1},{5,7},{7,5},{8,10},{10,8},{12,... | collective-permute-start | bytes 196616 | tf_op jit(solution)/shard_map/ppermute | solution.py:424
  16.5 4.6 %collective-permute-start.12 = (bf16[64,512]{1,0:T(8,128)(2,1)S(1)}, bf16[64,512]{1,0:T(8,128)(2,1)S(1)}, u32[]{:S(2)}, u32[]{:S(2)}) collective-permute-start(bf16[64,512]{1,0:T(8,128)(2,1)S(1)} %ratio_chunk.1.refs_0_.ratio_ref), channel_id=1, source_target_pairs={{0,8},{8,0},{16,24},{24,16},{1,9},{9,1},{17,25},{25,17},{2,10},{10... | collective-permute-start | bytes 196616 | tf_op jit(solution)/shard_map/ppermute | solution.py:424
  16.6 7.3 %collective-permute-start.5 = (bf16[64,512]{1,0:T(8,128)(2,1)S(1)}, bf16[64,512]{1,0:T(8,128)(2,1)S(1)}, u32[]{:S(2)}, u32[]{:S(2)}) collective-permute-start(bf16[64,512]{1,0:T(8,128)(2,1)S(1)} %ratio_chunk.1.refs_0_.ratio_ref), channel_id=1, source_target_pairs={{0,4},{2,6},{4,0},{6,2},{1,5},{3,7},{5,1},{7,3},{8,12},{10,14},{12... | collective-permute-start | bytes 196616 | tf_op jit(solution)/shard_map/ppermute | solution.py:424
  19.4 6.7 %collective-permute-start.4 = (bf16[64,512]{1,0:T(8,128)(2,1)S(1)}, bf16[64,512]{1,0:T(8,128)(2,1)S(1)}, u32[]{:S(2)}, u32[]{:S(2)}) collective-permute-start(bf16[64,512]{1,0:T(8,128)(2,1)S(1)} %ratio_chunk.1.refs_0_.ratio_ref), channel_id=1, source_target_pairs={{0,6},{2,4},{4,2},{6,0},{1,7},{3,5},{5,3},{7,1},{8,14},{10,12},{12... | collective-permute-start | bytes 196616 | tf_op jit(solution)/shard_map/ppermute | solution.py:424
  20.1 6.1 %collective-permute-start.3 = (bf16[64,512]{1,0:T(8,128)(2,1)S(1)}, bf16[64,512]{1,0:T(8,128)(2,1)S(1)}, u32[]{:S(2)}, u32[]{:S(2)}) collective-permute-start(bf16[64,512]{1,0:T(8,128)(2,1)S(1)} %ratio_chunk.1.refs_0_.ratio_ref), channel_id=1, source_target_pairs={{0,2},{2,0},{4,6},{6,4},{1,3},{3,1},{5,7},{7,5},{8,10},{10,8},{12,... | collective-permute-start | bytes 196616 | tf_op jit(solution)/shard_map/ppermute | solution.py:424
  21.6 8.2 %collective-permute-start.13 = (bf16[64,2048]{1,0:T(8,128)(2,1)S(1)}, bf16[64,2048]{1,0:T(8,128)(2,1)S(1)}, u32[]{:S(2)}, u32[]{:S(2)}) collective-permute-start(bf16[64,2048]{1,0:T(8,128)(2,1)S(1)} %beta_pieces.3.own_ref), channel_id=1, source_target_pairs={{0,16},{8,24},{16,0},{24,8},{1,17},{9,25},{17,1},{25,9},{2,18},{10... | collective-permute-start | bytes 786440 | tf_op jit(solution)/shard_map/ppermute | solution.py:424
  23.9 14.9 %collective-permute-start.9 = (bf16[128,2048]{1,0:T(8,128)(2,1)S(1)}, bf16[128,2048]{1,0:T(8,128)(2,1)S(1)}, u32[]{:S(2)}, u32[]{:S(2)}) collective-permute-start(bf16[128,2048]{1,0:T(8,128)(2,1)S(1)} %hold.2), channel_id=1, source_target_pairs={{0,1},{1,0},{2,3},{3,2},{4,5},{5,4},{6,7},{7,6},{8,9},{9,8},{10,11... | collective-permute-start | bytes 1572872 | tf_op jit(solution)/shard_map/ppermute | solution.py:420
  26.3 1.5 %collective-permute-start.6 = (bf16[192,512]{1,0:T(8,128)(2,1)S(1)}, bf16[192,512]{1,0:T(8,128)(2,1)S(1)}, u32[]{:S(2)}, u32[]{:S(2)}) collective-permute-start(bf16[192,512]{1,0:T(8,128)(2,1)S(1)} %stack_rows.1.ratio_ref), channel_id=1, source_target_pairs={{0,8},{8,0},{16,24},{24,16},{1,9},{9,1},{17,25},{25,17},{2,10},{10... | collective-permute-start | bytes 589832 | tf_op jit(solution)/shard_map/ppermute | solution.py:424
  29.8 16.9 %collective-permute-start.14 = (bf16[128,2048]{1,0:T(8,128)(2,1)S(1)}, bf16[128,2048]{1,0:T(8,128)(2,1)S(1)}, u32[]{:S(2)}, u32[]{:S(2)}) collective-permute-start(bf16[128,2048]{1,0:T(8,128)(2,1)S(1)} %hold.3), channel_id=1, source_target_pairs={{0,16},{8,24},{16,0},{24,8},{1,17},{9,25},{17,1},{25,9},{2,18},{10... | collective-permute-start | bytes 1572872 | tf_op jit(solution)/shard_map/ppermute | solution.py:424
  31.4 11.4 %collective-permute-start.8 = (bf16[256,512]{1,0:T(8,128)(2,1)S(1)}, bf16[256,512]{1,0:T(8,128)(2,1)S(1)}, u32[]{:S(2)}, u32[]{:S(2)}) collective-permute-start(bf16[256,512]{1,0:T(8,128)(2,1)S(1)} %join_ratio.1.refs_0_), channel_id=1, source_target_pairs={{0,1},{1,0},{2,3},{3,2},{4,5},{5,4},{6,7},{7,6},{8,9},{9,8},{10,11... | collective-permute-start | bytes 786440 | tf_op jit(solution)/shard_map/ppermute | solution.py:420
  38.8 4.2 %collective-permute-start.10 = (bf16[64,2048]{1,0:T(8,128)(2,1)S(1)}, bf16[64,2048]{1,0:T(8,128)(2,1)S(1)}, u32[]{:S(2)}, u32[]{:S(2)}) collective-permute-start(bf16[64,2048]{1,0:T(8,128)(2,1)S(1)} %get-tuple-element.30.refs_3_), channel_id=1, source_target_pairs={{0,8},{8,0},{16,24},{24,16},{1,9},{9,1},{17,25},{25,17},{2,10},{10... | collective-permute-start | bytes 786440 | tf_op jit(solution)/shard_map/ppermute | solution.py:424
  38.9 4.1 %collective-permute-start.11 = (bf16[64,2048]{1,0:T(8,128)(2,1)S(1)}, bf16[64,2048]{1,0:T(8,128)(2,1)S(1)}, u32[]{:S(2)}, u32[]{:S(2)}) collective-permute-start(bf16[64,2048]{1,0:T(8,128)(2,1)S(1)} %get-tuple-element.31.refs_4_), channel_id=1, source_target_pairs={{0,8},{8,0},{16,24},{24,16},{1,9},{9,1},{17,25},{25,17},{2,10},{10... | collective-permute-start | bytes 786440 | tf_op jit(solution)/shard_map/ppermute | solution.py:424
  39.4 8.9 %collective-permute-start.15 = (bf16[64,2048]{1,0:T(8,128)(2,1)S(1)}, bf16[64,2048]{1,0:T(8,128)(2,1)S(1)}, u32[]{:S(2)}, u32[]{:S(2)}) collective-permute-start(bf16[64,2048]{1,0:T(8,128)(2,1)S(1)} %get-tuple-element.35.own_ref), channel_id=1, source_target_pairs={{0,16},{8,24},{16,0},{24,8},{1,17},{9,25},{17,1},{25,9},{2,18},{10... | collective-permute-start | bytes 786440 | tf_op jit(solution)/shard_map/ppermute | solution.py:424
  46.8 3.2 %collective-permute-start.17 = (bf16[128,2048]{1,0:T(8,128)(2,1)S(1)}, bf16[128,2048]{1,0:T(8,128)(2,1)S(1)}, u32[]{:S(2)}, u32[]{:S(2)}) collective-permute-start(bf16[128,2048]{1,0:T(8,128)(2,1)S(1)} %add_pair.4.refs_1_), channel_id=1, source_target_pairs={{0,8},{8,0},{16,24},{24,16},{1,9},{9,1},{17,25},{25,17},{2,10},{10... | collective-permute-start | bytes 1572872 | tf_op jit(solution)/shard_map/ppermute | solution.py:424
  46.9 2.2 %collective-permute-start.16 = (bf16[64,2048]{1,0:T(8,128)(2,1)S(1)}, bf16[64,2048]{1,0:T(8,128)(2,1)S(1)}, u32[]{:S(2)}, u32[]{:S(2)}) collective-permute-start(bf16[64,2048]{1,0:T(8,128)(2,1)S(1)} %add_pair.3.refs_0_), channel_id=1, source_target_pairs={{0,8},{8,0},{16,24},{24,16},{1,9},{9,1},{17,25},{25,17},{2,10},{10... | collective-permute-start | bytes 786440 | tf_op jit(solution)/shard_map/ppermute | solution.py:424
  48.4 1.6 %collective-permute-start.18 = (bf16[64,2048]{1,0:T(8,128)(2,1)S(1)}, bf16[64,2048]{1,0:T(8,128)(2,1)S(1)}, u32[]{:S(2)}, u32[]{:S(2)}) collective-permute-start(bf16[64,2048]{1,0:T(8,128)(2,1)S(1)} %add_pair.5.refs_2_), channel_id=1, source_target_pairs={{0,8},{8,0},{16,24},{24,16},{1,9},{9,1},{17,25},{25,17},{2,10},{10... | collective-permute-start | bytes 786440 | tf_op jit(solution)/shard_map/ppermute | solution.py:424

commit v15 on v13

--- a/solution.py
+++ b/solution.py
@@ -10,7 +10,8 @@
 BF16 = jnp.bfloat16
 F32 = jnp.float32
 MIB = 1024 * 1024
-HOLD_COST = 15 * 10**7
+ADD_COST = 22 * 10**8
+KERNEL_COST = 125 * 10**7
 TURN_COST = 10**9
 ANY = pl.BlockSpec(memory_space=pl.ANY)
 HBM = pl.BlockSpec(memory_space=pltpu.HBM)
@@ -202,7 +203,7 @@
         in_specs=[VMEM, VMEM],
         out_specs=VMEM,
         compiler_params=call_params(),
-        cost_estimate=cost(2 * words * docs * width, 2 * docs * width + 4 * words * width),
+        cost_estimate=cost(KERNEL_COST, 1) if words > 64 else cost(2 * words * docs * width, 2 * docs * width + 4 * words * width),
         name="own_product",
     )(ratio, docs_held)
 
@@ -230,7 +231,7 @@
         in_specs=[SMEM] + [VMEM] * 4,
         out_specs=[VMEM] * len(flips),
         compiler_params=call_params(),
-        cost_estimate=cost(2 * words * docs * side_width, 2 * (4 * words + docs) * side_width),
+        cost_estimate=cost(KERNEL_COST, 1) if len(flips) > 1 else cost(2 * words * docs * side_width, 2 * (4 * words + docs) * side_width),
         name="beta_pieces",
     )(here, product, ratio, docs_held, prob_held)
 
@@ -271,7 +272,7 @@
     )(array, *after)
 
 
-def add_pair(own, other, after=()):
+def add_pair(own, other, after=(), flops=1):
     def kernel(own_ref, other_ref, *rest):
         rest[-1][...] = (own_ref[...].astype(F32) + other_ref[...].astype(F32)).astype(BF16)
 
@@ -281,7 +282,7 @@
         in_specs=[VMEM, VMEM] + [ANY] * len(after),
         out_specs=VMEM,
         compiler_params=call_params(),
-        cost_estimate=cost(own.size, 6 * own.size),
+        cost_estimate=cost(max(flops, own.size), 6 * own.size),
         name="add_pair",
     )(own, other, *after)
 
@@ -422,21 +423,25 @@
     gathered = [swap(own_ratio, "topic", s) for s in order]
     far_bits = [1 << b for b in range(1, sizes.doc.bit_length() - 1)]
 
-    def beta(ratio, flips, after):
+    def beta(chunks, flips):
+        ratio, sibling_ratio = chunks[0], swap(chunks[0], "doc", 1)
+        if len(chunks) > 1:
+            ratio = stack_rows(chunks, [])
+            sibling_ratio = stack_rows([sibling_ratio] + [swap(chunk, "doc", 1) for chunk in chunks[1:]], [])
         pieces = beta_pieces(
-            sizes, here, own_product(ratio, docs_held), swap(ratio, "doc", 1), sibling_docs, prob_held, flips
+            sizes, here, own_product(ratio, docs_held), sibling_ratio, sibling_docs, prob_held, flips
         )
         for bit in far_bits[:-1]:
             pieces = [add_pair(part, swap(part, "doc", bit)) for part in pieces]
-        sent = [hold(pieces[0], after, HOLD_COST) if after else pieces[0], *pieces[1:]]
-        return [(part, swap(copy, "doc", far_bits[-1])) for part, copy in zip(pieces, sent)]
+        return [(part, swap(part, "doc", far_bits[-1])) for part in pieces]
 
     flips = [[0]] + [piece for piece in (order[:-1], order[-1:]) if piece]
-    pairs = beta(own_ratio, flips[:1], [])
+    pairs = beta([own_ratio], flips[:1])
     near_logits = [shift(hold(part, gathered[-1:]), s) for s, part in enumerate(near_logits, 1)]
-    pairs += beta(stack_rows(gathered, []), flips[1:], [pairs[0][1]])
-
-    ratio = join_ratio(sizes, here, [own_ratio] + gathered, [0] + order, [pairs[1][0]])
+    pairs += beta(gathered, flips[1:])
+    first = add_pair(*pairs[0], [], ADD_COST)
+
+    ratio = join_ratio(sizes, here, [own_ratio] + gathered, [0] + order, [first])
     far_ratios = [shift(ratio, s) for s in range(1, sizes.vocab)]
     far_logits = []
     for part in near_logits:
@@ -445,7 +450,7 @@
     turned = turn_ratios(sizes, here, ratio, far_ratios)
     theta, theta_done = theta_grad(sizes, here, turned, prob_held, far_logits, norm_held)
 
-    sums = [add_pair(*pair, [theta_done] if p else []) for p, pair in enumerate(pairs)]
+    sums = [first] + [add_pair(*pair, [theta_done]) for pair in pairs[1:]]
     out = place_pieces(sizes, here, sums, [swap(part, "doc", 1) for part in sums], flips, word_logits.shape)
     return theta, out
 

time: 51.6 us -> 51.3 us (level)
    ppermute x17 -> x19, waiting for transfers between devices: 10.4 us -> 8.32 us  [swap(): return lax.ppermute(array, axis, [(i, i ^ bits) for i in range(count)])]
    ppermute x2, waiting for transfers between devices: 7.64 us -> 9.16 us  [shift(): lax.ppermute(array, 'vocab', [(i, (i + by) % sizes.vocab) for i in range(...]
    ppermute x17 -> x19, starting transfers between devices: 15.8 us -> 16.1 us  [swap(): return lax.ppermute(array, axis, [(i, i ^ bits) for i in range(count)])]
  transfers between devices with their start and end apart: 19 -> 21, of which waited for: 13 -> 13; matrix products, arithmetic and copies ran while one was open for 0% -> 0% of each run, Pallas kernels for 14% -> 14%
where the time goes in v15:
time: 51.3 us; the launch traced here: 51.1 us
  starting transfers between devices  19.3 us (38%)
  waiting for transfers between devices  17.5 us (34%)
  Pallas kernels  13.5 us (26%)
  between operations  0.81 us (2%)
    ppermute x19, starting transfers between devices, swap(): return lax.ppermute(array, axis, [(i, i ^ bits) for i in range(count)])  16.1 us
    ppermute x2, waiting for transfers between devices, shift(): lax.ppermute(array, 'vocab', [(i, (i + by) % sizes.vocab) for i in range(...  9.16 us
    ppermute x19, waiting for transfers between devices, swap(): return lax.ppermute(array, axis, [(i, i ^ bits) for i in range(count)])  8.32 us
    pallas_call x1, Pallas kernels, rate_partial(): pl.pallas_call(kernel, out_shape=[jax.ShapeDtypeStruct((chunk, docs), BF1...  4.78 us
    pallas_call x1, Pallas kernels, theta_grad(): pl.pallas_call(kernel, out_shape=[jax.ShapeDtypeStruct((docs, share), F32...  3.66 us
    ppermute x2, starting transfers between devices, shift(): lax.ppermute(array, 'vocab', [(i, (i + by) % sizes.vocab) for i in range(...  3.24 us
    pallas_call x1, Pallas kernels, place_pieces(): pl.pallas_call(kernel, out_shape=jax.ShapeDtypeStruct(shape, BF16), in_sp...  1.37 us
    pallas_call x2, Pallas kernels, beta_pieces(): pl.pallas_call(kernel, out_shape=[jax.ShapeDtypeStruct((rows * len(piece)...  1.15 us
  transfers between devices with their start and end apart: 21, of which 13 were waited for; matrix products, arithmetic and copies ran while one was open for 0% of the time, Pallas kernels for 14%

profile of v15, /device:TPU:0, one launch (start us, length us, event | category | flops | bytes accessed | tf_op | source)
XLA Modules:
  0.0 51.1 jit_solution(16000619363693825904)
XLA Ops:
  0.6 4.8 %rate_partial.1 = (bf16[64,512]{1,0:T(8,128)(2,1)S(1)}, bf16[64,512]{1,0:T(8,128)(2,1)S(1)}, bf16[64,512]{1,0:T(8,128)(2,1)S(1)}, bf16[64,512]{1,0:T(8,128)(2,1)...) custom-call(s32[1]{0:T(128)} %bitcast.here_ref, ...), custom_call_target="tpu_custom_call" | custom-call | flops 1073741824 | bytes 6291456 | tf_op jit(solution)/shard_map/rate_partial/pallas_call | solution.py:104
  5.4 0.5 %collective-permute-start.7 = (bf16[512,2048]{1,0:T(8,128)(2,1)S(1)}, bf16[512,2048]{1,0:T(8,128)(2,1)S(1)}, u32[]{:S(2)}, u32[]{:S(2)}) collective-permute-start(bf16[512,2048]{1,0:T(8,128)(2,1)S(1)} %get-tuple-element.24), channel_id=1, source_target_pairs={{0,8},{8,0},{16,24},{24,16},{1,9},{9,1},{17,25},{25,17},{2,10},{10... | collective-permute-start | bytes 6291464 | tf_op jit(solution)/shard_map/ppermute | solution.py:412
  6.0 3.7 %collective-permute-start = (bf16[64,512]{1,0:T(8,128)(2,1)S(1)}, bf16[64,512]{1,0:T(8,128)(2,1)S(1)}, u32[]{:S(2)}, u32[]{:S(2)}) collective-permute-start(bf16[64,512]{1,0:T(8,128)(2,1)S(1)} %get-tuple-element.20), channel_id=1, source_target_pairs={{0,4},{2,6},{4,0},{6,2},{1,5},{3,7},{5,1},{7,3},{8,12},{10,14},{12... | collective-permute-start | bytes 196616 | tf_op jit(solution)/shard_map/ppermute | solution.py:412
  9.6 1.3 %collective-permute-start.1 = (bf16[64,512]{1,0:T(8,128)(2,1)S(1)}, bf16[64,512]{1,0:T(8,128)(2,1)S(1)}, u32[]{:S(2)}, u32[]{:S(2)}) collective-permute-start(bf16[64,512]{1,0:T(8,128)(2,1)S(1)} %get-tuple-element.21), channel_id=1, source_target_pairs={{0,6},{2,4},{4,2},{6,0},{1,7},{3,5},{5,3},{7,1},{8,14},{10,12},{12... | collective-permute-start | bytes 196616 | tf_op jit(solution)/shard_map/ppermute | solution.py:412
  11.0 0.2 collective-permute-start.2
  11.2 0.8 %chunk_counts.1.refs_4_ = f32[64,512]{1,0:T(8,128)S(1)} custom-call(s32[1]{0:T(128)} %bitcast.here_ref, s32[16]{0:T(128)} %doc_at.1, s32[16]{0:T(128)} %word_at.1, s32[16,64,128]{2,1,0:T(8,128)S(1)} %copy-done), custom_call_target="tpu_custom_call" | custom-call | flops 131072 | bytes 524288 | tf_op jit(solution)/shard_map/chunk_counts/pallas_call | solution.py:143
  12.0 1.8 %collective-permute-done.refs_1_ = bf16[64,512]{1,0:T(8,128)(2,1)S(1)} collective-permute-done((bf16[64,512]{1,0:T(8,128)(2,1)S(1)}, bf16[64,512]{1,0:T(8,128)(2,1)S(1)}, u32[]{:S(2)}, u32[]{:S(2)}) %collective-permute-start) | collective-permute-done | bytes 65568 | tf_op jit(solution)/shard_map/ppermute | solution.py:412
  13.9 2.4 %collective-permute-done.1.refs_2_ = bf16[64,512]{1,0:T(8,128)(2,1)S(1)} collective-permute-done((bf16[64,512]{1,0:T(8,128)(2,1)S(1)}, bf16[64,512]{1,0:T(8,128)(2,1)S(1)}, u32[]{:S(2)}, u32[]{:S(2)}) %collective-permute-start.1) | collective-permute-done | bytes 65568 | tf_op jit(solution)/shard_map/ppermute | solution.py:412
  16.6 2.8 %collective-permute-start.5 = (bf16[64,512]{1,0:T(8,128)(2,1)S(1)}, bf16[64,512]{1,0:T(8,128)(2,1)S(1)}, u32[]{:S(2)}, u32[]{:S(2)}) collective-permute-start(bf16[64,512]{1,0:T(8,128)(2,1)S(1)} %ratio_chunk.1.ratio_ref.refs_0_), channel_id=1, source_target_pairs={{0,4},{2,6},{4,0},{6,2},{1,5},{3,7},{5,1},{7,3},{8,12},{10,14},{12... | collective-permute-start | bytes 196616 | tf_op jit(solution)/shard_map/ppermute | solution.py:412
  19.4 0.7 %collective-permute-start.4 = (bf16[64,512]{1,0:T(8,128)(2,1)S(1)}, bf16[64,512]{1,0:T(8,128)(2,1)S(1)}, u32[]{:S(2)}, u32[]{:S(2)}) collective-permute-start(bf16[64,512]{1,0:T(8,128)(2,1)S(1)} %ratio_chunk.1.ratio_ref.refs_0_), channel_id=1, source_target_pairs={{0,6},{2,4},{4,2},{6,0},{1,7},{3,5},{5,3},{7,1},{8,14},{10,12},{12... | collective-permute-start | bytes 196616 | tf_op jit(solution)/shard_map/ppermute | solution.py:412
  20.1 0.5 collective-permute-start.3
  20.6 0.5 own_product.2.product_ref
  21.1 0.5 beta_pieces.2.own_ref
  21.6 1.6 %collective-permute-start.8 = (bf16[64,2048]{1,0:T(8,128)(2,1)S(1)}, bf16[64,2048]{1,0:T(8,128)(2,1)S(1)}, u32[]{:S(2)}, u32[]{:S(2)}) collective-permute-start(bf16[64,2048]{1,0:T(8,128)(2,1)S(1)} %beta_pieces.2.own_ref), channel_id=1, source_target_pairs={{0,16},{8,24},{16,0},{24,8},{1,17},{9,25},{17,1},{25,9},{2,18},{10... | collective-permute-start | bytes 786440 | tf_op jit(solution)/shard_map/ppermute | solution.py:412
  23.2 0.7 %collective-permute-done.5.refs_3_.rest_0_.refs_2_ = bf16[64,512]{1,0:T(8,128)(2,1)S(1)} collective-permute-done((bf16[64,512]{1,0:T(8,128)(2,1)S(1)}, bf16[64,512]{1,0:T(8,128)(2,1)S(1)}, u32[]{:S(2)}, u32[]{:S(2)}) %collective-permute-start.5) | collective-permute-done | bytes 65568 | tf_op jit(solution)/shard_map/ppermute | solution.py:412
  23.9 1.7 %collective-permute-start.10 = (bf16[128,2048]{1,0:T(8,128)(2,1)S(1)}, bf16[128,2048]{1,0:T(8,128)(2,1)S(1)}, u32[]{:S(2)}, u32[]{:S(2)}) collective-permute-start(bf16[128,2048]{1,0:T(8,128)(2,1)S(1)} %hold.1), channel_id=1, source_target_pairs={{0,1},{1,0},{2,3},{3,2},{4,5},{5,4},{6,7},{7,6},{8,9},{9,8},{10,11... | collective-permute-start | bytes 1572872 | tf_op jit(solution)/shard_map/ppermute | solution.py:408
  25.6 0.5 %collective-permute-done.4.refs_2_.refs_1_ = bf16[64,512]{1,0:T(8,128)(2,1)S(1)} collective-permute-done((bf16[64,512]{1,0:T(8,128)(2,1)S(1)}, bf16[64,512]{1,0:T(8,128)(2,1)S(1)}, u32[]{:S(2)}, u32[]{:S(2)}) %collective-permute-start.4) | collective-permute-done | bytes 65568 | tf_op jit(solution)/shard_map/ppermute | solution.py:412
  26.3 0.3 collective-permute-start.11
  26.6 0.6 %own_product.3.product_ref = f32[192,2048]{1,0:T(8,128)S(1)} custom-call(bf16[192,512]{1,0:T(8,128)(2,1)S(1)} %stack_rows.2.ratio_ref, bf16[512,2048]{1,0:T(8,128)(2,1)S(1)} %get-tuple-element.23.doc_ref), custom_call_target="tpu_custom_call" | custom-call | flops 1250000000 | bytes 1 | tf_op jit(solution)/shard_map/own_product/pallas_call | solution.py:200
  27.6 0.7 %beta_pieces.3 = (bf16[128,2048]{1,0:T(8,128)(2,1)S(1)}, bf16[64,2048]{1,0:T(8,128)(2,1)S(1)}) custom-call(s32[1]{0:T(128)} %bitcast.here_ref, f32[192,2048]{1,0:T(8,128)S(1)} %own_product.3.product_ref, bf16[192,512]{1,0:T(8,128)(2,1)S(1)} %stack_rows.3.ratio_ref, bf16[512,2048]{1,0:T(8,128)(2,1)S(1)} %collective-permute-done.7.doc_ref, ...), custom_call_target="tpu_custom_call" | custom-call | flops 1250000000 | bytes 1 | tf_op jit(solution)/shard_map/beta_pieces/pallas_call | solution.py:228
  28.2 1.6 %collective-permute-start.16 = (bf16[128,2048]{1,0:T(8,128)(2,1)S(1)}, bf16[128,2048]{1,0:T(8,128)(2,1)S(1)}, u32[]{:S(2)}, u32[]{:S(2)}) collective-permute-start(bf16[128,2048]{1,0:T(8,128)(2,1)S(1)} %get-tuple-element.29.rest_0_.own_ref), channel_id=1, source_target_pairs={{0,16},{8,24},{16,0},{24,8},{1,17},{9,25},{17,1},{25,9},{2,18},{10... | collective-permute-start | bytes 1572872 | tf_op jit(solution)/shard_map/ppermute | solution.py:412
  29.9 1.6 %collective-permute-start.9 = (bf16[256,512]{1,0:T(8,128)(2,1)S(1)}, bf16[256,512]{1,0:T(8,128)(2,1)S(1)}, u32[]{:S(2)}, u32[]{:S(2)}) collective-permute-start(bf16[256,512]{1,0:T(8,128)(2,1)S(1)} %join_ratio.1.refs_0_), channel_id=1, source_target_pairs={{0,1},{1,0},{2,3},{3,2},{4,5},{5,4},{6,7},{7,6},{8,9},{9,8},{10,11... | collective-permute-start | bytes 786440 | tf_op jit(solution)/shard_map/ppermute | solution.py:408
  31.5 7.4 %collective-permute-done.10.in_ref = bf16[128,2048]{1,0:T(8,128)(2,1)S(1)} collective-permute-done((bf16[128,2048]{1,0:T(8,128)(2,1)S(1)}, bf16[128,2048]{1,0:T(8,128)(2,1)S(1)}, u32[]{:S(2)}, u32[]{:S(2)}) %collective-permute-start.10) | collective-permute-done | bytes 524320 | tf_op jit(solution)/shard_map/ppermute | solution.py:408
  39.0 0.5 collective-permute-start.15
  39.5 1.6 %collective-permute-start.17 = (bf16[64,2048]{1,0:T(8,128)(2,1)S(1)}, bf16[64,2048]{1,0:T(8,128)(2,1)S(1)}, u32[]{:S(2)}, u32[]{:S(2)}) collective-permute-start(bf16[64,2048]{1,0:T(8,128)(2,1)S(1)} %get-tuple-element.35.own_ref), channel_id=1, source_target_pairs={{0,16},{8,24},{16,0},{24,8},{1,17},{9,25},{17,1},{25,9},{2,18},{10... | collective-permute-start | bytes 786440 | tf_op jit(solution)/shard_map/ppermute | solution.py:412
  41.0 1.8 %collective-permute-done.9.refs_1_ = bf16[256,512]{1,0:T(8,128)(2,1)S(1)} collective-permute-done((bf16[256,512]{1,0:T(8,128)(2,1)S(1)}, bf16[256,512]{1,0:T(8,128)(2,1)S(1)}, u32[]{:S(2)}, u32[]{:S(2)}) %collective-permute-start.9) | collective-permute-done | bytes 262176 | tf_op jit(solution)/shard_map/ppermute | solution.py:408
  43.1 3.7 %theta_grad.1 = (f32[512,2048]{1,0:T(8,128)}, f32[8,128]{1,0:T(8,128)S(1)}) custom-call(s32[1]{0:T(128)} %bitcast.here_ref, bf16[512,256]{1,0:T(8,128)(2,1)S(1)} %get-tuple-element.26.refs_0_, bf16[512,256]{1,0:T(8,128)(2,1)S(1)} %get-tuple-element.27.refs_1_, bf16[256,4096]{1,0:T(8,128)(2,1)S(1)} %get-tuple-element.25.prob_ref.refs_2_, ...), custom_call_target="tpu_custom_call" | custom-call | flops 1 | bytes 1 | tf_op jit(solution)/shard_map/theta_grad/pallas_call | solution.py:351
  46.9 0.5 collective-permute-start.18
  47.4 0.6 %collective-permute-done.17.other_ref = bf16[64,2048]{1,0:T(8,128)(2,1)S(1)} collective-permute-done((bf16[64,2048]{1,0:T(8,128)(2,1)S(1)}, bf16[64,2048]{1,0:T(8,128)(2,1)S(1)}, u32[]{:S(2)}, u32[]{:S(2)}) %collective-permute-start.17) | collective-permute-done | bytes 262176 | tf_op jit(solution)/shard_map/ppermute | solution.py:412
  48.2 1.0 %collective-permute-done.18.refs_3_ = bf16[64,2048]{1,0:T(8,128)(2,1)S(1)} collective-permute-done((bf16[64,2048]{1,0:T(8,128)(2,1)S(1)}, bf16[64,2048]{1,0:T(8,128)(2,1)S(1)}, u32[]{:S(2)}, u32[]{:S(2)}) %collective-permute-start.18) | collective-permute-done | bytes 262176 | tf_op jit(solution)/shard_map/ppermute | solution.py:412
  49.2 0.5 %collective-permute-done.20.refs_5_ = bf16[64,2048]{1,0:T(8,128)(2,1)S(1)} collective-permute-done((bf16[64,2048]{1,0:T(8,128)(2,1)S(1)}, bf16[64,2048]{1,0:T(8,128)(2,1)S(1)}, u32[]{:S(2)}, u32[]{:S(2)}) %collective-permute-start.20) | collective-permute-done | bytes 262176 | tf_op jit(solution)/shard_map/ppermute | solution.py:412
  49.7 1.4 %place_pieces.1 = bf16[256,4096]{1,0:T(8,128)(2,1)} custom-call(s32[1]{0:T(128)} %bitcast.here_ref, bf16[64,2048]{1,0:T(8,128)(2,1)S(1)} %add_pair.3.refs_4_.refs_0_, bf16[128,2048]{1,0:T(8,128)(2,1)S(1)} %add_pair.4.refs_1_, bf16[64,2048]{1,0:T(8,128)(2,1)S(1)} %add_pair.5.refs_2_, bf16[64,2048]{1,0:T(8,128)(2,1)S(1)} %collective-permute-done.18.refs_3_, ...), custom_call_target="tpu_custom_call" | custom-call | bytes 4194304 | tf_op jit(solution)/shard_map/place_pieces/pallas_call | solution.py:389
  (30 shorter events, 1.6 us)
Async XLA Ops:
  0.6 10.6 %copy-start = (s32[16,64,128]{2,1,0:T(8,128)S(1)}, s32[16,64,128]{2,1,0:T(8,128)}, u32[]{:S(2)}) copy-start(s32[16,64,128]{2,1,0:T(8,128)} %count_ref.1) | copy-start | bytes 1572868
  5.4 15.7 %collective-permute-start.7 = (bf16[512,2048]{1,0:T(8,128)(2,1)S(1)}, bf16[512,2048]{1,0:T(8,128)(2,1)S(1)}, u32[]{:S(2)}, u32[]{:S(2)}) collective-permute-start(bf16[512,2048]{1,0:T(8,128)(2,1)S(1)} %get-tuple-element.24), channel_id=1, source_target_pairs={{0,8},{8,0},{16,24},{24,16},{1,9},{9,1},{17,25},{25,17},{2,10},{10... | collective-permute-start | bytes 6291464 | tf_op jit(solution)/shard_map/ppermute | solution.py:412
  6.0 7.9 %collective-permute-start = (bf16[64,512]{1,0:T(8,128)(2,1)S(1)}, bf16[64,512]{1,0:T(8,128)(2,1)S(1)}, u32[]{:S(2)}, u32[]{:S(2)}) collective-permute-start(bf16[64,512]{1,0:T(8,128)(2,1)S(1)} %get-tuple-element.20), channel_id=1, source_target_pairs={{0,4},{2,6},{4,0},{6,2},{1,5},{3,7},{5,1},{7,3},{8,12},{10,14},{12... | collective-permute-start | bytes 196616 | tf_op jit(solution)/shard_map/ppermute | solution.py:412
  9.6 6.7 %collective-permute-start.1 = (bf16[64,512]{1,0:T(8,128)(2,1)S(1)}, bf16[64,512]{1,0:T(8,128)(2,1)S(1)}, u32[]{:S(2)}, u32[]{:S(2)}) collective-permute-start(bf16[64,512]{1,0:T(8,128)(2,1)S(1)} %get-tuple-element.21), channel_id=1, source_target_pairs={{0,6},{2,4},{4,2},{6,0},{1,7},{3,5},{5,3},{7,1},{8,14},{10,12},{12... | collective-permute-start | bytes 196616 | tf_op jit(solution)/shard_map/ppermute | solution.py:412
  11.0 5.5 %collective-permute-start.2 = (bf16[64,512]{1,0:T(8,128)(2,1)S(1)}, bf16[64,512]{1,0:T(8,128)(2,1)S(1)}, u32[]{:S(2)}, u32[]{:S(2)}) collective-permute-start(bf16[64,512]{1,0:T(8,128)(2,1)S(1)} %get-tuple-element.22), channel_id=1, source_target_pairs={{0,2},{2,0},{4,6},{6,4},{1,3},{3,1},{5,7},{7,5},{8,10},{10,8},{12,... | collective-permute-start | bytes 196616 | tf_op jit(solution)/shard_map/ppermute | solution.py:412
  16.5 4.6 %collective-permute-start.6 = (bf16[64,512]{1,0:T(8,128)(2,1)S(1)}, bf16[64,512]{1,0:T(8,128)(2,1)S(1)}, u32[]{:S(2)}, u32[]{:S(2)}) collective-permute-start(bf16[64,512]{1,0:T(8,128)(2,1)S(1)} %ratio_chunk.1.ratio_ref.refs_0_), channel_id=1, source_target_pairs={{0,8},{8,0},{16,24},{24,16},{1,9},{9,1},{17,25},{25,17},{2,10},{10... | collective-permute-start | bytes 196616 | tf_op jit(solution)/shard_map/ppermute | solution.py:412
  16.6 7.3 %collective-permute-start.5 = (bf16[64,512]{1,0:T(8,128)(2,1)S(1)}, bf16[64,512]{1,0:T(8,128)(2,1)S(1)}, u32[]{:S(2)}, u32[]{:S(2)}) collective-permute-start(bf16[64,512]{1,0:T(8,128)(2,1)S(1)} %ratio_chunk.1.ratio_ref.refs_0_), channel_id=1, source_target_pairs={{0,4},{2,6},{4,0},{6,2},{1,5},{3,7},{5,1},{7,3},{8,12},{10,14},{12... | collective-permute-start | bytes 196616 | tf_op jit(solution)/shard_map/ppermute | solution.py:412
  19.4 6.7 %collective-permute-start.4 = (bf16[64,512]{1,0:T(8,128)(2,1)S(1)}, bf16[64,512]{1,0:T(8,128)(2,1)S(1)}, u32[]{:S(2)}, u32[]{:S(2)}) collective-permute-start(bf16[64,512]{1,0:T(8,128)(2,1)S(1)} %ratio_chunk.1.ratio_ref.refs_0_), channel_id=1, source_target_pairs={{0,6},{2,4},{4,2},{6,0},{1,7},{3,5},{5,3},{7,1},{8,14},{10,12},{12... | collective-permute-start | bytes 196616 | tf_op jit(solution)/shard_map/ppermute | solution.py:412
  20.1 6.1 %collective-permute-start.3 = (bf16[64,512]{1,0:T(8,128)(2,1)S(1)}, bf16[64,512]{1,0:T(8,128)(2,1)S(1)}, u32[]{:S(2)}, u32[]{:S(2)}) collective-permute-start(bf16[64,512]{1,0:T(8,128)(2,1)S(1)} %ratio_chunk.1.ratio_ref.refs_0_), channel_id=1, source_target_pairs={{0,2},{2,0},{4,6},{6,4},{1,3},{3,1},{5,7},{7,5},{8,10},{10,8},{12,... | collective-permute-start | bytes 196616 | tf_op jit(solution)/shard_map/ppermute | solution.py:412
  21.6 8.2 %collective-permute-start.8 = (bf16[64,2048]{1,0:T(8,128)(2,1)S(1)}, bf16[64,2048]{1,0:T(8,128)(2,1)S(1)}, u32[]{:S(2)}, u32[]{:S(2)}) collective-permute-start(bf16[64,2048]{1,0:T(8,128)(2,1)S(1)} %beta_pieces.2.own_ref), channel_id=1, source_target_pairs={{0,16},{8,24},{16,0},{24,8},{1,17},{9,25},{17,1},{25,9},{2,18},{10... | collective-permute-start | bytes 786440 | tf_op jit(solution)/shard_map/ppermute | solution.py:412
  23.9 14.9 %collective-permute-start.10 = (bf16[128,2048]{1,0:T(8,128)(2,1)S(1)}, bf16[128,2048]{1,0:T(8,128)(2,1)S(1)}, u32[]{:S(2)}, u32[]{:S(2)}) collective-permute-start(bf16[128,2048]{1,0:T(8,128)(2,1)S(1)} %hold.1), channel_id=1, source_target_pairs={{0,1},{1,0},{2,3},{3,2},{4,5},{5,4},{6,7},{7,6},{8,9},{9,8},{10,11... | collective-permute-start | bytes 1572872 | tf_op jit(solution)/shard_map/ppermute | solution.py:408
  25.6 1.7 %collective-permute-start.13 = (bf16[64,512]{1,0:T(8,128)(2,1)S(1)}, bf16[64,512]{1,0:T(8,128)(2,1)S(1)}, u32[]{:S(2)}, u32[]{:S(2)}) collective-permute-start(bf16[64,512]{1,0:T(8,128)(2,1)S(1)} %collective-permute-done.5.refs_3_.rest_0_.refs_2_), channel_id=1, source_target_pairs={{0,8},{8,0},{16,24},{24,16},{1,9},{9,1},{17,25},{25,17},{2,10},{10... | collective-permute-start | bytes 196616 | tf_op jit(solution)/shard_map/ppermute | solution.py:412
  26.1 1.3 %collective-permute-start.12 = (bf16[64,512]{1,0:T(8,128)(2,1)S(1)}, bf16[64,512]{1,0:T(8,128)(2,1)S(1)}, u32[]{:S(2)}, u32[]{:S(2)}) collective-permute-start(bf16[64,512]{1,0:T(8,128)(2,1)S(1)} %collective-permute-done.4.refs_2_.refs_1_), channel_id=1, source_target_pairs={{0,8},{8,0},{16,24},{24,16},{1,9},{9,1},{17,25},{25,17},{2,10},{10... | collective-permute-start | bytes 196616 | tf_op jit(solution)/shard_map/ppermute | solution.py:412
  26.3 1.3 %collective-permute-start.11 = (bf16[64,512]{1,0:T(8,128)(2,1)S(1)}, bf16[64,512]{1,0:T(8,128)(2,1)S(1)}, u32[]{:S(2)}, u32[]{:S(2)}) collective-permute-start(bf16[64,512]{1,0:T(8,128)(2,1)S(1)} %collective-permute-done.3.refs_1_.refs_0_), channel_id=1, source_target_pairs={{0,8},{8,0},{16,24},{24,16},{1,9},{9,1},{17,25},{25,17},{2,10},{10... | collective-permute-start | bytes 196616 | tf_op jit(solution)/shard_map/ppermute | solution.py:412
  28.2 18.5 %collective-permute-start.16 = (bf16[128,2048]{1,0:T(8,128)(2,1)S(1)}, bf16[128,2048]{1,0:T(8,128)(2,1)S(1)}, u32[]{:S(2)}, u32[]{:S(2)}) collective-permute-start(bf16[128,2048]{1,0:T(8,128)(2,1)S(1)} %get-tuple-element.29.rest_0_.own_ref), channel_id=1, source_target_pairs={{0,16},{8,24},{16,0},{24,8},{1,17},{9,25},{17,1},{25,9},{2,18},{10... | collective-permute-start | bytes 1572872 | tf_op jit(solution)/shard_map/ppermute | solution.py:412
  29.9 12.9 %collective-permute-start.9 = (bf16[256,512]{1,0:T(8,128)(2,1)S(1)}, bf16[256,512]{1,0:T(8,128)(2,1)S(1)}, u32[]{:S(2)}, u32[]{:S(2)}) collective-permute-start(bf16[256,512]{1,0:T(8,128)(2,1)S(1)} %join_ratio.1.refs_0_), channel_id=1, source_target_pairs={{0,1},{1,0},{2,3},{3,2},{4,5},{5,4},{6,7},{7,6},{8,9},{9,8},{10,11... | collective-permute-start | bytes 786440 | tf_op jit(solution)/shard_map/ppermute | solution.py:408
  38.9 4.2 %collective-permute-start.14 = (bf16[64,2048]{1,0:T(8,128)(2,1)S(1)}, bf16[64,2048]{1,0:T(8,128)(2,1)S(1)}, u32[]{:S(2)}, u32[]{:S(2)}) collective-permute-start(bf16[64,2048]{1,0:T(8,128)(2,1)S(1)} %get-tuple-element.30.refs_3_), channel_id=1, source_target_pairs={{0,8},{8,0},{16,24},{24,16},{1,9},{9,1},{17,25},{25,17},{2,10},{10... | collective-permute-start | bytes 786440 | tf_op jit(solution)/shard_map/ppermute | solution.py:412
  39.0 4.1 %collective-permute-start.15 = (bf16[64,2048]{1,0:T(8,128)(2,1)S(1)}, bf16[64,2048]{1,0:T(8,128)(2,1)S(1)}, u32[]{:S(2)}, u32[]{:S(2)}) collective-permute-start(bf16[64,2048]{1,0:T(8,128)(2,1)S(1)} %get-tuple-element.31.refs_4_), channel_id=1, source_target_pairs={{0,8},{8,0},{16,24},{24,16},{1,9},{9,1},{17,25},{25,17},{2,10},{10... | collective-permute-start | bytes 786440 | tf_op jit(solution)/shard_map/ppermute | solution.py:412
  39.5 8.6 %collective-permute-start.17 = (bf16[64,2048]{1,0:T(8,128)(2,1)S(1)}, bf16[64,2048]{1,0:T(8,128)(2,1)S(1)}, u32[]{:S(2)}, u32[]{:S(2)}) collective-permute-start(bf16[64,2048]{1,0:T(8,128)(2,1)S(1)} %get-tuple-element.35.own_ref), channel_id=1, source_target_pairs={{0,16},{8,24},{16,0},{24,8},{1,17},{9,25},{17,1},{25,9},{2,18},{10... | collective-permute-start | bytes 786440 | tf_op jit(solution)/shard_map/ppermute | solution.py:412
  46.9 2.9 %collective-permute-start.19 = (bf16[128,2048]{1,0:T(8,128)(2,1)S(1)}, bf16[128,2048]{1,0:T(8,128)(2,1)S(1)}, u32[]{:S(2)}, u32[]{:S(2)}) collective-permute-start(bf16[128,2048]{1,0:T(8,128)(2,1)S(1)} %add_pair.4.refs_1_), channel_id=1, source_target_pairs={{0,8},{8,0},{16,24},{24,16},{1,9},{9,1},{17,25},{25,17},{2,10},{10... | collective-permute-start | bytes 1572872 | tf_op jit(solution)/shard_map/ppermute | solution.py:412
  46.9 2.3 %collective-permute-start.18 = (bf16[64,2048]{1,0:T(8,128)(2,1)S(1)}, bf16[64,2048]{1,0:T(8,128)(2,1)S(1)}, u32[]{:S(2)}, u32[]{:S(2)}) collective-permute-start(bf16[64,2048]{1,0:T(8,128)(2,1)S(1)} %add_pair.3.refs_4_.refs_0_), channel_id=1, source_target_pairs={{0,8},{8,0},{16,24},{24,16},{1,9},{9,1},{17,25},{25,17},{2,10},{10... | collective-permute-start | bytes 786440 | tf_op jit(solution)/shard_map/ppermute | solution.py:412
  48.1 1.6 %collective-permute-start.20 = (bf16[64,2048]{1,0:T(8,128)(2,1)S(1)}, bf16[64,2048]{1,0:T(8,128)(2,1)S(1)}, u32[]{:S(2)}, u32[]{:S(2)}) collective-permute-start(bf16[64,2048]{1,0:T(8,128)(2,1)S(1)} %add_pair.5.refs_2_), channel_id=1, source_target_pairs={{0,8},{8,0},{16,24},{24,16},{1,9},{9,1},{17,25},{25,17},{2,10},{10... | collective-permute-start | bytes 786440 | tf_op jit(solution)/shard_map/ppermute | solution.py:412

commit v16 on v15

--- a/solution.py
+++ b/solution.py
@@ -325,7 +325,7 @@
     )(here, ratio, *far_ratios)
 
 
-def theta_grad(sizes, here, turned, prob_held, far_logits, log_norm):
+def theta_grad(sizes, here, turned, prob_held, far_logits, log_norm, after):
     docs, words = turned[0].shape
     cuts = len(far_logits[0])
     rows, share = far_logits[0][0].shape
@@ -335,7 +335,7 @@
 
     def kernel(here_ref, *refs):
         turned_refs, prob_ref = refs[:count], refs[count]
-        logit_refs, norm_ref = refs[count + 1 : -3], refs[-3]
+        logit_refs, norm_ref = refs[count + 1 : -3 - len(after)], refs[-3 - len(after)]
         out_ref, done_ref = refs[-2:]
         done_ref[...] = jnp.zeros_like(done_ref)
         summed = jnp.dot(turned_refs[0][...], prob_ref[...], preferred_element_type=F32)
@@ -357,21 +357,26 @@
             in_specs=[pl.BlockSpec((docs, words), whole)] * count
             + [pl.BlockSpec((words, span), held)]
             + [pl.BlockSpec((rows, span), column)] * (cuts * (count - 1))
-            + [pl.BlockSpec((1, span), held)],
+            + [pl.BlockSpec((1, span), held)]
+            + [ANY] * len(after),
             out_specs=[pl.BlockSpec((docs, span), column), pl.BlockSpec((8, 128), whole)],
         ),
         compiler_params=call_params(16),
         cost_estimate=cost(1, 1),
         name="theta_grad",
-    )(here, *turned, prob_held, *sum(far_logits, []), log_norm)
-
-
-def place_pieces(sizes, here, own, other, flips, shape):
+    )(here, *turned, prob_held, *sum(far_logits, []), log_norm, *after)
+
+
+def place_pieces(sizes, here, own, other, flips, shape, so_far=None):
     pieces = len(own)
     side_width = shape[1] // 2
+    before = [] if so_far is None else [so_far]
 
     def kernel(here_ref, *refs):
-        own_refs, other_refs, (out_ref, sems) = refs[:pieces], refs[pieces : 2 * pieces], refs[-2:]
+        own_refs, other_refs = refs[:pieces], refs[pieces : 2 * pieces]
+        out_ref, sems = refs[2 * pieces + len(before)], refs[-1]
+        if not before:
+            refs[-2][...] = jnp.zeros_like(refs[-2])
         side, topic_at = sizes.side(here_ref), sizes.topic_at(here_ref)
         copies = []
         for p in range(pieces):
@@ -388,14 +393,15 @@
 
     return pl.pallas_call(
         kernel,
-        out_shape=jax.ShapeDtypeStruct(shape, BF16),
-        in_specs=[SMEM] + [VMEM] * (2 * pieces),
-        out_specs=HBM,
+        out_shape=[jax.ShapeDtypeStruct(shape, BF16)] + ([] if before else [jax.ShapeDtypeStruct((8, 128), F32)]),
+        in_specs=[SMEM] + [VMEM] * (2 * pieces) + [HBM] * len(before),
+        out_specs=[HBM] + ([] if before else [VMEM]),
         scratch_shapes=[pltpu.SemaphoreType.DMA((2 * sum(map(len, flips)),))],
-        compiler_params=call_params(),
-        cost_estimate=cost(0, 4 * shape[0] * shape[1]),
+        input_output_aliases={2 * pieces + 1: 0} if before else {},
+        compiler_params=call_params(),
+        cost_estimate=cost(0, 4 * sum(part.size for part in own)),
         name="place_pieces",
-    )(here, *own, *other)
+    )(here, *own, *other, *before)
 
 
 def on_device(sizes, doc_topics, word_logits, log_norm, tile_doc, tile_word, word_counts):
@@ -419,7 +425,7 @@
     arrived = [swap(parts[s], "topic", s) for s in order]
     counts = chunk_counts(sizes, here, word_counts, tile_doc, tile_word, docs, words)
     own_ratio = ratio_chunk([parts[0]] + arrived, counts, word_tile)
-    order.reverse()
+    order = order[1:] + order[:1]
     gathered = [swap(own_ratio, "topic", s) for s in order]
     far_bits = [1 << b for b in range(1, sizes.doc.bit_length() - 1)]
 
@@ -448,10 +454,11 @@
         pieces = list(cut_rows(part, 2, [pairs[1][0]]))
         far_logits.append(pieces + [swap(piece, "doc", 1) for piece in pieces])
     turned = turn_ratios(sizes, here, ratio, far_ratios)
-    theta, theta_done = theta_grad(sizes, here, turned, prob_held, far_logits, norm_held)
-
-    sums = [first] + [add_pair(*pair, [theta_done]) for pair in pairs[1:]]
-    out = place_pieces(sizes, here, sums, [swap(part, "doc", 1) for part in sums], flips, word_logits.shape)
+    out, early_done = place_pieces(sizes, here, [first], [swap(first, "doc", 1)], flips[:1], word_logits.shape)
+    theta, theta_done = theta_grad(sizes, here, turned, prob_held, far_logits, norm_held, [early_done])
+    sums = [add_pair(*pair, [theta_done]) for pair in pairs[1:]]
+    siblings = [swap(part, "doc", 1) for part in sums]
+    (out,) = place_pieces(sizes, here, sums, siblings, flips[1:], word_logits.shape, out)
     return theta, out
 
 

time: 51.3 us -> 51.3 us (level)
  Pallas kernels: 13.5 us -> 14.1 us
    ppermute x2, waiting for transfers between devices: 9.16 us -> 7.85 us  [shift(): lax.ppermute(array, 'vocab', [(i, (i + by) % sizes.vocab) for i in range(...]
    ppermute x19, waiting for transfers between devices: 8.32 us -> 9.28 us  [swap(): return lax.ppermute(array, axis, [(i, i ^ bits) for i in range(count)])]
    pallas_call x1 -> x2, Pallas kernels: 1.37 us -> 1.99 us  [place_pieces(): pl.pallas_call(kernel, out_shape=[jax.ShapeDtypeStruct(shape, BF16)] + ([...]
  transfers between devices with their start and end apart: 21 -> 21, of which waited for: 13 -> 12; matrix products, arithmetic and copies ran while one was open for 0% -> 0% of each run, Pallas kernels for 14% -> 16%
where the time goes in v16:
time: 51.3 us; the launch traced here: 51.2 us
  starting transfers between devices  19.1 us (37%)
  waiting for transfers between devices  17.1 us (33%)
  Pallas kernels  14.1 us (27%)
  between operations  0.82 us (2%)
    ppermute x19, starting transfers between devices, swap(): return lax.ppermute(array, axis, [(i, i ^ bits) for i in range(count)])  15.9 us
    ppermute x19, waiting for transfers between devices, swap(): return lax.ppermute(array, axis, [(i, i ^ bits) for i in range(count)])  9.28 us
    ppermute x2, waiting for transfers between devices, shift(): lax.ppermute(array, 'vocab', [(i, (i + by) % sizes.vocab) for i in range(...  7.85 us
    pallas_call x1, Pallas kernels, rate_partial(): pl.pallas_call(kernel, out_shape=[jax.ShapeDtypeStruct((chunk, docs), BF1...  4.78 us
    pallas_call x1, Pallas kernels, theta_grad(): pl.pallas_call(kernel, out_shape=[jax.ShapeDtypeStruct((docs, share), F32...  3.65 us
    ppermute x2, starting transfers between devices, shift(): lax.ppermute(array, 'vocab', [(i, (i + by) % sizes.vocab) for i in range(...  3.24 us
    pallas_call x2, Pallas kernels, place_pieces(): pl.pallas_call(kernel, out_shape=[jax.ShapeDtypeStruct(shape, BF16)] + ([...  1.99 us
    pallas_call x2, Pallas kernels, beta_pieces(): pl.pallas_call(kernel, out_shape=[jax.ShapeDtypeStruct((rows * len(piece)...  1.15 us
  transfers between devices with their start and end apart: 21, of which 12 were waited for; matrix products, arithmetic and copies ran while one was open for 0% of the time, Pallas kernels for 16%

profile of v16, /device:TPU:0, one launch (start us, length us, event | category | flops | bytes accessed | tf_op | source)
XLA Modules:
  0.0 51.2 jit_solution(6986516754150666114)
XLA Ops:
  0.6 4.8 %rate_partial.1 = (bf16[64,512]{1,0:T(8,128)(2,1)S(1)}, bf16[64,512]{1,0:T(8,128)(2,1)S(1)}, bf16[64,512]{1,0:T(8,128)(2,1)S(1)}, bf16[64,512]{1,0:T(8,128)(2,1)...) custom-call(s32[1]{0:T(128)} %bitcast.here_ref, ...), custom_call_target="tpu_custom_call" | custom-call | flops 1073741824 | bytes 6291456 | tf_op jit(solution)/shard_map/rate_partial/pallas_call | solution.py:104
  5.4 0.5 %collective-permute-start.7 = (bf16[512,2048]{1,0:T(8,128)(2,1)S(1)}, bf16[512,2048]{1,0:T(8,128)(2,1)S(1)}, u32[]{:S(2)}, u32[]{:S(2)}) collective-permute-start(bf16[512,2048]{1,0:T(8,128)(2,1)S(1)} %get-tuple-element.26), channel_id=1, source_target_pairs={{0,8},{8,0},{16,24},{24,16},{1,9},{9,1},{17,25},{25,17},{2,10},{10... | collective-permute-start | bytes 6291464 | tf_op jit(solution)/shard_map/ppermute | solution.py:418
  6.0 3.7 %collective-permute-start = (bf16[64,512]{1,0:T(8,128)(2,1)S(1)}, bf16[64,512]{1,0:T(8,128)(2,1)S(1)}, u32[]{:S(2)}, u32[]{:S(2)}) collective-permute-start(bf16[64,512]{1,0:T(8,128)(2,1)S(1)} %get-tuple-element.22), channel_id=1, source_target_pairs={{0,4},{2,6},{4,0},{6,2},{1,5},{3,7},{5,1},{7,3},{8,12},{10,14},{12... | collective-permute-start | bytes 196616 | tf_op jit(solution)/shard_map/ppermute | solution.py:418
  9.6 1.3 %collective-permute-start.1 = (bf16[64,512]{1,0:T(8,128)(2,1)S(1)}, bf16[64,512]{1,0:T(8,128)(2,1)S(1)}, u32[]{:S(2)}, u32[]{:S(2)}) collective-permute-start(bf16[64,512]{1,0:T(8,128)(2,1)S(1)} %get-tuple-element.23), channel_id=1, source_target_pairs={{0,6},{2,4},{4,2},{6,0},{1,7},{3,5},{5,3},{7,1},{8,14},{10,12},{12... | collective-permute-start | bytes 196616 | tf_op jit(solution)/shard_map/ppermute | solution.py:418
  11.0 0.2 collective-permute-start.2
  11.2 0.8 %chunk_counts.1.refs_4_ = f32[64,512]{1,0:T(8,128)S(1)} custom-call(s32[1]{0:T(128)} %bitcast.here_ref, s32[16]{0:T(128)} %doc_at.1, s32[16]{0:T(128)} %word_at.1, s32[16,64,128]{2,1,0:T(8,128)S(1)} %copy-done), custom_call_target="tpu_custom_call" | custom-call | flops 131072 | bytes 524288 | tf_op jit(solution)/shard_map/chunk_counts/pallas_call | solution.py:143
  12.0 1.8 %collective-permute-done.refs_1_ = bf16[64,512]{1,0:T(8,128)(2,1)S(1)} collective-permute-done((bf16[64,512]{1,0:T(8,128)(2,1)S(1)}, bf16[64,512]{1,0:T(8,128)(2,1)S(1)}, u32[]{:S(2)}, u32[]{:S(2)}) %collective-permute-start) | collective-permute-done | bytes 65568 | tf_op jit(solution)/shard_map/ppermute | solution.py:418
  13.9 2.4 %collective-permute-done.1.refs_2_ = bf16[64,512]{1,0:T(8,128)(2,1)S(1)} collective-permute-done((bf16[64,512]{1,0:T(8,128)(2,1)S(1)}, bf16[64,512]{1,0:T(8,128)(2,1)S(1)}, u32[]{:S(2)}, u32[]{:S(2)}) %collective-permute-start.1) | collective-permute-done | bytes 65568 | tf_op jit(solution)/shard_map/ppermute | solution.py:418
  16.6 2.8 %collective-permute-start.5 = (bf16[64,512]{1,0:T(8,128)(2,1)S(1)}, bf16[64,512]{1,0:T(8,128)(2,1)S(1)}, u32[]{:S(2)}, u32[]{:S(2)}) collective-permute-start(bf16[64,512]{1,0:T(8,128)(2,1)S(1)} %ratio_chunk.1.ratio_ref.refs_0_), channel_id=1, source_target_pairs={{0,4},{2,6},{4,0},{6,2},{1,5},{3,7},{5,1},{7,3},{8,12},{10,14},{12... | collective-permute-start | bytes 196616 | tf_op jit(solution)/shard_map/ppermute | solution.py:418
  19.4 0.7 %collective-permute-start.3 = (bf16[64,512]{1,0:T(8,128)(2,1)S(1)}, bf16[64,512]{1,0:T(8,128)(2,1)S(1)}, u32[]{:S(2)}, u32[]{:S(2)}) collective-permute-start(bf16[64,512]{1,0:T(8,128)(2,1)S(1)} %ratio_chunk.1.ratio_ref.refs_0_), channel_id=1, source_target_pairs={{0,6},{2,4},{4,2},{6,0},{1,7},{3,5},{5,3},{7,1},{8,14},{10,12},{12... | collective-permute-start | bytes 196616 | tf_op jit(solution)/shard_map/ppermute | solution.py:418
  20.1 0.5 collective-permute-start.4
  20.6 0.5 own_product.2.product_ref
  21.1 0.5 beta_pieces.2.own_ref
  21.6 1.6 %collective-permute-start.8 = (bf16[64,2048]{1,0:T(8,128)(2,1)S(1)}, bf16[64,2048]{1,0:T(8,128)(2,1)S(1)}, u32[]{:S(2)}, u32[]{:S(2)}) collective-permute-start(bf16[64,2048]{1,0:T(8,128)(2,1)S(1)} %beta_pieces.2.own_ref), channel_id=1, source_target_pairs={{0,16},{8,24},{16,0},{24,8},{1,17},{9,25},{17,1},{25,9},{2,18},{10... | collective-permute-start | bytes 786440 | tf_op jit(solution)/shard_map/ppermute | solution.py:418
  23.2 0.7 %collective-permute-done.5.refs_3_.rest_0_.refs_2_ = bf16[64,512]{1,0:T(8,128)(2,1)S(1)} collective-permute-done((bf16[64,512]{1,0:T(8,128)(2,1)S(1)}, bf16[64,512]{1,0:T(8,128)(2,1)S(1)}, u32[]{:S(2)}, u32[]{:S(2)}) %collective-permute-start.5) | collective-permute-done | bytes 65568 | tf_op jit(solution)/shard_map/ppermute | solution.py:418
  23.9 1.7 %collective-permute-start.10 = (bf16[128,2048]{1,0:T(8,128)(2,1)S(1)}, bf16[128,2048]{1,0:T(8,128)(2,1)S(1)}, u32[]{:S(2)}, u32[]{:S(2)}) collective-permute-start(bf16[128,2048]{1,0:T(8,128)(2,1)S(1)} %hold.1), channel_id=1, source_target_pairs={{0,1},{1,0},{2,3},{3,2},{4,5},{5,4},{6,7},{7,6},{8,9},{9,8},{10,11... | collective-permute-start | bytes 1572872 | tf_op jit(solution)/shard_map/ppermute | solution.py:414
  25.6 0.5 %collective-permute-done.3.refs_1_.refs_0_ = bf16[64,512]{1,0:T(8,128)(2,1)S(1)} collective-permute-done((bf16[64,512]{1,0:T(8,128)(2,1)S(1)}, bf16[64,512]{1,0:T(8,128)(2,1)S(1)}, u32[]{:S(2)}, u32[]{:S(2)}) %collective-permute-start.3) | collective-permute-done | bytes 65568 | tf_op jit(solution)/shard_map/ppermute | solution.py:418
  26.3 0.4 collective-permute-start.12
  26.9 0.6 %own_product.3.product_ref = f32[192,2048]{1,0:T(8,128)S(1)} custom-call(bf16[192,512]{1,0:T(8,128)(2,1)S(1)} %stack_rows.2.ratio_ref, bf16[512,2048]{1,0:T(8,128)(2,1)S(1)} %get-tuple-element.25.doc_ref), custom_call_target="tpu_custom_call" | custom-call | flops 1250000000 | bytes 1 | tf_op jit(solution)/shard_map/own_product/pallas_call | solution.py:200
  27.6 0.3 collective-permute-done.13.refs_2_
  28.0 0.7 %beta_pieces.3 = (bf16[128,2048]{1,0:T(8,128)(2,1)S(1)}, bf16[64,2048]{1,0:T(8,128)(2,1)S(1)}) custom-call(s32[1]{0:T(128)} %bitcast.here_ref, f32[192,2048]{1,0:T(8,128)S(1)} %own_product.3.product_ref, bf16[192,512]{1,0:T(8,128)(2,1)S(1)} %stack_rows.3.ratio_ref, bf16[512,2048]{1,0:T(8,128)(2,1)S(1)} %collective-permute-done.7.doc_ref, ...), custom_call_target="tpu_custom_call" | custom-call | flops 1250000000 | bytes 1 | tf_op jit(solution)/shard_map/beta_pieces/pallas_call | solution.py:228
  28.6 1.6 %collective-permute-start.17 = (bf16[128,2048]{1,0:T(8,128)(2,1)S(1)}, bf16[128,2048]{1,0:T(8,128)(2,1)S(1)}, u32[]{:S(2)}, u32[]{:S(2)}) collective-permute-start(bf16[128,2048]{1,0:T(8,128)(2,1)S(1)} %get-tuple-element.31.rest_0_.own_ref), channel_id=1, source_target_pairs={{0,16},{8,24},{16,0},{24,8},{1,17},{9,25},{17,1},{25,9},{2,18},{10... | collective-permute-start | bytes 1572872 | tf_op jit(solution)/shard_map/ppermute | solution.py:418
  30.4 1.6 %collective-permute-start.9 = (bf16[256,512]{1,0:T(8,128)(2,1)S(1)}, bf16[256,512]{1,0:T(8,128)(2,1)S(1)}, u32[]{:S(2)}, u32[]{:S(2)}) collective-permute-start(bf16[256,512]{1,0:T(8,128)(2,1)S(1)} %join_ratio.1.refs_0_), channel_id=1, source_target_pairs={{0,1},{1,0},{2,3},{3,2},{4,5},{5,4},{6,7},{7,6},{8,9},{9,8},{10,11... | collective-permute-start | bytes 786440 | tf_op jit(solution)/shard_map/ppermute | solution.py:414
  32.0 6.9 %collective-permute-done.10.in_ref = bf16[128,2048]{1,0:T(8,128)(2,1)S(1)} collective-permute-done((bf16[128,2048]{1,0:T(8,128)(2,1)S(1)}, bf16[128,2048]{1,0:T(8,128)(2,1)S(1)}, u32[]{:S(2)}, u32[]{:S(2)}) %collective-permute-start.10) | collective-permute-done | bytes 524320 | tf_op jit(solution)/shard_map/ppermute | solution.py:414
  39.0 0.5 collective-permute-start.15
  39.5 1.6 %collective-permute-start.18 = (bf16[64,2048]{1,0:T(8,128)(2,1)S(1)}, bf16[64,2048]{1,0:T(8,128)(2,1)S(1)}, u32[]{:S(2)}, u32[]{:S(2)}) collective-permute-start(bf16[64,2048]{1,0:T(8,128)(2,1)S(1)} %get-tuple-element.38.own_ref), channel_id=1, source_target_pairs={{0,16},{8,24},{16,0},{24,8},{1,17},{9,25},{17,1},{25,9},{2,18},{10... | collective-permute-start | bytes 786440 | tf_op jit(solution)/shard_map/ppermute | solution.py:418
  41.0 0.8 %place_pieces.2 = (bf16[256,4096]{1,0:T(8,128)(2,1)}, f32[8,128]{1,0:T(8,128)S(1)}) custom-call(s32[1]{0:T(128)} %bitcast.here_ref, bf16[64,2048]{1,0:T(8,128)(2,1)S(1)} %add_pair.3.refs_4_.refs_0_, bf16[64,2048]{1,0:T(8,128)(2,1)S(1)} %collective-permute-done.16.refs_1_), custom_call_target="tpu_custom_call" | custom-call | bytes 524288 | tf_op jit(solution)/shard_map/place_pieces/pallas_call | solution.py:394
  41.8 1.0 %collective-permute-done.9.refs_1_ = bf16[256,512]{1,0:T(8,128)(2,1)S(1)} collective-permute-done((bf16[256,512]{1,0:T(8,128)(2,1)S(1)}, bf16[256,512]{1,0:T(8,128)(2,1)S(1)}, u32[]{:S(2)}, u32[]{:S(2)}) %collective-permute-start.9) | collective-permute-done | bytes 262176 | tf_op jit(solution)/shard_map/ppermute | solution.py:414
  43.1 3.6 %theta_grad.1 = (f32[512,2048]{1,0:T(8,128)}, f32[8,128]{1,0:T(8,128)S(1)}) custom-call(s32[1]{0:T(128)} %bitcast.here_ref, bf16[512,256]{1,0:T(8,128)(2,1)S(1)} %get-tuple-element.28.refs_0_, bf16[512,256]{1,0:T(8,128)(2,1)S(1)} %get-tuple-element.29.refs_1_, bf16[256,4096]{1,0:T(8,128)(2,1)S(1)} %get-tuple-element.27.prob_ref.refs_2_, ...), custom_call_target="tpu_custom_call" | custom-call | flops 1 | bytes 1 | tf_op jit(solution)/shard_map/theta_grad/pallas_call | solution.py:351
  46.9 1.4 %collective-permute-done.18.other_ref = bf16[64,2048]{1,0:T(8,128)(2,1)S(1)} collective-permute-done((bf16[64,2048]{1,0:T(8,128)(2,1)S(1)}, bf16[64,2048]{1,0:T(8,128)(2,1)S(1)}, u32[]{:S(2)}, u32[]{:S(2)}) %collective-permute-start.18) | collective-permute-done | bytes 262176 | tf_op jit(solution)/shard_map/ppermute | solution.py:418
  48.5 1.5 %collective-permute-done.20.refs_3_ = bf16[64,2048]{1,0:T(8,128)(2,1)S(1)} collective-permute-done((bf16[64,2048]{1,0:T(8,128)(2,1)S(1)}, bf16[64,2048]{1,0:T(8,128)(2,1)S(1)}, u32[]{:S(2)}, u32[]{:S(2)}) %collective-permute-start.20) | collective-permute-done | bytes 262176 | tf_op jit(solution)/shard_map/ppermute | solution.py:418
  50.0 1.2 %place_pieces.3 = bf16[256,4096]{1,0:T(8,128)(2,1)} custom-call(s32[1]{0:T(128)} %bitcast.here_ref, bf16[128,2048]{1,0:T(8,128)(2,1)S(1)} %add_pair.4.refs_0_, bf16[64,2048]{1,0:T(8,128)(2,1)S(1)} %add_pair.5.refs_1_, bf16[128,2048]{1,0:T(8,128)(2,1)S(1)} %collective-permute-done.19.refs_2_, ...), custom_call_target="tpu_custom_call", output_to_operand_aliasing={{}: (5, {})} | custom-call | bytes 1572864 | tf_op jit(solution)/shard_map/place_pieces/pallas_call | solution.py:394
  (31 shorter events, 1.7 us)
Async XLA Ops:
  0.6 10.6 %copy-start = (s32[16,64,128]{2,1,0:T(8,128)S(1)}, s32[16,64,128]{2,1,0:T(8,128)}, u32[]{:S(2)}) copy-start(s32[16,64,128]{2,1,0:T(8,128)} %count_ref.1) | copy-start | bytes 1572868
  5.4 15.7 %collective-permute-start.7 = (bf16[512,2048]{1,0:T(8,128)(2,1)S(1)}, bf16[512,2048]{1,0:T(8,128)(2,1)S(1)}, u32[]{:S(2)}, u32[]{:S(2)}) collective-permute-start(bf16[512,2048]{1,0:T(8,128)(2,1)S(1)} %get-tuple-element.26), channel_id=1, source_target_pairs={{0,8},{8,0},{16,24},{24,16},{1,9},{9,1},{17,25},{25,17},{2,10},{10... | collective-permute-start | bytes 6291464 | tf_op jit(solution)/shard_map/ppermute | solution.py:418
  6.0 7.9 %collective-permute-start = (bf16[64,512]{1,0:T(8,128)(2,1)S(1)}, bf16[64,512]{1,0:T(8,128)(2,1)S(1)}, u32[]{:S(2)}, u32[]{:S(2)}) collective-permute-start(bf16[64,512]{1,0:T(8,128)(2,1)S(1)} %get-tuple-element.22), channel_id=1, source_target_pairs={{0,4},{2,6},{4,0},{6,2},{1,5},{3,7},{5,1},{7,3},{8,12},{10,14},{12... | collective-permute-start | bytes 196616 | tf_op jit(solution)/shard_map/ppermute | solution.py:418
  9.6 6.7 %collective-permute-start.1 = (bf16[64,512]{1,0:T(8,128)(2,1)S(1)}, bf16[64,512]{1,0:T(8,128)(2,1)S(1)}, u32[]{:S(2)}, u32[]{:S(2)}) collective-permute-start(bf16[64,512]{1,0:T(8,128)(2,1)S(1)} %get-tuple-element.23), channel_id=1, source_target_pairs={{0,6},{2,4},{4,2},{6,0},{1,7},{3,5},{5,3},{7,1},{8,14},{10,12},{12... | collective-permute-start | bytes 196616 | tf_op jit(solution)/shard_map/ppermute | solution.py:418
  11.0 5.5 %collective-permute-start.2 = (bf16[64,512]{1,0:T(8,128)(2,1)S(1)}, bf16[64,512]{1,0:T(8,128)(2,1)S(1)}, u32[]{:S(2)}, u32[]{:S(2)}) collective-permute-start(bf16[64,512]{1,0:T(8,128)(2,1)S(1)} %get-tuple-element.24), channel_id=1, source_target_pairs={{0,2},{2,0},{4,6},{6,4},{1,3},{3,1},{5,7},{7,5},{8,10},{10,8},{12,... | collective-permute-start | bytes 196616 | tf_op jit(solution)/shard_map/ppermute | solution.py:418
  16.5 4.6 %collective-permute-start.6 = (bf16[64,512]{1,0:T(8,128)(2,1)S(1)}, bf16[64,512]{1,0:T(8,128)(2,1)S(1)}, u32[]{:S(2)}, u32[]{:S(2)}) collective-permute-start(bf16[64,512]{1,0:T(8,128)(2,1)S(1)} %ratio_chunk.1.ratio_ref.refs_0_), channel_id=1, source_target_pairs={{0,8},{8,0},{16,24},{24,16},{1,9},{9,1},{17,25},{25,17},{2,10},{10... | collective-permute-start | bytes 196616 | tf_op jit(solution)/shard_map/ppermute | solution.py:418
  16.6 7.3 %collective-permute-start.5 = (bf16[64,512]{1,0:T(8,128)(2,1)S(1)}, bf16[64,512]{1,0:T(8,128)(2,1)S(1)}, u32[]{:S(2)}, u32[]{:S(2)}) collective-permute-start(bf16[64,512]{1,0:T(8,128)(2,1)S(1)} %ratio_chunk.1.ratio_ref.refs_0_), channel_id=1, source_target_pairs={{0,4},{2,6},{4,0},{6,2},{1,5},{3,7},{5,1},{7,3},{8,12},{10,14},{12... | collective-permute-start | bytes 196616 | tf_op jit(solution)/shard_map/ppermute | solution.py:418
  19.4 6.7 %collective-permute-start.3 = (bf16[64,512]{1,0:T(8,128)(2,1)S(1)}, bf16[64,512]{1,0:T(8,128)(2,1)S(1)}, u32[]{:S(2)}, u32[]{:S(2)}) collective-permute-start(bf16[64,512]{1,0:T(8,128)(2,1)S(1)} %ratio_chunk.1.ratio_ref.refs_0_), channel_id=1, source_target_pairs={{0,6},{2,4},{4,2},{6,0},{1,7},{3,5},{5,3},{7,1},{8,14},{10,12},{12... | collective-permute-start | bytes 196616 | tf_op jit(solution)/shard_map/ppermute | solution.py:418
  20.1 6.1 %collective-permute-start.4 = (bf16[64,512]{1,0:T(8,128)(2,1)S(1)}, bf16[64,512]{1,0:T(8,128)(2,1)S(1)}, u32[]{:S(2)}, u32[]{:S(2)}) collective-permute-start(bf16[64,512]{1,0:T(8,128)(2,1)S(1)} %ratio_chunk.1.ratio_ref.refs_0_), channel_id=1, source_target_pairs={{0,2},{2,0},{4,6},{6,4},{1,3},{3,1},{5,7},{7,5},{8,10},{10,8},{12,... | collective-permute-start | bytes 196616 | tf_op jit(solution)/shard_map/ppermute | solution.py:418
  21.6 8.6 %collective-permute-start.8 = (bf16[64,2048]{1,0:T(8,128)(2,1)S(1)}, bf16[64,2048]{1,0:T(8,128)(2,1)S(1)}, u32[]{:S(2)}, u32[]{:S(2)}) collective-permute-start(bf16[64,2048]{1,0:T(8,128)(2,1)S(1)} %beta_pieces.2.own_ref), channel_id=1, source_target_pairs={{0,16},{8,24},{16,0},{24,8},{1,17},{9,25},{17,1},{25,9},{2,18},{10... | collective-permute-start | bytes 786440 | tf_op jit(solution)/shard_map/ppermute | solution.py:418
  23.9 14.9 %collective-permute-start.10 = (bf16[128,2048]{1,0:T(8,128)(2,1)S(1)}, bf16[128,2048]{1,0:T(8,128)(2,1)S(1)}, u32[]{:S(2)}, u32[]{:S(2)}) collective-permute-start(bf16[128,2048]{1,0:T(8,128)(2,1)S(1)} %hold.1), channel_id=1, source_target_pairs={{0,1},{1,0},{2,3},{3,2},{4,5},{5,4},{6,7},{7,6},{8,9},{9,8},{10,11... | collective-permute-start | bytes 1572872 | tf_op jit(solution)/shard_map/ppermute | solution.py:414
  26.1 1.4 %collective-permute-start.11 = (bf16[64,512]{1,0:T(8,128)(2,1)S(1)}, bf16[64,512]{1,0:T(8,128)(2,1)S(1)}, u32[]{:S(2)}, u32[]{:S(2)}) collective-permute-start(bf16[64,512]{1,0:T(8,128)(2,1)S(1)} %collective-permute-done.3.refs_1_.refs_0_), channel_id=1, source_target_pairs={{0,8},{8,0},{16,24},{24,16},{1,9},{9,1},{17,25},{25,17},{2,10},{10... | collective-permute-start | bytes 196616 | tf_op jit(solution)/shard_map/ppermute | solution.py:418
  26.3 1.3 %collective-permute-start.12 = (bf16[64,512]{1,0:T(8,128)(2,1)S(1)}, bf16[64,512]{1,0:T(8,128)(2,1)S(1)}, u32[]{:S(2)}, u32[]{:S(2)}) collective-permute-start(bf16[64,512]{1,0:T(8,128)(2,1)S(1)} %collective-permute-done.4.refs_2_.refs_1_), channel_id=1, source_target_pairs={{0,8},{8,0},{16,24},{24,16},{1,9},{9,1},{17,25},{25,17},{2,10},{10... | collective-permute-start | bytes 196616 | tf_op jit(solution)/shard_map/ppermute | solution.py:418
  26.7 1.3 %collective-permute-start.13 = (bf16[64,512]{1,0:T(8,128)(2,1)S(1)}, bf16[64,512]{1,0:T(8,128)(2,1)S(1)}, u32[]{:S(2)}, u32[]{:S(2)}) collective-permute-start(bf16[64,512]{1,0:T(8,128)(2,1)S(1)} %collective-permute-done.5.refs_3_.rest_0_.refs_2_), channel_id=1, source_target_pairs={{0,8},{8,0},{16,24},{24,16},{1,9},{9,1},{17,25},{25,17},{2,10},{10... | collective-permute-start | bytes 196616 | tf_op jit(solution)/shard_map/ppermute | solution.py:418
  28.6 18.1 %collective-permute-start.17 = (bf16[128,2048]{1,0:T(8,128)(2,1)S(1)}, bf16[128,2048]{1,0:T(8,128)(2,1)S(1)}, u32[]{:S(2)}, u32[]{:S(2)}) collective-permute-start(bf16[128,2048]{1,0:T(8,128)(2,1)S(1)} %get-tuple-element.31.rest_0_.own_ref), channel_id=1, source_target_pairs={{0,16},{8,24},{16,0},{24,8},{1,17},{9,25},{17,1},{25,9},{2,18},{10... | collective-permute-start | bytes 1572872 | tf_op jit(solution)/shard_map/ppermute | solution.py:418
  30.3 9.2 %collective-permute-start.16 = (bf16[64,2048]{1,0:T(8,128)(2,1)S(1)}, bf16[64,2048]{1,0:T(8,128)(2,1)S(1)}, u32[]{:S(2)}, u32[]{:S(2)}) collective-permute-start(bf16[64,2048]{1,0:T(8,128)(2,1)S(1)} %add_pair.3.refs_4_.refs_0_), channel_id=1, source_target_pairs={{0,8},{8,0},{16,24},{24,16},{1,9},{9,1},{17,25},{25,17},{2,10},{10... | collective-permute-start | bytes 786440 | tf_op jit(solution)/shard_map/ppermute | solution.py:418
  30.4 12.4 %collective-permute-start.9 = (bf16[256,512]{1,0:T(8,128)(2,1)S(1)}, bf16[256,512]{1,0:T(8,128)(2,1)S(1)}, u32[]{:S(2)}, u32[]{:S(2)}) collective-permute-start(bf16[256,512]{1,0:T(8,128)(2,1)S(1)} %join_ratio.1.refs_0_), channel_id=1, source_target_pairs={{0,1},{1,0},{2,3},{3,2},{4,5},{5,4},{6,7},{7,6},{8,9},{9,8},{10,11... | collective-permute-start | bytes 786440 | tf_op jit(solution)/shard_map/ppermute | solution.py:414
  38.9 4.2 %collective-permute-start.14 = (bf16[64,2048]{1,0:T(8,128)(2,1)S(1)}, bf16[64,2048]{1,0:T(8,128)(2,1)S(1)}, u32[]{:S(2)}, u32[]{:S(2)}) collective-permute-start(bf16[64,2048]{1,0:T(8,128)(2,1)S(1)} %get-tuple-element.32.refs_3_), channel_id=1, source_target_pairs={{0,8},{8,0},{16,24},{24,16},{1,9},{9,1},{17,25},{25,17},{2,10},{10... | collective-permute-start | bytes 786440 | tf_op jit(solution)/shard_map/ppermute | solution.py:418
  39.0 4.1 %collective-permute-start.15 = (bf16[64,2048]{1,0:T(8,128)(2,1)S(1)}, bf16[64,2048]{1,0:T(8,128)(2,1)S(1)}, u32[]{:S(2)}, u32[]{:S(2)}) collective-permute-start(bf16[64,2048]{1,0:T(8,128)(2,1)S(1)} %get-tuple-element.33.refs_4_), channel_id=1, source_target_pairs={{0,8},{8,0},{16,24},{24,16},{1,9},{9,1},{17,25},{25,17},{2,10},{10... | collective-permute-start | bytes 786440 | tf_op jit(solution)/shard_map/ppermute | solution.py:418
  39.5 8.9 %collective-permute-start.18 = (bf16[64,2048]{1,0:T(8,128)(2,1)S(1)}, bf16[64,2048]{1,0:T(8,128)(2,1)S(1)}, u32[]{:S(2)}, u32[]{:S(2)}) collective-permute-start(bf16[64,2048]{1,0:T(8,128)(2,1)S(1)} %get-tuple-element.38.own_ref), channel_id=1, source_target_pairs={{0,16},{8,24},{16,0},{24,8},{1,17},{9,25},{17,1},{25,9},{2,18},{10... | collective-permute-start | bytes 786440 | tf_op jit(solution)/shard_map/ppermute | solution.py:418
  46.8 3.2 %collective-permute-start.19 = (bf16[128,2048]{1,0:T(8,128)(2,1)S(1)}, bf16[128,2048]{1,0:T(8,128)(2,1)S(1)}, u32[]{:S(2)}, u32[]{:S(2)}) collective-permute-start(bf16[128,2048]{1,0:T(8,128)(2,1)S(1)} %add_pair.4.refs_0_), channel_id=1, source_target_pairs={{0,8},{8,0},{16,24},{24,16},{1,9},{9,1},{17,25},{25,17},{2,10},{10... | collective-permute-start | bytes 1572872 | tf_op jit(solution)/shard_map/ppermute | solution.py:418
  48.4 1.6 %collective-permute-start.20 = (bf16[64,2048]{1,0:T(8,128)(2,1)S(1)}, bf16[64,2048]{1,0:T(8,128)(2,1)S(1)}, u32[]{:S(2)}, u32[]{:S(2)}) collective-permute-start(bf16[64,2048]{1,0:T(8,128)(2,1)S(1)} %add_pair.5.refs_1_), channel_id=1, source_target_pairs={{0,8},{8,0},{16,24},{24,16},{1,9},{9,1},{17,25},{25,17},{2,10},{10... | collective-permute-start | bytes 786440 | tf_op jit(solution)/shard_map/ppermute | solution.py:418

commit v17 on v16

--- a/solution.py
+++ b/solution.py
@@ -10,7 +10,7 @@
 BF16 = jnp.bfloat16
 F32 = jnp.float32
 MIB = 1024 * 1024
-ADD_COST = 22 * 10**8
+ADD_COST = 28 * 10**8
 KERNEL_COST = 125 * 10**7
 TURN_COST = 10**9
 ANY = pl.BlockSpec(memory_space=pl.ANY)
@@ -231,7 +231,7 @@
         in_specs=[SMEM] + [VMEM] * 4,
         out_specs=[VMEM] * len(flips),
         compiler_params=call_params(),
-        cost_estimate=cost(KERNEL_COST, 1) if len(flips) > 1 else cost(2 * words * docs * side_width, 2 * (4 * words + docs) * side_width),
+        cost_estimate=cost(KERNEL_COST, 1) if len(flips[0]) > 1 else cost(2 * words * docs * side_width, 2 * (4 * words + docs) * side_width),
         name="beta_pieces",
     )(here, product, ratio, docs_held, prob_held)
 
@@ -441,13 +441,15 @@
             pieces = [add_pair(part, swap(part, "doc", bit)) for part in pieces]
         return [(part, swap(part, "doc", far_bits[-1])) for part in pieces]
 
-    flips = [[0]] + [piece for piece in (order[:-1], order[-1:]) if piece]
+    flips = [[0]] + [piece for piece in (order[-1:] + order[:-2], order[-2:-1]) if piece]
     pairs = beta([own_ratio], flips[:1])
     near_logits = [shift(hold(part, gathered[-1:]), s) for s, part in enumerate(near_logits, 1)]
-    pairs += beta(gathered, flips[1:])
+    ratios = dict(zip(order, gathered))
+    for piece in flips[1:]:
+        pairs += beta([ratios[s] for s in piece], [piece])
     first = add_pair(*pairs[0], [], ADD_COST)
 
-    ratio = join_ratio(sizes, here, [own_ratio] + gathered, [0] + order, [first])
+    ratio = join_ratio(sizes, here, [own_ratio] + gathered, [0] + order, [first, pairs[-1][0]])
     far_ratios = [shift(ratio, s) for s in range(1, sizes.vocab)]
     far_logits = []
     for part in near_logits:

time: 51.3 us -> 51 us (level)
  waiting for transfers between devices: 17.1 us -> 15.9 us
  Pallas kernels: 14.1 us -> 14.8 us
    ppermute x19, waiting for transfers between devices: 9.28 us -> 8.12 us  [swap(): return lax.ppermute(array, axis, [(i, i ^ bits) for i in range(count)])]
    pallas_call x2 -> x3, Pallas kernels: 1.15 us -> 1.5 us  [beta_pieces(): pl.pallas_call(kernel, out_shape=[jax.ShapeDtypeStruct((rows * len(piece)...]
    pallas_call x2 -> x3, Pallas kernels: 1.09 us -> 1.44 us  [own_product(): pl.pallas_call(kernel, out_shape=jax.ShapeDtypeStruct((words, width), F32...]
  transfers between devices with their start and end apart: 21 -> 21, of which waited for: 12 -> 9; matrix products, arithmetic and copies ran while one was open for 0% -> 0% of each run, Pallas kernels for 16% -> 17%
where the time goes in v17:
time: 51 us; the launch traced here: 50.9 us
  starting transfers between devices  19.3 us (38%)
  waiting for transfers between devices  15.9 us (31%)
  Pallas kernels  14.8 us (29%)
  between operations  0.84 us (2%)
    ppermute x19, starting transfers between devices, swap(): return lax.ppermute(array, axis, [(i, i ^ bits) for i in range(count)])  16 us
    ppermute x19, waiting for transfers between devices, swap(): return lax.ppermute(array, axis, [(i, i ^ bits) for i in range(count)])  8.12 us
    ppermute x2, waiting for transfers between devices, shift(): lax.ppermute(array, 'vocab', [(i, (i + by) % sizes.vocab) for i in range(...  7.82 us
    pallas_call x1, Pallas kernels, rate_partial(): pl.pallas_call(kernel, out_shape=[jax.ShapeDtypeStruct((chunk, docs), BF1...  4.78 us
    pallas_call x1, Pallas kernels, theta_grad(): pl.pallas_call(kernel, out_shape=[jax.ShapeDtypeStruct((docs, share), F32...  3.65 us
    ppermute x2, starting transfers between devices, shift(): lax.ppermute(array, 'vocab', [(i, (i + by) % sizes.vocab) for i in range(...  3.25 us
    pallas_call x2, Pallas kernels, place_pieces(): pl.pallas_call(kernel, out_shape=[jax.ShapeDtypeStruct(shape, BF16)] + ([...  1.99 us
    pallas_call x3, Pallas kernels, beta_pieces(): pl.pallas_call(kernel, out_shape=[jax.ShapeDtypeStruct((rows * len(piece)...  1.5 us
  transfers between devices with their start and end apart: 21, of which 9 were waited for; matrix products, arithmetic and copies ran while one was open for 0% of the time, Pallas kernels for 17%

profile of v17, /device:TPU:0, one launch (start us, length us, event | category | flops | bytes accessed | tf_op | source)
XLA Modules:
  0.0 50.9 jit_solution(15620990062621685944)
XLA Ops:
  0.6 4.8 %rate_partial.1 = (bf16[64,512]{1,0:T(8,128)(2,1)S(1)}, bf16[64,512]{1,0:T(8,128)(2,1)S(1)}, bf16[64,512]{1,0:T(8,128)(2,1)S(1)}, bf16[64,512]{1,0:T(8,128)(2,1)...) custom-call(s32[1]{0:T(128)} %bitcast.here_ref, ...), custom_call_target="tpu_custom_call" | custom-call | flops 1073741824 | bytes 6291456 | tf_op jit(solution)/shard_map/rate_partial/pallas_call | solution.py:104
  5.4 0.5 %collective-permute-start.7 = (bf16[512,2048]{1,0:T(8,128)(2,1)S(1)}, bf16[512,2048]{1,0:T(8,128)(2,1)S(1)}, u32[]{:S(2)}, u32[]{:S(2)}) collective-permute-start(bf16[512,2048]{1,0:T(8,128)(2,1)S(1)} %get-tuple-element.24), channel_id=1, source_target_pairs={{0,8},{8,0},{16,24},{24,16},{1,9},{9,1},{17,25},{25,17},{2,10},{10... | collective-permute-start | bytes 6291464 | tf_op jit(solution)/shard_map/ppermute | solution.py:418
  6.0 3.7 %collective-permute-start = (bf16[64,512]{1,0:T(8,128)(2,1)S(1)}, bf16[64,512]{1,0:T(8,128)(2,1)S(1)}, u32[]{:S(2)}, u32[]{:S(2)}) collective-permute-start(bf16[64,512]{1,0:T(8,128)(2,1)S(1)} %get-tuple-element.20), channel_id=1, source_target_pairs={{0,4},{2,6},{4,0},{6,2},{1,5},{3,7},{5,1},{7,3},{8,12},{10,14},{12... | collective-permute-start | bytes 196616 | tf_op jit(solution)/shard_map/ppermute | solution.py:418
  9.6 1.4 %collective-permute-start.1 = (bf16[64,512]{1,0:T(8,128)(2,1)S(1)}, bf16[64,512]{1,0:T(8,128)(2,1)S(1)}, u32[]{:S(2)}, u32[]{:S(2)}) collective-permute-start(bf16[64,512]{1,0:T(8,128)(2,1)S(1)} %get-tuple-element.21), channel_id=1, source_target_pairs={{0,6},{2,4},{4,2},{6,0},{1,7},{3,5},{5,3},{7,1},{8,14},{10,12},{12... | collective-permute-start | bytes 196616 | tf_op jit(solution)/shard_map/ppermute | solution.py:418
  11.2 0.8 %chunk_counts.1.refs_4_ = f32[64,512]{1,0:T(8,128)S(1)} custom-call(s32[1]{0:T(128)} %bitcast.here_ref, s32[16]{0:T(128)} %doc_at.1, s32[16]{0:T(128)} %word_at.1, s32[16,64,128]{2,1,0:T(8,128)S(1)} %copy-done), custom_call_target="tpu_custom_call" | custom-call | flops 131072 | bytes 524288 | tf_op jit(solution)/shard_map/chunk_counts/pallas_call | solution.py:143
  12.0 1.8 %collective-permute-done.refs_1_ = bf16[64,512]{1,0:T(8,128)(2,1)S(1)} collective-permute-done((bf16[64,512]{1,0:T(8,128)(2,1)S(1)}, bf16[64,512]{1,0:T(8,128)(2,1)S(1)}, u32[]{:S(2)}, u32[]{:S(2)}) %collective-permute-start) | collective-permute-done | bytes 65568 | tf_op jit(solution)/shard_map/ppermute | solution.py:418
  13.9 2.4 %collective-permute-done.1.refs_2_ = bf16[64,512]{1,0:T(8,128)(2,1)S(1)} collective-permute-done((bf16[64,512]{1,0:T(8,128)(2,1)S(1)}, bf16[64,512]{1,0:T(8,128)(2,1)S(1)}, u32[]{:S(2)}, u32[]{:S(2)}) %collective-permute-start.1) | collective-permute-done | bytes 65568 | tf_op jit(solution)/shard_map/ppermute | solution.py:418
  16.6 2.8 %collective-permute-start.5 = (bf16[64,512]{1,0:T(8,128)(2,1)S(1)}, bf16[64,512]{1,0:T(8,128)(2,1)S(1)}, u32[]{:S(2)}, u32[]{:S(2)}) collective-permute-start(bf16[64,512]{1,0:T(8,128)(2,1)S(1)} %ratio_chunk.1.ratio_ref.refs_0_), channel_id=1, source_target_pairs={{0,4},{2,6},{4,0},{6,2},{1,5},{3,7},{5,1},{7,3},{8,12},{10,14},{12... | collective-permute-start | bytes 196616 | tf_op jit(solution)/shard_map/ppermute | solution.py:418
  19.4 0.7 %collective-permute-start.3 = (bf16[64,512]{1,0:T(8,128)(2,1)S(1)}, bf16[64,512]{1,0:T(8,128)(2,1)S(1)}, u32[]{:S(2)}, u32[]{:S(2)}) collective-permute-start(bf16[64,512]{1,0:T(8,128)(2,1)S(1)} %ratio_chunk.1.ratio_ref.refs_0_), channel_id=1, source_target_pairs={{0,6},{2,4},{4,2},{6,0},{1,7},{3,5},{5,3},{7,1},{8,14},{10,12},{12... | collective-permute-start | bytes 196616 | tf_op jit(solution)/shard_map/ppermute | solution.py:418
  20.1 0.5 own_product.3.product_ref
  20.6 0.5 beta_pieces.3.own_ref
  21.1 1.6 %collective-permute-start.8 = (bf16[64,2048]{1,0:T(8,128)(2,1)S(1)}, bf16[64,2048]{1,0:T(8,128)(2,1)S(1)}, u32[]{:S(2)}, u32[]{:S(2)}) collective-permute-start(bf16[64,2048]{1,0:T(8,128)(2,1)S(1)} %beta_pieces.3.own_ref), channel_id=1, source_target_pairs={{0,16},{8,24},{16,0},{24,8},{1,17},{9,25},{17,1},{25,9},{2,18},{10... | collective-permute-start | bytes 786440 | tf_op jit(solution)/shard_map/ppermute | solution.py:418
  22.7 0.5 collective-permute-start.4
  23.2 0.7 %collective-permute-done.5.refs_3_.rest_0_.refs_0_ = bf16[64,512]{1,0:T(8,128)(2,1)S(1)} collective-permute-done((bf16[64,512]{1,0:T(8,128)(2,1)S(1)}, bf16[64,512]{1,0:T(8,128)(2,1)S(1)}, u32[]{:S(2)}, u32[]{:S(2)}) %collective-permute-start.5) | collective-permute-done | bytes 65568 | tf_op jit(solution)/shard_map/ppermute | solution.py:418
  23.9 1.7 %collective-permute-start.11 = (bf16[128,2048]{1,0:T(8,128)(2,1)S(1)}, bf16[128,2048]{1,0:T(8,128)(2,1)S(1)}, u32[]{:S(2)}, u32[]{:S(2)}) collective-permute-start(bf16[128,2048]{1,0:T(8,128)(2,1)S(1)} %hold.1), channel_id=1, source_target_pairs={{0,1},{1,0},{2,3},{3,2},{4,5},{5,4},{6,7},{7,6},{8,9},{9,8},{10,11... | collective-permute-start | bytes 1572872 | tf_op jit(solution)/shard_map/ppermute | solution.py:414
  25.6 0.6 %collective-permute-start.13 = (bf16[64,512]{1,0:T(8,128)(2,1)S(1)}, bf16[64,512]{1,0:T(8,128)(2,1)S(1)}, u32[]{:S(2)}, u32[]{:S(2)}) collective-permute-start(bf16[64,512]{1,0:T(8,128)(2,1)S(1)} %collective-permute-done.3.refs_1_), channel_id=1, source_target_pairs={{0,8},{8,0},{16,24},{24,16},{1,9},{9,1},{17,25},{25,17},{2,10},{10... | collective-permute-start | bytes 196616 | tf_op jit(solution)/shard_map/ppermute | solution.py:418
  26.2 0.5 own_product.5.product_ref
  26.6 0.3 collective-permute-done.4.ratio_ref.refs_2_
  27.0 0.5 own_product.4.product_ref
  27.5 0.5 %beta_pieces.5.rest_0_.own_ref = bf16[128,2048]{1,0:T(8,128)(2,1)S(1)} custom-call(s32[1]{0:T(128)} %bitcast.here_ref, f32[128,2048]{1,0:T(8,128)S(1)} %own_product.5.product_ref, bf16[128,512]{1,0:T(8,128)(2,1)S(1)} %stack_rows.3.ratio_ref, bf16[512,2048]{1,0:T(8,128)(2,1)S(1)} %collective-permute-done.7.doc_ref, ...), custom_call_target="tpu_custom_call" | custom-call | flops 1250000000 | bytes 1 | tf_op jit(solution)/shard_map/beta_pieces/pallas_call | solution.py:228
  28.0 1.5 %collective-permute-start.17 = (bf16[128,2048]{1,0:T(8,128)(2,1)S(1)}, bf16[128,2048]{1,0:T(8,128)(2,1)S(1)}, u32[]{:S(2)}, u32[]{:S(2)}) collective-permute-start(bf16[128,2048]{1,0:T(8,128)(2,1)S(1)} %beta_pieces.5.rest_0_.own_ref), channel_id=1, source_target_pairs={{0,16},{8,24},{16,0},{24,8},{1,17},{9,25},{17,1},{25,9},{2,18},{10... | collective-permute-start | bytes 1572872 | tf_op jit(solution)/shard_map/ppermute | solution.py:418
  29.9 0.5 beta_pieces.4.refs_5_.own_ref
  30.4 1.6 %collective-permute-start.10 = (bf16[256,512]{1,0:T(8,128)(2,1)S(1)}, bf16[256,512]{1,0:T(8,128)(2,1)S(1)}, u32[]{:S(2)}, u32[]{:S(2)}) collective-permute-start(bf16[256,512]{1,0:T(8,128)(2,1)S(1)} %join_ratio.1.refs_0_), channel_id=1, source_target_pairs={{0,1},{1,0},{2,3},{3,2},{4,5},{5,4},{6,7},{7,6},{8,9},{9,8},{10,11... | collective-permute-start | bytes 786440 | tf_op jit(solution)/shard_map/ppermute | solution.py:414
  32.0 6.8 %collective-permute-done.11.in_ref = bf16[128,2048]{1,0:T(8,128)(2,1)S(1)} collective-permute-done((bf16[128,2048]{1,0:T(8,128)(2,1)S(1)}, bf16[128,2048]{1,0:T(8,128)(2,1)S(1)}, u32[]{:S(2)}, u32[]{:S(2)}) %collective-permute-start.11) | collective-permute-done | bytes 524320 | tf_op jit(solution)/shard_map/ppermute | solution.py:414
  38.9 0.5 collective-permute-start.15
  39.4 1.6 %collective-permute-start.18 = (bf16[64,2048]{1,0:T(8,128)(2,1)S(1)}, bf16[64,2048]{1,0:T(8,128)(2,1)S(1)}, u32[]{:S(2)}, u32[]{:S(2)}) collective-permute-start(bf16[64,2048]{1,0:T(8,128)(2,1)S(1)} %beta_pieces.4.refs_5_.own_ref), channel_id=1, source_target_pairs={{0,16},{8,24},{16,0},{24,8},{1,17},{9,25},{17,1},{25,9},{2,18},{10... | collective-permute-start | bytes 786440 | tf_op jit(solution)/shard_map/ppermute | solution.py:418
  41.0 0.8 %place_pieces.2 = (bf16[256,4096]{1,0:T(8,128)(2,1)}, f32[8,128]{1,0:T(8,128)S(1)}) custom-call(s32[1]{0:T(128)} %bitcast.here_ref, bf16[64,2048]{1,0:T(8,128)(2,1)S(1)} %add_pair.3.refs_4_.refs_0_, bf16[64,2048]{1,0:T(8,128)(2,1)S(1)} %collective-permute-done.16.refs_1_), custom_call_target="tpu_custom_call" | custom-call | bytes 524288 | tf_op jit(solution)/shard_map/place_pieces/pallas_call | solution.py:394
  41.8 1.0 %collective-permute-done.10.refs_1_ = bf16[256,512]{1,0:T(8,128)(2,1)S(1)} collective-permute-done((bf16[256,512]{1,0:T(8,128)(2,1)S(1)}, bf16[256,512]{1,0:T(8,128)(2,1)S(1)}, u32[]{:S(2)}, u32[]{:S(2)}) %collective-permute-start.10) | collective-permute-done | bytes 262176 | tf_op jit(solution)/shard_map/ppermute | solution.py:414
  43.1 3.7 %theta_grad.1 = (f32[512,2048]{1,0:T(8,128)}, f32[8,128]{1,0:T(8,128)S(1)}) custom-call(s32[1]{0:T(128)} %bitcast.here_ref, bf16[512,256]{1,0:T(8,128)(2,1)S(1)} %get-tuple-element.26.refs_0_, bf16[512,256]{1,0:T(8,128)(2,1)S(1)} %get-tuple-element.27.refs_1_, bf16[256,4096]{1,0:T(8,128)(2,1)S(1)} %get-tuple-element.25.prob_ref.refs_2_, ...), custom_call_target="tpu_custom_call" | custom-call | flops 1 | bytes 1 | tf_op jit(solution)/shard_map/theta_grad/pallas_call | solution.py:351
  46.9 1.1 %collective-permute-done.18.other_ref = bf16[64,2048]{1,0:T(8,128)(2,1)S(1)} collective-permute-done((bf16[64,2048]{1,0:T(8,128)(2,1)S(1)}, bf16[64,2048]{1,0:T(8,128)(2,1)S(1)}, u32[]{:S(2)}, u32[]{:S(2)}) %collective-permute-start.18) | collective-permute-done | bytes 262176 | tf_op jit(solution)/shard_map/ppermute | solution.py:418
  48.2 1.5 %collective-permute-done.20.refs_3_ = bf16[64,2048]{1,0:T(8,128)(2,1)S(1)} collective-permute-done((bf16[64,2048]{1,0:T(8,128)(2,1)S(1)}, bf16[64,2048]{1,0:T(8,128)(2,1)S(1)}, u32[]{:S(2)}, u32[]{:S(2)}) %collective-permute-start.20) | collective-permute-done | bytes 262176 | tf_op jit(solution)/shard_map/ppermute | solution.py:418
  49.7 1.2 %place_pieces.3 = bf16[256,4096]{1,0:T(8,128)(2,1)} custom-call(s32[1]{0:T(128)} %bitcast.here_ref, bf16[128,2048]{1,0:T(8,128)(2,1)S(1)} %add_pair.4.refs_0_, bf16[64,2048]{1,0:T(8,128)(2,1)S(1)} %add_pair.5.refs_1_, bf16[128,2048]{1,0:T(8,128)(2,1)S(1)} %collective-permute-done.19.refs_2_, ...), custom_call_target="tpu_custom_call", output_to_operand_aliasing={{}: (5, {})} | custom-call | bytes 1572864 | tf_op jit(solution)/shard_map/place_pieces/pallas_call | solution.py:394
  (33 shorter events, 1.6 us)
Async XLA Ops:
  0.6 10.6 %copy-start = (s32[16,64,128]{2,1,0:T(8,128)S(1)}, s32[16,64,128]{2,1,0:T(8,128)}, u32[]{:S(2)}) copy-start(s32[16,64,128]{2,1,0:T(8,128)} %count_ref.1) | copy-start | bytes 1572868
  5.4 15.2 %collective-permute-start.7 = (bf16[512,2048]{1,0:T(8,128)(2,1)S(1)}, bf16[512,2048]{1,0:T(8,128)(2,1)S(1)}, u32[]{:S(2)}, u32[]{:S(2)}) collective-permute-start(bf16[512,2048]{1,0:T(8,128)(2,1)S(1)} %get-tuple-element.24), channel_id=1, source_target_pairs={{0,8},{8,0},{16,24},{24,16},{1,9},{9,1},{17,25},{25,17},{2,10},{10... | collective-permute-start | bytes 6291464 | tf_op jit(solution)/shard_map/ppermute | solution.py:418
  6.0 7.9 %collective-permute-start = (bf16[64,512]{1,0:T(8,128)(2,1)S(1)}, bf16[64,512]{1,0:T(8,128)(2,1)S(1)}, u32[]{:S(2)}, u32[]{:S(2)}) collective-permute-start(bf16[64,512]{1,0:T(8,128)(2,1)S(1)} %get-tuple-element.20), channel_id=1, source_target_pairs={{0,4},{2,6},{4,0},{6,2},{1,5},{3,7},{5,1},{7,3},{8,12},{10,14},{12... | collective-permute-start | bytes 196616 | tf_op jit(solution)/shard_map/ppermute | solution.py:418
  9.6 6.7 %collective-permute-start.1 = (bf16[64,512]{1,0:T(8,128)(2,1)S(1)}, bf16[64,512]{1,0:T(8,128)(2,1)S(1)}, u32[]{:S(2)}, u32[]{:S(2)}) collective-permute-start(bf16[64,512]{1,0:T(8,128)(2,1)S(1)} %get-tuple-element.21), channel_id=1, source_target_pairs={{0,6},{2,4},{4,2},{6,0},{1,7},{3,5},{5,3},{7,1},{8,14},{10,12},{12... | collective-permute-start | bytes 196616 | tf_op jit(solution)/shard_map/ppermute | solution.py:418
  11.0 5.5 %collective-permute-start.2 = (bf16[64,512]{1,0:T(8,128)(2,1)S(1)}, bf16[64,512]{1,0:T(8,128)(2,1)S(1)}, u32[]{:S(2)}, u32[]{:S(2)}) collective-permute-start(bf16[64,512]{1,0:T(8,128)(2,1)S(1)} %get-tuple-element.22), channel_id=1, source_target_pairs={{0,2},{2,0},{4,6},{6,4},{1,3},{3,1},{5,7},{7,5},{8,10},{10,8},{12,... | collective-permute-start | bytes 196616 | tf_op jit(solution)/shard_map/ppermute | solution.py:418
  16.5 4.1 %collective-permute-start.6 = (bf16[64,512]{1,0:T(8,128)(2,1)S(1)}, bf16[64,512]{1,0:T(8,128)(2,1)S(1)}, u32[]{:S(2)}, u32[]{:S(2)}) collective-permute-start(bf16[64,512]{1,0:T(8,128)(2,1)S(1)} %ratio_chunk.1.ratio_ref.refs_0_), channel_id=1, source_target_pairs={{0,8},{8,0},{16,24},{24,16},{1,9},{9,1},{17,25},{25,17},{2,10},{10... | collective-permute-start | bytes 196616 | tf_op jit(solution)/shard_map/ppermute | solution.py:418
  16.6 7.3 %collective-permute-start.5 = (bf16[64,512]{1,0:T(8,128)(2,1)S(1)}, bf16[64,512]{1,0:T(8,128)(2,1)S(1)}, u32[]{:S(2)}, u32[]{:S(2)}) collective-permute-start(bf16[64,512]{1,0:T(8,128)(2,1)S(1)} %ratio_chunk.1.ratio_ref.refs_0_), channel_id=1, source_target_pairs={{0,4},{2,6},{4,0},{6,2},{1,5},{3,7},{5,1},{7,3},{8,12},{10,14},{12... | collective-permute-start | bytes 196616 | tf_op jit(solution)/shard_map/ppermute | solution.py:418
  19.4 6.1 %collective-permute-start.3 = (bf16[64,512]{1,0:T(8,128)(2,1)S(1)}, bf16[64,512]{1,0:T(8,128)(2,1)S(1)}, u32[]{:S(2)}, u32[]{:S(2)}) collective-permute-start(bf16[64,512]{1,0:T(8,128)(2,1)S(1)} %ratio_chunk.1.ratio_ref.refs_0_), channel_id=1, source_target_pairs={{0,6},{2,4},{4,2},{6,0},{1,7},{3,5},{5,3},{7,1},{8,14},{10,12},{12... | collective-permute-start | bytes 196616 | tf_op jit(solution)/shard_map/ppermute | solution.py:418
  21.1 8.4 %collective-permute-start.8 = (bf16[64,2048]{1,0:T(8,128)(2,1)S(1)}, bf16[64,2048]{1,0:T(8,128)(2,1)S(1)}, u32[]{:S(2)}, u32[]{:S(2)}) collective-permute-start(bf16[64,2048]{1,0:T(8,128)(2,1)S(1)} %beta_pieces.3.own_ref), channel_id=1, source_target_pairs={{0,16},{8,24},{16,0},{24,8},{1,17},{9,25},{17,1},{25,9},{2,18},{10... | collective-permute-start | bytes 786440 | tf_op jit(solution)/shard_map/ppermute | solution.py:418
  22.7 4.3 %collective-permute-start.4 = (bf16[64,512]{1,0:T(8,128)(2,1)S(1)}, bf16[64,512]{1,0:T(8,128)(2,1)S(1)}, u32[]{:S(2)}, u32[]{:S(2)}) collective-permute-start(bf16[64,512]{1,0:T(8,128)(2,1)S(1)} %ratio_chunk.1.ratio_ref.refs_0_), channel_id=1, source_target_pairs={{0,2},{2,0},{4,6},{6,4},{1,3},{3,1},{5,7},{7,5},{8,10},{10,8},{12,... | collective-permute-start | bytes 196616 | tf_op jit(solution)/shard_map/ppermute | solution.py:418
  23.9 14.9 %collective-permute-start.11 = (bf16[128,2048]{1,0:T(8,128)(2,1)S(1)}, bf16[128,2048]{1,0:T(8,128)(2,1)S(1)}, u32[]{:S(2)}, u32[]{:S(2)}) collective-permute-start(bf16[128,2048]{1,0:T(8,128)(2,1)S(1)} %hold.1), channel_id=1, source_target_pairs={{0,1},{1,0},{2,3},{3,2},{4,5},{5,4},{6,7},{7,6},{8,9},{9,8},{10,11... | collective-permute-start | bytes 1572872 | tf_op jit(solution)/shard_map/ppermute | solution.py:414
  25.6 1.9 %collective-permute-start.12 = (bf16[64,512]{1,0:T(8,128)(2,1)S(1)}, bf16[64,512]{1,0:T(8,128)(2,1)S(1)}, u32[]{:S(2)}, u32[]{:S(2)}) collective-permute-start(bf16[64,512]{1,0:T(8,128)(2,1)S(1)} %collective-permute-done.5.refs_3_.rest_0_.refs_0_), channel_id=1, source_target_pairs={{0,8},{8,0},{16,24},{24,16},{1,9},{9,1},{17,25},{25,17},{2,10},{10... | collective-permute-start | bytes 196616 | tf_op jit(solution)/shard_map/ppermute | solution.py:418
  25.6 1.9 %collective-permute-start.13 = (bf16[64,512]{1,0:T(8,128)(2,1)S(1)}, bf16[64,512]{1,0:T(8,128)(2,1)S(1)}, u32[]{:S(2)}, u32[]{:S(2)}) collective-permute-start(bf16[64,512]{1,0:T(8,128)(2,1)S(1)} %collective-permute-done.3.refs_1_), channel_id=1, source_target_pairs={{0,8},{8,0},{16,24},{24,16},{1,9},{9,1},{17,25},{25,17},{2,10},{10... | collective-permute-start | bytes 196616 | tf_op jit(solution)/shard_map/ppermute | solution.py:418
  27.0 2.9 %collective-permute-start.9 = (bf16[64,512]{1,0:T(8,128)(2,1)S(1)}, bf16[64,512]{1,0:T(8,128)(2,1)S(1)}, u32[]{:S(2)}, u32[]{:S(2)}) collective-permute-start(bf16[64,512]{1,0:T(8,128)(2,1)S(1)} %collective-permute-done.4.ratio_ref.refs_2_), channel_id=1, source_target_pairs={{0,8},{8,0},{16,24},{24,16},{1,9},{9,1},{17,25},{25,17},{2,10},{10... | collective-permute-start | bytes 196616 | tf_op jit(solution)/shard_map/ppermute | solution.py:418
  28.0 18.7 %collective-permute-start.17 = (bf16[128,2048]{1,0:T(8,128)(2,1)S(1)}, bf16[128,2048]{1,0:T(8,128)(2,1)S(1)}, u32[]{:S(2)}, u32[]{:S(2)}) collective-permute-start(bf16[128,2048]{1,0:T(8,128)(2,1)S(1)} %beta_pieces.5.rest_0_.own_ref), channel_id=1, source_target_pairs={{0,16},{8,24},{16,0},{24,8},{1,17},{9,25},{17,1},{25,9},{2,18},{10... | collective-permute-start | bytes 1572872 | tf_op jit(solution)/shard_map/ppermute | solution.py:418
  29.6 9.9 %collective-permute-start.16 = (bf16[64,2048]{1,0:T(8,128)(2,1)S(1)}, bf16[64,2048]{1,0:T(8,128)(2,1)S(1)}, u32[]{:S(2)}, u32[]{:S(2)}) collective-permute-start(bf16[64,2048]{1,0:T(8,128)(2,1)S(1)} %add_pair.3.refs_4_.refs_0_), channel_id=1, source_target_pairs={{0,8},{8,0},{16,24},{24,16},{1,9},{9,1},{17,25},{25,17},{2,10},{10... | collective-permute-start | bytes 786440 | tf_op jit(solution)/shard_map/ppermute | solution.py:418
  30.4 12.4 %collective-permute-start.10 = (bf16[256,512]{1,0:T(8,128)(2,1)S(1)}, bf16[256,512]{1,0:T(8,128)(2,1)S(1)}, u32[]{:S(2)}, u32[]{:S(2)}) collective-permute-start(bf16[256,512]{1,0:T(8,128)(2,1)S(1)} %join_ratio.1.refs_0_), channel_id=1, source_target_pairs={{0,1},{1,0},{2,3},{3,2},{4,5},{5,4},{6,7},{7,6},{8,9},{9,8},{10,11... | collective-permute-start | bytes 786440 | tf_op jit(solution)/shard_map/ppermute | solution.py:414
  38.9 4.2 %collective-permute-start.14 = (bf16[64,2048]{1,0:T(8,128)(2,1)S(1)}, bf16[64,2048]{1,0:T(8,128)(2,1)S(1)}, u32[]{:S(2)}, u32[]{:S(2)}) collective-permute-start(bf16[64,2048]{1,0:T(8,128)(2,1)S(1)} %get-tuple-element.29.refs_3_), channel_id=1, source_target_pairs={{0,8},{8,0},{16,24},{24,16},{1,9},{9,1},{17,25},{25,17},{2,10},{10... | collective-permute-start | bytes 786440 | tf_op jit(solution)/shard_map/ppermute | solution.py:418
  38.9 4.1 %collective-permute-start.15 = (bf16[64,2048]{1,0:T(8,128)(2,1)S(1)}, bf16[64,2048]{1,0:T(8,128)(2,1)S(1)}, u32[]{:S(2)}, u32[]{:S(2)}) collective-permute-start(bf16[64,2048]{1,0:T(8,128)(2,1)S(1)} %get-tuple-element.30.refs_4_), channel_id=1, source_target_pairs={{0,8},{8,0},{16,24},{24,16},{1,9},{9,1},{17,25},{25,17},{2,10},{10... | collective-permute-start | bytes 786440 | tf_op jit(solution)/shard_map/ppermute | solution.py:418
  39.4 8.6 %collective-permute-start.18 = (bf16[64,2048]{1,0:T(8,128)(2,1)S(1)}, bf16[64,2048]{1,0:T(8,128)(2,1)S(1)}, u32[]{:S(2)}, u32[]{:S(2)}) collective-permute-start(bf16[64,2048]{1,0:T(8,128)(2,1)S(1)} %beta_pieces.4.refs_5_.own_ref), channel_id=1, source_target_pairs={{0,16},{8,24},{16,0},{24,8},{1,17},{9,25},{17,1},{25,9},{2,18},{10... | collective-permute-start | bytes 786440 | tf_op jit(solution)/shard_map/ppermute | solution.py:418
  46.8 2.9 %collective-permute-start.19 = (bf16[128,2048]{1,0:T(8,128)(2,1)S(1)}, bf16[128,2048]{1,0:T(8,128)(2,1)S(1)}, u32[]{:S(2)}, u32[]{:S(2)}) collective-permute-start(bf16[128,2048]{1,0:T(8,128)(2,1)S(1)} %add_pair.4.refs_0_), channel_id=1, source_target_pairs={{0,8},{8,0},{16,24},{24,16},{1,9},{9,1},{17,25},{25,17},{2,10},{10... | collective-permute-start | bytes 1572872 | tf_op jit(solution)/shard_map/ppermute | solution.py:418
  48.1 1.6 %collective-permute-start.20 = (bf16[64,2048]{1,0:T(8,128)(2,1)S(1)}, bf16[64,2048]{1,0:T(8,128)(2,1)S(1)}, u32[]{:S(2)}, u32[]{:S(2)}) collective-permute-start(bf16[64,2048]{1,0:T(8,128)(2,1)S(1)} %add_pair.5.refs_1_), channel_id=1, source_target_pairs={{0,8},{8,0},{16,24},{24,16},{1,9},{9,1},{17,25},{25,17},{2,10},{10... | collective-permute-start | bytes 786440 | tf_op jit(solution)/shard_map/ppermute | solution.py:418

commit v18 on v17

--- a/solution.py
+++ b/solution.py
@@ -53,7 +53,7 @@
     docs, width = doc_topics.shape
     words = word_logits.shape[0]
     side_width = width // 2
-    span = min(side_width, 512)
+    span = min(side_width, 1024)
     steps = side_width // span
     count, far = sizes.topic, sizes.vocab - 1
     chunk, half, share = words // count, words // 2, width // sizes.vocab

time: 51 us -> 50.3 us (0.986)
  Pallas kernels: 14.8 us -> 14.1 us
    pallas_call x1, Pallas kernels: 4.78 us -> 4.03 us  [rate_partial(): pl.pallas_call(kernel, out_shape=[jax.ShapeDtypeStruct((chunk, docs), BF1...]
  transfers between devices with their start and end apart: 21 -> 21, of which waited for: 9 -> 9; matrix products, arithmetic and copies ran while one was open for 0% -> 0% of each run, Pallas kernels for 17% -> 18%
where the time goes in v18:
time: 50.3 us; the launch traced here: 50.1 us
  starting transfers between devices  19.3 us (38%)
  waiting for transfers between devices  15.9 us (32%)
  Pallas kernels  14.1 us (28%)
  between operations  0.84 us (2%)
    ppermute x19, starting transfers between devices, swap(): return lax.ppermute(array, axis, [(i, i ^ bits) for i in range(count)])  16 us
    ppermute x19, waiting for transfers between devices, swap(): return lax.ppermute(array, axis, [(i, i ^ bits) for i in range(count)])  8.09 us
    ppermute x2, waiting for transfers between devices, shift(): lax.ppermute(array, 'vocab', [(i, (i + by) % sizes.vocab) for i in range(...  7.81 us
    pallas_call x1, Pallas kernels, rate_partial(): pl.pallas_call(kernel, out_shape=[jax.ShapeDtypeStruct((chunk, docs), BF1...  4.03 us
    pallas_call x1, Pallas kernels, theta_grad(): pl.pallas_call(kernel, out_shape=[jax.ShapeDtypeStruct((docs, share), F32...  3.66 us
    ppermute x2, starting transfers between devices, shift(): lax.ppermute(array, 'vocab', [(i, (i + by) % sizes.vocab) for i in range(...  3.26 us
    pallas_call x2, Pallas kernels, place_pieces(): pl.pallas_call(kernel, out_shape=[jax.ShapeDtypeStruct(shape, BF16)] + ([...  1.99 us
    pallas_call x3, Pallas kernels, beta_pieces(): pl.pallas_call(kernel, out_shape=[jax.ShapeDtypeStruct((rows * len(piece)...  1.51 us
  transfers between devices with their start and end apart: 21, of which 9 were waited for; matrix products, arithmetic and copies ran while one was open for 0% of the time, Pallas kernels for 18%

profile of v18, /device:TPU:0, one launch (start us, length us, event | category | flops | bytes accessed | tf_op | source)
XLA Modules:
  0.0 50.1 jit_solution(4884806107896728659)
XLA Ops:
  0.6 4.0 %rate_partial.1 = (bf16[64,512]{1,0:T(8,128)(2,1)S(1)}, bf16[64,512]{1,0:T(8,128)(2,1)S(1)}, bf16[64,512]{1,0:T(8,128)(2,1)S(1)}, bf16[64,512]{1,0:T(8,128)(2,1)...) custom-call(s32[1]{0:T(128)} %bitcast.here_ref, ...), custom_call_target="tpu_custom_call" | custom-call | flops 1073741824 | bytes 6291456 | tf_op jit(solution)/shard_map/rate_partial/pallas_call | solution.py:104
  4.7 0.5 %collective-permute-start.7 = (bf16[512,2048]{1,0:T(8,128)(2,1)S(1)}, bf16[512,2048]{1,0:T(8,128)(2,1)S(1)}, u32[]{:S(2)}, u32[]{:S(2)}) collective-permute-start(bf16[512,2048]{1,0:T(8,128)(2,1)S(1)} %get-tuple-element.24), channel_id=1, source_target_pairs={{0,8},{8,0},{16,24},{24,16},{1,9},{9,1},{17,25},{25,17},{2,10},{10... | collective-permute-start | bytes 6291464 | tf_op jit(solution)/shard_map/ppermute | solution.py:418
  5.2 3.7 %collective-permute-start = (bf16[64,512]{1,0:T(8,128)(2,1)S(1)}, bf16[64,512]{1,0:T(8,128)(2,1)S(1)}, u32[]{:S(2)}, u32[]{:S(2)}) collective-permute-start(bf16[64,512]{1,0:T(8,128)(2,1)S(1)} %get-tuple-element.20), channel_id=1, source_target_pairs={{0,4},{2,6},{4,0},{6,2},{1,5},{3,7},{5,1},{7,3},{8,12},{10,14},{12... | collective-permute-start | bytes 196616 | tf_op jit(solution)/shard_map/ppermute | solution.py:418
  8.9 1.4 %collective-permute-start.1 = (bf16[64,512]{1,0:T(8,128)(2,1)S(1)}, bf16[64,512]{1,0:T(8,128)(2,1)S(1)}, u32[]{:S(2)}, u32[]{:S(2)}) collective-permute-start(bf16[64,512]{1,0:T(8,128)(2,1)S(1)} %get-tuple-element.21), channel_id=1, source_target_pairs={{0,6},{2,4},{4,2},{6,0},{1,7},{3,5},{5,3},{7,1},{8,14},{10,12},{12... | collective-permute-start | bytes 196616 | tf_op jit(solution)/shard_map/ppermute | solution.py:418
  10.4 0.8 %chunk_counts.1.refs_4_ = f32[64,512]{1,0:T(8,128)S(1)} custom-call(s32[1]{0:T(128)} %bitcast.here_ref, s32[16]{0:T(128)} %doc_at.1, s32[16]{0:T(128)} %word_at.1, s32[16,64,128]{2,1,0:T(8,128)S(1)} %copy-done), custom_call_target="tpu_custom_call" | custom-call | flops 131072 | bytes 524288 | tf_op jit(solution)/shard_map/chunk_counts/pallas_call | solution.py:143
  11.3 1.8 %collective-permute-done.refs_1_ = bf16[64,512]{1,0:T(8,128)(2,1)S(1)} collective-permute-done((bf16[64,512]{1,0:T(8,128)(2,1)S(1)}, bf16[64,512]{1,0:T(8,128)(2,1)S(1)}, u32[]{:S(2)}, u32[]{:S(2)}) %collective-permute-start) | collective-permute-done | bytes 65568 | tf_op jit(solution)/shard_map/ppermute | solution.py:418
  13.1 2.4 %collective-permute-done.1.refs_2_ = bf16[64,512]{1,0:T(8,128)(2,1)S(1)} collective-permute-done((bf16[64,512]{1,0:T(8,128)(2,1)S(1)}, bf16[64,512]{1,0:T(8,128)(2,1)S(1)}, u32[]{:S(2)}, u32[]{:S(2)}) %collective-permute-start.1) | collective-permute-done | bytes 65568 | tf_op jit(solution)/shard_map/ppermute | solution.py:418
  15.9 2.8 %collective-permute-start.5 = (bf16[64,512]{1,0:T(8,128)(2,1)S(1)}, bf16[64,512]{1,0:T(8,128)(2,1)S(1)}, u32[]{:S(2)}, u32[]{:S(2)}) collective-permute-start(bf16[64,512]{1,0:T(8,128)(2,1)S(1)} %ratio_chunk.1.ratio_ref.refs_0_), channel_id=1, source_target_pairs={{0,4},{2,6},{4,0},{6,2},{1,5},{3,7},{5,1},{7,3},{8,12},{10,14},{12... | collective-permute-start | bytes 196616 | tf_op jit(solution)/shard_map/ppermute | solution.py:418
  18.7 0.7 %collective-permute-start.3 = (bf16[64,512]{1,0:T(8,128)(2,1)S(1)}, bf16[64,512]{1,0:T(8,128)(2,1)S(1)}, u32[]{:S(2)}, u32[]{:S(2)}) collective-permute-start(bf16[64,512]{1,0:T(8,128)(2,1)S(1)} %ratio_chunk.1.ratio_ref.refs_0_), channel_id=1, source_target_pairs={{0,6},{2,4},{4,2},{6,0},{1,7},{3,5},{5,3},{7,1},{8,14},{10,12},{12... | collective-permute-start | bytes 196616 | tf_op jit(solution)/shard_map/ppermute | solution.py:418
  19.4 0.5 own_product.3.product_ref
  19.9 0.5 beta_pieces.3.own_ref
  20.4 1.6 %collective-permute-start.8 = (bf16[64,2048]{1,0:T(8,128)(2,1)S(1)}, bf16[64,2048]{1,0:T(8,128)(2,1)S(1)}, u32[]{:S(2)}, u32[]{:S(2)}) collective-permute-start(bf16[64,2048]{1,0:T(8,128)(2,1)S(1)} %beta_pieces.3.own_ref), channel_id=1, source_target_pairs={{0,16},{8,24},{16,0},{24,8},{1,17},{9,25},{17,1},{25,9},{2,18},{10... | collective-permute-start | bytes 786440 | tf_op jit(solution)/shard_map/ppermute | solution.py:418
  21.9 0.5 collective-permute-start.4
  22.4 0.7 %collective-permute-done.5.refs_3_.rest_0_.refs_0_ = bf16[64,512]{1,0:T(8,128)(2,1)S(1)} collective-permute-done((bf16[64,512]{1,0:T(8,128)(2,1)S(1)}, bf16[64,512]{1,0:T(8,128)(2,1)S(1)}, u32[]{:S(2)}, u32[]{:S(2)}) %collective-permute-start.5) | collective-permute-done | bytes 65568 | tf_op jit(solution)/shard_map/ppermute | solution.py:418
  23.2 1.7 %collective-permute-start.11 = (bf16[128,2048]{1,0:T(8,128)(2,1)S(1)}, bf16[128,2048]{1,0:T(8,128)(2,1)S(1)}, u32[]{:S(2)}, u32[]{:S(2)}) collective-permute-start(bf16[128,2048]{1,0:T(8,128)(2,1)S(1)} %hold.1), channel_id=1, source_target_pairs={{0,1},{1,0},{2,3},{3,2},{4,5},{5,4},{6,7},{7,6},{8,9},{9,8},{10,11... | collective-permute-start | bytes 1572872 | tf_op jit(solution)/shard_map/ppermute | solution.py:414
  24.8 0.6 %collective-permute-start.13 = (bf16[64,512]{1,0:T(8,128)(2,1)S(1)}, bf16[64,512]{1,0:T(8,128)(2,1)S(1)}, u32[]{:S(2)}, u32[]{:S(2)}) collective-permute-start(bf16[64,512]{1,0:T(8,128)(2,1)S(1)} %collective-permute-done.3.refs_1_), channel_id=1, source_target_pairs={{0,8},{8,0},{16,24},{24,16},{1,9},{9,1},{17,25},{25,17},{2,10},{10... | collective-permute-start | bytes 196616 | tf_op jit(solution)/shard_map/ppermute | solution.py:418
  25.4 0.5 own_product.5.product_ref
  25.9 0.3 collective-permute-done.4.ratio_ref.refs_2_
  26.2 0.5 own_product.4.product_ref
  26.7 0.5 %beta_pieces.5.rest_0_.own_ref = bf16[128,2048]{1,0:T(8,128)(2,1)S(1)} custom-call(s32[1]{0:T(128)} %bitcast.here_ref, f32[128,2048]{1,0:T(8,128)S(1)} %own_product.5.product_ref, bf16[128,512]{1,0:T(8,128)(2,1)S(1)} %stack_rows.3.ratio_ref, bf16[512,2048]{1,0:T(8,128)(2,1)S(1)} %collective-permute-done.7.doc_ref, ...), custom_call_target="tpu_custom_call" | custom-call | flops 1250000000 | bytes 1 | tf_op jit(solution)/shard_map/beta_pieces/pallas_call | solution.py:228
  27.3 1.5 %collective-permute-start.17 = (bf16[128,2048]{1,0:T(8,128)(2,1)S(1)}, bf16[128,2048]{1,0:T(8,128)(2,1)S(1)}, u32[]{:S(2)}, u32[]{:S(2)}) collective-permute-start(bf16[128,2048]{1,0:T(8,128)(2,1)S(1)} %beta_pieces.5.rest_0_.own_ref), channel_id=1, source_target_pairs={{0,16},{8,24},{16,0},{24,8},{1,17},{9,25},{17,1},{25,9},{2,18},{10... | collective-permute-start | bytes 1572872 | tf_op jit(solution)/shard_map/ppermute | solution.py:418
  29.1 0.5 %beta_pieces.4.refs_5_.own_ref = bf16[64,2048]{1,0:T(8,128)(2,1)S(1)} custom-call(s32[1]{0:T(128)} %bitcast.here_ref, f32[64,2048]{1,0:T(8,128)S(1)} %own_product.4.product_ref, bf16[64,512]{1,0:T(8,128)(2,1)S(1)} %collective-permute-done.9.ratio_ref, bf16[512,2048]{1,0:T(8,128)(2,1)S(1)} %collective-permute-done.7.doc_ref, ...), custom_call_target="tpu_custom_call" | custom-call | flops 134217728 | bytes 3145728 | tf_op jit(solution)/shard_map/beta_pieces/pallas_call | solution.py:228
  29.7 1.6 %collective-permute-start.10 = (bf16[256,512]{1,0:T(8,128)(2,1)S(1)}, bf16[256,512]{1,0:T(8,128)(2,1)S(1)}, u32[]{:S(2)}, u32[]{:S(2)}) collective-permute-start(bf16[256,512]{1,0:T(8,128)(2,1)S(1)} %join_ratio.1.refs_0_), channel_id=1, source_target_pairs={{0,1},{1,0},{2,3},{3,2},{4,5},{5,4},{6,7},{7,6},{8,9},{9,8},{10,11... | collective-permute-start | bytes 786440 | tf_op jit(solution)/shard_map/ppermute | solution.py:414
  31.2 6.8 %collective-permute-done.11.in_ref = bf16[128,2048]{1,0:T(8,128)(2,1)S(1)} collective-permute-done((bf16[128,2048]{1,0:T(8,128)(2,1)S(1)}, bf16[128,2048]{1,0:T(8,128)(2,1)S(1)}, u32[]{:S(2)}, u32[]{:S(2)}) %collective-permute-start.11) | collective-permute-done | bytes 524320 | tf_op jit(solution)/shard_map/ppermute | solution.py:414
  38.2 0.5 collective-permute-start.15
  38.7 1.6 %collective-permute-start.18 = (bf16[64,2048]{1,0:T(8,128)(2,1)S(1)}, bf16[64,2048]{1,0:T(8,128)(2,1)S(1)}, u32[]{:S(2)}, u32[]{:S(2)}) collective-permute-start(bf16[64,2048]{1,0:T(8,128)(2,1)S(1)} %beta_pieces.4.refs_5_.own_ref), channel_id=1, source_target_pairs={{0,16},{8,24},{16,0},{24,8},{1,17},{9,25},{17,1},{25,9},{2,18},{10... | collective-permute-start | bytes 786440 | tf_op jit(solution)/shard_map/ppermute | solution.py:418
  40.3 0.8 %place_pieces.2 = (bf16[256,4096]{1,0:T(8,128)(2,1)}, f32[8,128]{1,0:T(8,128)S(1)}) custom-call(s32[1]{0:T(128)} %bitcast.here_ref, bf16[64,2048]{1,0:T(8,128)(2,1)S(1)} %add_pair.3.refs_4_.refs_0_, bf16[64,2048]{1,0:T(8,128)(2,1)S(1)} %collective-permute-done.16.refs_1_), custom_call_target="tpu_custom_call" | custom-call | bytes 524288 | tf_op jit(solution)/shard_map/place_pieces/pallas_call | solution.py:394
  41.1 1.0 %collective-permute-done.10.refs_1_ = bf16[256,512]{1,0:T(8,128)(2,1)S(1)} collective-permute-done((bf16[256,512]{1,0:T(8,128)(2,1)S(1)}, bf16[256,512]{1,0:T(8,128)(2,1)S(1)}, u32[]{:S(2)}, u32[]{:S(2)}) %collective-permute-start.10) | collective-permute-done | bytes 262176 | tf_op jit(solution)/shard_map/ppermute | solution.py:414
  42.3 3.7 %theta_grad.1 = (f32[512,2048]{1,0:T(8,128)}, f32[8,128]{1,0:T(8,128)S(1)}) custom-call(s32[1]{0:T(128)} %bitcast.here_ref, bf16[512,256]{1,0:T(8,128)(2,1)S(1)} %get-tuple-element.26.refs_0_, bf16[512,256]{1,0:T(8,128)(2,1)S(1)} %get-tuple-element.27.refs_1_, bf16[256,4096]{1,0:T(8,128)(2,1)S(1)} %get-tuple-element.25.prob_ref.refs_2_, ...), custom_call_target="tpu_custom_call" | custom-call | flops 1 | bytes 1 | tf_op jit(solution)/shard_map/theta_grad/pallas_call | solution.py:351
  46.2 1.1 %collective-permute-done.18.other_ref = bf16[64,2048]{1,0:T(8,128)(2,1)S(1)} collective-permute-done((bf16[64,2048]{1,0:T(8,128)(2,1)S(1)}, bf16[64,2048]{1,0:T(8,128)(2,1)S(1)}, u32[]{:S(2)}, u32[]{:S(2)}) %collective-permute-start.18) | collective-permute-done | bytes 262176 | tf_op jit(solution)/shard_map/ppermute | solution.py:418
  47.4 1.5 %collective-permute-done.20.refs_3_ = bf16[64,2048]{1,0:T(8,128)(2,1)S(1)} collective-permute-done((bf16[64,2048]{1,0:T(8,128)(2,1)S(1)}, bf16[64,2048]{1,0:T(8,128)(2,1)S(1)}, u32[]{:S(2)}, u32[]{:S(2)}) %collective-permute-start.20) | collective-permute-done | bytes 262176 | tf_op jit(solution)/shard_map/ppermute | solution.py:418
  48.9 1.2 %place_pieces.3 = bf16[256,4096]{1,0:T(8,128)(2,1)} custom-call(s32[1]{0:T(128)} %bitcast.here_ref, bf16[128,2048]{1,0:T(8,128)(2,1)S(1)} %add_pair.4.refs_0_, bf16[64,2048]{1,0:T(8,128)(2,1)S(1)} %add_pair.5.refs_1_, bf16[128,2048]{1,0:T(8,128)(2,1)S(1)} %collective-permute-done.19.refs_2_, ...), custom_call_target="tpu_custom_call", output_to_operand_aliasing={{}: (5, {})} | custom-call | bytes 1572864 | tf_op jit(solution)/shard_map/place_pieces/pallas_call | solution.py:394
  (33 shorter events, 1.7 us)
Async XLA Ops:
  0.6 9.8 %copy-start = (s32[16,64,128]{2,1,0:T(8,128)S(1)}, s32[16,64,128]{2,1,0:T(8,128)}, u32[]{:S(2)}) copy-start(s32[16,64,128]{2,1,0:T(8,128)} %count_ref.1) | copy-start | bytes 1572868
  4.7 15.2 %collective-permute-start.7 = (bf16[512,2048]{1,0:T(8,128)(2,1)S(1)}, bf16[512,2048]{1,0:T(8,128)(2,1)S(1)}, u32[]{:S(2)}, u32[]{:S(2)}) collective-permute-start(bf16[512,2048]{1,0:T(8,128)(2,1)S(1)} %get-tuple-element.24), channel_id=1, source_target_pairs={{0,8},{8,0},{16,24},{24,16},{1,9},{9,1},{17,25},{25,17},{2,10},{10... | collective-permute-start | bytes 6291464 | tf_op jit(solution)/shard_map/ppermute | solution.py:418
  5.2 7.9 %collective-permute-start = (bf16[64,512]{1,0:T(8,128)(2,1)S(1)}, bf16[64,512]{1,0:T(8,128)(2,1)S(1)}, u32[]{:S(2)}, u32[]{:S(2)}) collective-permute-start(bf16[64,512]{1,0:T(8,128)(2,1)S(1)} %get-tuple-element.20), channel_id=1, source_target_pairs={{0,4},{2,6},{4,0},{6,2},{1,5},{3,7},{5,1},{7,3},{8,12},{10,14},{12... | collective-permute-start | bytes 196616 | tf_op jit(solution)/shard_map/ppermute | solution.py:418
  8.9 6.7 %collective-permute-start.1 = (bf16[64,512]{1,0:T(8,128)(2,1)S(1)}, bf16[64,512]{1,0:T(8,128)(2,1)S(1)}, u32[]{:S(2)}, u32[]{:S(2)}) collective-permute-start(bf16[64,512]{1,0:T(8,128)(2,1)S(1)} %get-tuple-element.21), channel_id=1, source_target_pairs={{0,6},{2,4},{4,2},{6,0},{1,7},{3,5},{5,3},{7,1},{8,14},{10,12},{12... | collective-permute-start | bytes 196616 | tf_op jit(solution)/shard_map/ppermute | solution.py:418
  10.2 5.5 %collective-permute-start.2 = (bf16[64,512]{1,0:T(8,128)(2,1)S(1)}, bf16[64,512]{1,0:T(8,128)(2,1)S(1)}, u32[]{:S(2)}, u32[]{:S(2)}) collective-permute-start(bf16[64,512]{1,0:T(8,128)(2,1)S(1)} %get-tuple-element.22), channel_id=1, source_target_pairs={{0,2},{2,0},{4,6},{6,4},{1,3},{3,1},{5,7},{7,5},{8,10},{10,8},{12,... | collective-permute-start | bytes 196616 | tf_op jit(solution)/shard_map/ppermute | solution.py:418
  15.8 4.1 %collective-permute-start.6 = (bf16[64,512]{1,0:T(8,128)(2,1)S(1)}, bf16[64,512]{1,0:T(8,128)(2,1)S(1)}, u32[]{:S(2)}, u32[]{:S(2)}) collective-permute-start(bf16[64,512]{1,0:T(8,128)(2,1)S(1)} %ratio_chunk.1.ratio_ref.refs_0_), channel_id=1, source_target_pairs={{0,8},{8,0},{16,24},{24,16},{1,9},{9,1},{17,25},{25,17},{2,10},{10... | collective-permute-start | bytes 196616 | tf_op jit(solution)/shard_map/ppermute | solution.py:418
  15.9 7.3 %collective-permute-start.5 = (bf16[64,512]{1,0:T(8,128)(2,1)S(1)}, bf16[64,512]{1,0:T(8,128)(2,1)S(1)}, u32[]{:S(2)}, u32[]{:S(2)}) collective-permute-start(bf16[64,512]{1,0:T(8,128)(2,1)S(1)} %ratio_chunk.1.ratio_ref.refs_0_), channel_id=1, source_target_pairs={{0,4},{2,6},{4,0},{6,2},{1,5},{3,7},{5,1},{7,3},{8,12},{10,14},{12... | collective-permute-start | bytes 196616 | tf_op jit(solution)/shard_map/ppermute | solution.py:418
  18.7 6.2 %collective-permute-start.3 = (bf16[64,512]{1,0:T(8,128)(2,1)S(1)}, bf16[64,512]{1,0:T(8,128)(2,1)S(1)}, u32[]{:S(2)}, u32[]{:S(2)}) collective-permute-start(bf16[64,512]{1,0:T(8,128)(2,1)S(1)} %ratio_chunk.1.ratio_ref.refs_0_), channel_id=1, source_target_pairs={{0,6},{2,4},{4,2},{6,0},{1,7},{3,5},{5,3},{7,1},{8,14},{10,12},{12... | collective-permute-start | bytes 196616 | tf_op jit(solution)/shard_map/ppermute | solution.py:418
  20.4 8.4 %collective-permute-start.8 = (bf16[64,2048]{1,0:T(8,128)(2,1)S(1)}, bf16[64,2048]{1,0:T(8,128)(2,1)S(1)}, u32[]{:S(2)}, u32[]{:S(2)}) collective-permute-start(bf16[64,2048]{1,0:T(8,128)(2,1)S(1)} %beta_pieces.3.own_ref), channel_id=1, source_target_pairs={{0,16},{8,24},{16,0},{24,8},{1,17},{9,25},{17,1},{25,9},{2,18},{10... | collective-permute-start | bytes 786440 | tf_op jit(solution)/shard_map/ppermute | solution.py:418
  21.9 4.3 %collective-permute-start.4 = (bf16[64,512]{1,0:T(8,128)(2,1)S(1)}, bf16[64,512]{1,0:T(8,128)(2,1)S(1)}, u32[]{:S(2)}, u32[]{:S(2)}) collective-permute-start(bf16[64,512]{1,0:T(8,128)(2,1)S(1)} %ratio_chunk.1.ratio_ref.refs_0_), channel_id=1, source_target_pairs={{0,2},{2,0},{4,6},{6,4},{1,3},{3,1},{5,7},{7,5},{8,10},{10,8},{12,... | collective-permute-start | bytes 196616 | tf_op jit(solution)/shard_map/ppermute | solution.py:418
  23.2 14.9 %collective-permute-start.11 = (bf16[128,2048]{1,0:T(8,128)(2,1)S(1)}, bf16[128,2048]{1,0:T(8,128)(2,1)S(1)}, u32[]{:S(2)}, u32[]{:S(2)}) collective-permute-start(bf16[128,2048]{1,0:T(8,128)(2,1)S(1)} %hold.1), channel_id=1, source_target_pairs={{0,1},{1,0},{2,3},{3,2},{4,5},{5,4},{6,7},{7,6},{8,9},{9,8},{10,11... | collective-permute-start | bytes 1572872 | tf_op jit(solution)/shard_map/ppermute | solution.py:414
  24.8 1.9 %collective-permute-start.12 = (bf16[64,512]{1,0:T(8,128)(2,1)S(1)}, bf16[64,512]{1,0:T(8,128)(2,1)S(1)}, u32[]{:S(2)}, u32[]{:S(2)}) collective-permute-start(bf16[64,512]{1,0:T(8,128)(2,1)S(1)} %collective-permute-done.5.refs_3_.rest_0_.refs_0_), channel_id=1, source_target_pairs={{0,8},{8,0},{16,24},{24,16},{1,9},{9,1},{17,25},{25,17},{2,10},{10... | collective-permute-start | bytes 196616 | tf_op jit(solution)/shard_map/ppermute | solution.py:418
  24.8 1.9 %collective-permute-start.13 = (bf16[64,512]{1,0:T(8,128)(2,1)S(1)}, bf16[64,512]{1,0:T(8,128)(2,1)S(1)}, u32[]{:S(2)}, u32[]{:S(2)}) collective-permute-start(bf16[64,512]{1,0:T(8,128)(2,1)S(1)} %collective-permute-done.3.refs_1_), channel_id=1, source_target_pairs={{0,8},{8,0},{16,24},{24,16},{1,9},{9,1},{17,25},{25,17},{2,10},{10... | collective-permute-start | bytes 196616 | tf_op jit(solution)/shard_map/ppermute | solution.py:418
  26.2 2.9 %collective-permute-start.9 = (bf16[64,512]{1,0:T(8,128)(2,1)S(1)}, bf16[64,512]{1,0:T(8,128)(2,1)S(1)}, u32[]{:S(2)}, u32[]{:S(2)}) collective-permute-start(bf16[64,512]{1,0:T(8,128)(2,1)S(1)} %collective-permute-done.4.ratio_ref.refs_2_), channel_id=1, source_target_pairs={{0,8},{8,0},{16,24},{24,16},{1,9},{9,1},{17,25},{25,17},{2,10},{10... | collective-permute-start | bytes 196616 | tf_op jit(solution)/shard_map/ppermute | solution.py:418
  27.3 18.7 %collective-permute-start.17 = (bf16[128,2048]{1,0:T(8,128)(2,1)S(1)}, bf16[128,2048]{1,0:T(8,128)(2,1)S(1)}, u32[]{:S(2)}, u32[]{:S(2)}) collective-permute-start(bf16[128,2048]{1,0:T(8,128)(2,1)S(1)} %beta_pieces.5.rest_0_.own_ref), channel_id=1, source_target_pairs={{0,16},{8,24},{16,0},{24,8},{1,17},{9,25},{17,1},{25,9},{2,18},{10... | collective-permute-start | bytes 1572872 | tf_op jit(solution)/shard_map/ppermute | solution.py:418
  28.8 9.9 %collective-permute-start.16 = (bf16[64,2048]{1,0:T(8,128)(2,1)S(1)}, bf16[64,2048]{1,0:T(8,128)(2,1)S(1)}, u32[]{:S(2)}, u32[]{:S(2)}) collective-permute-start(bf16[64,2048]{1,0:T(8,128)(2,1)S(1)} %add_pair.3.refs_4_.refs_0_), channel_id=1, source_target_pairs={{0,8},{8,0},{16,24},{24,16},{1,9},{9,1},{17,25},{25,17},{2,10},{10... | collective-permute-start | bytes 786440 | tf_op jit(solution)/shard_map/ppermute | solution.py:418
  29.7 12.4 %collective-permute-start.10 = (bf16[256,512]{1,0:T(8,128)(2,1)S(1)}, bf16[256,512]{1,0:T(8,128)(2,1)S(1)}, u32[]{:S(2)}, u32[]{:S(2)}) collective-permute-start(bf16[256,512]{1,0:T(8,128)(2,1)S(1)} %join_ratio.1.refs_0_), channel_id=1, source_target_pairs={{0,1},{1,0},{2,3},{3,2},{4,5},{5,4},{6,7},{7,6},{8,9},{9,8},{10,11... | collective-permute-start | bytes 786440 | tf_op jit(solution)/shard_map/ppermute | solution.py:414
  38.1 4.2 %collective-permute-start.14 = (bf16[64,2048]{1,0:T(8,128)(2,1)S(1)}, bf16[64,2048]{1,0:T(8,128)(2,1)S(1)}, u32[]{:S(2)}, u32[]{:S(2)}) collective-permute-start(bf16[64,2048]{1,0:T(8,128)(2,1)S(1)} %get-tuple-element.29.refs_3_), channel_id=1, source_target_pairs={{0,8},{8,0},{16,24},{24,16},{1,9},{9,1},{17,25},{25,17},{2,10},{10... | collective-permute-start | bytes 786440 | tf_op jit(solution)/shard_map/ppermute | solution.py:418
  38.2 4.1 %collective-permute-start.15 = (bf16[64,2048]{1,0:T(8,128)(2,1)S(1)}, bf16[64,2048]{1,0:T(8,128)(2,1)S(1)}, u32[]{:S(2)}, u32[]{:S(2)}) collective-permute-start(bf16[64,2048]{1,0:T(8,128)(2,1)S(1)} %get-tuple-element.30.refs_4_), channel_id=1, source_target_pairs={{0,8},{8,0},{16,24},{24,16},{1,9},{9,1},{17,25},{25,17},{2,10},{10... | collective-permute-start | bytes 786440 | tf_op jit(solution)/shard_map/ppermute | solution.py:418
  38.7 8.6 %collective-permute-start.18 = (bf16[64,2048]{1,0:T(8,128)(2,1)S(1)}, bf16[64,2048]{1,0:T(8,128)(2,1)S(1)}, u32[]{:S(2)}, u32[]{:S(2)}) collective-permute-start(bf16[64,2048]{1,0:T(8,128)(2,1)S(1)} %beta_pieces.4.refs_5_.own_ref), channel_id=1, source_target_pairs={{0,16},{8,24},{16,0},{24,8},{1,17},{9,25},{17,1},{25,9},{2,18},{10... | collective-permute-start | bytes 786440 | tf_op jit(solution)/shard_map/ppermute | solution.py:418
  46.1 2.8 %collective-permute-start.19 = (bf16[128,2048]{1,0:T(8,128)(2,1)S(1)}, bf16[128,2048]{1,0:T(8,128)(2,1)S(1)}, u32[]{:S(2)}, u32[]{:S(2)}) collective-permute-start(bf16[128,2048]{1,0:T(8,128)(2,1)S(1)} %add_pair.4.refs_0_), channel_id=1, source_target_pairs={{0,8},{8,0},{16,24},{24,16},{1,9},{9,1},{17,25},{25,17},{2,10},{10... | collective-permute-start | bytes 1572872 | tf_op jit(solution)/shard_map/ppermute | solution.py:418
  47.3 1.6 %collective-permute-start.20 = (bf16[64,2048]{1,0:T(8,128)(2,1)S(1)}, bf16[64,2048]{1,0:T(8,128)(2,1)S(1)}, u32[]{:S(2)}, u32[]{:S(2)}) collective-permute-start(bf16[64,2048]{1,0:T(8,128)(2,1)S(1)} %add_pair.5.refs_1_), channel_id=1, source_target_pairs={{0,8},{8,0},{16,24},{24,16},{1,9},{9,1},{17,25},{25,17},{2,10},{10... | collective-permute-start | bytes 786440 | tf_op jit(solution)/shard_map/ppermute | solution.py:418

commit v19 on v18

--- a/solution.py
+++ b/solution.py
@@ -53,7 +53,7 @@
     docs, width = doc_topics.shape
     words = word_logits.shape[0]
     side_width = width // 2
-    span = min(side_width, 1024)
+    span = min(side_width, 2048)
     steps = side_width // span
     count, far = sizes.topic, sizes.vocab - 1
     chunk, half, share = words // count, words // 2, width // sizes.vocab

time: 50.3 us -> 50.1 us (level)
  no operation moved by 1% of the time
where the time goes in v19:
time: 50.1 us; the launch traced here: 49.9 us
  starting transfers between devices  19.3 us (39%)
  waiting for transfers between devices  15.9 us (32%)
  Pallas kernels  13.9 us (28%)
  between operations  0.84 us (2%)
    ppermute x19, starting transfers between devices, swap(): return lax.ppermute(array, axis, [(i, i ^ bits) for i in range(count)])  16 us
    ppermute x19, waiting for transfers between devices, swap(): return lax.ppermute(array, axis, [(i, i ^ bits) for i in range(count)])  8.1 us
    ppermute x2, waiting for transfers between devices, shift(): lax.ppermute(array, 'vocab', [(i, (i + by) % sizes.vocab) for i in range(...  7.82 us
    pallas_call x1, Pallas kernels, rate_partial(): pl.pallas_call(kernel, out_shape=[jax.ShapeDtypeStruct((chunk, docs), BF1...  3.81 us
    pallas_call x1, Pallas kernels, theta_grad(): pl.pallas_call(kernel, out_shape=[jax.ShapeDtypeStruct((docs, share), F32...  3.65 us
    ppermute x2, starting transfers between devices, shift(): lax.ppermute(array, 'vocab', [(i, (i + by) % sizes.vocab) for i in range(...  3.26 us
    pallas_call x2, Pallas kernels, place_pieces(): pl.pallas_call(kernel, out_shape=[jax.ShapeDtypeStruct(shape, BF16)] + ([...  1.99 us
    pallas_call x3, Pallas kernels, beta_pieces(): pl.pallas_call(kernel, out_shape=[jax.ShapeDtypeStruct((rows * len(piece)...  1.51 us
  transfers between devices with their start and end apart: 21, of which 9 were waited for; matrix products, arithmetic and copies ran while one was open for 0% of the time, Pallas kernels for 18%

profile of v19, /device:TPU:0, one launch (start us, length us, event | category | flops | bytes accessed | tf_op | source)
XLA Modules:
  0.0 49.9 jit_solution(8692965466301689032)
XLA Ops:
  0.6 3.8 %rate_partial.1 = (bf16[64,512]{1,0:T(8,128)(2,1)S(1)}, bf16[64,512]{1,0:T(8,128)(2,1)S(1)}, bf16[64,512]{1,0:T(8,128)(2,1)S(1)}, bf16[64,512]{1,0:T(8,128)(2,1)...) custom-call(s32[1]{0:T(128)} %bitcast.here_ref, ...), custom_call_target="tpu_custom_call" | custom-call | flops 1073741824 | bytes 6291456 | tf_op jit(solution)/shard_map/rate_partial/pallas_call | solution.py:104
  4.5 0.5 %collective-permute-start.7 = (bf16[512,2048]{1,0:T(8,128)(2,1)S(1)}, bf16[512,2048]{1,0:T(8,128)(2,1)S(1)}, u32[]{:S(2)}, u32[]{:S(2)}) collective-permute-start(bf16[512,2048]{1,0:T(8,128)(2,1)S(1)} %get-tuple-element.24), channel_id=1, source_target_pairs={{0,8},{8,0},{16,24},{24,16},{1,9},{9,1},{17,25},{25,17},{2,10},{10... | collective-permute-start | bytes 6291464 | tf_op jit(solution)/shard_map/ppermute | solution.py:418
  5.0 3.7 %collective-permute-start = (bf16[64,512]{1,0:T(8,128)(2,1)S(1)}, bf16[64,512]{1,0:T(8,128)(2,1)S(1)}, u32[]{:S(2)}, u32[]{:S(2)}) collective-permute-start(bf16[64,512]{1,0:T(8,128)(2,1)S(1)} %get-tuple-element.20), channel_id=1, source_target_pairs={{0,4},{2,6},{4,0},{6,2},{1,5},{3,7},{5,1},{7,3},{8,12},{10,14},{12... | collective-permute-start | bytes 196616 | tf_op jit(solution)/shard_map/ppermute | solution.py:418
  8.7 1.3 %collective-permute-start.1 = (bf16[64,512]{1,0:T(8,128)(2,1)S(1)}, bf16[64,512]{1,0:T(8,128)(2,1)S(1)}, u32[]{:S(2)}, u32[]{:S(2)}) collective-permute-start(bf16[64,512]{1,0:T(8,128)(2,1)S(1)} %get-tuple-element.21), channel_id=1, source_target_pairs={{0,6},{2,4},{4,2},{6,0},{1,7},{3,5},{5,3},{7,1},{8,14},{10,12},{12... | collective-permute-start | bytes 196616 | tf_op jit(solution)/shard_map/ppermute | solution.py:418
  10.2 0.8 %chunk_counts.1.refs_4_ = f32[64,512]{1,0:T(8,128)S(1)} custom-call(s32[1]{0:T(128)} %bitcast.here_ref, s32[16]{0:T(128)} %doc_at.1, s32[16]{0:T(128)} %word_at.1, s32[16,64,128]{2,1,0:T(8,128)S(1)} %copy-done), custom_call_target="tpu_custom_call" | custom-call | flops 131072 | bytes 524288 | tf_op jit(solution)/shard_map/chunk_counts/pallas_call | solution.py:143
  11.1 1.8 %collective-permute-done.refs_1_ = bf16[64,512]{1,0:T(8,128)(2,1)S(1)} collective-permute-done((bf16[64,512]{1,0:T(8,128)(2,1)S(1)}, bf16[64,512]{1,0:T(8,128)(2,1)S(1)}, u32[]{:S(2)}, u32[]{:S(2)}) %collective-permute-start) | collective-permute-done | bytes 65568 | tf_op jit(solution)/shard_map/ppermute | solution.py:418
  12.9 2.4 %collective-permute-done.1.refs_2_ = bf16[64,512]{1,0:T(8,128)(2,1)S(1)} collective-permute-done((bf16[64,512]{1,0:T(8,128)(2,1)S(1)}, bf16[64,512]{1,0:T(8,128)(2,1)S(1)}, u32[]{:S(2)}, u32[]{:S(2)}) %collective-permute-start.1) | collective-permute-done | bytes 65568 | tf_op jit(solution)/shard_map/ppermute | solution.py:418
  15.6 2.8 %collective-permute-start.5 = (bf16[64,512]{1,0:T(8,128)(2,1)S(1)}, bf16[64,512]{1,0:T(8,128)(2,1)S(1)}, u32[]{:S(2)}, u32[]{:S(2)}) collective-permute-start(bf16[64,512]{1,0:T(8,128)(2,1)S(1)} %ratio_chunk.1.ratio_ref.refs_0_), channel_id=1, source_target_pairs={{0,4},{2,6},{4,0},{6,2},{1,5},{3,7},{5,1},{7,3},{8,12},{10,14},{12... | collective-permute-start | bytes 196616 | tf_op jit(solution)/shard_map/ppermute | solution.py:418
  18.5 0.7 %collective-permute-start.3 = (bf16[64,512]{1,0:T(8,128)(2,1)S(1)}, bf16[64,512]{1,0:T(8,128)(2,1)S(1)}, u32[]{:S(2)}, u32[]{:S(2)}) collective-permute-start(bf16[64,512]{1,0:T(8,128)(2,1)S(1)} %ratio_chunk.1.ratio_ref.refs_0_), channel_id=1, source_target_pairs={{0,6},{2,4},{4,2},{6,0},{1,7},{3,5},{5,3},{7,1},{8,14},{10,12},{12... | collective-permute-start | bytes 196616 | tf_op jit(solution)/shard_map/ppermute | solution.py:418
  19.2 0.5 own_product.3.product_ref
  19.7 0.5 beta_pieces.3.own_ref
  20.2 1.6 %collective-permute-start.8 = (bf16[64,2048]{1,0:T(8,128)(2,1)S(1)}, bf16[64,2048]{1,0:T(8,128)(2,1)S(1)}, u32[]{:S(2)}, u32[]{:S(2)}) collective-permute-start(bf16[64,2048]{1,0:T(8,128)(2,1)S(1)} %beta_pieces.3.own_ref), channel_id=1, source_target_pairs={{0,16},{8,24},{16,0},{24,8},{1,17},{9,25},{17,1},{25,9},{2,18},{10... | collective-permute-start | bytes 786440 | tf_op jit(solution)/shard_map/ppermute | solution.py:418
  21.7 0.5 collective-permute-start.4
  22.2 0.7 %collective-permute-done.5.refs_3_.rest_0_.refs_0_ = bf16[64,512]{1,0:T(8,128)(2,1)S(1)} collective-permute-done((bf16[64,512]{1,0:T(8,128)(2,1)S(1)}, bf16[64,512]{1,0:T(8,128)(2,1)S(1)}, u32[]{:S(2)}, u32[]{:S(2)}) %collective-permute-start.5) | collective-permute-done | bytes 65568 | tf_op jit(solution)/shard_map/ppermute | solution.py:418
  22.9 1.7 %collective-permute-start.11 = (bf16[128,2048]{1,0:T(8,128)(2,1)S(1)}, bf16[128,2048]{1,0:T(8,128)(2,1)S(1)}, u32[]{:S(2)}, u32[]{:S(2)}) collective-permute-start(bf16[128,2048]{1,0:T(8,128)(2,1)S(1)} %hold.1), channel_id=1, source_target_pairs={{0,1},{1,0},{2,3},{3,2},{4,5},{5,4},{6,7},{7,6},{8,9},{9,8},{10,11... | collective-permute-start | bytes 1572872 | tf_op jit(solution)/shard_map/ppermute | solution.py:414
  24.6 0.6 %collective-permute-start.13 = (bf16[64,512]{1,0:T(8,128)(2,1)S(1)}, bf16[64,512]{1,0:T(8,128)(2,1)S(1)}, u32[]{:S(2)}, u32[]{:S(2)}) collective-permute-start(bf16[64,512]{1,0:T(8,128)(2,1)S(1)} %collective-permute-done.3.refs_1_), channel_id=1, source_target_pairs={{0,8},{8,0},{16,24},{24,16},{1,9},{9,1},{17,25},{25,17},{2,10},{10... | collective-permute-start | bytes 196616 | tf_op jit(solution)/shard_map/ppermute | solution.py:418
  25.2 0.5 own_product.5.product_ref
  25.7 0.3 collective-permute-done.4.ratio_ref.refs_2_
  26.0 0.5 own_product.4.product_ref
  26.5 0.5 %beta_pieces.5.rest_0_.own_ref = bf16[128,2048]{1,0:T(8,128)(2,1)S(1)} custom-call(s32[1]{0:T(128)} %bitcast.here_ref, f32[128,2048]{1,0:T(8,128)S(1)} %own_product.5.product_ref, bf16[128,512]{1,0:T(8,128)(2,1)S(1)} %stack_rows.3.ratio_ref, bf16[512,2048]{1,0:T(8,128)(2,1)S(1)} %collective-permute-done.7.doc_ref, ...), custom_call_target="tpu_custom_call" | custom-call | flops 1250000000 | bytes 1 | tf_op jit(solution)/shard_map/beta_pieces/pallas_call | solution.py:228
  27.0 1.5 %collective-permute-start.17 = (bf16[128,2048]{1,0:T(8,128)(2,1)S(1)}, bf16[128,2048]{1,0:T(8,128)(2,1)S(1)}, u32[]{:S(2)}, u32[]{:S(2)}) collective-permute-start(bf16[128,2048]{1,0:T(8,128)(2,1)S(1)} %beta_pieces.5.rest_0_.own_ref), channel_id=1, source_target_pairs={{0,16},{8,24},{16,0},{24,8},{1,17},{9,25},{17,1},{25,9},{2,18},{10... | collective-permute-start | bytes 1572872 | tf_op jit(solution)/shard_map/ppermute | solution.py:418
  28.9 0.5 %beta_pieces.4.refs_5_.own_ref = bf16[64,2048]{1,0:T(8,128)(2,1)S(1)} custom-call(s32[1]{0:T(128)} %bitcast.here_ref, f32[64,2048]{1,0:T(8,128)S(1)} %own_product.4.product_ref, bf16[64,512]{1,0:T(8,128)(2,1)S(1)} %collective-permute-done.9.ratio_ref, bf16[512,2048]{1,0:T(8,128)(2,1)S(1)} %collective-permute-done.7.doc_ref, ...), custom_call_target="tpu_custom_call" | custom-call | flops 134217728 | bytes 3145728 | tf_op jit(solution)/shard_map/beta_pieces/pallas_call | solution.py:228
  29.4 1.6 %collective-permute-start.10 = (bf16[256,512]{1,0:T(8,128)(2,1)S(1)}, bf16[256,512]{1,0:T(8,128)(2,1)S(1)}, u32[]{:S(2)}, u32[]{:S(2)}) collective-permute-start(bf16[256,512]{1,0:T(8,128)(2,1)S(1)} %join_ratio.1.refs_0_), channel_id=1, source_target_pairs={{0,1},{1,0},{2,3},{3,2},{4,5},{5,4},{6,7},{7,6},{8,9},{9,8},{10,11... | collective-permute-start | bytes 786440 | tf_op jit(solution)/shard_map/ppermute | solution.py:414
  31.0 6.8 %collective-permute-done.11.in_ref = bf16[128,2048]{1,0:T(8,128)(2,1)S(1)} collective-permute-done((bf16[128,2048]{1,0:T(8,128)(2,1)S(1)}, bf16[128,2048]{1,0:T(8,128)(2,1)S(1)}, u32[]{:S(2)}, u32[]{:S(2)}) %collective-permute-start.11) | collective-permute-done | bytes 524320 | tf_op jit(solution)/shard_map/ppermute | solution.py:414
  38.0 0.5 collective-permute-start.15
  38.5 1.6 %collective-permute-start.18 = (bf16[64,2048]{1,0:T(8,128)(2,1)S(1)}, bf16[64,2048]{1,0:T(8,128)(2,1)S(1)}, u32[]{:S(2)}, u32[]{:S(2)}) collective-permute-start(bf16[64,2048]{1,0:T(8,128)(2,1)S(1)} %beta_pieces.4.refs_5_.own_ref), channel_id=1, source_target_pairs={{0,16},{8,24},{16,0},{24,8},{1,17},{9,25},{17,1},{25,9},{2,18},{10... | collective-permute-start | bytes 786440 | tf_op jit(solution)/shard_map/ppermute | solution.py:418
  40.1 0.8 %place_pieces.2 = (bf16[256,4096]{1,0:T(8,128)(2,1)}, f32[8,128]{1,0:T(8,128)S(1)}) custom-call(s32[1]{0:T(128)} %bitcast.here_ref, bf16[64,2048]{1,0:T(8,128)(2,1)S(1)} %add_pair.3.refs_4_.refs_0_, bf16[64,2048]{1,0:T(8,128)(2,1)S(1)} %collective-permute-done.16.refs_1_), custom_call_target="tpu_custom_call" | custom-call | bytes 524288 | tf_op jit(solution)/shard_map/place_pieces/pallas_call | solution.py:394
  40.9 1.0 %collective-permute-done.10.refs_1_ = bf16[256,512]{1,0:T(8,128)(2,1)S(1)} collective-permute-done((bf16[256,512]{1,0:T(8,128)(2,1)S(1)}, bf16[256,512]{1,0:T(8,128)(2,1)S(1)}, u32[]{:S(2)}, u32[]{:S(2)}) %collective-permute-start.10) | collective-permute-done | bytes 262176 | tf_op jit(solution)/shard_map/ppermute | solution.py:414
  42.1 3.7 %theta_grad.1 = (f32[512,2048]{1,0:T(8,128)}, f32[8,128]{1,0:T(8,128)S(1)}) custom-call(s32[1]{0:T(128)} %bitcast.here_ref, bf16[512,256]{1,0:T(8,128)(2,1)S(1)} %get-tuple-element.26.refs_0_, bf16[512,256]{1,0:T(8,128)(2,1)S(1)} %get-tuple-element.27.refs_1_, bf16[256,4096]{1,0:T(8,128)(2,1)S(1)} %get-tuple-element.25.prob_ref.refs_2_, ...), custom_call_target="tpu_custom_call" | custom-call | flops 1 | bytes 1 | tf_op jit(solution)/shard_map/theta_grad/pallas_call | solution.py:351
  45.9 1.1 %collective-permute-done.18.other_ref = bf16[64,2048]{1,0:T(8,128)(2,1)S(1)} collective-permute-done((bf16[64,2048]{1,0:T(8,128)(2,1)S(1)}, bf16[64,2048]{1,0:T(8,128)(2,1)S(1)}, u32[]{:S(2)}, u32[]{:S(2)}) %collective-permute-start.18) | collective-permute-done | bytes 262176 | tf_op jit(solution)/shard_map/ppermute | solution.py:418
  47.2 1.5 %collective-permute-done.20.refs_3_ = bf16[64,2048]{1,0:T(8,128)(2,1)S(1)} collective-permute-done((bf16[64,2048]{1,0:T(8,128)(2,1)S(1)}, bf16[64,2048]{1,0:T(8,128)(2,1)S(1)}, u32[]{:S(2)}, u32[]{:S(2)}) %collective-permute-start.20) | collective-permute-done | bytes 262176 | tf_op jit(solution)/shard_map/ppermute | solution.py:418
  48.7 1.2 %place_pieces.3 = bf16[256,4096]{1,0:T(8,128)(2,1)} custom-call(s32[1]{0:T(128)} %bitcast.here_ref, bf16[128,2048]{1,0:T(8,128)(2,1)S(1)} %add_pair.4.refs_0_, bf16[64,2048]{1,0:T(8,128)(2,1)S(1)} %add_pair.5.refs_1_, bf16[128,2048]{1,0:T(8,128)(2,1)S(1)} %collective-permute-done.19.refs_2_, ...), custom_call_target="tpu_custom_call", output_to_operand_aliasing={{}: (5, {})} | custom-call | bytes 1572864 | tf_op jit(solution)/shard_map/place_pieces/pallas_call | solution.py:394
  (33 shorter events, 1.7 us)
Async XLA Ops:
  0.6 9.6 %copy-start = (s32[16,64,128]{2,1,0:T(8,128)S(1)}, s32[16,64,128]{2,1,0:T(8,128)}, u32[]{:S(2)}) copy-start(s32[16,64,128]{2,1,0:T(8,128)} %count_ref.1) | copy-start | bytes 1572868
  4.5 15.2 %collective-permute-start.7 = (bf16[512,2048]{1,0:T(8,128)(2,1)S(1)}, bf16[512,2048]{1,0:T(8,128)(2,1)S(1)}, u32[]{:S(2)}, u32[]{:S(2)}) collective-permute-start(bf16[512,2048]{1,0:T(8,128)(2,1)S(1)} %get-tuple-element.24), channel_id=1, source_target_pairs={{0,8},{8,0},{16,24},{24,16},{1,9},{9,1},{17,25},{25,17},{2,10},{10... | collective-permute-start | bytes 6291464 | tf_op jit(solution)/shard_map/ppermute | solution.py:418
  5.0 7.9 %collective-permute-start = (bf16[64,512]{1,0:T(8,128)(2,1)S(1)}, bf16[64,512]{1,0:T(8,128)(2,1)S(1)}, u32[]{:S(2)}, u32[]{:S(2)}) collective-permute-start(bf16[64,512]{1,0:T(8,128)(2,1)S(1)} %get-tuple-element.20), channel_id=1, source_target_pairs={{0,4},{2,6},{4,0},{6,2},{1,5},{3,7},{5,1},{7,3},{8,12},{10,14},{12... | collective-permute-start | bytes 196616 | tf_op jit(solution)/shard_map/ppermute | solution.py:418
  8.7 6.7 %collective-permute-start.1 = (bf16[64,512]{1,0:T(8,128)(2,1)S(1)}, bf16[64,512]{1,0:T(8,128)(2,1)S(1)}, u32[]{:S(2)}, u32[]{:S(2)}) collective-permute-start(bf16[64,512]{1,0:T(8,128)(2,1)S(1)} %get-tuple-element.21), channel_id=1, source_target_pairs={{0,6},{2,4},{4,2},{6,0},{1,7},{3,5},{5,3},{7,1},{8,14},{10,12},{12... | collective-permute-start | bytes 196616 | tf_op jit(solution)/shard_map/ppermute | solution.py:418
  10.0 5.5 %collective-permute-start.2 = (bf16[64,512]{1,0:T(8,128)(2,1)S(1)}, bf16[64,512]{1,0:T(8,128)(2,1)S(1)}, u32[]{:S(2)}, u32[]{:S(2)}) collective-permute-start(bf16[64,512]{1,0:T(8,128)(2,1)S(1)} %get-tuple-element.22), channel_id=1, source_target_pairs={{0,2},{2,0},{4,6},{6,4},{1,3},{3,1},{5,7},{7,5},{8,10},{10,8},{12,... | collective-permute-start | bytes 196616 | tf_op jit(solution)/shard_map/ppermute | solution.py:418
  15.6 4.1 %collective-permute-start.6 = (bf16[64,512]{1,0:T(8,128)(2,1)S(1)}, bf16[64,512]{1,0:T(8,128)(2,1)S(1)}, u32[]{:S(2)}, u32[]{:S(2)}) collective-permute-start(bf16[64,512]{1,0:T(8,128)(2,1)S(1)} %ratio_chunk.1.ratio_ref.refs_0_), channel_id=1, source_target_pairs={{0,8},{8,0},{16,24},{24,16},{1,9},{9,1},{17,25},{25,17},{2,10},{10... | collective-permute-start | bytes 196616 | tf_op jit(solution)/shard_map/ppermute | solution.py:418
  15.6 7.2 %collective-permute-start.5 = (bf16[64,512]{1,0:T(8,128)(2,1)S(1)}, bf16[64,512]{1,0:T(8,128)(2,1)S(1)}, u32[]{:S(2)}, u32[]{:S(2)}) collective-permute-start(bf16[64,512]{1,0:T(8,128)(2,1)S(1)} %ratio_chunk.1.ratio_ref.refs_0_), channel_id=1, source_target_pairs={{0,4},{2,6},{4,0},{6,2},{1,5},{3,7},{5,1},{7,3},{8,12},{10,14},{12... | collective-permute-start | bytes 196616 | tf_op jit(solution)/shard_map/ppermute | solution.py:418
  18.5 6.2 %collective-permute-start.3 = (bf16[64,512]{1,0:T(8,128)(2,1)S(1)}, bf16[64,512]{1,0:T(8,128)(2,1)S(1)}, u32[]{:S(2)}, u32[]{:S(2)}) collective-permute-start(bf16[64,512]{1,0:T(8,128)(2,1)S(1)} %ratio_chunk.1.ratio_ref.refs_0_), channel_id=1, source_target_pairs={{0,6},{2,4},{4,2},{6,0},{1,7},{3,5},{5,3},{7,1},{8,14},{10,12},{12... | collective-permute-start | bytes 196616 | tf_op jit(solution)/shard_map/ppermute | solution.py:418
  20.2 8.4 %collective-permute-start.8 = (bf16[64,2048]{1,0:T(8,128)(2,1)S(1)}, bf16[64,2048]{1,0:T(8,128)(2,1)S(1)}, u32[]{:S(2)}, u32[]{:S(2)}) collective-permute-start(bf16[64,2048]{1,0:T(8,128)(2,1)S(1)} %beta_pieces.3.own_ref), channel_id=1, source_target_pairs={{0,16},{8,24},{16,0},{24,8},{1,17},{9,25},{17,1},{25,9},{2,18},{10... | collective-permute-start | bytes 786440 | tf_op jit(solution)/shard_map/ppermute | solution.py:418
  21.7 4.3 %collective-permute-start.4 = (bf16[64,512]{1,0:T(8,128)(2,1)S(1)}, bf16[64,512]{1,0:T(8,128)(2,1)S(1)}, u32[]{:S(2)}, u32[]{:S(2)}) collective-permute-start(bf16[64,512]{1,0:T(8,128)(2,1)S(1)} %ratio_chunk.1.ratio_ref.refs_0_), channel_id=1, source_target_pairs={{0,2},{2,0},{4,6},{6,4},{1,3},{3,1},{5,7},{7,5},{8,10},{10,8},{12,... | collective-permute-start | bytes 196616 | tf_op jit(solution)/shard_map/ppermute | solution.py:418
  22.9 14.9 %collective-permute-start.11 = (bf16[128,2048]{1,0:T(8,128)(2,1)S(1)}, bf16[128,2048]{1,0:T(8,128)(2,1)S(1)}, u32[]{:S(2)}, u32[]{:S(2)}) collective-permute-start(bf16[128,2048]{1,0:T(8,128)(2,1)S(1)} %hold.1), channel_id=1, source_target_pairs={{0,1},{1,0},{2,3},{3,2},{4,5},{5,4},{6,7},{7,6},{8,9},{9,8},{10,11... | collective-permute-start | bytes 1572872 | tf_op jit(solution)/shard_map/ppermute | solution.py:414
  24.6 1.9 %collective-permute-start.12 = (bf16[64,512]{1,0:T(8,128)(2,1)S(1)}, bf16[64,512]{1,0:T(8,128)(2,1)S(1)}, u32[]{:S(2)}, u32[]{:S(2)}) collective-permute-start(bf16[64,512]{1,0:T(8,128)(2,1)S(1)} %collective-permute-done.5.refs_3_.rest_0_.refs_0_), channel_id=1, source_target_pairs={{0,8},{8,0},{16,24},{24,16},{1,9},{9,1},{17,25},{25,17},{2,10},{10... | collective-permute-start | bytes 196616 | tf_op jit(solution)/shard_map/ppermute | solution.py:418
  24.6 1.9 %collective-permute-start.13 = (bf16[64,512]{1,0:T(8,128)(2,1)S(1)}, bf16[64,512]{1,0:T(8,128)(2,1)S(1)}, u32[]{:S(2)}, u32[]{:S(2)}) collective-permute-start(bf16[64,512]{1,0:T(8,128)(2,1)S(1)} %collective-permute-done.3.refs_1_), channel_id=1, source_target_pairs={{0,8},{8,0},{16,24},{24,16},{1,9},{9,1},{17,25},{25,17},{2,10},{10... | collective-permute-start | bytes 196616 | tf_op jit(solution)/shard_map/ppermute | solution.py:418
  26.0 2.9 %collective-permute-start.9 = (bf16[64,512]{1,0:T(8,128)(2,1)S(1)}, bf16[64,512]{1,0:T(8,128)(2,1)S(1)}, u32[]{:S(2)}, u32[]{:S(2)}) collective-permute-start(bf16[64,512]{1,0:T(8,128)(2,1)S(1)} %collective-permute-done.4.ratio_ref.refs_2_), channel_id=1, source_target_pairs={{0,8},{8,0},{16,24},{24,16},{1,9},{9,1},{17,25},{25,17},{2,10},{10... | collective-permute-start | bytes 196616 | tf_op jit(solution)/shard_map/ppermute | solution.py:418
  27.0 18.7 %collective-permute-start.17 = (bf16[128,2048]{1,0:T(8,128)(2,1)S(1)}, bf16[128,2048]{1,0:T(8,128)(2,1)S(1)}, u32[]{:S(2)}, u32[]{:S(2)}) collective-permute-start(bf16[128,2048]{1,0:T(8,128)(2,1)S(1)} %beta_pieces.5.rest_0_.own_ref), channel_id=1, source_target_pairs={{0,16},{8,24},{16,0},{24,8},{1,17},{9,25},{17,1},{25,9},{2,18},{10... | collective-permute-start | bytes 1572872 | tf_op jit(solution)/shard_map/ppermute | solution.py:418
  28.6 9.9 %collective-permute-start.16 = (bf16[64,2048]{1,0:T(8,128)(2,1)S(1)}, bf16[64,2048]{1,0:T(8,128)(2,1)S(1)}, u32[]{:S(2)}, u32[]{:S(2)}) collective-permute-start(bf16[64,2048]{1,0:T(8,128)(2,1)S(1)} %add_pair.3.refs_4_.refs_0_), channel_id=1, source_target_pairs={{0,8},{8,0},{16,24},{24,16},{1,9},{9,1},{17,25},{25,17},{2,10},{10... | collective-permute-start | bytes 786440 | tf_op jit(solution)/shard_map/ppermute | solution.py:418
  29.4 12.4 %collective-permute-start.10 = (bf16[256,512]{1,0:T(8,128)(2,1)S(1)}, bf16[256,512]{1,0:T(8,128)(2,1)S(1)}, u32[]{:S(2)}, u32[]{:S(2)}) collective-permute-start(bf16[256,512]{1,0:T(8,128)(2,1)S(1)} %join_ratio.1.refs_0_), channel_id=1, source_target_pairs={{0,1},{1,0},{2,3},{3,2},{4,5},{5,4},{6,7},{7,6},{8,9},{9,8},{10,11... | collective-permute-start | bytes 786440 | tf_op jit(solution)/shard_map/ppermute | solution.py:414
  37.9 4.2 %collective-permute-start.14 = (bf16[64,2048]{1,0:T(8,128)(2,1)S(1)}, bf16[64,2048]{1,0:T(8,128)(2,1)S(1)}, u32[]{:S(2)}, u32[]{:S(2)}) collective-permute-start(bf16[64,2048]{1,0:T(8,128)(2,1)S(1)} %get-tuple-element.29.refs_3_), channel_id=1, source_target_pairs={{0,8},{8,0},{16,24},{24,16},{1,9},{9,1},{17,25},{25,17},{2,10},{10... | collective-permute-start | bytes 786440 | tf_op jit(solution)/shard_map/ppermute | solution.py:418
  38.0 4.1 %collective-permute-start.15 = (bf16[64,2048]{1,0:T(8,128)(2,1)S(1)}, bf16[64,2048]{1,0:T(8,128)(2,1)S(1)}, u32[]{:S(2)}, u32[]{:S(2)}) collective-permute-start(bf16[64,2048]{1,0:T(8,128)(2,1)S(1)} %get-tuple-element.30.refs_4_), channel_id=1, source_target_pairs={{0,8},{8,0},{16,24},{24,16},{1,9},{9,1},{17,25},{25,17},{2,10},{10... | collective-permute-start | bytes 786440 | tf_op jit(solution)/shard_map/ppermute | solution.py:418
  38.5 8.6 %collective-permute-start.18 = (bf16[64,2048]{1,0:T(8,128)(2,1)S(1)}, bf16[64,2048]{1,0:T(8,128)(2,1)S(1)}, u32[]{:S(2)}, u32[]{:S(2)}) collective-permute-start(bf16[64,2048]{1,0:T(8,128)(2,1)S(1)} %beta_pieces.4.refs_5_.own_ref), channel_id=1, source_target_pairs={{0,16},{8,24},{16,0},{24,8},{1,17},{9,25},{17,1},{25,9},{2,18},{10... | collective-permute-start | bytes 786440 | tf_op jit(solution)/shard_map/ppermute | solution.py:418
  45.9 2.9 %collective-permute-start.19 = (bf16[128,2048]{1,0:T(8,128)(2,1)S(1)}, bf16[128,2048]{1,0:T(8,128)(2,1)S(1)}, u32[]{:S(2)}, u32[]{:S(2)}) collective-permute-start(bf16[128,2048]{1,0:T(8,128)(2,1)S(1)} %add_pair.4.refs_0_), channel_id=1, source_target_pairs={{0,8},{8,0},{16,24},{24,16},{1,9},{9,1},{17,25},{25,17},{2,10},{10... | collective-permute-start | bytes 1572872 | tf_op jit(solution)/shard_map/ppermute | solution.py:418
  47.1 1.6 %collective-permute-start.20 = (bf16[64,2048]{1,0:T(8,128)(2,1)S(1)}, bf16[64,2048]{1,0:T(8,128)(2,1)S(1)}, u32[]{:S(2)}, u32[]{:S(2)}) collective-permute-start(bf16[64,2048]{1,0:T(8,128)(2,1)S(1)} %add_pair.5.refs_1_), channel_id=1, source_target_pairs={{0,8},{8,0},{16,24},{24,16},{1,9},{9,1},{17,25},{25,17},{2,10},{10... | collective-permute-start | bytes 786440 | tf_op jit(solution)/shard_map/ppermute | solution.py:418
